TPU v7x, 32 devices: a whole 2x2x4 slice. The times are simulated.
32 devices in a mesh: dp: 16 (over z, x, core), space: 2 (over y).
Axes of the slice: x: 2, y: 2, z: 4, core: 2. Of those that a mesh axis runs over, the one named last changes fastest.
Arguments:
- fields: bfloat16 [16, 126, 252, 192], P('dp', 'space'), may hold values from -6 to 6
- cotangent: bfloat16 [16, 126, 252, 192], P('dp', 'space'), may hold values from -1.796875 to 1.796875
- spec_real: bfloat16 [126, 192], replicated, may hold values from -4.1875 to 4.1875
- spec_imag: bfloat16 [126, 192], replicated, may hold values from -4.1875 to 4.1875
Outputs:
- grad_real: float32 [126, 192], replicated
- grad_imag: float32 [126, 192], replicated
All inputs are finite; a program needn't handle non-finite values.
Results may differ from a plain program's by a relative error of at most 0.015.
Values may be sent and summed in bfloat16 or wider, within the bound.
No kernel may reach another device: no remote copies, remote signals or barrier semaphores. Data moves between devices by JAX's collectives and lax.ppermute only.
A program may use at most 128 MiB of HBM per device.

v0:
```python
import math

import jax
import jax.numpy as jnp
from jax import lax
from jax.sharding import PartitionSpec as P

NLAT = 126
NLON = 252
MODES = 126


def grid_tables():
    latitude = jnp.arange(NLAT, dtype=jnp.float32)
    colatitude = math.pi * (latitude + 0.5) / NLAT
    sin_theta = jnp.sin(colatitude)
    quad_weight = math.pi / NLAT * (2.0 * math.pi / NLON) * sin_theta
    return (jnp.cos(colatitude), sin_theta, quad_weight)


def fourier_tables(orders):
    longitude = jnp.arange(NLON, dtype=jnp.int32)
    phase_index = orders[:, None] * longitude[None, :] % NLON
    angles = 2.0 * math.pi / NLON * phase_index.astype(jnp.float32)
    basis_rows = jnp.stack([jnp.cos(angles), -jnp.sin(angles)], axis=1)
    factor = jnp.where(orders == 0, 1.0, 2.0).astype(jnp.float32)
    return (
        basis_rows.astype(jnp.bfloat16),
        (basis_rows * factor[:, None, None]).astype(jnp.bfloat16),
    )


def legendre(orders, cos_theta, sin_theta):
    counters = jnp.arange(1, MODES, dtype=jnp.float32)
    log_steps = 0.5 * jnp.log((2.0 * counters + 1.0) / (2.0 * counters))
    log_table = jnp.concatenate([jnp.zeros((1,), jnp.float32), jnp.cumsum(log_steps)])
    order_float = orders.astype(jnp.float32)[:, None]
    log_diagonal = (
        0.5 * jnp.log(1.0 / (4.0 * math.pi))
        + log_table[orders][:, None]
        + order_float * jnp.log(sin_theta)[None, :]
    )
    diagonal_start = jnp.exp(log_diagonal)
    cos_row = cos_theta[None, :]

    def advance(state_pair, degree):
        previous, earlier = state_pair
        degree_float = degree.astype(jnp.float32)
        growth = jnp.sqrt(
            jnp.maximum(4.0 * degree_float * degree_float - 1.0, 0.0)
            / jnp.maximum(degree_float * degree_float - order_float * order_float, 1.0)
        )
        below = degree_float - 1.0
        damping = jnp.sqrt(
            jnp.maximum(below * below - order_float * order_float, 0.0)
            / jnp.maximum(4.0 * below * below - 1.0, 1.0)
        )
        recurrence = growth * (cos_row * previous - damping * earlier)
        current = jnp.where(
            degree_float == order_float,
            diagonal_start,
            jnp.where(degree_float > order_float, recurrence, 0.0),
        )
        return ((current, previous), current)

    empty_rows = jnp.zeros_like(diagonal_start)
    final_state, stacked = lax.scan(
        advance, (empty_rows, empty_rows), jnp.arange(MODES, dtype=jnp.int32), unroll=6
    )
    return jnp.swapaxes(stacked, 0, 1)


def gelu_slope(values):
    cumulative = 0.5 * (1.0 + lax.erf(values / math.sqrt(2.0)))
    density = jnp.exp(-0.5 * values * values) / math.sqrt(2.0 * math.pi)
    return cumulative + values * density


def block_analysis(tables, coeffs):
    return jnp.einsum("qlj,sqjc->sqlc", tables, coeffs, preferred_element_type=jnp.float32)


def block_synthesis(tables, spectral):
    return jnp.einsum("qlj,sqlc->sqjc", tables, spectral, preferred_element_type=jnp.float32)


def apply_filter(spectral, real_rows, imag_rows):
    channels = real_rows.shape[-1]
    spec_values = spectral.astype(jnp.float32)
    real_part = spec_values[..., :channels]
    imag_part = spec_values[..., channels:]
    return jnp.concatenate(
        [
            real_part * real_rows - imag_part * imag_rows,
            real_part * imag_rows + imag_part * real_rows,
        ],
        axis=-1,
    ).astype(jnp.bfloat16)


def row_products(spectral, back_spectral):
    channels = spectral.shape[-1] // 2
    spec_values = spectral.astype(jnp.float32)
    back_values = back_spectral.astype(jnp.float32)
    real_term = (
        spec_values[..., :channels] * back_values[..., :channels]
        + spec_values[..., channels:] * back_values[..., channels:]
    )
    imag_term = (
        spec_values[..., :channels] * back_values[..., channels:]
        - spec_values[..., channels:] * back_values[..., :channels]
    )
    return (real_term, imag_term)


def grid_to_modes(grid_values, basis):
    cosine_part = jnp.einsum(
        "salc,ml->smac", grid_values, basis[:, 0], preferred_element_type=jnp.float32
    ).astype(jnp.bfloat16)
    sine_part = jnp.einsum(
        "salc,ml->smac", grid_values, basis[:, 1], preferred_element_type=jnp.float32
    ).astype(jnp.bfloat16)
    return jnp.concatenate([cosine_part, sine_part], axis=-1)


def modes_to_grid(mode_values, basis):
    channels = mode_values.shape[-1] // 2
    cosine_part = jnp.einsum(
        "smac,ml->salc",
        mode_values[..., :channels],
        basis[:, 0],
        preferred_element_type=jnp.float32,
    )
    sine_part = jnp.einsum(
        "smac,ml->salc",
        mode_values[..., channels:],
        basis[:, 1],
        preferred_element_type=jnp.float32,
    )
    return cosine_part + sine_part


def to_orders(grid_coeffs):
    return lax.all_to_all(grid_coeffs, "space", split_axis=1, concat_axis=2, tiled=True)


def on_device(fields, cotangent, spec_real, spec_imag):
    space_parts = lax.axis_size("space")
    band_index = lax.axis_index("space")
    slot_count = MODES // space_parts
    positions = jnp.arange(MODES, dtype=jnp.int32)
    slot_range = jnp.arange(slot_count, dtype=jnp.int32)
    local_orders = band_index * slot_count + slot_range
    forward_basis, inverse_basis = fourier_tables(positions)
    cos_theta, sin_theta, quad_weight = grid_tables()
    associated = legendre(local_orders, cos_theta, sin_theta)
    weighted = (associated * quad_weight[None, None, :]).astype(jnp.bfloat16)
    plain = associated.astype(jnp.bfloat16)
    real_rows = spec_real.astype(jnp.float32)
    imag_rows = spec_imag.astype(jnp.float32)

    def degree_sums(term):
        return jnp.sum(term, axis=(0, 1))

    coeffs = grid_to_modes(fields, forward_basis)
    by_order = to_orders(coeffs)
    spectral = block_analysis(weighted, by_order).astype(jnp.bfloat16)
    mixed = apply_filter(spectral, real_rows, imag_rows)
    synthesized = block_synthesis(plain, mixed).astype(jnp.bfloat16)
    by_band = lax.all_to_all(synthesized, "space", split_axis=2, concat_axis=1, tiled=True)
    signal = modes_to_grid(by_band, inverse_basis)
    upstream = (cotangent.astype(jnp.float32) * gelu_slope(signal)).astype(jnp.bfloat16)
    back_coeffs = grid_to_modes(upstream, inverse_basis)
    back_order = to_orders(back_coeffs)
    back_spectral = block_analysis(plain, back_order).astype(jnp.bfloat16)
    real_term, imag_term = row_products(spectral, back_spectral)
    part_real = degree_sums(real_term)
    part_imag = degree_sums(imag_term)
    summed_real, summed_imag = lax.psum((part_real, part_imag), ("dp", "space"))
    batch_total = fields.shape[0] * lax.axis_size("dp")
    return (summed_real / batch_total, summed_imag / batch_total)


def solution(mesh):
    in_specs = (P("dp", "space", None, None), P("dp", "space", None, None), P(), P())
    out_specs = (P(), P())
    return jax.shard_map(
        on_device, mesh=mesh, in_specs=in_specs, out_specs=out_specs, check_vma=False
    )
```

profile of v0, /device:TPU:0, one launch (start us, length us, event | category | flops | bytes accessed | tf_op | source)
XLA Modules:
  0.0 592.6 jit_solution(1087648713569418819)
XLA Ops:
  7.8 4.7 fusion.57
  12.5 1.8 fusion.58
  15.4 4.5 pad_maximum_fusion
  19.9 9.0 %copy.23 = bf16[1,126,63,384]{3,2,0,1:T(8,128)(2,1)} copy(bf16[1,126,63,384]{1,3,2,0:T(8,128)(2,1)} %pad_maximum_fusion) | data formatting | bytes 12192768 | tf_op jit(solution)/shard_map/concatenate | solution.py:123
  28.9 6.3 %all-to-all-start = ((bf16[1,126,63,384]{3,2,0,1:T(8,128)(2,1)}), bf16[1,126,63,384]{3,2,0,1:T(8,128)(2,1)}, u32[]{:S(2)}, u32[]{:S(2)}) async-start(bf16[1,126,63,384]{3,2,0,1:T(8,128)(2,1)} %copy.23), calls=%async_computation | async-start | bytes 12386304 | tf_op jit(solution)/shard_map/all_to_all | solution.py:144
  35.8 0.8 gather_fusion
  36.6 140.8 %while.21 = (s32[]{:T(128)}, f32[63,126]{1,0:T(8,128)S(1)}, f32[63,126]{1,0:T(8,128)S(1)}, f32[21,6,63,126]{3,2,1,0:T(8,128)}, s32[21,6]{0,1:T(8,128)S(1)}, /*in...) while((s32[]{:T(128)}, f32[63,126]{1,0:T(8,128)S(1)}, ...), condition=%wide.region_2.3_spmd.clone.clone.clone.clone, body=%wide.region_1.2_spmd.clone.clone.clone.clone.sunk | while | flops 894296 | bytes 1152597 | solution.py:67
  37.1 0.6 fusion.78
  43.0 0.7 bitcast_dynamic-update-slice_fusion.20
  43.8 0.6 fusion.78
  49.7 0.7 bitcast_dynamic-update-slice_fusion.20
  50.5 0.6 fusion.78
  56.4 0.7 bitcast_dynamic-update-slice_fusion.20
  57.2 0.6 fusion.78
  63.1 0.7 bitcast_dynamic-update-slice_fusion.20
  63.9 0.6 fusion.78
  69.8 0.7 bitcast_dynamic-update-slice_fusion.20
  70.6 0.6 fusion.78
  76.5 0.7 bitcast_dynamic-update-slice_fusion.20
  77.3 0.6 fusion.78
  83.1 0.7 bitcast_dynamic-update-slice_fusion.20
  83.9 0.6 fusion.78
  89.8 0.7 bitcast_dynamic-update-slice_fusion.20
  90.6 0.6 fusion.78
  96.5 0.7 bitcast_dynamic-update-slice_fusion.20
  97.3 0.6 fusion.78
  103.2 0.7 bitcast_dynamic-update-slice_fusion.20
  104.0 0.6 fusion.78
  109.8 0.7 bitcast_dynamic-update-slice_fusion.20
  116.5 0.7 bitcast_dynamic-update-slice_fusion.20
  123.2 0.7 bitcast_dynamic-update-slice_fusion.20
  129.9 0.7 bitcast_dynamic-update-slice_fusion.20
  136.6 0.7 bitcast_dynamic-update-slice_fusion.20
  143.2 0.7 bitcast_dynamic-update-slice_fusion.20
  149.9 0.7 bitcast_dynamic-update-slice_fusion.20
  156.6 0.7 bitcast_dynamic-update-slice_fusion.20
  163.3 0.7 bitcast_dynamic-update-slice_fusion.20
  169.9 0.7 bitcast_dynamic-update-slice_fusion.20
  176.6 0.7 bitcast_dynamic-update-slice_fusion.20
  177.4 6.6 %copy.24 = bf16[1,63,2,63,384]{4,1,3,2,0:T(8,128)(2,1)S(1)} copy(bf16[1,63,2,63,384]{4,3,1,2,0:T(8,128)(2,1)} %bitcast.12) | data formatting | bytes 12192768 | tf_op jit(solution)/shard_map/all_to_all | solution.py:144
  184.0 13.7 %convert_bitcast_fusion.1 = f32[1,63,126,384]{2,3,1,0:T(8,128)} fusion(bf16[63,126,384]{2,0,1:T(8,128)(2,1)S(1)} %bitcast.243, f32[126,63,126]{2,1,0:T(8,128)S(1)} %bitcast.247, f32[126]{0:T(128)S(1)} %broadcast_multiply_fusion.2), kind=kOutput, calls=%fused_computation.63 | convolution fusion | flops 776241152 | bytes 22290408 | tf_op jit(solution)/shard_map/qlj,sqjc->sqlc/dot_general | solution.py:80
  197.8 7.3 %fusion.40 = (bf16[63,126,192]{1,2,0:T(8,128)(2,1)}, bf16[63,126,192]{1,2,0:T(8,128)(2,1)}) fusion(f32[1,63,126,384]{2,3,1,0:T(8,128)} %convert_bitcast_fusion.1, f32[126,192]{0,1:T(8,128)S(1)} %convert_element_type.205, f32[126,192]{0,1:T(8,128)S(1)} %convert_element_type.204), kind=kLoop, calls=%fused_computation.81 | loop fusion | flops 12192768 | bytes 18482688 | tf_op jit(solution)/shard_map/concatenate | solution.py:92
  205.1 8.9 %convert_bitcast_fusion.2 = bf16[1,63,126,384]{2,3,1,0:T(8,128)(2,1)} fusion(bf16[63,126,192]{1,2,0:T(8,128)(2,1)} %get-tuple-element.358, bf16[63,126,192]{1,2,0:T(8,128)(2,1)} %get-tuple-element.357, f32[126,63,126]{2,1,0:T(8,128)S(1)} %bitcast.248), kind=kOutput, calls=%fused_computation.76 | convolution fusion | flops 783385344 | bytes 16193520 | tf_op jit(solution)/shard_map/qlj,sqlc->sqjc/dot_general | solution.py:84
  214.0 9.0 %copy.28 = bf16[1,63,126,384]{3,1,0,2:T(8,128)(2,1)} copy(bf16[1,63,126,384]{2,3,1,0:T(8,128)(2,1)} %convert_bitcast_fusion.2) | data formatting | bytes 12192768 | tf_op jit(solution)/shard_map/convert_element_type | solution.py:169
  223.0 6.2 %all-to-all-start.1 = ((bf16[1,63,126,384]{3,1,0,2:T(8,128)(2,1)}), bf16[1,63,126,384]{3,1,0,2:T(8,128)(2,1)}, u32[]{:S(2)}, u32[]{:S(2)}) async-start(bf16[1,63,126,384]{3,1,0,2:T(8,128)(2,1)} %copy.28), calls=%async_computation.1 | async-start | bytes 12386304 | tf_op jit(solution)/shard_map/all_to_all | solution.py:170
  229.4 70.1 %all-to-all-done.1 = bf16[1,63,126,384]{3,1,0,2:T(8,128)(2,1)} async-done(((bf16[1,63,126,384]{3,1,0,2:T(8,128)(2,1)}), bf16[1,63,126,384]{3,1,0,2:T(8,128)(2,1)}, u32[]{:S(2)}, u32[]{:S(2)}) %all-to-all-start.1) | async-done | bytes 6096416 | tf_op jit(solution)/shard_map/all_to_all | solution.py:170
  299.4 6.4 %copy.29 = bf16[1,2,63,63,384]{4,3,2,1,0:T(8,128)(2,1)S(1)} copy(bf16[1,2,63,63,384]{4,2,3,1,0:T(8,128)(2,1)} %bitcast.27) | data formatting | bytes 12192768 | tf_op jit(solution)/shard_map/all_to_all | solution.py:170
  305.9 4.7 fusion.70
  310.6 8.5 %copy.36 = bf16[1,126,63,192]{1,3,2,0:T(8,128)(2,1)S(1)} copy(bf16[1,126,63,192]{3,2,1,0:T(8,128)(2,1)} %get-tuple-element.359) | data formatting | bytes 6096384
  319.1 6.8 %copy.35 = bf16[1,126,63,192]{1,3,2,0:T(8,128)(2,1)} copy(bf16[1,126,63,192]{3,2,1,0:T(8,128)(2,1)} %get-tuple-element.360) | data formatting | bytes 6096384
  325.9 3.6 fusion.60
  329.5 1.7 fusion.62
  331.3 8.2 %fusion.22 = bf16[1,63,252,192]{2,3,1,0:T(8,128)(2,1)S(1)} fusion(f32[252,63,192]{0,2,1:T(8,128)S(1)} %bitcast.231, f32[252,63,192]{0,2,1:T(8,128)S(1)} %bitcast.232, bf16[1,63,252,192]{2,3,1,0:T(8,128)(2,1)} %param.7), kind=kLoop, calls=%fused_computation.57 | loop fusion | flops 36578304 | bytes 36578304 | tf_op jit(solution)/shard_map/convert_element_type | solution.py:172
  339.5 1.8 fusion.61
  341.2 1.8 fusion.59
  344.1 4.4 pad_maximum_fusion.1
  348.6 9.0 %copy.32 = bf16[1,126,63,384]{3,2,0,1:T(8,128)(2,1)} copy(bf16[1,126,63,384]{1,3,2,0:T(8,128)(2,1)} %pad_maximum_fusion.1) | data formatting | bytes 12192768 | tf_op jit(solution)/shard_map/concatenate | solution.py:123
  357.6 73.1 %all_to_all.48 = bf16[1,126,63,384]{3,2,0,1:T(8,128)(2,1)S(1)} all-to-all(bf16[1,126,63,384]{3,2,0,1:T(8,128)(2,1)} %copy.32), channel_id=1, replica_groups=mesh['dp'=16,'space'=2] {'space'}, dimensions={1} | all-to-all | bytes 12192768 | tf_op jit(solution)/shard_map/all_to_all | solution.py:144
  430.6 3.7 copy.33
  434.4 13.6 %convert_bitcast_fusion = f32[1,63,126,384]{2,3,1,0:T(8,128)} fusion(bf16[63,126,384]{2,0,1:T(8,128)(2,1)S(1)} %bitcast.244, f32[126,63,126]{2,1,0:T(8,128)S(1)} %bitcast.249), kind=kOutput, calls=%fused_computation.58 | convolution fusion | flops 774240768 | bytes 22289904 | tf_op jit(solution)/shard_map/qlj,sqjc->sqlc/dot_general | solution.py:80
  448.0 10.4 %subtract_reduce_fusion = (f32[126,192]{0,1:T(8,128)}, f32[126,192]{0,1:T(8,128)}) fusion(f32[1,63,126,384]{2,3,1,0:T(8,128)} %convert_bitcast_fusion, f32[1,63,126,384]{2,3,1,0:T(8,128)} %convert_bitcast_fusion.1), kind=kLoop, calls=%fused_computation.74 | loop fusion | flops 12144384 | bytes 24579072 | tf_op jit(solution)/shard_map/reduce_sum | solution.py:163
  458.4 123.8 %all-reduce.3.cloned.1.call-done = (f32[126,192]{0,1:T(8,128)}, f32[126,192]{0,1:T(8,128)}) async-done(((f32[126,192]{0,1:T(8,128)}, f32[126,192]{0,1:T(8,128)}), (f32[126,192]{0,1:T(8,128)}, f32[126,192]{0,1:T(8,128)})) %all-reduce.3.cloned.1.call-update) | async-done | bytes 193552 | tf_op jit(solution)/shard_map/psum | solution.py:179
  582.2 1.5 broadcast_multiply_fusion.1
  583.8 1.5 broadcast_multiply_fusion
  (470 shorter events, 37.5 us)
Async XLA Ops:
  7.7 4.7 slice-start
  7.8 4.7 slice-start.1
  28.9 148.5 %all-to-all-start = ((bf16[1,126,63,384]{3,2,0,1:T(8,128)(2,1)}), bf16[1,126,63,384]{3,2,0,1:T(8,128)(2,1)}, u32[]{:S(2)}, u32[]{:S(2)}) async-start(bf16[1,126,63,384]{3,2,0,1:T(8,128)(2,1)} %copy.23), calls=%async_computation | async-start | bytes 12386304 | tf_op jit(solution)/shard_map/all_to_all | solution.py:144
  35.2 142.1 %copy-start.2 = (bf16[126,192]{0,1:T(8,128)(2,1)S(1)}, bf16[126,192]{0,1:T(8,128)(2,1)}, u32[]{:S(2)}) copy-start(bf16[126,192]{0,1:T(8,128)(2,1)} %param.8) | copy-start | bytes 145156
  35.2 142.1 %copy-start.3 = (bf16[126,192]{0,1:T(8,128)(2,1)S(1)}, bf16[126,192]{0,1:T(8,128)(2,1)}, u32[]{:S(2)}) copy-start(bf16[126,192]{0,1:T(8,128)(2,1)} %param.9) | copy-start | bytes 145156
  177.4 6.6 %copy-start = (f32[21,6,63,126]{3,2,1,0:T(8,128)S(1)}, f32[21,6,63,126]{3,2,1,0:T(8,128)}, u32[]{:S(2)}) copy-start(f32[21,6,63,126]{3,2,1,0:T(8,128)} %get-tuple-element.177) | copy-start | bytes 12002260
  223.0 76.5 %all-to-all-start.1 = ((bf16[1,63,126,384]{3,1,0,2:T(8,128)(2,1)}), bf16[1,63,126,384]{3,1,0,2:T(8,128)(2,1)}, u32[]{:S(2)}, u32[]{:S(2)}) async-start(bf16[1,63,126,384]{3,1,0,2:T(8,128)(2,1)} %copy.28), calls=%async_computation.1 | async-start | bytes 12386304 | tf_op jit(solution)/shard_map/all_to_all | solution.py:170
  229.2 353.0 %all-reduce.3.cloned.1.call-start = ((), (), s32[]{:S(2)}) async-start(), calls=%async_computation.3 | async-start | bytes 393216 | tf_op jit(solution)/shard_map/psum | solution.py:179
  430.6 3.7 copy-start.1
Sparse Core Ops, SparseCore 0:
  458.5 123.6 all-reduce.2
where the time goes:
time: 601 us; the launch traced here: 593 us
  waiting for transfers between devices  194 us (32%)
  local copies, waits for them, and re-layouts  93.5 us (16%)
  loops' own time  85.5 us (14%)
  blocking collectives  73.1 us (12%)
  other arithmetic  67.6 us (11%)
  matrix products  51.6 us (9%)
  between operations  14.8 us (2%)
  starting transfers between devices  12.6 us (2%)
    psum x1, waiting for transfers between devices, on_device(): summed_real, summed_imag = lax.psum((part_real, part_imag), ('dp', 'space'))  124 us
    another operation x1, loops' own time, legendre(): lax.scan(advance, (empty_rows, empty_rows), jnp.arange(MODES, dtype=jnp.i...  85.5 us
    all_to_all x1, blocking collectives, to_orders(): lax.all_to_all(grid_coeffs, 'space', split_axis=1, concat_axis=2, tiled=T...  73.1 us
    all_to_all x1, waiting for transfers between devices, on_device(): lax.all_to_all(synthesized, 'space', split_axis=2, concat_axis=1, tiled=T...  70.1 us
    dot_general x2, matrix products, block_analysis(): jnp.einsum('qlj,sqjc->sqlc', tables, coeffs, preferred_element_type=jnp.f...  27.4 us
    while x105, other arithmetic  19.2 us
    concatenate x2, local copies, waits for them, and re-layouts, grid_to_modes(): return jnp.concatenate([cosine_part, sine_part], axis=-1)  18 us
    unnamed x14, local copies, waits for them, and re-layouts  15.4 us
  transfers between devices with their start and end apart: 3, of which 2 were waited for; matrix products, arithmetic and copies ran while one was open for 10% of the time, Pallas kernels for 0%

commit v1 on v0

v1 whole, which is shorter than its diff:
```python
import functools
import math

import jax
import jax.numpy as jnp
import ml_dtypes
import numpy as np
from jax import lax
from jax.experimental import pallas as pl
from jax.experimental.pallas import tpu as pltpu
from jax.sharding import PartitionSpec as P

NLAT = 126
NLON = 252
MODES = 126
LANES = 128
GROUP = 16
PAIRS = 8
VMEM = 56 * 1024 * 1024


def round_up(value, step):
    return -(-value // step) * step


def legendre_table():
    colatitude = math.pi * (np.arange(NLAT) + 0.5) / NLAT
    cos_theta, sin_theta = np.cos(colatitude), np.sin(colatitude)
    counters = np.arange(1, MODES)
    log_steps = 0.5 * np.log((2.0 * counters + 1.0) / (2.0 * counters))
    log_table = np.concatenate([[0.0], np.cumsum(log_steps)])
    table = np.zeros((MODES, MODES, NLAT))
    for order in range(MODES):
        table[order, order] = np.exp(
            0.5 * math.log(1.0 / (4.0 * math.pi)) + log_table[order] + order * np.log(sin_theta)
        )
        for degree in range(order + 1, MODES):
            growth = math.sqrt((4.0 * degree**2 - 1.0) / (degree**2 - order**2))
            below = degree - 1
            current = cos_theta * table[order, below]
            if below > order:
                damping = math.sqrt((below**2 - order**2) / (4.0 * below**2 - 1.0))
                current = current - damping * table[order, degree - 2]
            table[order, degree] = growth * current
    weight = math.pi / NLAT * (2.0 * math.pi / NLON) * sin_theta
    return table, table * weight


def to_bf16(array):
    return np.where(np.abs(array) < 2.0**-126, 0.0, array).astype(ml_dtypes.bfloat16)


class Layout:
    def __init__(self, parts, local):
        self.parts, self.local = parts, local
        self.rows = round_up(local + 1, 16)
        self.half = self.rows // 2
        self.low = max(MODES - local, 0)
        high = MODES - self.low
        self.pairs = (high + 1) // 2
        self.blocks = self.low + self.pairs
        self.slots = round_up(self.low + 2 * self.pairs, 8)
        self.degrees = round_up(MODES, 16)
        self.first_natural = self.rows - MODES + self.low
        self.partner = MODES - 1 + self.low
        orders = list(range(self.low))
        for pair in range(self.pairs):
            order = self.low + pair
            orders += [order, self.partner - order if self.partner - order != order else -1]
        self.orders = np.array(orders + [-1] * (self.slots - len(orders)))


@functools.lru_cache(maxsize=None)
def fourier_constants(parts, local):
    layout = Layout(parts, local)
    orders = np.maximum(layout.orders, 0)
    angles = 2.0 * math.pi / NLON * (orders[:, None] * np.arange(NLON)[None] % NLON)
    live = (layout.orders >= 0)[:, None]
    basis = np.concatenate([np.cos(angles) * live, -np.sin(angles) * live])
    factor = np.where(layout.orders == 0, 1.0, 2.0)[:, None]
    inverse = basis * np.concatenate([factor, factor])
    return to_bf16(basis), to_bf16(inverse), to_bf16(inverse.T)


@functools.lru_cache(maxsize=None)
def legendre_constants(parts, local):
    layout = Layout(parts, local)
    plain, weighted = legendre_table()
    rows, degrees, low, pairs = layout.rows, layout.degrees, layout.low, layout.pairs
    analysis = np.zeros((low, 2 * parts * rows, degrees))
    synth_low = np.zeros((low, parts * rows, degrees))
    pair_fwd = np.zeros((parts, pairs, rows, 2 * rows))
    pair_back = np.zeros((parts, pairs, rows, 2 * rows))
    for part in range(parts):
        own = slice(part * local, (part + 1) * local)
        start = part * rows
        synth_low[:, start : start + local, :MODES] = np.swapaxes(plain[:low, :, own], 1, 2)
        for turn in (1, 2):
            start = (turn * parts - 1 - part) * rows
            analysis[:, start : start + local, :MODES] = np.swapaxes(weighted[:low, :, own], 1, 2)
        for pair in range(pairs):
            order = low + pair
            mate = layout.partner - order
            for target, table in ((pair_fwd, weighted), (pair_back, plain)):
                count = MODES - order
                target[part, pair, rows - count :, :local] = table[order, order:, own]
                if mate != order:
                    count = MODES - mate
                    target[part, pair, :count, rows : rows + local] = table[mate, mate:, own][::-1]
    place = np.zeros((degrees, 2 * rows))
    for row in range(rows):
        if row >= rows - MODES + low:
            place[MODES - rows + row, row] = 1.0
        if MODES - 1 - row >= 0:
            place[MODES - 1 - row, rows + row] = 1.0
    return {
        "analysis": to_bf16(analysis),
        "synth_low": to_bf16(synth_low),
        "pair_fwd": to_bf16(pair_fwd),
        "pair_back": to_bf16(pair_back),
        "pair_synth": to_bf16(np.swapaxes(pair_back, -1, -2)),
        "place": place.astype(np.float32),
    }


def dot(left, right):
    return jnp.dot(left, right, preferred_element_type=jnp.float32)


def swap_halves(values):
    return pltpu.roll(values, LANES // 2, 1)


def interleave(first, second):
    lane = lax.broadcasted_iota(jnp.int32, first.shape, 1)
    below = lane < LANES // 2
    return (
        jnp.where(below, first, swap_halves(second)),
        jnp.where(below, swap_halves(first), second),
    )


def gelu_slope(values):
    size = jnp.abs(values)
    step = 1.0 / (1.0 + 0.2316419 * size)
    scale = 1.0 / math.sqrt(2.0 * math.pi)
    series = 1.330274429 * scale
    for term in (-1.821255978, 1.781477937, -0.356563782, 0.319381530):
        series = series * step + term * scale
    below = jnp.exp(-0.5 * values * values) * (series * step - scale * size)
    return jnp.where(values >= 0.0, 1.0 - below, below)


def grid_rows(layout, side, north, south, quad, group):
    low, width = side * (LANES // 2), LANES // 2
    columns = []
    for pair in (2 * quad, 2 * quad + 1):
        columns.append(north[0, pair][:, low : low + width])
        values = south[0, pair][:, low : low + width]
        if layout.rows > layout.local:
            latitude = layout.half + group * PAIRS + pair
            values = jnp.where(latitude < layout.local, values, jnp.zeros_like(values))
        columns.append(values)
    return jnp.concatenate(columns, axis=1)


def scatter_rows(layout, values, scratch, quad, group):
    slots = layout.slots
    for which in range(2):
        columns = slice(which * LANES, (which + 1) * LANES)
        upper, lower = interleave(values[:slots, columns], values[slots:, columns])
        latitude = group * PAIRS + 2 * quad + which
        scratch[pl.ds(latitude, slots, stride=layout.rows), :] = upper
        scratch[pl.ds(latitude + layout.half, slots, stride=layout.rows), :] = lower


def gather_rows(layout, scratch, quad, group):
    slots = layout.slots
    cosine, sine = [], []
    for which in range(2):
        latitude = group * PAIRS + 2 * quad + which
        upper = scratch[pl.ds(latitude, slots, stride=layout.rows), :]
        lower = scratch[pl.ds(latitude + layout.half, slots, stride=layout.rows), :]
        first, second = interleave(upper, lower)
        cosine.append(first.astype(jnp.bfloat16))
        sine.append(second.astype(jnp.bfloat16))
    return jnp.concatenate(
        [jnp.concatenate(cosine, axis=1), jnp.concatenate(sine, axis=1)], axis=0
    )


def order_rows(layout, scratch, first, count):
    start = pl.multiple_of(first * layout.rows, layout.rows)
    return scratch[pl.ds(start, count * layout.rows), :].astype(jnp.bfloat16)


def forward_kernel(layout, side, north, south, basis, pair_fwd, out, scratch):
    group = pl.program_id(0)
    for quad in range(PAIRS // 2):
        grid = grid_rows(layout, side, north, south, quad, group)
        scatter_rows(layout, dot(basis[...], grid), scratch, quad, group)

    @pl.when(group == pl.num_programs(0) - 1)
    def _():
        def low_block(order, carry):
            out[order] = order_rows(layout, scratch, order, 1)
            return carry

        def pair_block(pair, carry):
            values = order_rows(layout, scratch, layout.low + 2 * pair, 2)
            out[layout.low + pair] = dot(pair_fwd[pair], values).astype(jnp.bfloat16)
            return carry

        lax.fori_loop(0, layout.low, low_block, 0, unroll=4)
        lax.fori_loop(0, layout.pairs, pair_block, 0, unroll=4)


def mix(spectral, real_rows, imag_rows):
    return (spectral * real_rows + swap_halves(spectral) * imag_rows).astype(jnp.bfloat16)


def spectral_kernel(layout, side, *refs):
    own, others = refs[0], refs[1 : layout.parts]
    north, south, basis, basis_t, analysis, synth_low, back_low = refs[layout.parts : layout.parts + 7]
    pair_synth, pair_back, place, real_ref, imag_ref = refs[layout.parts + 7 : layout.parts + 12]
    out, scratch, spec_low, spec_pair = refs[layout.parts + 12 :]
    group = pl.program_id(0)
    rows, degrees, low = layout.rows, layout.degrees, layout.low

    def groups():
        for start in range(0, low, GROUP):
            yield start, min(start + GROUP, low), start // 16 * 16

    @pl.when(group == 0)
    def _():
        for start, stop, top in groups():
            real_rows = real_ref[top:degrees, :]
            imag_rows = imag_ref[top:degrees, :]

            def low_block(order, carry):
                values = jnp.concatenate([own[order]] + [ref[order] for ref in others], axis=0)
                spectral = dot(analysis[order, top:degrees, :], values).astype(jnp.bfloat16)
                spec_low[order, top:degrees, :] = spectral
                mixed = mix(spectral.astype(jnp.float32), real_rows, imag_rows)
                begin = pl.multiple_of(order * rows, rows)
                scratch[pl.ds(begin, rows), :] = dot(synth_low[order, :, top:degrees], mixed)
                return carry

            lax.fori_loop(start, stop, low_block, 0, unroll=4)

        line = lax.broadcasted_iota(jnp.int32, (rows, LANES), 0)

        def pair_block(pair, carry):
            total = own[low + pair].astype(jnp.float32)
            for ref in others:
                total = total + ref[low + pair].astype(jnp.float32)
            spectral = total.astype(jnp.bfloat16)
            spec_pair[pair] = spectral
            natural = line >= layout.first_natural + pair
            real_rows = jnp.where(natural, real_ref[degrees : degrees + rows, :], real_ref[degrees + rows :, :])
            imag_rows = jnp.where(natural, imag_ref[degrees : degrees + rows, :], imag_ref[degrees + rows :, :])
            mixed = mix(spectral.astype(jnp.float32), real_rows, imag_rows)
            begin = pl.multiple_of((low + 2 * pair) * rows, rows)
            scratch[pl.ds(begin, 2 * rows), :] = dot(pair_synth[pair], mixed)
            return carry

        lax.fori_loop(0, layout.pairs, pair_block, 0, unroll=4)
        used = (low + 2 * layout.pairs) * rows
        if used < layout.slots * rows:
            scratch[used:, :] = jnp.zeros((layout.slots * rows - used, LANES), jnp.float32)

    for quad in range(PAIRS // 2):
        modes = gather_rows(layout, scratch, quad, group)
        signal = dot(basis_t[...], modes)
        incoming = grid_rows(layout, side, north, south, quad, group).astype(jnp.float32)
        upstream = (incoming * gelu_slope(signal)).astype(jnp.bfloat16)
        scatter_rows(layout, dot(basis[...], upstream), scratch, quad, group)

    @pl.when(group == pl.num_programs(0) - 1)
    def _():
        def products(spectral, back):
            spectral = spectral.astype(jnp.float32)
            back = back.astype(jnp.bfloat16).astype(jnp.float32)
            return spectral * back, spectral * swap_halves(back)

        zeros = jnp.zeros((degrees, LANES), jnp.float32)
        same, cross = zeros, zeros
        for start, stop, top in groups():

            def low_block(order, carry):
                back = dot(back_low[order, top:degrees, :], order_rows(layout, scratch, order, 1))
                first, second = products(spec_low[order, top:degrees, :], back)
                return carry[0] + first, carry[1] + second

            part = jnp.zeros((degrees - top, LANES), jnp.float32)
            first, second = lax.fori_loop(start, stop, low_block, (part, part), unroll=4)
            if top:
                empty = jnp.zeros((top, LANES), jnp.float32)
                first = jnp.concatenate([empty, first], axis=0)
                second = jnp.concatenate([empty, second], axis=0)
            same, cross = same + first, cross + second

        line = lax.broadcasted_iota(jnp.int32, (rows, LANES), 0)

        def pair_block(pair, carry):
            values = order_rows(layout, scratch, low + 2 * pair, 2)
            first, second = products(spec_pair[pair], dot(pair_back[pair], values))
            natural = line >= layout.first_natural + pair
            return (
                carry[0] + jnp.where(natural, first, 0.0),
                carry[1] + jnp.where(natural, second, 0.0),
                carry[2] + jnp.where(natural, 0.0, first),
                carry[3] + jnp.where(natural, 0.0, second),
            )

        part = jnp.zeros((rows, LANES), jnp.float32)
        sums = lax.fori_loop(0, layout.pairs, pair_block, (part,) * 4, unroll=4)
        placed = jnp.dot(
            place[...],
            jnp.concatenate(
                [jnp.concatenate(sums[:2], axis=1), jnp.concatenate(sums[2:], axis=1)], axis=0
            ),
            preferred_element_type=jnp.float32,
            precision=lax.Precision.HIGHEST,
        )
        same = same + placed[:, :LANES]
        cross = cross + placed[:, LANES:]
        real = same + swap_halves(same)
        imag = swap_halves(cross) - cross
        lane = lax.broadcasted_iota(jnp.int32, real.shape, 1)
        out[...] = jnp.where(lane < LANES // 2, real, imag)


def grid_specs(layout, tile):
    last = -(-layout.local // PAIRS) - 1
    shift = layout.half // PAIRS
    block = (1, PAIRS, NLON, LANES)
    return [
        pl.BlockSpec(block, lambda g: (0, jnp.minimum(g, last), 0, tile)),
        pl.BlockSpec(block, lambda g: (0, jnp.minimum(shift + g, last), 0, tile)),
    ]


def whole():
    return pl.BlockSpec(memory_space=pltpu.VMEM)


def forward_call(layout, chunk, fields, basis, pair_fwd):
    work = 2 * 2 * layout.slots * NLON * layout.rows * LANES // 2
    return pl.pallas_call(
        functools.partial(forward_kernel, layout, chunk % 2),
        grid=(layout.half // PAIRS,),
        in_specs=grid_specs(layout, chunk // 2) + [whole()] * 2,
        out_specs=whole(),
        out_shape=jax.ShapeDtypeStruct((layout.blocks, layout.rows, LANES), jnp.bfloat16),
        scratch_shapes=[pltpu.VMEM((layout.slots * layout.rows, LANES), jnp.float32)],
        compiler_params=pltpu.CompilerParams(vmem_limit_bytes=VMEM),
        cost_estimate=pl.CostEstimate(flops=2 * work, bytes_accessed=8_000_000, transcendentals=0),
        name=f"forward_{chunk}",
    )(fields, fields, basis, pair_fwd)


def spectral_call(layout, chunk, coeffs, cotangent, tables, real_rows, imag_rows):
    work = 2 * 2 * layout.slots * NLON * layout.rows * LANES // 2
    operands = list(coeffs) + [cotangent, cotangent] + list(tables) + [real_rows, imag_rows]
    return pl.pallas_call(
        functools.partial(spectral_kernel, layout, chunk % 2),
        grid=(layout.half // PAIRS,),
        in_specs=[whole()] * layout.parts
        + grid_specs(layout, chunk // 2)
        + [whole()] * (len(tables) + 2),
        out_specs=whole(),
        out_shape=jax.ShapeDtypeStruct((layout.degrees, LANES), jnp.float32),
        scratch_shapes=[
            pltpu.VMEM((layout.slots * layout.rows, LANES), jnp.float32),
            pltpu.VMEM((layout.low, layout.degrees, LANES), jnp.bfloat16),
            pltpu.VMEM((layout.pairs, layout.rows, LANES), jnp.bfloat16),
        ],
        compiler_params=pltpu.CompilerParams(vmem_limit_bytes=VMEM),
        cost_estimate=pl.CostEstimate(flops=6 * work, bytes_accessed=16_000_000, transcendentals=0),
        name=f"spectral_{chunk}",
    )(*operands)


def radices(size):
    found, factor = [], 2
    while size > 1:
        while size % factor == 0:
            found.append(factor)
            size //= factor
        factor += 1
    return found


def sum_over(value, axis):
    size = lax.axis_size(axis)
    stride = 1
    for radix in radices(size):
        total = value
        for turn in range(1, radix):
            pairs = []
            for index in range(size):
                digit = index // stride % radix
                pairs.append((index, index + ((digit + turn) % radix - digit) * stride))
            total = total + lax.ppermute(value, axis, pairs)
        value = total
        stride *= radix
    return value


def filter_rows(layout, spec):
    padded = jnp.pad(spec, ((0, layout.degrees - MODES), (0, 0)))
    front = jnp.pad(spec, ((layout.rows, layout.rows), (0, 0)))
    natural = front[MODES : MODES + layout.rows]
    backward = front[layout.rows + MODES - layout.rows : layout.rows + MODES][::-1]
    return jnp.concatenate([padded, natural, backward], axis=0).astype(jnp.float32)


def on_device(fields, cotangent, spec_real, spec_imag):
    parts = lax.axis_size("space")
    index = lax.axis_index("space")
    layout = Layout(parts, fields.shape[1])
    width = LANES // 2
    chunks = fields.shape[-1] // width
    basis, inverse, inverse_t = (jnp.asarray(a) for a in fourier_constants(parts, layout.local))
    constants = legendre_constants(parts, layout.local)

    def local_table(name):
        return lax.dynamic_index_in_dim(jnp.asarray(constants[name]), index, keepdims=False)

    pair_fwd = local_table("pair_fwd")
    def bands(name, first, count):
        table = jnp.asarray(constants[name])
        return lax.optimization_barrier(
            lax.dynamic_slice_in_dim(table, first * layout.rows, count * layout.rows, 1)
        )

    analysis = jnp.swapaxes(bands("analysis", parts - 1 - index, parts), 1, 2)
    synth_low = bands("synth_low", index, 1)
    back_low = jnp.swapaxes(synth_low, 1, 2)
    pair_tables = [local_table(name) for name in ("pair_synth", "pair_back")]
    tables = [inverse, inverse_t, analysis, synth_low, back_low] + pair_tables + [jnp.asarray(constants["place"])]
    real_all = filter_rows(layout, spec_real)
    imag_all = filter_rows(layout, spec_imag)

    received = []
    for chunk in range(chunks):
        own = forward_call(layout, chunk, fields, basis, pair_fwd)
        blocks = [own]
        for shift in range(1, parts):
            route = [(source, (source + shift) % parts) for source in range(parts)]
            blocks.append(lax.ppermute(own, "space", route))
        received.append(blocks)

    totals = []
    for chunk in range(chunks):
        columns = slice(chunk * width, (chunk + 1) * width)
        real, imag = real_all[:, columns], imag_all[:, columns]
        real_rows = jnp.concatenate([real, real], axis=1)
        imag_rows = jnp.concatenate([-imag, imag], axis=1)
        grads = spectral_call(layout, chunk, received[chunk], cotangent, tables, real_rows, imag_rows)
        totals.append(sum_over(sum_over(grads, "dp"), "space"))

    batch_total = fields.shape[0] * lax.axis_size("dp")
    real = jnp.concatenate([total[:MODES, :width] for total in totals], axis=1)
    imag = jnp.concatenate([total[:MODES, width:] for total in totals], axis=1)
    return (real / batch_total, imag / batch_total)


def solution(mesh):
    in_specs = (P("dp", "space", None, None), P("dp", "space", None, None), P(), P())
    out_specs = (P(), P())
    return jax.shard_map(
        on_device, mesh=mesh, in_specs=in_specs, out_specs=out_specs, check_vma=False
    )
```

time: 601 us -> 207 us (0.34); the launches traced: 593 us -> 206 us
  waiting for transfers between devices: 194 us -> 7.72 us
  Pallas kernels: 0 us -> 138 us
  loops' own time: 85.5 us -> 0 us
  blocking collectives: 73.1 us -> 0 us
  other arithmetic: 67.6 us -> 3.91 us
  local copies, waits for them, and re-layouts: 93.5 us -> 34 us
  matrix products: 51.6 us -> 0 us
  between operations: 14.8 us -> 0.85 us
  starting transfers between devices: 12.6 us -> 21.8 us
    pallas_call x0 -> x6, Pallas kernels: none -> 138 us  [the longest x3 110 us: spectral_call(): pl.pallas_call(functools.partial(spectral_kernel, layout, chunk % 2), gri...]
    psum x1 -> x0, waiting for transfers between devices: 124 us -> none  [on_device(): summed_real, summed_imag = lax.psum((part_real, part_imag), ('dp', 'space'))]
    another operation x1 -> x0, loops' own time: 85.5 us -> none  [legendre(): lax.scan(advance, (empty_rows, empty_rows), jnp.arange(MODES, dtype=jnp.i...]
    all_to_all x1 -> x0, blocking collectives: 73.1 us -> none  [to_orders(): lax.all_to_all(grid_coeffs, 'space', split_axis=1, concat_axis=2, tiled=T...]
    all_to_all x2 -> x0, waiting for transfers between devices: 70.1 us -> none  [the longest x1 70.1 us: on_device(): lax.all_to_all(synthesized, 'space', split_axis=2, concat_axis=1, tiled=T...]
    dot_general x3 -> x0, matrix products: 36.2 us -> none  [the longest x2 27.4 us: block_analysis(): jnp.einsum('qlj,sqjc->sqlc', tables, coeffs, preferred_element_type=jnp.f...]
    ppermute x0 -> x18, starting transfers between devices: none -> 21.8 us  [the longest x15 16.8 us: sum_over(): total = total + lax.ppermute(value, axis, pairs)]
    while x105 -> x0, other arithmetic: 19.2 us -> none
  transfers between devices with their start and end apart: 3 -> 18, of which waited for: 2 -> 7; matrix products, arithmetic and copies ran while one was open for 10% -> 12% of each run, Pallas kernels for 0% -> 62%
where the time goes in v1:
time: 207 us; the launch traced here: 206 us
  Pallas kernels  138 us (67%)
  local copies, waits for them, and re-layouts  34 us (16%)
  starting transfers between devices  21.8 us (11%)
  waiting for transfers between devices  7.72 us (4%)
  other arithmetic  3.91 us (2%)
    pallas_call x3, Pallas kernels, spectral_call(): pl.pallas_call(functools.partial(spectral_kernel, layout, chunk % 2), gri...  110 us
    pallas_call x3, Pallas kernels, forward_call(): pl.pallas_call(functools.partial(forward_kernel, layout, chunk % 2), grid...  27.8 us
    unnamed x22, local copies, waits for them, and re-layouts  22 us
    ppermute x15, starting transfers between devices, sum_over(): total = total + lax.ppermute(value, axis, pairs)  16.8 us
    ppermute x15, waiting for transfers between devices, sum_over(): total = total + lax.ppermute(value, axis, pairs)  7.71 us
    dynamic_slice x2, local copies, waits for them, and re-layouts, bands(): lax.dynamic_slice_in_dim(table, first * layout.rows, count * layout.rows, 1)  6.57 us
    ppermute x3, starting transfers between devices, on_device(): blocks.append(lax.ppermute(own, 'space', route))  4.99 us
  transfers between devices with their start and end apart: 18, of which 7 were waited for; matrix products, arithmetic and copies ran while one was open for 12% of the time, Pallas kernels for 62%

profile of v1, /device:TPU:0, one launch (start us, length us, event | category | flops | bytes accessed | tf_op | source)
XLA Modules:
  0.0 206.4 jit_solution(6183230172856546289)
XLA Ops:
  0.6 0.0 copy-start.5
  0.6 10.2 %copy.15.north.south = bf16[1,63,252,192]{3,2,1,0:T(8,128)(2,1)} copy(bf16[1,63,252,192]{2,3,1,0:T(8,128)(2,1)} %param.13) | data formatting | bytes 12192768 | tf_op args[0]
  10.8 0.8 dynamic-slice_bitcast_fusion.2.pair_fwd
  11.7 9.3 %forward_0.1.refs_0_ = bf16[95,64,128]{2,1,0:T(8,128)(2,1)} custom-call(bf16[1,63,252,192]{3,2,1,0:T(8,128)(2,1)} %copy.15.north.south, bf16[1,63,252,192]{3,2,1,0:T(8,128)(2,1)} %copy.15.north.south, bf16[256,252]{1,0:T(8,128)(2,1)} %constant.49.clone.basis, bf16[32,64,128]{2,1,0:T(8,128)(2,1)} %dynamic-slice_bitcast_fusion.2.pair_fwd), custom_call_target="tpu_custom_call" | custom-call | flops 1056964608 | bytes 8000000 | tf_op jit(solution)/shard_map/forward_0/pallas_call | solution.py:350
  20.9 3.0 %collective-permute-start = (bf16[95,64,128]{2,1,0:T(8,128)(2,1)}, bf16[95,64,128]{2,1,0:T(8,128)(2,1)}, u32[]{:S(2)}, u32[]{:S(2)}) collective-permute-start(bf16[95,64,128]{2,1,0:T(8,128)(2,1)} %forward_0.1.refs_0_), channel_id=1, source_target_pairs={{0,1},{1,0},{2,3},{3,2},{4,5},{5,4},{6,7},{7,6},{8,9},{9,8},{10,11... | collective-permute-start | bytes 4669448 | tf_op jit(solution)/shard_map/ppermute | solution.py:452
  23.9 9.3 %forward_1.1.refs_0_ = bf16[95,64,128]{2,1,0:T(8,128)(2,1)} custom-call(bf16[1,63,252,192]{3,2,1,0:T(8,128)(2,1)} %copy.15.north.south, bf16[1,63,252,192]{3,2,1,0:T(8,128)(2,1)} %copy.15.north.south, bf16[256,252]{1,0:T(8,128)(2,1)} %constant.49.clone.basis, bf16[32,64,128]{2,1,0:T(8,128)(2,1)} %dynamic-slice_bitcast_fusion.2.pair_fwd), custom_call_target="tpu_custom_call" | custom-call | flops 1056964608 | bytes 8000000 | tf_op jit(solution)/shard_map/forward_1/pallas_call | solution.py:350
  33.2 0.0 collective-permute-start.6
  33.2 9.3 %forward_2.1.refs_0_ = bf16[95,64,128]{2,1,0:T(8,128)(2,1)} custom-call(bf16[1,63,252,192]{3,2,1,0:T(8,128)(2,1)} %copy.15.north.south, bf16[1,63,252,192]{3,2,1,0:T(8,128)(2,1)} %copy.15.north.south, bf16[256,252]{1,0:T(8,128)(2,1)} %constant.49.clone.basis, bf16[32,64,128]{2,1,0:T(8,128)(2,1)} %dynamic-slice_bitcast_fusion.2.pair_fwd), custom_call_target="tpu_custom_call" | custom-call | flops 1056964608 | bytes 8000000 | tf_op jit(solution)/shard_map/forward_2/pallas_call | solution.py:350
  42.5 2.0 collective-permute-start.12
  44.5 4.3 %constant_dynamic-slice_fusion.1 = bf16[63,128,128]{1,2,0:T(8,128)(2,1)} fusion(bf16[63,256,128]{1,2,0:T(8,128)(2,1)} %constant.53.clone, s32[]{:T(128)S(6)} %select_n.14), kind=kLoop, calls=%fused_computation.21 | loop fusion | bytes 4128772 | tf_op jit(solution)/shard_map/dynamic_slice | solution.py:435
  48.8 0.1 copy.17
  48.9 0.1 rev.6
  49.0 0.0 copy-start.7
  49.0 2.2 %constant_dynamic-slice_fusion = bf16[63,64,128]{1,2,0:T(8,128)(2,1)S(1)} fusion(bf16[63,128,128]{1,2,0:T(8,128)(2,1)} %constant.54.clone, s32[]{:T(128)S(6)} %select_n.15), kind=kLoop, calls=%fused_computation.20 | loop fusion | bytes 2064388 | tf_op jit(solution)/shard_map/dynamic_slice | solution.py:435
  51.3 0.1 copy.19
  51.5 0.1 rev.7
  51.6 2.2 %copy.23.refs_7_ = bf16[63,64,128]{2,1,0:T(8,128)(2,1)} copy(bf16[63,64,128]{1,2,0:T(8,128)(2,1)S(1)} %constant_dynamic-slice_fusion) | data formatting | bytes 2064384 | tf_op jit(solution)/shard_map/optimization_barrier | solution.py:434
  53.7 10.1 %copy.21.refs_2_.refs_3_ = bf16[1,63,252,192]{3,2,1,0:T(8,128)(2,1)} copy(bf16[1,63,252,192]{2,3,1,0:T(8,128)(2,1)} %param.14) | data formatting | bytes 12192768 | tf_op args[1]
  63.8 0.1 fusion.8
  63.9 0.0 copy-start.1
  63.9 0.1 slice_negate_fusion.2
  64.1 0.9 pad_maximum_fusion
  64.9 0.9 pad_maximum_fusion.2
  65.8 0.9 pad_maximum_fusion.4
  66.6 0.8 dynamic-slice_bitcast_fusion.1.refs_10_
  67.5 1.1 dynamic-slice_bitcast_fusion.refs_9_
  68.5 36.7 %spectral_0.1 = f32[128,128]{1,0:T(8,128)} custom-call(bf16[95,64,128]{2,1,0:T(8,128)(2,1)} %forward_0.1.refs_0_, bf16[95,64,128]{2,1,0:T(8,128)(2,1)} %collective-permute-done.refs_1_, bf16[1,63,252,192]{3,2,1,0:T(8,128)(2,1)} %copy.21.refs_2_.refs_3_, bf16[1,63,252,192]{3,2,1,0:T(8,128)(2,1)} %copy.21.refs_2_.refs_3_, ...), custom_call_target="tpu_custom_call" | custom-call | flops 3170893824 | bytes 16000000 | tf_op jit(solution)/shard_map/spectral_0/pallas_call | solution.py:366
  105.2 0.0 collective-permute-start.1
  105.3 36.9 %spectral_1.1 = f32[128,128]{1,0:T(8,128)} custom-call(bf16[95,64,128]{2,1,0:T(8,128)(2,1)} %forward_1.1.refs_0_, bf16[95,64,128]{2,1,0:T(8,128)(2,1)} %collective-permute-done.6.refs_1_, bf16[1,63,252,192]{3,2,1,0:T(8,128)(2,1)} %copy.21.refs_2_.refs_3_, bf16[1,63,252,192]{3,2,1,0:T(8,128)(2,1)} %copy.21.refs_2_.refs_3_, ...), custom_call_target="tpu_custom_call" | custom-call | flops 3170893824 | bytes 16000000 | tf_op jit(solution)/shard_map/spectral_1/pallas_call | solution.py:366
  142.1 0.5 collective-permute-start.7
  142.6 36.7 %spectral_2.1 = f32[128,128]{1,0:T(8,128)} custom-call(bf16[95,64,128]{2,1,0:T(8,128)(2,1)} %forward_2.1.refs_0_, bf16[95,64,128]{2,1,0:T(8,128)(2,1)} %collective-permute-done.12.refs_1_, bf16[1,63,252,192]{3,2,1,0:T(8,128)(2,1)} %copy.21.refs_2_.refs_3_, bf16[1,63,252,192]{3,2,1,0:T(8,128)(2,1)} %copy.21.refs_2_.refs_3_, ...), custom_call_target="tpu_custom_call" | custom-call | flops 3170893824 | bytes 16000000 | tf_op jit(solution)/shard_map/spectral_2/pallas_call | solution.py:366
  179.3 0.0 collective-permute-start.13
  179.4 1.6 collective-permute-start.2
  181.0 0.0 collective-permute-done.7
  181.0 0.6 collective-permute-start.8
  181.6 0.0 collective-permute-done.13
  181.6 0.9 add.75
  182.4 1.6 collective-permute-start.14
  184.0 0.1 collective-permute-done.2
  184.1 1.7 collective-permute-start.3
  185.7 0.0 collective-permute-done.8
  185.8 1.7 collective-permute-start.9
  187.4 0.0 collective-permute-done.14
  187.4 1.0 collective-permute-start.15
  188.4 0.7 collective-permute-done.3
  189.1 2.7 %collective-permute-start.4 = (f32[128,128]{1,0:T(8,128)S(1)}, f32[128,128]{1,0:T(8,128)S(1)}, u32[]{:S(2)}, u32[]{:S(2)}) collective-permute-start(f32[128,128]{1,0:T(8,128)S(1)} %add.67), channel_id=1, source_target_pairs={{0,16},{2,18},{4,20},{6,22},{8,24},{10,26},{12,28},{14,30},{16,0},... | collective-permute-start | bytes 196616 | tf_op jit(solution)/shard_map/ppermute | solution.py:405
  191.8 1.7 collective-permute-start.10
  193.6 1.3 collective-permute-start.16
  194.9 2.2 %collective-permute-done.4 = f32[128,128]{1,0:T(8,128)S(1)} collective-permute-done((f32[128,128]{1,0:T(8,128)S(1)}, f32[128,128]{1,0:T(8,128)S(1)}, u32[]{:S(2)}, u32[]{:S(2)}) %collective-permute-start.4) | collective-permute-done | bytes 65568 | tf_op jit(solution)/shard_map/ppermute | solution.py:405
  197.1 0.5 collective-permute-start.5
  197.6 2.0 collective-permute-done.10
  199.6 0.6 collective-permute-start.11
  200.1 0.1 collective-permute-done.16
  200.3 1.5 collective-permute-start.17
  201.7 0.0 collective-permute-done.5
  201.8 0.1 fusion.9
  201.8 2.1 collective-permute-done.11
  203.9 0.1 fusion.10
  204.0 0.6 collective-permute-done.17
  204.6 0.1 fusion.11
  204.7 0.1 maximum_multiply_fusion.1
  204.8 0.7 copy.35
  205.6 0.1 maximum_multiply_fusion
  205.7 0.7 copy.34
  (37 shorter events, 0.2 us)
Async XLA Ops:
  0.6 10.2 %copy-start.5 = (bf16[2,32,64,128]{3,2,1,0:T(8,128)(2,1)S(1)}, bf16[2,32,64,128]{3,2,1,0:T(8,128)(2,1)}, u32[]{:S(2)}) copy-start(bf16[2,32,64,128]{3,2,1,0:T(8,128)(2,1)} %constant.52.clone) | copy-start | bytes 3145732
  20.9 47.6 %collective-permute-start = (bf16[95,64,128]{2,1,0:T(8,128)(2,1)}, bf16[95,64,128]{2,1,0:T(8,128)(2,1)}, u32[]{:S(2)}, u32[]{:S(2)}) collective-permute-start(bf16[95,64,128]{2,1,0:T(8,128)(2,1)} %forward_0.1.refs_0_), channel_id=1, source_target_pairs={{0,1},{1,0},{2,3},{3,2},{4,5},{5,4},{6,7},{7,6},{8,9},{9,8},{10,11... | collective-permute-start | bytes 4669448 | tf_op jit(solution)/shard_map/ppermute | solution.py:452
  33.2 72.1 %collective-permute-start.6 = (bf16[95,64,128]{2,1,0:T(8,128)(2,1)}, bf16[95,64,128]{2,1,0:T(8,128)(2,1)}, u32[]{:S(2)}, u32[]{:S(2)}) collective-permute-start(bf16[95,64,128]{2,1,0:T(8,128)(2,1)} %forward_1.1.refs_0_), channel_id=1, source_target_pairs={{0,1},{1,0},{2,3},{3,2},{4,5},{5,4},{6,7},{7,6},{8,9},{9,8},{10,11... | collective-permute-start | bytes 4669448 | tf_op jit(solution)/shard_map/ppermute | solution.py:452
  42.5 100.1 %collective-permute-start.12 = (bf16[95,64,128]{2,1,0:T(8,128)(2,1)}, bf16[95,64,128]{2,1,0:T(8,128)(2,1)}, u32[]{:S(2)}, u32[]{:S(2)}) collective-permute-start(bf16[95,64,128]{2,1,0:T(8,128)(2,1)} %forward_2.1.refs_0_), channel_id=1, source_target_pairs={{0,1},{1,0},{2,3},{3,2},{4,5},{5,4},{6,7},{7,6},{8,9},{9,8},{10,11... | collective-permute-start | bytes 4669448 | tf_op jit(solution)/shard_map/ppermute | solution.py:452
  44.5 4.3 %copy-start.6 = (bf16[126,192]{0,1:T(8,128)(2,1)S(1)}, bf16[126,192]{0,1:T(8,128)(2,1)}, u32[]{:S(2)}) copy-start(bf16[126,192]{0,1:T(8,128)(2,1)} %param.15) | copy-start | bytes 145156
  49.0 2.3 %copy-start.7 = (bf16[126,192]{0,1:T(8,128)(2,1)S(1)}, bf16[126,192]{0,1:T(8,128)(2,1)}, u32[]{:S(2)}) copy-start(bf16[126,192]{0,1:T(8,128)(2,1)} %param.16) | copy-start | bytes 145156
  51.3 12.5 %copy-start = (bf16[63,64,128]{1,2,0:T(8,128)(2,1)}, bf16[63,64,128]{1,2,0:T(8,128)(2,1)S(1)}, u32[]{:S(2)}) copy-start(bf16[63,64,128]{1,2,0:T(8,128)(2,1)S(1)} %constant_dynamic-slice_fusion) | copy-start | bytes 3096580
  63.8 2.8 %copy-start.4 = (bf16[2,32,64,128]{3,2,1,0:T(8,128)(2,1)S(1)}, bf16[2,32,64,128]{3,2,1,0:T(8,128)(2,1)}, u32[]{:S(2)}) copy-start(bf16[2,32,64,128]{3,2,1,0:T(8,128)(2,1)} %constant.56.clone) | copy-start | bytes 3145732
  63.9 3.5 %copy-start.1 = (bf16[2,32,128,64]{3,2,1,0:T(8,128)(2,1)S(1)}, bf16[2,32,128,64]{3,2,1,0:T(8,128)(2,1)}, u32[]{:S(2)}) copy-start(bf16[2,32,128,64]{3,2,1,0:T(8,128)(2,1)} %constant.55.clone) | copy-start | bytes 3145732
  105.2 74.1 %collective-permute-start.1 = (f32[128,128]{1,0:T(8,128)}, f32[128,128]{1,0:T(8,128)S(1)}, u32[]{:S(2)}, u32[]{:S(2)}) collective-permute-start(f32[128,128]{1,0:T(8,128)} %spectral_0.1), channel_id=1, source_target_pairs={{0,2},{2,0},{4,6},{6,4},{8,10},{10,8},{12,14},{14,12},{16,18},{18,... | collective-permute-start | bytes 196616 | tf_op jit(solution)/shard_map/ppermute | solution.py:405
  142.1 38.8 %collective-permute-start.7 = (f32[128,128]{1,0:T(8,128)}, f32[128,128]{1,0:T(8,128)S(1)}, u32[]{:S(2)}, u32[]{:S(2)}) collective-permute-start(f32[128,128]{1,0:T(8,128)} %spectral_1.1), channel_id=1, source_target_pairs={{0,2},{2,0},{4,6},{6,4},{8,10},{10,8},{12,14},{14,12},{16,18},{18,... | collective-permute-start | bytes 196616 | tf_op jit(solution)/shard_map/ppermute | solution.py:405
  142.6 36.8 %copy-start.2 = (f32[128,128]{1,0:T(8,128)S(1)}, f32[128,128]{1,0:T(8,128)}, u32[]{:S(2)}) copy-start(f32[128,128]{1,0:T(8,128)} %spectral_0.1) | copy-start | bytes 196612
  142.6 38.3 %copy-start.3 = (f32[128,128]{1,0:T(8,128)S(1)}, f32[128,128]{1,0:T(8,128)}, u32[]{:S(2)}) copy-start(f32[128,128]{1,0:T(8,128)} %spectral_1.1) | copy-start | bytes 196612
  179.3 2.2 %collective-permute-start.13 = (f32[128,128]{1,0:T(8,128)}, f32[128,128]{1,0:T(8,128)S(1)}, u32[]{:S(2)}, u32[]{:S(2)}) collective-permute-start(f32[128,128]{1,0:T(8,128)} %spectral_2.1), channel_id=1, source_target_pairs={{0,2},{2,0},{4,6},{6,4},{8,10},{10,8},{12,14},{14,12},{16,18},{18,... | collective-permute-start | bytes 196616 | tf_op jit(solution)/shard_map/ppermute | solution.py:405
  179.4 4.7 %collective-permute-start.2 = (f32[128,128]{1,0:T(8,128)S(1)}, f32[128,128]{1,0:T(8,128)S(1)}, u32[]{:S(2)}, u32[]{:S(2)}) collective-permute-start(f32[128,128]{1,0:T(8,128)S(1)} %add.65), channel_id=1, source_target_pairs={{0,4},{2,6},{4,0},{6,2},{8,12},{10,14},{12,8},{14,10},{16,20},{18,... | collective-permute-start | bytes 196616 | tf_op jit(solution)/shard_map/ppermute | solution.py:405
  181.0 4.8 %collective-permute-start.8 = (f32[128,128]{1,0:T(8,128)S(1)}, f32[128,128]{1,0:T(8,128)S(1)}, u32[]{:S(2)}, u32[]{:S(2)}) collective-permute-start(f32[128,128]{1,0:T(8,128)S(1)} %add.70), channel_id=1, source_target_pairs={{0,4},{2,6},{4,0},{6,2},{8,12},{10,14},{12,8},{14,10},{16,20},{18,... | collective-permute-start | bytes 196616 | tf_op jit(solution)/shard_map/ppermute | solution.py:405
  182.4 5.0 %collective-permute-start.14 = (f32[128,128]{1,0:T(8,128)S(1)}, f32[128,128]{1,0:T(8,128)S(1)}, u32[]{:S(2)}, u32[]{:S(2)}) collective-permute-start(f32[128,128]{1,0:T(8,128)S(1)} %add.75), channel_id=1, source_target_pairs={{0,4},{2,6},{4,0},{6,2},{8,12},{10,14},{12,8},{14,10},{16,20},{18,... | collective-permute-start | bytes 196616 | tf_op jit(solution)/shard_map/ppermute | solution.py:405
  184.1 5.0 %collective-permute-start.3 = (f32[128,128]{1,0:T(8,128)S(1)}, f32[128,128]{1,0:T(8,128)S(1)}, u32[]{:S(2)}, u32[]{:S(2)}) collective-permute-start(f32[128,128]{1,0:T(8,128)S(1)} %add.66), channel_id=1, source_target_pairs={{0,8},{2,10},{4,12},{6,14},{8,0},{10,2},{12,4},{14,6},{16,24},{18,... | collective-permute-start | bytes 196616 | tf_op jit(solution)/shard_map/ppermute | solution.py:405
  185.8 6.0 %collective-permute-start.9 = (f32[128,128]{1,0:T(8,128)S(1)}, f32[128,128]{1,0:T(8,128)S(1)}, u32[]{:S(2)}, u32[]{:S(2)}) collective-permute-start(f32[128,128]{1,0:T(8,128)S(1)} %add.71), channel_id=1, source_target_pairs={{0,8},{2,10},{4,12},{6,14},{8,0},{10,2},{12,4},{14,6},{16,24},{18,... | collective-permute-start | bytes 196616 | tf_op jit(solution)/shard_map/ppermute | solution.py:405
  187.4 6.1 %collective-permute-start.15 = (f32[128,128]{1,0:T(8,128)S(1)}, f32[128,128]{1,0:T(8,128)S(1)}, u32[]{:S(2)}, u32[]{:S(2)}) collective-permute-start(f32[128,128]{1,0:T(8,128)S(1)} %add.76), channel_id=1, source_target_pairs={{0,8},{2,10},{4,12},{6,14},{8,0},{10,2},{12,4},{14,6},{16,24},{18,... | collective-permute-start | bytes 196616 | tf_op jit(solution)/shard_map/ppermute | solution.py:405
  189.1 8.0 %collective-permute-start.4 = (f32[128,128]{1,0:T(8,128)S(1)}, f32[128,128]{1,0:T(8,128)S(1)}, u32[]{:S(2)}, u32[]{:S(2)}) collective-permute-start(f32[128,128]{1,0:T(8,128)S(1)} %add.67), channel_id=1, source_target_pairs={{0,16},{2,18},{4,20},{6,22},{8,24},{10,26},{12,28},{14,30},{16,0},... | collective-permute-start | bytes 196616 | tf_op jit(solution)/shard_map/ppermute | solution.py:405
  191.8 7.7 %collective-permute-start.10 = (f32[128,128]{1,0:T(8,128)S(1)}, f32[128,128]{1,0:T(8,128)S(1)}, u32[]{:S(2)}, u32[]{:S(2)}) collective-permute-start(f32[128,128]{1,0:T(8,128)S(1)} %add.72), channel_id=1, source_target_pairs={{0,16},{2,18},{4,20},{6,22},{8,24},{10,26},{12,28},{14,30},{16,0},... | collective-permute-start | bytes 196616 | tf_op jit(solution)/shard_map/ppermute | solution.py:405
  193.6 6.7 %collective-permute-start.16 = (f32[128,128]{1,0:T(8,128)S(1)}, f32[128,128]{1,0:T(8,128)S(1)}, u32[]{:S(2)}, u32[]{:S(2)}) collective-permute-start(f32[128,128]{1,0:T(8,128)S(1)} %add.77), channel_id=1, source_target_pairs={{0,16},{2,18},{4,20},{6,22},{8,24},{10,26},{12,28},{14,30},{16,0},... | collective-permute-start | bytes 196616 | tf_op jit(solution)/shard_map/ppermute | solution.py:405
  197.1 4.7 %collective-permute-start.5 = (f32[128,128]{1,0:T(8,128)S(1)}, f32[128,128]{1,0:T(8,128)S(1)}, u32[]{:S(2)}, u32[]{:S(2)}) collective-permute-start(f32[128,128]{1,0:T(8,128)S(1)} %add.68), channel_id=1, source_target_pairs={{0,1},{1,0},{2,3},{3,2},{4,5},{5,4},{6,7},{7,6},{8,9},{9,8},{10,11... | collective-permute-start | bytes 196616 | tf_op jit(solution)/shard_map/ppermute | solution.py:405
  199.6 4.3 %collective-permute-start.11 = (f32[128,128]{1,0:T(8,128)S(1)}, f32[128,128]{1,0:T(8,128)S(1)}, u32[]{:S(2)}, u32[]{:S(2)}) collective-permute-start(f32[128,128]{1,0:T(8,128)S(1)} %add.73), channel_id=1, source_target_pairs={{0,1},{1,0},{2,3},{3,2},{4,5},{5,4},{6,7},{7,6},{8,9},{9,8},{10,11... | collective-permute-start | bytes 196616 | tf_op jit(solution)/shard_map/ppermute | solution.py:405
  200.3 4.3 %collective-permute-start.17 = (f32[128,128]{1,0:T(8,128)S(1)}, f32[128,128]{1,0:T(8,128)S(1)}, u32[]{:S(2)}, u32[]{:S(2)}) collective-permute-start(f32[128,128]{1,0:T(8,128)S(1)} %add.78), channel_id=1, source_target_pairs={{0,1},{1,0},{2,3},{3,2},{4,5},{5,4},{6,7},{7,6},{8,9},{9,8},{10,11... | collective-permute-start | bytes 196616 | tf_op jit(solution)/shard_map/ppermute | solution.py:405

commit v2 on v1

--- a/solution.py
+++ b/solution.py
@@ -16,7 +16,7 @@
 LANES = 128
 GROUP = 16
 PAIRS = 8
-VMEM = 56 * 1024 * 1024
+VMEM = 30 * 1024 * 1024
 
 
 def round_up(value, step):
@@ -55,6 +55,7 @@
         self.parts, self.local = parts, local
         self.rows = round_up(local + 1, 16)
         self.half = self.rows // 2
+        self.pitch = self.rows + 8
         self.low = max(MODES - local, 0)
         high = MODES - self.low
         self.pairs = (high + 1) // 2
@@ -79,7 +80,7 @@
     basis = np.concatenate([np.cos(angles) * live, -np.sin(angles) * live])
     factor = np.where(layout.orders == 0, 1.0, 2.0)[:, None]
     inverse = basis * np.concatenate([factor, factor])
-    return to_bf16(basis), to_bf16(inverse), to_bf16(inverse.T)
+    return to_bf16(basis), to_bf16(inverse)
 
 
 @functools.lru_cache(maxsize=None)
@@ -123,8 +124,9 @@
     }
 
 
-def dot(left, right):
-    return jnp.dot(left, right, preferred_element_type=jnp.float32)
+def dot(left, right, sides=(1, 0)):
+    contract = (((sides[0],), (sides[1],)), ((), ()))
+    return lax.dot_general(left, right, contract, preferred_element_type=jnp.float32)
 
 
 def swap_halves(values):
@@ -151,17 +153,16 @@
     return jnp.where(values >= 0.0, 1.0 - below, below)
 
 
-def grid_rows(layout, side, north, south, quad, group):
-    low, width = side * (LANES // 2), LANES // 2
-    columns = []
+def grid_rows(layout, north, south, quad, group):
+    rows = []
     for pair in (2 * quad, 2 * quad + 1):
-        columns.append(north[0, pair][:, low : low + width])
-        values = south[0, pair][:, low : low + width]
+        rows.append(north[0, pair])
+        values = south[0, pair]
         if layout.rows > layout.local:
             latitude = layout.half + group * PAIRS + pair
             values = jnp.where(latitude < layout.local, values, jnp.zeros_like(values))
-        columns.append(values)
-    return jnp.concatenate(columns, axis=1)
+        rows.append(values)
+    return jnp.concatenate(rows, axis=0)
 
 
 def scatter_rows(layout, values, scratch, quad, group):
@@ -170,8 +171,8 @@
         columns = slice(which * LANES, (which + 1) * LANES)
         upper, lower = interleave(values[:slots, columns], values[slots:, columns])
         latitude = group * PAIRS + 2 * quad + which
-        scratch[pl.ds(latitude, slots, stride=layout.rows), :] = upper
-        scratch[pl.ds(latitude + layout.half, slots, stride=layout.rows), :] = lower
+        scratch[pl.ds(latitude, slots, stride=layout.pitch), :] = upper
+        scratch[pl.ds(latitude + layout.half, slots, stride=layout.pitch), :] = lower
 
 
 def gather_rows(layout, scratch, quad, group):
@@ -179,8 +180,8 @@
     cosine, sine = [], []
     for which in range(2):
         latitude = group * PAIRS + 2 * quad + which
-        upper = scratch[pl.ds(latitude, slots, stride=layout.rows), :]
-        lower = scratch[pl.ds(latitude + layout.half, slots, stride=layout.rows), :]
+        upper = scratch[pl.ds(latitude, slots, stride=layout.pitch), :]
+        lower = scratch[pl.ds(latitude + layout.half, slots, stride=layout.pitch), :]
         first, second = interleave(upper, lower)
         cosine.append(first.astype(jnp.bfloat16))
         sine.append(second.astype(jnp.bfloat16))
@@ -190,15 +191,18 @@
 
 
 def order_rows(layout, scratch, first, count):
-    start = pl.multiple_of(first * layout.rows, layout.rows)
-    return scratch[pl.ds(start, count * layout.rows), :].astype(jnp.bfloat16)
-
-
-def forward_kernel(layout, side, north, south, basis, pair_fwd, out, scratch):
+    parts = []
+    for order in range(count):
+        start = pl.multiple_of((first + order) * layout.pitch, 8)
+        parts.append(scratch[pl.ds(start, layout.rows), :])
+    return jnp.concatenate(parts, axis=0).astype(jnp.bfloat16)
+
+
+def forward_kernel(layout, north, south, basis, pair_fwd, out, scratch):
     group = pl.program_id(0)
     for quad in range(PAIRS // 2):
-        grid = grid_rows(layout, side, north, south, quad, group)
-        scatter_rows(layout, dot(basis[...], grid), scratch, quad, group)
+        grid = grid_rows(layout, north, south, quad, group)
+        scatter_rows(layout, dot(basis[...], grid, (1, 1)), scratch, quad, group)
 
     @pl.when(group == pl.num_programs(0) - 1)
     def _():
@@ -211,19 +215,19 @@
             out[layout.low + pair] = dot(pair_fwd[pair], values).astype(jnp.bfloat16)
             return carry
 
-        lax.fori_loop(0, layout.low, low_block, 0, unroll=4)
-        lax.fori_loop(0, layout.pairs, pair_block, 0, unroll=4)
-
-
-def mix(spectral, real_rows, imag_rows):
-    return (spectral * real_rows + swap_halves(spectral) * imag_rows).astype(jnp.bfloat16)
-
-
-def spectral_kernel(layout, side, *refs):
+        lax.fori_loop(0, layout.low, low_block, 0, unroll=8)
+        lax.fori_loop(0, layout.pairs, pair_block, 0, unroll=8)
+
+
+def mix(spectral, swapped, real_rows, imag_rows):
+    return (spectral * real_rows + swapped * imag_rows).astype(jnp.bfloat16)
+
+
+def spectral_kernel(layout, *refs):
     own, others = refs[0], refs[1 : layout.parts]
-    north, south, basis, basis_t, analysis, synth_low, back_low = refs[layout.parts : layout.parts + 7]
-    pair_synth, pair_back, place, real_ref, imag_ref = refs[layout.parts + 7 : layout.parts + 12]
-    out, scratch, spec_low, spec_pair = refs[layout.parts + 12 :]
+    north, south, basis, analysis, synth_low, back_low = refs[layout.parts : layout.parts + 6]
+    pair_synth, pair_back, place, real_ref, imag_ref = refs[layout.parts + 6 : layout.parts + 11]
+    out, scratch, returned, spec_low, swap_low, spec_pair, swap_pair = refs[layout.parts + 11 :]
     group = pl.program_id(0)
     rows, degrees, low = layout.rows, layout.degrees, layout.low
 
@@ -241,12 +245,19 @@
                 values = jnp.concatenate([own[order]] + [ref[order] for ref in others], axis=0)
                 spectral = dot(analysis[order, top:degrees, :], values).astype(jnp.bfloat16)
                 spec_low[order, top:degrees, :] = spectral
-                mixed = mix(spectral.astype(jnp.float32), real_rows, imag_rows)
-                begin = pl.multiple_of(order * rows, rows)
+                return carry
+
+            def mix_block(order, carry):
+                spectral = spec_low[order, top:degrees, :].astype(jnp.float32)
+                swapped = swap_halves(spectral)
+                swap_low[order, top:degrees, :] = swapped.astype(jnp.bfloat16)
+                mixed = mix(spectral, swapped, real_rows, imag_rows)
+                begin = pl.multiple_of(order * layout.pitch, 8)
                 scratch[pl.ds(begin, rows), :] = dot(synth_low[order, :, top:degrees], mixed)
                 return carry
 
-            lax.fori_loop(start, stop, low_block, 0, unroll=4)
+            lax.fori_loop(start, stop, low_block, 0, unroll=8)
+            lax.fori_loop(start, stop, mix_block, 0, unroll=8)
 
         line = lax.broadcasted_iota(jnp.int32, (rows, LANES), 0)
 
@@ -259,41 +270,48 @@
             natural = line >= layout.first_natural + pair
             real_rows = jnp.where(natural, real_ref[degrees : degrees + rows, :], real_ref[degrees + rows :, :])
             imag_rows = jnp.where(natural, imag_ref[degrees : degrees + rows, :], imag_ref[degrees + rows :, :])
-            mixed = mix(spectral.astype(jnp.float32), real_rows, imag_rows)
-            begin = pl.multiple_of((low + 2 * pair) * rows, rows)
-            scratch[pl.ds(begin, 2 * rows), :] = dot(pair_synth[pair], mixed)
+            spectral = spectral.astype(jnp.float32)
+            swapped = swap_halves(spectral)
+            swap_pair[pair] = swapped.astype(jnp.bfloat16)
+            mixed = mix(spectral, swapped, real_rows, imag_rows)
+            values = dot(pair_synth[pair], mixed)
+            for which in range(2):
+                begin = pl.multiple_of((low + 2 * pair + which) * layout.pitch, 8)
+                scratch[pl.ds(begin, rows), :] = values[which * rows : (which + 1) * rows]
             return carry
 
-        lax.fori_loop(0, layout.pairs, pair_block, 0, unroll=4)
-        used = (low + 2 * layout.pairs) * rows
-        if used < layout.slots * rows:
-            scratch[used:, :] = jnp.zeros((layout.slots * rows - used, LANES), jnp.float32)
+        lax.fori_loop(0, layout.pairs, pair_block, 0, unroll=8)
+        used = (low + 2 * layout.pairs) * layout.pitch
+        if used < layout.slots * layout.pitch:
+            scratch[used : layout.slots * layout.pitch, :] = jnp.zeros(
+                (layout.slots * layout.pitch - used, LANES), jnp.float32
+            )
 
     for quad in range(PAIRS // 2):
         modes = gather_rows(layout, scratch, quad, group)
-        signal = dot(basis_t[...], modes)
-        incoming = grid_rows(layout, side, north, south, quad, group).astype(jnp.float32)
+        signal = dot(modes, basis[...], (0, 0))
+        incoming = grid_rows(layout, north, south, quad, group).astype(jnp.float32)
         upstream = (incoming * gelu_slope(signal)).astype(jnp.bfloat16)
-        scatter_rows(layout, dot(basis[...], upstream), scratch, quad, group)
+        scatter_rows(layout, dot(basis[...], upstream, (1, 1)), returned, quad, group)
 
     @pl.when(group == pl.num_programs(0) - 1)
     def _():
-        def products(spectral, back):
-            spectral = spectral.astype(jnp.float32)
-            back = back.astype(jnp.bfloat16).astype(jnp.float32)
-            return spectral * back, spectral * swap_halves(back)
+        def products(spectral, swapped, back):
+            return spectral.astype(jnp.float32) * back, swapped.astype(jnp.float32) * back
 
         zeros = jnp.zeros((degrees, LANES), jnp.float32)
         same, cross = zeros, zeros
         for start, stop, top in groups():
 
             def low_block(order, carry):
-                back = dot(back_low[order, top:degrees, :], order_rows(layout, scratch, order, 1))
-                first, second = products(spec_low[order, top:degrees, :], back)
+                back = dot(back_low[order, top:degrees, :], order_rows(layout, returned, order, 1))
+                first, second = products(
+                    spec_low[order, top:degrees, :], swap_low[order, top:degrees, :], back
+                )
                 return carry[0] + first, carry[1] + second
 
             part = jnp.zeros((degrees - top, LANES), jnp.float32)
-            first, second = lax.fori_loop(start, stop, low_block, (part, part), unroll=4)
+            first, second = lax.fori_loop(start, stop, low_block, (part, part), unroll=8)
             if top:
                 empty = jnp.zeros((top, LANES), jnp.float32)
                 first = jnp.concatenate([empty, first], axis=0)
@@ -303,8 +321,8 @@
         line = lax.broadcasted_iota(jnp.int32, (rows, LANES), 0)
 
         def pair_block(pair, carry):
-            values = order_rows(layout, scratch, low + 2 * pair, 2)
-            first, second = products(spec_pair[pair], dot(pair_back[pair], values))
+            back = dot(pair_back[pair], order_rows(layout, returned, low + 2 * pair, 2))
+            first, second = products(spec_pair[pair], swap_pair[pair], back)
             natural = line >= layout.first_natural + pair
             return (
                 carry[0] + jnp.where(natural, first, 0.0),
@@ -314,7 +332,7 @@
             )
 
         part = jnp.zeros((rows, LANES), jnp.float32)
-        sums = lax.fori_loop(0, layout.pairs, pair_block, (part,) * 4, unroll=4)
+        sums = lax.fori_loop(0, layout.pairs, pair_block, (part,) * 4, unroll=8)
         placed = jnp.dot(
             place[...],
             jnp.concatenate(
@@ -326,18 +344,18 @@
         same = same + placed[:, :LANES]
         cross = cross + placed[:, LANES:]
         real = same + swap_halves(same)
-        imag = swap_halves(cross) - cross
+        imag = cross - swap_halves(cross)
         lane = lax.broadcasted_iota(jnp.int32, real.shape, 1)
         out[...] = jnp.where(lane < LANES // 2, real, imag)
 
 
-def grid_specs(layout, tile):
+def grid_specs(layout, chunk):
     last = -(-layout.local // PAIRS) - 1
     shift = layout.half // PAIRS
-    block = (1, PAIRS, NLON, LANES)
+    block = (1, PAIRS, LANES // 2, NLON)
     return [
-        pl.BlockSpec(block, lambda g: (0, jnp.minimum(g, last), 0, tile)),
-        pl.BlockSpec(block, lambda g: (0, jnp.minimum(shift + g, last), 0, tile)),
+        pl.BlockSpec(block, lambda g: (0, jnp.minimum(g, last), chunk, 0)),
+        pl.BlockSpec(block, lambda g: (0, jnp.minimum(shift + g, last), chunk, 0)),
     ]
 
 
@@ -348,12 +366,12 @@
 def forward_call(layout, chunk, fields, basis, pair_fwd):
     work = 2 * 2 * layout.slots * NLON * layout.rows * LANES // 2
     return pl.pallas_call(
-        functools.partial(forward_kernel, layout, chunk % 2),
+        functools.partial(forward_kernel, layout),
         grid=(layout.half // PAIRS,),
-        in_specs=grid_specs(layout, chunk // 2) + [whole()] * 2,
+        in_specs=grid_specs(layout, chunk) + [whole()] * 2,
         out_specs=whole(),
         out_shape=jax.ShapeDtypeStruct((layout.blocks, layout.rows, LANES), jnp.bfloat16),
-        scratch_shapes=[pltpu.VMEM((layout.slots * layout.rows, LANES), jnp.float32)],
+        scratch_shapes=[pltpu.VMEM((layout.slots * layout.pitch, LANES), jnp.float32)],
         compiler_params=pltpu.CompilerParams(vmem_limit_bytes=VMEM),
         cost_estimate=pl.CostEstimate(flops=2 * work, bytes_accessed=8_000_000, transcendentals=0),
         name=f"forward_{chunk}",
@@ -364,16 +382,19 @@
     work = 2 * 2 * layout.slots * NLON * layout.rows * LANES // 2
     operands = list(coeffs) + [cotangent, cotangent] + list(tables) + [real_rows, imag_rows]
     return pl.pallas_call(
-        functools.partial(spectral_kernel, layout, chunk % 2),
+        functools.partial(spectral_kernel, layout),
         grid=(layout.half // PAIRS,),
         in_specs=[whole()] * layout.parts
-        + grid_specs(layout, chunk // 2)
+        + grid_specs(layout, chunk)
         + [whole()] * (len(tables) + 2),
         out_specs=whole(),
         out_shape=jax.ShapeDtypeStruct((layout.degrees, LANES), jnp.float32),
         scratch_shapes=[
-            pltpu.VMEM((layout.slots * layout.rows, LANES), jnp.float32),
+            pltpu.VMEM((layout.slots * layout.pitch, LANES), jnp.float32),
+            pltpu.VMEM((layout.slots * layout.pitch, LANES), jnp.float32),
             pltpu.VMEM((layout.low, layout.degrees, LANES), jnp.bfloat16),
+            pltpu.VMEM((layout.low, layout.degrees, LANES), jnp.bfloat16),
+            pltpu.VMEM((layout.pairs, layout.rows, LANES), jnp.bfloat16),
             pltpu.VMEM((layout.pairs, layout.rows, LANES), jnp.bfloat16),
         ],
         compiler_params=pltpu.CompilerParams(vmem_limit_bytes=VMEM),
@@ -422,7 +443,7 @@
     layout = Layout(parts, fields.shape[1])
     width = LANES // 2
     chunks = fields.shape[-1] // width
-    basis, inverse, inverse_t = (jnp.asarray(a) for a in fourier_constants(parts, layout.local))
+    basis, inverse = (jnp.asarray(a) for a in fourier_constants(parts, layout.local))
     constants = legendre_constants(parts, layout.local)
 
     def local_table(name):
@@ -439,7 +460,8 @@
     synth_low = bands("synth_low", index, 1)
     back_low = jnp.swapaxes(synth_low, 1, 2)
     pair_tables = [local_table(name) for name in ("pair_synth", "pair_back")]
-    tables = [inverse, inverse_t, analysis, synth_low, back_low] + pair_tables + [jnp.asarray(constants["place"])]
+    tables = [inverse, analysis, synth_low, back_low] + pair_tables + [jnp.asarray(constants["place"])]
+    fields, cotangent = jnp.swapaxes(fields, 2, 3), jnp.swapaxes(cotangent, 2, 3)
     real_all = filter_rows(layout, spec_real)
     imag_all = filter_rows(layout, spec_imag)
 

time: 207 us -> 163 us (0.79)
  Pallas kernels: 138 us -> 73.6 us
  waiting for transfers between devices: 7.72 us -> 42.6 us
  local copies, waits for them, and re-layouts: 34 us -> 19.5 us
  starting transfers between devices: 21.8 us -> 24.9 us
  other arithmetic: 3.91 us -> 0.89 us
    pallas_call x6, Pallas kernels: 138 us -> 73.6 us  [the longest x3 59.6 us: spectral_call(): pl.pallas_call(functools.partial(spectral_kernel, layout), grid=(layout.h...]
    ppermute x3, waiting for transfers between devices: 0.01 us -> 36 us  [on_device(): blocks.append(lax.ppermute(own, 'space', route))]
    unnamed x22 -> x28, local copies, waits for them, and re-layouts: 22 us -> 9.39 us
    ppermute x15, starting transfers between devices: 16.8 us -> 19.9 us  [sum_over(): total = total + lax.ppermute(value, axis, pairs)]
    concatenate x3, other arithmetic: 2.57 us -> 0.4 us  [on_device(): real_rows = jnp.concatenate([real, real], axis=1)]
  transfers between devices with their start and end apart: 18 -> 18, of which waited for: 7 -> 9; matrix products, arithmetic and copies ran while one was open for 12% -> 6% of each run, Pallas kernels for 62% -> 42%
where the time goes in v2:
time: 163 us
  Pallas kernels  73.6 us (45%)
  waiting for transfers between devices  42.6 us (26%)
  starting transfers between devices  24.9 us (15%)
  local copies, waits for them, and re-layouts  19.5 us (12%)
    pallas_call x3, Pallas kernels, spectral_call(): pl.pallas_call(functools.partial(spectral_kernel, layout), grid=(layout.h...  59.6 us
    ppermute x3, waiting for transfers between devices, on_device(): blocks.append(lax.ppermute(own, 'space', route))  36 us
    ppermute x15, starting transfers between devices, sum_over(): total = total + lax.ppermute(value, axis, pairs)  19.9 us
    pallas_call x3, Pallas kernels, forward_call(): pl.pallas_call(functools.partial(forward_kernel, layout), grid=(layout.ha...  14 us
    unnamed x28, local copies, waits for them, and re-layouts  9.39 us
    ppermute x15, waiting for transfers between devices, sum_over(): total = total + lax.ppermute(value, axis, pairs)  6.61 us
    dynamic_slice x2, local copies, waits for them, and re-layouts, bands(): lax.dynamic_slice_in_dim(table, first * layout.rows, count * layout.rows, 1)  6.53 us
    ppermute x3, starting transfers between devices, on_device(): blocks.append(lax.ppermute(own, 'space', route))  4.99 us
  transfers between devices with their start and end apart: 18, of which 9 were waited for; matrix products, arithmetic and copies ran while one was open for 6% of the time, Pallas kernels for 42%

profile of v2, /device:TPU:0, one launch (start us, length us, event | category | flops | bytes accessed | tf_op | source)
XLA Modules:
  0.0 162.6 jit_solution(7566632695473890788)
XLA Ops:
  0.6 1.1 dynamic-slice_bitcast_fusion.2.pair_fwd
  1.7 0.0 copy-start
  1.7 2.7 %copy-done = bf16[1,63,252,192]{2,3,1,0:T(8,128)(2,1)S(1)} copy-done((bf16[1,63,252,192]{2,3,1,0:T(8,128)(2,1)S(1)}, bf16[1,63,252,192]{2,3,1,0:T(8,128)(2,1)}, u32[]{:S(2)}) %copy-start) | copy-done | bytes 6096408
  4.5 0.9 copy-done.4
  5.4 4.7 %forward_0.1.refs_0_ = bf16[95,64,128]{2,1,0:T(8,128)(2,1)} custom-call(bf16[1,63,192,252]{3,2,1,0:T(8,128)(2,1)S(1)} %bitcast.10, bf16[1,63,192,252]{3,2,1,0:T(8,128)(2,1)S(1)} %bitcast.11, bf16[256,252]{1,0:T(8,128)(2,1)S(1)} %copy-done.4, bf16[32,64,128]{2,1,0:T(8,128)(2,1)S(1)} %dynamic-slice_bitcast_fusion.2.pair_fwd), custom_call_target="tpu_custom_call" | custom-call | flops 1056964608 | bytes 8000000 | tf_op jit(solution)/shard_map/forward_0/pallas_call | solution.py:368
  10.1 3.0 %collective-permute-start = (bf16[95,64,128]{2,1,0:T(8,128)(2,1)}, bf16[95,64,128]{2,1,0:T(8,128)(2,1)}, u32[]{:S(2)}, u32[]{:S(2)}) collective-permute-start(bf16[95,64,128]{2,1,0:T(8,128)(2,1)} %forward_0.1.refs_0_), channel_id=1, source_target_pairs={{0,1},{1,0},{2,3},{3,2},{4,5},{5,4},{6,7},{7,6},{8,9},{9,8},{10,11... | collective-permute-start | bytes 4669448 | tf_op jit(solution)/shard_map/ppermute | solution.py:474
  13.0 4.7 %forward_1.1.refs_0_ = bf16[95,64,128]{2,1,0:T(8,128)(2,1)} custom-call(bf16[1,63,192,252]{3,2,1,0:T(8,128)(2,1)S(1)} %bitcast.12, bf16[1,63,192,252]{3,2,1,0:T(8,128)(2,1)S(1)} %bitcast.13, bf16[256,252]{1,0:T(8,128)(2,1)S(1)} %copy-done.4, bf16[32,64,128]{2,1,0:T(8,128)(2,1)S(1)} %dynamic-slice_bitcast_fusion.2.pair_fwd), custom_call_target="tpu_custom_call" | custom-call | flops 1056964608 | bytes 8000000 | tf_op jit(solution)/shard_map/forward_1/pallas_call | solution.py:368
  17.7 4.6 %forward_2.1.refs_0_ = bf16[95,64,128]{2,1,0:T(8,128)(2,1)} custom-call(bf16[1,63,192,252]{3,2,1,0:T(8,128)(2,1)S(1)} %bitcast.14, bf16[1,63,192,252]{3,2,1,0:T(8,128)(2,1)S(1)} %bitcast.15, bf16[256,252]{1,0:T(8,128)(2,1)S(1)} %copy-done.4, bf16[32,64,128]{2,1,0:T(8,128)(2,1)S(1)} %dynamic-slice_bitcast_fusion.2.pair_fwd), custom_call_target="tpu_custom_call" | custom-call | flops 1056964608 | bytes 8000000 | tf_op jit(solution)/shard_map/forward_2/pallas_call | solution.py:368
  22.3 2.0 %collective-permute-start.12 = (bf16[95,64,128]{2,1,0:T(8,128)(2,1)}, bf16[95,64,128]{2,1,0:T(8,128)(2,1)}, u32[]{:S(2)}, u32[]{:S(2)}) collective-permute-start(bf16[95,64,128]{2,1,0:T(8,128)(2,1)} %forward_2.1.refs_0_), channel_id=1, source_target_pairs={{0,1},{1,0},{2,3},{3,2},{4,5},{5,4},{6,7},{7,6},{8,9},{9,8},{10,11... | collective-permute-start | bytes 4669448 | tf_op jit(solution)/shard_map/ppermute | solution.py:474
  24.4 2.2 %constant_dynamic-slice_fusion = bf16[63,64,128]{1,2,0:T(8,128)(2,1)S(1)} fusion(bf16[63,128,128]{1,2,0:T(8,128)(2,1)} %constant.51.clone, s32[]{:T(128)S(6)} %select_n.15), kind=kLoop, calls=%fused_computation.20 | loop fusion | bytes 2064388 | tf_op jit(solution)/shard_map/dynamic_slice | solution.py:456
  26.6 0.1 copy.14
  26.8 0.1 rev.6
  26.9 4.3 %constant_dynamic-slice_fusion.1 = bf16[63,128,128]{1,2,0:T(8,128)(2,1)} fusion(bf16[63,256,128]{1,2,0:T(8,128)(2,1)} %constant.50.clone, s32[]{:T(128)S(6)} %select_n.14), kind=kLoop, calls=%fused_computation.21 | loop fusion | bytes 4128772 | tf_op jit(solution)/shard_map/dynamic_slice | solution.py:456
  31.2 0.1 copy.16
  31.3 0.1 rev.7
  31.4 1.9 %copy.18.refs_6_ = bf16[63,64,128]{2,1,0:T(8,128)(2,1)S(1)} copy(bf16[63,64,128]{1,2,0:T(8,128)(2,1)S(1)} %constant_dynamic-slice_fusion) | data formatting | bytes 2064384 | tf_op jit(solution)/shard_map/optimization_barrier | solution.py:455
  33.3 0.0 copy-start.7
  33.3 0.1 fusion.8
  33.5 0.0 copy-start.6
  33.5 0.1 slice_negate_fusion.2
  33.6 0.1 pad_maximum_fusion
  33.7 0.1 pad_maximum_fusion.2
  33.9 0.0 copy-start.3
  33.9 0.0 copy-start.5
  33.9 0.1 pad_maximum_fusion.4
  34.0 0.5 copy-done.7
  34.6 0.7 copy-done.6
  35.3 0.1 dynamic-slice_bitcast_fusion.refs_8_
  35.4 12.9 %collective-permute-done.refs_1_ = bf16[95,64,128]{2,1,0:T(8,128)(2,1)} collective-permute-done((bf16[95,64,128]{2,1,0:T(8,128)(2,1)}, bf16[95,64,128]{2,1,0:T(8,128)(2,1)}, u32[]{:S(2)}, u32[]{:S(2)}) %collective-permute-start) | collective-permute-done | bytes 1556512 | tf_op jit(solution)/shard_map/ppermute | solution.py:474
  48.2 2.7 %copy-done.1 = bf16[1,63,252,192]{2,3,1,0:T(8,128)(2,1)S(1)} copy-done((bf16[1,63,252,192]{2,3,1,0:T(8,128)(2,1)S(1)}, bf16[1,63,252,192]{2,3,1,0:T(8,128)(2,1)}, u32[]{:S(2)}) %copy-start.1) | copy-done | bytes 6096408
  51.0 19.8 %spectral_0.1 = f32[128,128]{1,0:T(8,128)S(1)} custom-call(bf16[95,64,128]{2,1,0:T(8,128)(2,1)} %forward_0.1.refs_0_, bf16[95,64,128]{2,1,0:T(8,128)(2,1)} %collective-permute-done.refs_1_, bf16[1,63,192,252]{3,2,1,0:T(8,128)(2,1)S(1)} %bitcast.16, bf16[1,63,192,252]{3,2,1,0:T(8,128)(2,1)S(1)} %bitcast.17, bf16[256,252]{1,0:T(8,128)(2,1)S(1)} %copy-done.3, ...), custom_call_target="tpu_custom_call" | custom-call | flops 3170893824 | bytes 16000000 | tf_op jit(solution)/shard_map/spectral_0/pallas_call | solution.py:384
  70.8 0.1 collective-permute-start.1
  70.9 10.7 %collective-permute-done.6.refs_1_ = bf16[95,64,128]{2,1,0:T(8,128)(2,1)} collective-permute-done((bf16[95,64,128]{2,1,0:T(8,128)(2,1)}, bf16[95,64,128]{2,1,0:T(8,128)(2,1)}, u32[]{:S(2)}, u32[]{:S(2)}) %collective-permute-start.6) | collective-permute-done | bytes 1556512 | tf_op jit(solution)/shard_map/ppermute | solution.py:474
  81.6 20.0 %spectral_1.1 = f32[128,128]{1,0:T(8,128)S(1)} custom-call(bf16[95,64,128]{2,1,0:T(8,128)(2,1)} %forward_1.1.refs_0_, bf16[95,64,128]{2,1,0:T(8,128)(2,1)} %collective-permute-done.6.refs_1_, bf16[1,63,192,252]{3,2,1,0:T(8,128)(2,1)S(1)} %bitcast.18, bf16[1,63,192,252]{3,2,1,0:T(8,128)(2,1)S(1)} %bitcast.19, bf16[256,252]{1,0:T(8,128)(2,1)S(1)} %copy-done.3, ...), custom_call_target="tpu_custom_call" | custom-call | flops 3170893824 | bytes 16000000 | tf_op jit(solution)/shard_map/spectral_1/pallas_call | solution.py:384
  101.6 0.1 collective-permute-start.7
  101.6 12.5 %collective-permute-done.12.refs_1_ = bf16[95,64,128]{2,1,0:T(8,128)(2,1)} collective-permute-done((bf16[95,64,128]{2,1,0:T(8,128)(2,1)}, bf16[95,64,128]{2,1,0:T(8,128)(2,1)}, u32[]{:S(2)}, u32[]{:S(2)}) %collective-permute-start.12) | collective-permute-done | bytes 1556512 | tf_op jit(solution)/shard_map/ppermute | solution.py:474
  114.1 19.9 %spectral_2.1 = f32[128,128]{1,0:T(8,128)S(1)} custom-call(bf16[95,64,128]{2,1,0:T(8,128)(2,1)} %forward_2.1.refs_0_, bf16[95,64,128]{2,1,0:T(8,128)(2,1)} %collective-permute-done.12.refs_1_, bf16[1,63,192,252]{3,2,1,0:T(8,128)(2,1)S(1)} %bitcast.22, bf16[1,63,192,252]{3,2,1,0:T(8,128)(2,1)S(1)} %bitcast.23, bf16[256,252]{1,0:T(8,128)(2,1)S(1)} %copy-done.3, ...), custom_call_target="tpu_custom_call" | custom-call | flops 3170893824 | bytes 16000000 | tf_op jit(solution)/shard_map/spectral_2/pallas_call | solution.py:384
  134.0 0.1 collective-permute-start.13
  134.1 1.8 %collective-permute-start.2 = (f32[128,128]{1,0:T(8,128)S(1)}, f32[128,128]{1,0:T(8,128)S(1)}, u32[]{:S(2)}, u32[]{:S(2)}) collective-permute-start(f32[128,128]{1,0:T(8,128)S(1)} %add.65), channel_id=1, source_target_pairs={{0,4},{2,6},{4,0},{6,2},{8,12},{10,14},{12,8},{14,10},{16,20},{18,... | collective-permute-start | bytes 196616 | tf_op jit(solution)/shard_map/ppermute | solution.py:426
  135.9 0.4 collective-permute-start.8
  136.3 1.8 %collective-permute-start.14 = (f32[128,128]{1,0:T(8,128)S(1)}, f32[128,128]{1,0:T(8,128)S(1)}, u32[]{:S(2)}, u32[]{:S(2)}) collective-permute-start(f32[128,128]{1,0:T(8,128)S(1)} %add.75), channel_id=1, source_target_pairs={{0,4},{2,6},{4,0},{6,2},{8,12},{10,14},{12,8},{14,10},{16,20},{18,... | collective-permute-start | bytes 196616 | tf_op jit(solution)/shard_map/ppermute | solution.py:426
  138.0 0.6 collective-permute-done.2
  138.6 2.0 %collective-permute-start.3 = (f32[128,128]{1,0:T(8,128)S(1)}, f32[128,128]{1,0:T(8,128)S(1)}, u32[]{:S(2)}, u32[]{:S(2)}) collective-permute-start(f32[128,128]{1,0:T(8,128)S(1)} %add.66), channel_id=1, source_target_pairs={{0,8},{2,10},{4,12},{6,14},{8,0},{10,2},{12,4},{14,6},{16,24},{18,... | collective-permute-start | bytes 196616 | tf_op jit(solution)/shard_map/ppermute | solution.py:426
  140.6 0.2 collective-permute-done.8
  140.8 1.7 %collective-permute-start.9 = (f32[128,128]{1,0:T(8,128)S(1)}, f32[128,128]{1,0:T(8,128)S(1)}, u32[]{:S(2)}, u32[]{:S(2)}) collective-permute-start(f32[128,128]{1,0:T(8,128)S(1)} %add.71), channel_id=1, source_target_pairs={{0,8},{2,10},{4,12},{6,14},{8,0},{10,2},{12,4},{14,6},{16,24},{18,... | collective-permute-start | bytes 196616 | tf_op jit(solution)/shard_map/ppermute | solution.py:426
  142.5 0.8 collective-permute-start.15
  143.3 0.0 collective-permute-done.3
  143.3 3.3 %collective-permute-start.4 = (f32[128,128]{1,0:T(8,128)S(1)}, f32[128,128]{1,0:T(8,128)S(1)}, u32[]{:S(2)}, u32[]{:S(2)}) collective-permute-start(f32[128,128]{1,0:T(8,128)S(1)} %add.67), channel_id=1, source_target_pairs={{0,16},{2,18},{4,20},{6,22},{8,24},{10,26},{12,28},{14,30},{16,0},... | collective-permute-start | bytes 196616 | tf_op jit(solution)/shard_map/ppermute | solution.py:426
  146.7 1.9 %collective-permute-start.10 = (f32[128,128]{1,0:T(8,128)S(1)}, f32[128,128]{1,0:T(8,128)S(1)}, u32[]{:S(2)}, u32[]{:S(2)}) collective-permute-start(f32[128,128]{1,0:T(8,128)S(1)} %add.72), channel_id=1, source_target_pairs={{0,16},{2,18},{4,20},{6,22},{8,24},{10,26},{12,28},{14,30},{16,0},... | collective-permute-start | bytes 196616 | tf_op jit(solution)/shard_map/ppermute | solution.py:426
  148.6 1.1 collective-permute-start.16
  149.8 1.7 %collective-permute-done.4 = f32[128,128]{1,0:T(8,128)S(1)} collective-permute-done((f32[128,128]{1,0:T(8,128)S(1)}, f32[128,128]{1,0:T(8,128)S(1)}, u32[]{:S(2)}, u32[]{:S(2)}) %collective-permute-start.4) | collective-permute-done | bytes 65568 | tf_op jit(solution)/shard_map/ppermute | solution.py:426
  151.5 2.2 %collective-permute-start.5 = (f32[128,128]{1,0:T(8,128)S(1)}, f32[128,128]{1,0:T(8,128)S(1)}, u32[]{:S(2)}, u32[]{:S(2)}) collective-permute-start(f32[128,128]{1,0:T(8,128)S(1)} %add.68), channel_id=1, source_target_pairs={{0,1},{1,0},{2,3},{3,2},{4,5},{5,4},{6,7},{7,6},{8,9},{9,8},{10,11... | collective-permute-start | bytes 196616 | tf_op jit(solution)/shard_map/ppermute | solution.py:426
  153.7 0.6 collective-permute-done.10
  154.3 2.1 %collective-permute-start.11 = (f32[128,128]{1,0:T(8,128)S(1)}, f32[128,128]{1,0:T(8,128)S(1)}, u32[]{:S(2)}, u32[]{:S(2)}) collective-permute-start(f32[128,128]{1,0:T(8,128)S(1)} %add.73), channel_id=1, source_target_pairs={{0,1},{1,0},{2,3},{3,2},{4,5},{5,4},{6,7},{7,6},{8,9},{9,8},{10,11... | collective-permute-start | bytes 196616 | tf_op jit(solution)/shard_map/ppermute | solution.py:426
  156.4 0.7 collective-permute-start.17
  157.1 0.1 fusion.9
  157.2 1.8 %collective-permute-done.11 = f32[128,128]{1,0:T(8,128)S(1)} collective-permute-done((f32[128,128]{1,0:T(8,128)S(1)}, f32[128,128]{1,0:T(8,128)S(1)}, u32[]{:S(2)}, u32[]{:S(2)}) %collective-permute-start.11) | collective-permute-done | bytes 65568 | tf_op jit(solution)/shard_map/ppermute | solution.py:426
  159.0 0.1 fusion.10
  159.1 1.7 %collective-permute-done.17 = f32[128,128]{1,0:T(8,128)S(1)} collective-permute-done((f32[128,128]{1,0:T(8,128)S(1)}, f32[128,128]{1,0:T(8,128)S(1)}, u32[]{:S(2)}, u32[]{:S(2)}) %collective-permute-start.17) | collective-permute-done | bytes 65568 | tf_op jit(solution)/shard_map/ppermute | solution.py:426
  160.8 0.1 fusion.11
  160.8 0.1 maximum_multiply_fusion.1
  161.0 0.7 copy.22
  161.7 0.1 maximum_multiply_fusion
  161.8 0.7 copy.21
  (44 shorter events, 0.3 us)
Async XLA Ops:
  1.7 2.8 %copy-start = (bf16[1,63,252,192]{2,3,1,0:T(8,128)(2,1)S(1)}, bf16[1,63,252,192]{2,3,1,0:T(8,128)(2,1)}, u32[]{:S(2)}) copy-start(bf16[1,63,252,192]{2,3,1,0:T(8,128)(2,1)} %param.12) | copy-start | bytes 18289156
  4.5 0.9 copy-start.4
  10.1 38.2 %collective-permute-start = (bf16[95,64,128]{2,1,0:T(8,128)(2,1)}, bf16[95,64,128]{2,1,0:T(8,128)(2,1)}, u32[]{:S(2)}, u32[]{:S(2)}) collective-permute-start(bf16[95,64,128]{2,1,0:T(8,128)(2,1)} %forward_0.1.refs_0_), channel_id=1, source_target_pairs={{0,1},{1,0},{2,3},{3,2},{4,5},{5,4},{6,7},{7,6},{8,9},{9,8},{10,11... | collective-permute-start | bytes 4669448 | tf_op jit(solution)/shard_map/ppermute | solution.py:474
  17.7 63.9 %collective-permute-start.6 = (bf16[95,64,128]{2,1,0:T(8,128)(2,1)}, bf16[95,64,128]{2,1,0:T(8,128)(2,1)}, u32[]{:S(2)}, u32[]{:S(2)}) collective-permute-start(bf16[95,64,128]{2,1,0:T(8,128)(2,1)} %forward_1.1.refs_0_), channel_id=1, source_target_pairs={{0,1},{1,0},{2,3},{3,2},{4,5},{5,4},{6,7},{7,6},{8,9},{9,8},{10,11... | collective-permute-start | bytes 4669448 | tf_op jit(solution)/shard_map/ppermute | solution.py:474
  22.3 91.8 %collective-permute-start.12 = (bf16[95,64,128]{2,1,0:T(8,128)(2,1)}, bf16[95,64,128]{2,1,0:T(8,128)(2,1)}, u32[]{:S(2)}, u32[]{:S(2)}) collective-permute-start(bf16[95,64,128]{2,1,0:T(8,128)(2,1)} %forward_2.1.refs_0_), channel_id=1, source_target_pairs={{0,1},{1,0},{2,3},{3,2},{4,5},{5,4},{6,7},{7,6},{8,9},{9,8},{10,11... | collective-permute-start | bytes 4669448 | tf_op jit(solution)/shard_map/ppermute | solution.py:474
  24.4 2.2 %copy-start.8 = (bf16[126,192]{0,1:T(8,128)(2,1)S(1)}, bf16[126,192]{0,1:T(8,128)(2,1)}, u32[]{:S(2)}) copy-start(bf16[126,192]{0,1:T(8,128)(2,1)} %param.14) | copy-start | bytes 145156
  26.9 4.3 %copy-start.9 = (bf16[126,192]{0,1:T(8,128)(2,1)S(1)}, bf16[126,192]{0,1:T(8,128)(2,1)}, u32[]{:S(2)}) copy-start(bf16[126,192]{0,1:T(8,128)(2,1)} %param.15) | copy-start | bytes 145156
  33.3 1.2 copy-start.7
  33.5 1.8 %copy-start.6 = (bf16[2,32,128,64]{3,2,1,0:T(8,128)(2,1)S(1)}, bf16[2,32,128,64]{3,2,1,0:T(8,128)(2,1)}, u32[]{:S(2)}) copy-start(bf16[2,32,128,64]{3,2,1,0:T(8,128)(2,1)} %constant.52.clone) | copy-start | bytes 3145732
  33.9 14.3 %copy-start.2 = (bf16[63,128,128]{1,2,0:T(8,128)(2,1)S(1)}, bf16[63,128,128]{1,2,0:T(8,128)(2,1)}, u32[]{:S(2)}) copy-start(bf16[63,128,128]{1,2,0:T(8,128)(2,1)} %constant_dynamic-slice_fusion.1) | copy-start | bytes 6193156
  33.9 14.3 %copy-start.3 = (bf16[256,252]{1,0:T(8,128)(2,1)S(1)}, bf16[256,252]{1,0:T(8,128)(2,1)}, u32[]{:S(2)}) copy-start(bf16[256,252]{1,0:T(8,128)(2,1)} %constant.48.clone.refs_4_) | copy-start | bytes 387076
  33.9 14.3 %copy-start.5 = (f32[128,128]{1,0:T(8,128)S(1)}, f32[128,128]{1,0:T(8,128)}, u32[]{:S(2)}) copy-start(f32[128,128]{1,0:T(8,128)} %constant.54.clone.refs_10_) | copy-start | bytes 196612
  48.2 2.8 %copy-start.1 = (bf16[1,63,252,192]{2,3,1,0:T(8,128)(2,1)S(1)}, bf16[1,63,252,192]{2,3,1,0:T(8,128)(2,1)}, u32[]{:S(2)}) copy-start(bf16[1,63,252,192]{2,3,1,0:T(8,128)(2,1)} %param.13) | copy-start | bytes 18289156
  70.8 63.2 %collective-permute-start.1 = (f32[128,128]{1,0:T(8,128)S(1)}, f32[128,128]{1,0:T(8,128)S(1)}, u32[]{:S(2)}, u32[]{:S(2)}) collective-permute-start(f32[128,128]{1,0:T(8,128)S(1)} %spectral_0.1), channel_id=1, source_target_pairs={{0,2},{2,0},{4,6},{6,4},{8,10},{10,8},{12,14},{14,12},{16,18},{18,... | collective-permute-start | bytes 196616 | tf_op jit(solution)/shard_map/ppermute | solution.py:426
  81.6 32.5 %slice-start = ((s8[6193152]{0:T(1024)(128)(4,1)}), s8[4194304]{0:T(1024)(128)(4,1)S(1)}, s32[]{:S(2)}) async-start(s8[6193152]{0:T(1024)(128)(4,1)} %bitcast.20), calls=%async_computation | async-start | bytes 8388608
  81.6 32.5 %slice-start.1 = ((s8[6193152]{0:T(1024)(128)(4,1)}), s8[1998848]{0:T(1024)(128)(4,1)S(1)}, s32[]{:S(2)}) async-start(s8[6193152]{0:T(1024)(128)(4,1)} %bitcast.20), calls=%async_computation.1 | async-start | bytes 3997696
  101.6 34.3 %collective-permute-start.7 = (f32[128,128]{1,0:T(8,128)S(1)}, f32[128,128]{1,0:T(8,128)S(1)}, u32[]{:S(2)}, u32[]{:S(2)}) collective-permute-start(f32[128,128]{1,0:T(8,128)S(1)} %spectral_1.1), channel_id=1, source_target_pairs={{0,2},{2,0},{4,6},{6,4},{8,10},{10,8},{12,14},{14,12},{16,18},{18,... | collective-permute-start | bytes 196616 | tf_op jit(solution)/shard_map/ppermute | solution.py:426
  134.0 2.3 %collective-permute-start.13 = (f32[128,128]{1,0:T(8,128)S(1)}, f32[128,128]{1,0:T(8,128)S(1)}, u32[]{:S(2)}, u32[]{:S(2)}) collective-permute-start(f32[128,128]{1,0:T(8,128)S(1)} %spectral_2.1), channel_id=1, source_target_pairs={{0,2},{2,0},{4,6},{6,4},{8,10},{10,8},{12,14},{14,12},{16,18},{18,... | collective-permute-start | bytes 196616 | tf_op jit(solution)/shard_map/ppermute | solution.py:426
  134.1 4.5 %collective-permute-start.2 = (f32[128,128]{1,0:T(8,128)S(1)}, f32[128,128]{1,0:T(8,128)S(1)}, u32[]{:S(2)}, u32[]{:S(2)}) collective-permute-start(f32[128,128]{1,0:T(8,128)S(1)} %add.65), channel_id=1, source_target_pairs={{0,4},{2,6},{4,0},{6,2},{8,12},{10,14},{12,8},{14,10},{16,20},{18,... | collective-permute-start | bytes 196616 | tf_op jit(solution)/shard_map/ppermute | solution.py:426
  135.9 5.0 %collective-permute-start.8 = (f32[128,128]{1,0:T(8,128)S(1)}, f32[128,128]{1,0:T(8,128)S(1)}, u32[]{:S(2)}, u32[]{:S(2)}) collective-permute-start(f32[128,128]{1,0:T(8,128)S(1)} %add.70), channel_id=1, source_target_pairs={{0,4},{2,6},{4,0},{6,2},{8,12},{10,14},{12,8},{14,10},{16,20},{18,... | collective-permute-start | bytes 196616 | tf_op jit(solution)/shard_map/ppermute | solution.py:426
  136.3 6.3 %collective-permute-start.14 = (f32[128,128]{1,0:T(8,128)S(1)}, f32[128,128]{1,0:T(8,128)S(1)}, u32[]{:S(2)}, u32[]{:S(2)}) collective-permute-start(f32[128,128]{1,0:T(8,128)S(1)} %add.75), channel_id=1, source_target_pairs={{0,4},{2,6},{4,0},{6,2},{8,12},{10,14},{12,8},{14,10},{16,20},{18,... | collective-permute-start | bytes 196616 | tf_op jit(solution)/shard_map/ppermute | solution.py:426
  138.6 4.7 %collective-permute-start.3 = (f32[128,128]{1,0:T(8,128)S(1)}, f32[128,128]{1,0:T(8,128)S(1)}, u32[]{:S(2)}, u32[]{:S(2)}) collective-permute-start(f32[128,128]{1,0:T(8,128)S(1)} %add.66), channel_id=1, source_target_pairs={{0,8},{2,10},{4,12},{6,14},{8,0},{10,2},{12,4},{14,6},{16,24},{18,... | collective-permute-start | bytes 196616 | tf_op jit(solution)/shard_map/ppermute | solution.py:426
  140.8 5.8 %collective-permute-start.9 = (f32[128,128]{1,0:T(8,128)S(1)}, f32[128,128]{1,0:T(8,128)S(1)}, u32[]{:S(2)}, u32[]{:S(2)}) collective-permute-start(f32[128,128]{1,0:T(8,128)S(1)} %add.71), channel_id=1, source_target_pairs={{0,8},{2,10},{4,12},{6,14},{8,0},{10,2},{12,4},{14,6},{16,24},{18,... | collective-permute-start | bytes 196616 | tf_op jit(solution)/shard_map/ppermute | solution.py:426
  142.5 6.1 %collective-permute-start.15 = (f32[128,128]{1,0:T(8,128)S(1)}, f32[128,128]{1,0:T(8,128)S(1)}, u32[]{:S(2)}, u32[]{:S(2)}) collective-permute-start(f32[128,128]{1,0:T(8,128)S(1)} %add.76), channel_id=1, source_target_pairs={{0,8},{2,10},{4,12},{6,14},{8,0},{10,2},{12,4},{14,6},{16,24},{18,... | collective-permute-start | bytes 196616 | tf_op jit(solution)/shard_map/ppermute | solution.py:426
  143.3 8.1 %collective-permute-start.4 = (f32[128,128]{1,0:T(8,128)S(1)}, f32[128,128]{1,0:T(8,128)S(1)}, u32[]{:S(2)}, u32[]{:S(2)}) collective-permute-start(f32[128,128]{1,0:T(8,128)S(1)} %add.67), channel_id=1, source_target_pairs={{0,16},{2,18},{4,20},{6,22},{8,24},{10,26},{12,28},{14,30},{16,0},... | collective-permute-start | bytes 196616 | tf_op jit(solution)/shard_map/ppermute | solution.py:426
  146.7 7.6 %collective-permute-start.10 = (f32[128,128]{1,0:T(8,128)S(1)}, f32[128,128]{1,0:T(8,128)S(1)}, u32[]{:S(2)}, u32[]{:S(2)}) collective-permute-start(f32[128,128]{1,0:T(8,128)S(1)} %add.72), channel_id=1, source_target_pairs={{0,16},{2,18},{4,20},{6,22},{8,24},{10,26},{12,28},{14,30},{16,0},... | collective-permute-start | bytes 196616 | tf_op jit(solution)/shard_map/ppermute | solution.py:426
  148.6 7.8 %collective-permute-start.16 = (f32[128,128]{1,0:T(8,128)S(1)}, f32[128,128]{1,0:T(8,128)S(1)}, u32[]{:S(2)}, u32[]{:S(2)}) collective-permute-start(f32[128,128]{1,0:T(8,128)S(1)} %add.77), channel_id=1, source_target_pairs={{0,16},{2,18},{4,20},{6,22},{8,24},{10,26},{12,28},{14,30},{16,0},... | collective-permute-start | bytes 196616 | tf_op jit(solution)/shard_map/ppermute | solution.py:426
  151.5 5.6 %collective-permute-start.5 = (f32[128,128]{1,0:T(8,128)S(1)}, f32[128,128]{1,0:T(8,128)S(1)}, u32[]{:S(2)}, u32[]{:S(2)}) collective-permute-start(f32[128,128]{1,0:T(8,128)S(1)} %add.68), channel_id=1, source_target_pairs={{0,1},{1,0},{2,3},{3,2},{4,5},{5,4},{6,7},{7,6},{8,9},{9,8},{10,11... | collective-permute-start | bytes 196616 | tf_op jit(solution)/shard_map/ppermute | solution.py:426
  154.3 4.7 %collective-permute-start.11 = (f32[128,128]{1,0:T(8,128)S(1)}, f32[128,128]{1,0:T(8,128)S(1)}, u32[]{:S(2)}, u32[]{:S(2)}) collective-permute-start(f32[128,128]{1,0:T(8,128)S(1)} %add.73), channel_id=1, source_target_pairs={{0,1},{1,0},{2,3},{3,2},{4,5},{5,4},{6,7},{7,6},{8,9},{9,8},{10,11... | collective-permute-start | bytes 196616 | tf_op jit(solution)/shard_map/ppermute | solution.py:426
  156.4 4.3 %collective-permute-start.17 = (f32[128,128]{1,0:T(8,128)S(1)}, f32[128,128]{1,0:T(8,128)S(1)}, u32[]{:S(2)}, u32[]{:S(2)}) collective-permute-start(f32[128,128]{1,0:T(8,128)S(1)} %add.78), channel_id=1, source_target_pairs={{0,1},{1,0},{2,3},{3,2},{4,5},{5,4},{6,7},{7,6},{8,9},{9,8},{10,11... | collective-permute-start | bytes 196616 | tf_op jit(solution)/shard_map/ppermute | solution.py:426

commit v3 on v2

--- a/solution.py
+++ b/solution.py
@@ -17,6 +17,7 @@
 GROUP = 16
 PAIRS = 8
 VMEM = 30 * 1024 * 1024
+FORWARD_VMEM = 56 * 1024 * 1024
 
 
 def round_up(value, step):
@@ -198,32 +199,69 @@
     return jnp.concatenate(parts, axis=0).astype(jnp.bfloat16)
 
 
-def forward_kernel(layout, north, south, basis, pair_fwd, out, scratch):
-    group = pl.program_id(0)
-    for quad in range(PAIRS // 2):
-        grid = grid_rows(layout, north, south, quad, group)
-        scatter_rows(layout, dot(basis[...], grid, (1, 1)), scratch, quad, group)
-
-    @pl.when(group == pl.num_programs(0) - 1)
-    def _():
-        def low_block(order, carry):
-            out[order] = order_rows(layout, scratch, order, 1)
-            return carry
-
-        def pair_block(pair, carry):
-            values = order_rows(layout, scratch, layout.low + 2 * pair, 2)
-            out[layout.low + pair] = dot(pair_fwd[pair], values).astype(jnp.bfloat16)
-            return carry
-
-        lax.fori_loop(0, layout.low, low_block, 0, unroll=8)
-        lax.fori_loop(0, layout.pairs, pair_block, 0, unroll=8)
+def band_copies(layout, chunk, fields, buffer, sems):
+    width = LANES // 2
+    copies = []
+    for group in range(layout.half // PAIRS):
+        started = []
+        for side in range(2):
+            first = side * layout.half + group * PAIRS
+            count = min(PAIRS, layout.local - first)
+            if count > 0:
+                started.append(
+                    pltpu.make_async_copy(
+                        fields.at[0, pl.ds(first, count), pl.ds(chunk * width, width), :],
+                        buffer.at[pl.ds(first, count)],
+                        sems.at[2 * group + side],
+                    )
+                )
+        copies.append(started)
+    return copies
+
+
+def forward_kernel(layout, chunk, index, fields, basis, pair_all, out, scratch, buffer, pair_fwd, sems, pair_sem):
+    copies = band_copies(layout, chunk, fields, buffer, sems)
+    for started in copies:
+        for copy in started:
+            copy.start()
+    tables = pltpu.make_async_copy(pair_all.at[index[0]], pair_fwd, pair_sem)
+    tables.start()
+    if layout.rows > layout.local:
+        shape = (layout.rows - layout.local,) + buffer.shape[1:]
+        buffer[layout.local :] = jnp.zeros(shape, buffer.dtype)
+    for group, started in enumerate(copies):
+        for copy in started:
+            copy.wait()
+        for quad in range(PAIRS // 2):
+            rows = []
+            for which in range(2):
+                latitude = group * PAIRS + 2 * quad + which
+                rows += [buffer[latitude], buffer[latitude + layout.half]]
+            grid = jnp.concatenate(rows, axis=0)
+            scatter_rows(layout, dot(basis[...], grid, (1, 1)), scratch, quad, group)
+    tables.wait()
+
+    def low_block(order, carry):
+        out[order] = order_rows(layout, scratch, order, 1)
+        return carry
+
+    def pair_block(pair, carry):
+        values = order_rows(layout, scratch, layout.low + 2 * pair, 2)
+        out[layout.low + pair] = dot(pair_fwd[pair], values).astype(jnp.bfloat16)
+        return carry
+
+    lax.fori_loop(0, layout.low, low_block, 0, unroll=8)
+    lax.fori_loop(0, layout.pairs, pair_block, 0, unroll=8)
 
 
 def mix(spectral, swapped, real_rows, imag_rows):
     return (spectral * real_rows + swapped * imag_rows).astype(jnp.bfloat16)
 
 
-def spectral_kernel(layout, *refs):
+def spectral_kernel(layout, carries, *refs):
+    ahead = None
+    if carries:
+        ahead, refs = refs[0], refs[1:]
     own, others = refs[0], refs[1 : layout.parts]
     north, south, basis, analysis, synth_low, back_low = refs[layout.parts : layout.parts + 6]
     pair_synth, pair_back, place, real_ref, imag_ref = refs[layout.parts + 6 : layout.parts + 11]
@@ -346,7 +384,10 @@
         real = same + swap_halves(same)
         imag = cross - swap_halves(cross)
         lane = lax.broadcasted_iota(jnp.int32, real.shape, 1)
-        out[...] = jnp.where(lane < LANES // 2, real, imag)
+        grads = jnp.where(lane < LANES // 2, real, imag)
+        out[out.shape[0] - LANES :, :] = grads.T
+        if ahead is not None:
+            out[: out.shape[0] - LANES, :] = ahead[...]
 
 
 def grid_specs(layout, chunk):
@@ -363,32 +404,46 @@
     return pl.BlockSpec(memory_space=pltpu.VMEM)
 
 
-def forward_call(layout, chunk, fields, basis, pair_fwd):
+def forward_call(layout, chunk, index, fields, basis, pair_fwd):
     work = 2 * 2 * layout.slots * NLON * layout.rows * LANES // 2
+    groups = layout.half // PAIRS
     return pl.pallas_call(
-        functools.partial(forward_kernel, layout),
-        grid=(layout.half // PAIRS,),
-        in_specs=grid_specs(layout, chunk) + [whole()] * 2,
+        functools.partial(forward_kernel, layout, chunk),
+        in_specs=[
+            pl.BlockSpec(memory_space=pltpu.SMEM),
+            pl.BlockSpec(memory_space=pl.ANY),
+            whole(),
+            pl.BlockSpec(memory_space=pl.ANY),
+        ],
         out_specs=whole(),
         out_shape=jax.ShapeDtypeStruct((layout.blocks, layout.rows, LANES), jnp.bfloat16),
-        scratch_shapes=[pltpu.VMEM((layout.slots * layout.pitch, LANES), jnp.float32)],
-        compiler_params=pltpu.CompilerParams(vmem_limit_bytes=VMEM),
+        scratch_shapes=[
+            pltpu.VMEM((layout.slots * layout.pitch, LANES), jnp.float32),
+            pltpu.VMEM((layout.rows, LANES // 2, NLON), jnp.bfloat16),
+            pltpu.VMEM(pair_fwd.shape[1:], jnp.bfloat16),
+            pltpu.SemaphoreType.DMA((2 * groups,)),
+            pltpu.SemaphoreType.DMA,
+        ],
+        compiler_params=pltpu.CompilerParams(vmem_limit_bytes=FORWARD_VMEM),
         cost_estimate=pl.CostEstimate(flops=2 * work, bytes_accessed=8_000_000, transcendentals=0),
         name=f"forward_{chunk}",
-    )(fields, fields, basis, pair_fwd)
-
-
-def spectral_call(layout, chunk, coeffs, cotangent, tables, real_rows, imag_rows):
+    )(index, fields, basis, pair_fwd)
+
+
+def spectral_call(layout, chunk, coeffs, cotangent, tables, real_rows, imag_rows, ahead=None):
     work = 2 * 2 * layout.slots * NLON * layout.rows * LANES // 2
     operands = list(coeffs) + [cotangent, cotangent] + list(tables) + [real_rows, imag_rows]
+    specs = [whole()] * layout.parts + grid_specs(layout, chunk) + [whole()] * (len(tables) + 2)
+    height = LANES
+    if ahead is not None:
+        operands, specs = [ahead] + operands, [whole()] + specs
+        height += ahead.shape[0]
     return pl.pallas_call(
-        functools.partial(spectral_kernel, layout),
+        functools.partial(spectral_kernel, layout, ahead is not None),
         grid=(layout.half // PAIRS,),
-        in_specs=[whole()] * layout.parts
-        + grid_specs(layout, chunk)
-        + [whole()] * (len(tables) + 2),
+        in_specs=specs,
         out_specs=whole(),
-        out_shape=jax.ShapeDtypeStruct((layout.degrees, LANES), jnp.float32),
+        out_shape=jax.ShapeDtypeStruct((height, layout.degrees), jnp.float32),
         scratch_shapes=[
             pltpu.VMEM((layout.slots * layout.pitch, LANES), jnp.float32),
             pltpu.VMEM((layout.slots * layout.pitch, LANES), jnp.float32),
@@ -449,7 +504,8 @@
     def local_table(name):
         return lax.dynamic_index_in_dim(jnp.asarray(constants[name]), index, keepdims=False)
 
-    pair_fwd = local_table("pair_fwd")
+    pair_fwd = jnp.asarray(constants["pair_fwd"])
+    place = jnp.reshape(index, (1,)).astype(jnp.int32)
     def bands(name, first, count):
         table = jnp.asarray(constants[name])
         return lax.optimization_barrier(
@@ -467,26 +523,32 @@
 
     received = []
     for chunk in range(chunks):
-        own = forward_call(layout, chunk, fields, basis, pair_fwd)
+        own = forward_call(layout, chunk, place, fields, basis, pair_fwd)
         blocks = [own]
         for shift in range(1, parts):
             route = [(source, (source + shift) % parts) for source in range(parts)]
             blocks.append(lax.ppermute(own, "space", route))
         received.append(blocks)
 
-    totals = []
+    totals, ahead = [], None
     for chunk in range(chunks):
         columns = slice(chunk * width, (chunk + 1) * width)
         real, imag = real_all[:, columns], imag_all[:, columns]
         real_rows = jnp.concatenate([real, real], axis=1)
         imag_rows = jnp.concatenate([-imag, imag], axis=1)
-        grads = spectral_call(layout, chunk, received[chunk], cotangent, tables, real_rows, imag_rows)
-        totals.append(sum_over(sum_over(grads, "dp"), "space"))
+        coeffs = received[chunk]
+        if totals:
+            coeffs[0], totals[-1] = lax.optimization_barrier((coeffs[0], totals[-1]))
+        grads = spectral_call(layout, chunk, coeffs, cotangent, tables, real_rows, imag_rows, ahead)
+        if chunk == chunks - 2:
+            ahead = grads
+        else:
+            totals.append(sum_over(sum_over(grads, "dp"), "space"))
 
     batch_total = fields.shape[0] * lax.axis_size("dp")
-    real = jnp.concatenate([total[:MODES, :width] for total in totals], axis=1)
-    imag = jnp.concatenate([total[:MODES, width:] for total in totals], axis=1)
-    return (real / batch_total, imag / batch_total)
+    rows = jnp.concatenate(totals, axis=0).reshape(chunks, 2, width, layout.degrees)
+    real, imag = (rows[:, part, :, :MODES].reshape(chunks * width, MODES) for part in range(2))
+    return (real.T / batch_total, imag.T / batch_total)
 
 
 def solution(mesh):

time: 163 us -> 177 us (1.086)
  waiting for transfers between devices: 42.6 us -> 58.4 us
  Pallas kernels: 73.6 us -> 77.8 us
  local copies, waits for them, and re-layouts: 19.5 us -> 15.8 us
  starting transfers between devices: 24.9 us -> 22.5 us
    ppermute x15 -> x10, waiting for transfers between devices: 6.61 us -> 50.2 us  [sum_over(): total = total + lax.ppermute(value, axis, pairs)]
    ppermute x3, waiting for transfers between devices: 36 us -> 8.19 us  [on_device(): blocks.append(lax.ppermute(own, 'space', route))]
    unnamed x28, local copies, waits for them, and re-layouts: 9.39 us -> 4.45 us
    pallas_call x6, Pallas kernels: 73.6 us -> 77.8 us  [the longest x3 58.7 us: spectral_call(): pl.pallas_call(functools.partial(spectral_kernel, layout, ahead is not No...]
    ppermute x15 -> x10, starting transfers between devices: 19.9 us -> 17.3 us  [sum_over(): total = total + lax.ppermute(value, axis, pairs)]
  transfers between devices with their start and end apart: 18 -> 13, of which waited for: 9 -> 11; matrix products, arithmetic and copies ran while one was open for 6% -> 7% of each run, Pallas kernels for 42% -> 29%
where the time goes in v3:
time: 177 us
  Pallas kernels  77.8 us (44%)
  waiting for transfers between devices  58.4 us (33%)
  starting transfers between devices  22.5 us (13%)
  local copies, waits for them, and re-layouts  15.8 us (9%)
    pallas_call x3, Pallas kernels, spectral_call(): pl.pallas_call(functools.partial(spectral_kernel, layout, ahead is not No...  58.7 us
    ppermute x10, waiting for transfers between devices, sum_over(): total = total + lax.ppermute(value, axis, pairs)  50.2 us
    pallas_call x3, Pallas kernels, forward_call(): pl.pallas_call(functools.partial(forward_kernel, layout, chunk), in_specs...  19.1 us
    ppermute x10, starting transfers between devices, sum_over(): total = total + lax.ppermute(value, axis, pairs)  17.3 us
    ppermute x3, waiting for transfers between devices, on_device(): blocks.append(lax.ppermute(own, 'space', route))  8.19 us
    dynamic_slice x2, local copies, waits for them, and re-layouts, bands(): lax.dynamic_slice_in_dim(table, first * layout.rows, count * layout.rows, 1)  6.47 us
    ppermute x3, starting transfers between devices, on_device(): blocks.append(lax.ppermute(own, 'space', route))  5.18 us
    unnamed x28, local copies, waits for them, and re-layouts  4.45 us
  transfers between devices with their start and end apart: 13, of which 11 were waited for; matrix products, arithmetic and copies ran while one was open for 7% of the time, Pallas kernels for 29%

profile of v3, /device:TPU:0, one launch (start us, length us, event | category | flops | bytes accessed | tf_op | source)
XLA Modules:
  0.0 176.9 jit_solution(2189370972034171215)
XLA Ops:
  0.6 6.3 %forward_0.1.refs_0_ = bf16[95,64,128]{2,1,0:T(8,128)(2,1)} custom-call(s32[1]{0:T(128)} %bitcast.index, bf16[1,63,192,252]{3,2,1,0:T(8,128)(2,1)} %bitcast.30, bf16[256,252]{1,0:T(8,128)(2,1)} %constant.45.clone.basis, bf16[2,32,64,128]{3,2,1,0:T(8,128)(2,1)} %constant.47.clone.pair_all), custom_call_target="tpu_custom_call" | custom-call | flops 1056964608 | bytes 8000000 | tf_op jit(solution)/shard_map/forward_0/pallas_call | solution.py:410
  7.0 3.0 %collective-permute-start = (bf16[95,64,128]{2,1,0:T(8,128)(2,1)}, bf16[95,64,128]{2,1,0:T(8,128)(2,1)}, u32[]{:S(2)}, u32[]{:S(2)}) collective-permute-start(bf16[95,64,128]{2,1,0:T(8,128)(2,1)} %forward_0.1.refs_0_), channel_id=1, source_target_pairs={{0,1},{1,0},{2,3},{3,2},{4,5},{5,4},{6,7},{7,6},{8,9},{9,8},{10,11... | collective-permute-start | bytes 4669448 | tf_op jit(solution)/shard_map/ppermute | solution.py:530
  10.0 6.4 %forward_1.1.refs_0_ = bf16[95,64,128]{2,1,0:T(8,128)(2,1)} custom-call(s32[1]{0:T(128)} %bitcast.index, bf16[1,63,192,252]{3,2,1,0:T(8,128)(2,1)} %bitcast.31, bf16[256,252]{1,0:T(8,128)(2,1)} %constant.45.clone.basis, bf16[2,32,64,128]{3,2,1,0:T(8,128)(2,1)} %constant.47.clone.pair_all), custom_call_target="tpu_custom_call" | custom-call | flops 1056964608 | bytes 8000000 | tf_op jit(solution)/shard_map/forward_1/pallas_call | solution.py:410
  16.4 0.0 copy-start.9
  16.4 0.0 copy-start.10
  16.4 0.1 collective-permute-start.6
  16.5 6.4 %forward_2.1.refs_1_ = bf16[95,64,128]{2,1,0:T(8,128)(2,1)} custom-call(s32[1]{0:T(128)} %bitcast.index, bf16[1,63,192,252]{3,2,1,0:T(8,128)(2,1)} %bitcast.32, bf16[256,252]{1,0:T(8,128)(2,1)} %constant.45.clone.basis, bf16[2,32,64,128]{3,2,1,0:T(8,128)(2,1)} %constant.47.clone.pair_all), custom_call_target="tpu_custom_call" | custom-call | flops 1056964608 | bytes 8000000 | tf_op jit(solution)/shard_map/forward_2/pallas_call | solution.py:410
  22.9 2.1 %collective-permute-start.7 = (bf16[95,64,128]{2,1,0:T(8,128)(2,1)}, bf16[95,64,128]{2,1,0:T(8,128)(2,1)}, u32[]{:S(2)}, u32[]{:S(2)}) collective-permute-start(bf16[95,64,128]{2,1,0:T(8,128)(2,1)} %forward_2.1.refs_1_), channel_id=1, source_target_pairs={{0,1},{1,0},{2,3},{3,2},{4,5},{5,4},{6,7},{7,6},{8,9},{9,8},{10,11... | collective-permute-start | bytes 4669448 | tf_op jit(solution)/shard_map/ppermute | solution.py:530
  24.9 0.0 copy-done.9
  24.9 0.1 copy.16
  25.1 0.1 rev.7
  25.2 0.0 copy-done.10
  25.2 0.1 copy.14
  25.3 0.1 rev.6
  25.4 2.2 %constant_dynamic-slice_fusion = bf16[63,64,128]{1,2,0:T(8,128)(2,1)S(1)} fusion(bf16[63,128,128]{1,2,0:T(8,128)(2,1)} %constant.49.clone, s32[]{:T(128)S(6)} %select_n.13), kind=kLoop, calls=%fused_computation.20 | loop fusion | bytes 2064388 | tf_op jit(solution)/shard_map/dynamic_slice | solution.py:512
  27.7 1.9 %copy.18.refs_6_.refs_7_ = bf16[63,64,128]{2,1,0:T(8,128)(2,1)S(1)} copy(bf16[63,64,128]{1,2,0:T(8,128)(2,1)S(1)} %constant_dynamic-slice_fusion) | data formatting | bytes 2064384 | tf_op jit(solution)/shard_map/optimization_barrier | solution.py:511
  29.6 4.2 %constant_dynamic-slice_fusion.1 = bf16[63,128,128]{1,2,0:T(8,128)(2,1)} fusion(bf16[63,256,128]{1,2,0:T(8,128)(2,1)} %constant.48.clone, s32[]{:T(128)S(6)} %select_n.12), kind=kLoop, calls=%fused_computation.21 | loop fusion | bytes 4128772 | tf_op jit(solution)/shard_map/dynamic_slice | solution.py:512
  33.9 0.1 slice_negate_fusion
  34.0 0.0 copy-start.3
  34.0 0.1 fusion.8
  34.1 0.0 copy-start.7
  34.1 0.0 copy-start.8
  34.1 0.1 pad_maximum_fusion.1
  34.3 1.3 dynamic-slice_bitcast_fusion.1.refs_9_.refs_10_
  35.6 1.4 dynamic-slice_bitcast_fusion.refs_8_.refs_9_
  37.0 8.2 %collective-permute-done.refs_1_ = bf16[95,64,128]{2,1,0:T(8,128)(2,1)} collective-permute-done((bf16[95,64,128]{2,1,0:T(8,128)(2,1)}, bf16[95,64,128]{2,1,0:T(8,128)(2,1)}, u32[]{:S(2)}, u32[]{:S(2)}) %collective-permute-start) | collective-permute-done | bytes 1556512 | tf_op jit(solution)/shard_map/ppermute | solution.py:530
  45.2 0.0 copy-done.2
  45.2 0.0 copy-start
  45.2 2.7 %copy-done = bf16[1,63,252,192]{2,3,1,0:T(8,128)(2,1)S(1)} copy-done((bf16[1,63,252,192]{2,3,1,0:T(8,128)(2,1)S(1)}, bf16[1,63,252,192]{2,3,1,0:T(8,128)(2,1)}, u32[]{:S(2)}) %copy-start) | copy-done | bytes 6096408
  48.0 1.4 copy-done.6
  49.4 19.7 %spectral_0.1 = f32[128,128]{1,0:T(8,128)S(1)} custom-call(bf16[95,64,128]{2,1,0:T(8,128)(2,1)S(1)} %copy-done.6, bf16[95,64,128]{2,1,0:T(8,128)(2,1)} %collective-permute-done.refs_1_, bf16[1,63,192,252]{3,2,1,0:T(8,128)(2,1)S(1)} %bitcast.16, bf16[1,63,192,252]{3,2,1,0:T(8,128)(2,1)S(1)} %bitcast.17, bf16[256,252]{1,0:T(8,128)(2,1)S(1)} %copy-done.7, ...), custom_call_target="tpu_custom_call" | custom-call | flops 3170893824 | bytes 16000000 | tf_op jit(solution)/shard_map/spectral_0/pallas_call | solution.py:441
  69.1 0.0 copy-start.5
  69.1 0.1 collective-permute-start.1
  69.2 1.2 collective-permute-done.1
  70.5 2.1 %collective-permute-start.2 = (f32[128,128]{1,0:T(8,128)S(1)}, f32[128,128]{1,0:T(8,128)S(1)}, u32[]{:S(2)}, u32[]{:S(2)}) collective-permute-start(f32[128,128]{1,0:T(8,128)S(1)} %add.49), channel_id=1, source_target_pairs={{0,4},{2,6},{4,0},{6,2},{8,12},{10,14},{12,8},{14,10},{16,20},{18,... | collective-permute-start | bytes 196616 | tf_op jit(solution)/shard_map/ppermute | solution.py:481
  72.6 2.4 %collective-permute-done.2 = f32[128,128]{1,0:T(8,128)S(1)} collective-permute-done((f32[128,128]{1,0:T(8,128)S(1)}, f32[128,128]{1,0:T(8,128)S(1)}, u32[]{:S(2)}, u32[]{:S(2)}) %collective-permute-start.2) | collective-permute-done | bytes 65568 | tf_op jit(solution)/shard_map/ppermute | solution.py:481
  75.0 2.0 %collective-permute-start.3 = (f32[128,128]{1,0:T(8,128)S(1)}, f32[128,128]{1,0:T(8,128)S(1)}, u32[]{:S(2)}, u32[]{:S(2)}) collective-permute-start(f32[128,128]{1,0:T(8,128)S(1)} %add.50), channel_id=1, source_target_pairs={{0,8},{2,10},{4,12},{6,14},{8,0},{10,2},{12,4},{14,6},{16,24},{18,... | collective-permute-start | bytes 196616 | tf_op jit(solution)/shard_map/ppermute | solution.py:481
  77.0 2.3 %collective-permute-done.3 = f32[128,128]{1,0:T(8,128)S(1)} collective-permute-done((f32[128,128]{1,0:T(8,128)S(1)}, f32[128,128]{1,0:T(8,128)S(1)}, u32[]{:S(2)}, u32[]{:S(2)}) %collective-permute-start.3) | collective-permute-done | bytes 65568 | tf_op jit(solution)/shard_map/ppermute | solution.py:481
  79.3 3.0 %collective-permute-start.4 = (f32[128,128]{1,0:T(8,128)S(1)}, f32[128,128]{1,0:T(8,128)S(1)}, u32[]{:S(2)}, u32[]{:S(2)}) collective-permute-start(f32[128,128]{1,0:T(8,128)S(1)} %add.51), channel_id=1, source_target_pairs={{0,16},{2,18},{4,20},{6,22},{8,24},{10,26},{12,28},{14,30},{16,0},... | collective-permute-start | bytes 196616 | tf_op jit(solution)/shard_map/ppermute | solution.py:481
  82.3 0.1 pad_maximum_fusion.3
  82.5 2.1 %collective-permute-done.4 = f32[128,128]{1,0:T(8,128)S(1)} collective-permute-done((f32[128,128]{1,0:T(8,128)S(1)}, f32[128,128]{1,0:T(8,128)S(1)}, u32[]{:S(2)}, u32[]{:S(2)}) %collective-permute-start.4) | collective-permute-done | bytes 65568 | tf_op jit(solution)/shard_map/ppermute | solution.py:481
  84.6 1.9 %collective-permute-start.5 = (f32[128,128]{1,0:T(8,128)S(1)}, f32[128,128]{1,0:T(8,128)S(1)}, u32[]{:S(2)}, u32[]{:S(2)}) collective-permute-start(f32[128,128]{1,0:T(8,128)S(1)} %add.52), channel_id=1, source_target_pairs={{0,1},{1,0},{2,3},{3,2},{4,5},{5,4},{6,7},{7,6},{8,9},{9,8},{10,11... | collective-permute-start | bytes 196616 | tf_op jit(solution)/shard_map/ppermute | solution.py:481
  86.5 0.1 pad_maximum_fusion.4
  86.6 25.7 %collective-permute-done.5 = f32[128,128]{1,0:T(8,128)S(1)} collective-permute-done((f32[128,128]{1,0:T(8,128)S(1)}, f32[128,128]{1,0:T(8,128)S(1)}, u32[]{:S(2)}, u32[]{:S(2)}) %collective-permute-start.5) | collective-permute-done | bytes 65568 | tf_op jit(solution)/shard_map/ppermute | solution.py:481
  112.4 0.0 collective-permute-done.6.refs_1_
  112.4 0.0 slice-done
  112.4 0.0 slice-done.1
  112.4 0.0 copy-done.5
  112.4 0.0 copy-start.4
  112.4 19.5 %spectral_1.1.refs_0_ = f32[128,128]{1,0:T(8,128)S(1)} custom-call(bf16[95,64,128]{2,1,0:T(8,128)(2,1)S(1)} %copy-done.5, bf16[95,64,128]{2,1,0:T(8,128)(2,1)} %collective-permute-done.6.refs_1_, bf16[1,63,192,252]{3,2,1,0:T(8,128)(2,1)S(1)} %bitcast.20, bf16[1,63,192,252]{3,2,1,0:T(8,128)(2,1)S(1)} %bitcast.21, bf16[256,252]{1,0:T(8,128)(2,1)S(1)} %copy-done.7, ...), custom_call_target="tpu_custom_call" | custom-call | flops 3170893824 | bytes 16000000 | tf_op jit(solution)/shard_map/spectral_1/pallas_call | solution.py:441
  132.0 0.0 collective-permute-done.7.refs_2_
  132.0 0.0 copy-done.4
  132.0 19.5 %spectral_2.1 = f32[256,128]{1,0:T(8,128)S(1)} custom-call(f32[128,128]{1,0:T(8,128)S(1)} %spectral_1.1.refs_0_, bf16[95,64,128]{2,1,0:T(8,128)(2,1)S(1)} %copy-done.4, bf16[95,64,128]{2,1,0:T(8,128)(2,1)} %collective-permute-done.7.refs_2_, bf16[1,63,192,252]{3,2,1,0:T(8,128)(2,1)S(1)} %bitcast.22, bf16[1,63,192,252]{3,2,1,0:T(8,128)(2,1)S(1)} %bitcast.23, ...), custom_call_target="tpu_custom_call" | custom-call | flops 3170893824 | bytes 16000000 | tf_op jit(solution)/shard_map/spectral_2/pallas_call | solution.py:441
  151.5 0.1 collective-permute-start.8
  151.5 1.3 collective-permute-done.8
  152.9 1.8 %collective-permute-start.9 = (f32[256,128]{1,0:T(8,128)S(1)}, f32[256,128]{1,0:T(8,128)S(1)}, u32[]{:S(2)}, u32[]{:S(2)}) collective-permute-start(f32[256,128]{1,0:T(8,128)S(1)} %add.54), channel_id=1, source_target_pairs={{0,4},{2,6},{4,0},{6,2},{8,12},{10,14},{12,8},{14,10},{16,20},{18,... | collective-permute-start | bytes 393224 | tf_op jit(solution)/shard_map/ppermute | solution.py:481
  154.7 3.8 %collective-permute-done.9 = f32[256,128]{1,0:T(8,128)S(1)} collective-permute-done((f32[256,128]{1,0:T(8,128)S(1)}, f32[256,128]{1,0:T(8,128)S(1)}, u32[]{:S(2)}, u32[]{:S(2)}) %collective-permute-start.9) | collective-permute-done | bytes 131104 | tf_op jit(solution)/shard_map/ppermute | solution.py:481
  158.5 1.9 %collective-permute-start.10 = (f32[256,128]{1,0:T(8,128)S(1)}, f32[256,128]{1,0:T(8,128)S(1)}, u32[]{:S(2)}, u32[]{:S(2)}) collective-permute-start(f32[256,128]{1,0:T(8,128)S(1)} %add.55), channel_id=1, source_target_pairs={{0,8},{2,10},{4,12},{6,14},{8,0},{10,2},{12,4},{14,6},{16,24},{18,... | collective-permute-start | bytes 393224 | tf_op jit(solution)/shard_map/ppermute | solution.py:481
  160.4 3.2 %collective-permute-done.10 = f32[256,128]{1,0:T(8,128)S(1)} collective-permute-done((f32[256,128]{1,0:T(8,128)S(1)}, f32[256,128]{1,0:T(8,128)S(1)}, u32[]{:S(2)}, u32[]{:S(2)}) %collective-permute-start.10) | collective-permute-done | bytes 131104 | tf_op jit(solution)/shard_map/ppermute | solution.py:481
  163.6 2.9 %collective-permute-start.11 = (f32[256,128]{1,0:T(8,128)S(1)}, f32[256,128]{1,0:T(8,128)S(1)}, u32[]{:S(2)}, u32[]{:S(2)}) collective-permute-start(f32[256,128]{1,0:T(8,128)S(1)} %add.56), channel_id=1, source_target_pairs={{0,16},{2,18},{4,20},{6,22},{8,24},{10,26},{12,28},{14,30},{16,0},... | collective-permute-start | bytes 393224 | tf_op jit(solution)/shard_map/ppermute | solution.py:481
  166.5 4.6 %collective-permute-done.11 = f32[256,128]{1,0:T(8,128)S(1)} collective-permute-done((f32[256,128]{1,0:T(8,128)S(1)}, f32[256,128]{1,0:T(8,128)S(1)}, u32[]{:S(2)}, u32[]{:S(2)}) %collective-permute-start.11) | collective-permute-done | bytes 131104 | tf_op jit(solution)/shard_map/ppermute | solution.py:481
  171.1 1.6 collective-permute-start.12
  172.8 3.4 %collective-permute-done.12 = f32[256,128]{1,0:T(8,128)S(1)} collective-permute-done((f32[256,128]{1,0:T(8,128)S(1)}, f32[256,128]{1,0:T(8,128)S(1)}, u32[]{:S(2)}, u32[]{:S(2)}) %collective-permute-start.12) | collective-permute-done | bytes 131104 | tf_op jit(solution)/shard_map/ppermute | solution.py:481
  176.2 0.7 slice_multiply_fusion
  (25 shorter events, 0.2 us)
Async XLA Ops:
  7.0 38.2 %collective-permute-start = (bf16[95,64,128]{2,1,0:T(8,128)(2,1)}, bf16[95,64,128]{2,1,0:T(8,128)(2,1)}, u32[]{:S(2)}, u32[]{:S(2)}) collective-permute-start(bf16[95,64,128]{2,1,0:T(8,128)(2,1)} %forward_0.1.refs_0_), channel_id=1, source_target_pairs={{0,1},{1,0},{2,3},{3,2},{4,5},{5,4},{6,7},{7,6},{8,9},{9,8},{10,11... | collective-permute-start | bytes 4669448 | tf_op jit(solution)/shard_map/ppermute | solution.py:530
  16.4 8.6 %copy-start.9 = (bf16[126,192]{0,1:T(8,128)(2,1)S(1)}, bf16[126,192]{0,1:T(8,128)(2,1)}, u32[]{:S(2)}) copy-start(bf16[126,192]{0,1:T(8,128)(2,1)} %param.15) | copy-start | bytes 145156
  16.4 8.8 %copy-start.10 = (bf16[126,192]{0,1:T(8,128)(2,1)S(1)}, bf16[126,192]{0,1:T(8,128)(2,1)}, u32[]{:S(2)}) copy-start(bf16[126,192]{0,1:T(8,128)(2,1)} %param.14) | copy-start | bytes 145156
  16.4 96.0 %collective-permute-start.6 = (bf16[95,64,128]{2,1,0:T(8,128)(2,1)}, bf16[95,64,128]{2,1,0:T(8,128)(2,1)}, u32[]{:S(2)}, u32[]{:S(2)}) collective-permute-start(bf16[95,64,128]{2,1,0:T(8,128)(2,1)} %forward_1.1.refs_0_), channel_id=1, source_target_pairs={{0,1},{1,0},{2,3},{3,2},{4,5},{5,4},{6,7},{7,6},{8,9},{9,8},{10,11... | collective-permute-start | bytes 4669448 | tf_op jit(solution)/shard_map/ppermute | solution.py:530
  22.9 109.1 %collective-permute-start.7 = (bf16[95,64,128]{2,1,0:T(8,128)(2,1)}, bf16[95,64,128]{2,1,0:T(8,128)(2,1)}, u32[]{:S(2)}, u32[]{:S(2)}) collective-permute-start(bf16[95,64,128]{2,1,0:T(8,128)(2,1)} %forward_2.1.refs_1_), channel_id=1, source_target_pairs={{0,1},{1,0},{2,3},{3,2},{4,5},{5,4},{6,7},{7,6},{8,9},{9,8},{10,11... | collective-permute-start | bytes 4669448 | tf_op jit(solution)/shard_map/ppermute | solution.py:530
  27.7 6.1 %copy-start.1 = (bf16[63,64,128]{1,2,0:T(8,128)(2,1)}, bf16[63,64,128]{1,2,0:T(8,128)(2,1)S(1)}, u32[]{:S(2)}) copy-start(bf16[63,64,128]{1,2,0:T(8,128)(2,1)S(1)} %constant_dynamic-slice_fusion) | copy-start | bytes 3096580
  33.8 78.6 %slice-start = ((s8[6193152]{0:T(1024)(128)(4,1)}), s8[1998848]{0:T(1024)(128)(4,1)S(1)}, s32[]{:S(2)}) async-start(s8[6193152]{0:T(1024)(128)(4,1)} %bitcast.18), calls=%async_computation | async-start | bytes 3997696
  34.0 11.2 %copy-start.3 = (bf16[63,128,128]{1,2,0:T(8,128)(2,1)S(1)}, bf16[63,128,128]{1,2,0:T(8,128)(2,1)}, u32[]{:S(2)}) copy-start(bf16[63,128,128]{1,2,0:T(8,128)(2,1)} %constant_dynamic-slice_fusion.1) | copy-start | bytes 6193156
  34.1 11.1 %copy-start.2 = (bf16[63,64,128]{1,2,0:T(8,128)(2,1)S(1)}, bf16[63,64,128]{1,2,0:T(8,128)(2,1)}, u32[]{:S(2)}) copy-start(bf16[63,64,128]{1,2,0:T(8,128)(2,1)} %copy-done.1) | copy-start | bytes 3096580
  34.1 11.1 %copy-start.7 = (bf16[256,252]{1,0:T(8,128)(2,1)S(1)}, bf16[256,252]{1,0:T(8,128)(2,1)}, u32[]{:S(2)}) copy-start(bf16[256,252]{1,0:T(8,128)(2,1)} %constant.46.clone.refs_4_.refs_5_) | copy-start | bytes 387076
  34.1 11.1 %copy-start.8 = (f32[128,128]{1,0:T(8,128)S(1)}, f32[128,128]{1,0:T(8,128)}, u32[]{:S(2)}) copy-start(f32[128,128]{1,0:T(8,128)} %constant.52.clone.refs_10_.refs_11_) | copy-start | bytes 196612
  45.2 2.8 %copy-start = (bf16[1,63,252,192]{2,3,1,0:T(8,128)(2,1)S(1)}, bf16[1,63,252,192]{2,3,1,0:T(8,128)(2,1)}, u32[]{:S(2)}) copy-start(bf16[1,63,252,192]{2,3,1,0:T(8,128)(2,1)} %param.13) | copy-start | bytes 18289156
  48.0 1.4 copy-start.6
  49.4 63.0 %slice-start.1 = ((s8[6193152]{0:T(1024)(128)(4,1)}), s8[4194304]{0:T(1024)(128)(4,1)S(1)}, s32[]{:S(2)}) async-start(s8[6193152]{0:T(1024)(128)(4,1)} %bitcast.18), calls=%async_computation.1 | async-start | bytes 8388608
  69.1 43.3 %copy-start.5 = (bf16[95,64,128]{2,1,0:T(8,128)(2,1)S(1)}, bf16[95,64,128]{2,1,0:T(8,128)(2,1)}, u32[]{:S(2)}) copy-start(bf16[95,64,128]{2,1,0:T(8,128)(2,1)} %forward_1.1.refs_0_) | copy-start | bytes 4669444
  69.1 1.3 collective-permute-start.1
  70.5 4.5 %collective-permute-start.2 = (f32[128,128]{1,0:T(8,128)S(1)}, f32[128,128]{1,0:T(8,128)S(1)}, u32[]{:S(2)}, u32[]{:S(2)}) collective-permute-start(f32[128,128]{1,0:T(8,128)S(1)} %add.49), channel_id=1, source_target_pairs={{0,4},{2,6},{4,0},{6,2},{8,12},{10,14},{12,8},{14,10},{16,20},{18,... | collective-permute-start | bytes 196616 | tf_op jit(solution)/shard_map/ppermute | solution.py:481
  75.0 4.3 %collective-permute-start.3 = (f32[128,128]{1,0:T(8,128)S(1)}, f32[128,128]{1,0:T(8,128)S(1)}, u32[]{:S(2)}, u32[]{:S(2)}) collective-permute-start(f32[128,128]{1,0:T(8,128)S(1)} %add.50), channel_id=1, source_target_pairs={{0,8},{2,10},{4,12},{6,14},{8,0},{10,2},{12,4},{14,6},{16,24},{18,... | collective-permute-start | bytes 196616 | tf_op jit(solution)/shard_map/ppermute | solution.py:481
  79.3 5.3 %collective-permute-start.4 = (f32[128,128]{1,0:T(8,128)S(1)}, f32[128,128]{1,0:T(8,128)S(1)}, u32[]{:S(2)}, u32[]{:S(2)}) collective-permute-start(f32[128,128]{1,0:T(8,128)S(1)} %add.51), channel_id=1, source_target_pairs={{0,16},{2,18},{4,20},{6,22},{8,24},{10,26},{12,28},{14,30},{16,0},... | collective-permute-start | bytes 196616 | tf_op jit(solution)/shard_map/ppermute | solution.py:481
  84.6 27.8 %collective-permute-start.5 = (f32[128,128]{1,0:T(8,128)S(1)}, f32[128,128]{1,0:T(8,128)S(1)}, u32[]{:S(2)}, u32[]{:S(2)}) collective-permute-start(f32[128,128]{1,0:T(8,128)S(1)} %add.52), channel_id=1, source_target_pairs={{0,1},{1,0},{2,3},{3,2},{4,5},{5,4},{6,7},{7,6},{8,9},{9,8},{10,11... | collective-permute-start | bytes 196616 | tf_op jit(solution)/shard_map/ppermute | solution.py:481
  112.4 19.6 %copy-start.4 = (bf16[95,64,128]{2,1,0:T(8,128)(2,1)S(1)}, bf16[95,64,128]{2,1,0:T(8,128)(2,1)}, u32[]{:S(2)}) copy-start(bf16[95,64,128]{2,1,0:T(8,128)(2,1)} %forward_2.1.refs_1_) | copy-start | bytes 4669444
  151.5 1.4 collective-permute-start.8
  152.9 5.6 %collective-permute-start.9 = (f32[256,128]{1,0:T(8,128)S(1)}, f32[256,128]{1,0:T(8,128)S(1)}, u32[]{:S(2)}, u32[]{:S(2)}) collective-permute-start(f32[256,128]{1,0:T(8,128)S(1)} %add.54), channel_id=1, source_target_pairs={{0,4},{2,6},{4,0},{6,2},{8,12},{10,14},{12,8},{14,10},{16,20},{18,... | collective-permute-start | bytes 393224 | tf_op jit(solution)/shard_map/ppermute | solution.py:481
  158.5 5.0 %collective-permute-start.10 = (f32[256,128]{1,0:T(8,128)S(1)}, f32[256,128]{1,0:T(8,128)S(1)}, u32[]{:S(2)}, u32[]{:S(2)}) collective-permute-start(f32[256,128]{1,0:T(8,128)S(1)} %add.55), channel_id=1, source_target_pairs={{0,8},{2,10},{4,12},{6,14},{8,0},{10,2},{12,4},{14,6},{16,24},{18,... | collective-permute-start | bytes 393224 | tf_op jit(solution)/shard_map/ppermute | solution.py:481
  163.6 7.5 %collective-permute-start.11 = (f32[256,128]{1,0:T(8,128)S(1)}, f32[256,128]{1,0:T(8,128)S(1)}, u32[]{:S(2)}, u32[]{:S(2)}) collective-permute-start(f32[256,128]{1,0:T(8,128)S(1)} %add.56), channel_id=1, source_target_pairs={{0,16},{2,18},{4,20},{6,22},{8,24},{10,26},{12,28},{14,30},{16,0},... | collective-permute-start | bytes 393224 | tf_op jit(solution)/shard_map/ppermute | solution.py:481
  171.1 5.0 %collective-permute-start.12 = (f32[256,128]{1,0:T(8,128)S(1)}, f32[256,128]{1,0:T(8,128)S(1)}, u32[]{:S(2)}, u32[]{:S(2)}) collective-permute-start(f32[256,128]{1,0:T(8,128)S(1)} %add.57), channel_id=1, source_target_pairs={{0,1},{1,0},{2,3},{3,2},{4,5},{5,4},{6,7},{7,6},{8,9},{9,8},{10,11... | collective-permute-start | bytes 393224 | tf_op jit(solution)/shard_map/ppermute | solution.py:481

commit v4 on v3

--- a/solution.py
+++ b/solution.py
@@ -70,16 +70,27 @@
             order = self.low + pair
             orders += [order, self.partner - order if self.partner - order != order else -1]
         self.orders = np.array(orders + [-1] * (self.slots - len(orders)))
+        self.split = round_up(self.low // 2, GROUP)
+
+    def piece_slots(self, first, last):
+        start = first + max(first - self.low, 0)
+        stop = last + max(last - self.low, 0)
+        return start, round_up(stop - start, 8)
 
 
 @functools.lru_cache(maxsize=None)
-def fourier_constants(parts, local):
-    layout = Layout(parts, local)
-    orders = np.maximum(layout.orders, 0)
+def fourier_constants(layout, first, last):
+    start, slots = layout.piece_slots(first, last)
+    live_orders = np.full(slots, -1)
+    part = layout.orders[start : start + slots]
+    live_orders[: len(part)] = part
+    stop = last + max(last - layout.low, 0)
+    live_orders[stop - start :] = -1
+    orders = np.maximum(live_orders, 0)
     angles = 2.0 * math.pi / NLON * (orders[:, None] * np.arange(NLON)[None] % NLON)
-    live = (layout.orders >= 0)[:, None]
+    live = (live_orders >= 0)[:, None]
     basis = np.concatenate([np.cos(angles) * live, -np.sin(angles) * live])
-    factor = np.where(layout.orders == 0, 1.0, 2.0)[:, None]
+    factor = np.where(live_orders == 0, 1.0, 2.0)[:, None]
     inverse = basis * np.concatenate([factor, factor])
     return to_bf16(basis), to_bf16(inverse)
 
@@ -144,14 +155,9 @@
 
 
 def gelu_slope(values):
-    size = jnp.abs(values)
-    step = 1.0 / (1.0 + 0.2316419 * size)
-    scale = 1.0 / math.sqrt(2.0 * math.pi)
-    series = 1.330274429 * scale
-    for term in (-1.821255978, 1.781477937, -0.356563782, 0.319381530):
-        series = series * step + term * scale
-    below = jnp.exp(-0.5 * values * values) * (series * step - scale * size)
-    return jnp.where(values >= 0.0, 1.0 - below, below)
+    cumulative = 0.5 * (1.0 + lax.erf(values / math.sqrt(2.0)))
+    density = jnp.exp(-0.5 * values * values) / math.sqrt(2.0 * math.pi)
+    return cumulative + values * density
 
 
 def grid_rows(layout, north, south, quad, group):
@@ -167,7 +173,7 @@
 
 
 def scatter_rows(layout, values, scratch, quad, group):
-    slots = layout.slots
+    slots = values.shape[0] // 2
     for which in range(2):
         columns = slice(which * LANES, (which + 1) * LANES)
         upper, lower = interleave(values[:slots, columns], values[slots:, columns])
@@ -219,13 +225,14 @@
     return copies
 
 
-def forward_kernel(layout, chunk, index, fields, basis, pair_all, out, scratch, buffer, pair_fwd, sems, pair_sem):
+def forward_kernel(layout, chunk, first, last, index, fields, basis, pair_all, out, scratch, buffer, pair_fwd, sems, pair_sem):
     copies = band_copies(layout, chunk, fields, buffer, sems)
     for started in copies:
         for copy in started:
             copy.start()
-    tables = pltpu.make_async_copy(pair_all.at[index[0]], pair_fwd, pair_sem)
-    tables.start()
+    if last > layout.low:
+        tables = pltpu.make_async_copy(pair_all.at[index[0]], pair_fwd, pair_sem)
+        tables.start()
     if layout.rows > layout.local:
         shape = (layout.rows - layout.local,) + buffer.shape[1:]
         buffer[layout.local :] = jnp.zeros(shape, buffer.dtype)
@@ -239,33 +246,42 @@
                 rows += [buffer[latitude], buffer[latitude + layout.half]]
             grid = jnp.concatenate(rows, axis=0)
             scatter_rows(layout, dot(basis[...], grid, (1, 1)), scratch, quad, group)
-    tables.wait()
+    if last > layout.low:
+        tables.wait()
+
+    lows = min(last, layout.low) - first
 
     def low_block(order, carry):
         out[order] = order_rows(layout, scratch, order, 1)
         return carry
 
     def pair_block(pair, carry):
-        values = order_rows(layout, scratch, layout.low + 2 * pair, 2)
-        out[layout.low + pair] = dot(pair_fwd[pair], values).astype(jnp.bfloat16)
+        values = order_rows(layout, scratch, lows + 2 * pair, 2)
+        out[lows + pair] = dot(pair_fwd[pair], values).astype(jnp.bfloat16)
         return carry
 
-    lax.fori_loop(0, layout.low, low_block, 0, unroll=8)
-    lax.fori_loop(0, layout.pairs, pair_block, 0, unroll=8)
+    lax.fori_loop(0, lows, low_block, 0, unroll=8)
+    lax.fori_loop(0, last - first - lows, pair_block, 0, unroll=8)
 
 
 def mix(spectral, swapped, real_rows, imag_rows):
     return (spectral * real_rows + swapped * imag_rows).astype(jnp.bfloat16)
 
 
-def spectral_kernel(layout, carries, *refs):
+def spectral_kernel(layout, carries, bounds, *refs):
     ahead = None
     if carries:
         ahead, refs = refs[0], refs[1:]
-    own, others = refs[0], refs[1 : layout.parts]
-    north, south, basis, analysis, synth_low, back_low = refs[layout.parts : layout.parts + 6]
-    pair_synth, pair_back, place, real_ref, imag_ref = refs[layout.parts + 6 : layout.parts + 11]
-    out, scratch, returned, spec_low, swap_low, spec_pair, swap_pair = refs[layout.parts + 11 :]
+    pieces = [refs[at : at + layout.parts] for at in range(0, layout.parts * (len(bounds) - 1), layout.parts)]
+    refs = refs[layout.parts * len(pieces) :]
+
+    def sources(block):
+        at = max(at for at in range(len(pieces)) if bounds[at] <= block)
+        return pieces[at], bounds[at]
+
+    north, south, basis, analysis, synth_low, back_low = refs[:6]
+    pair_synth, pair_back, place, real_ref, imag_ref = refs[6:11]
+    out, scratch, returned, spec_low, swap_low, spec_pair, swap_pair = refs[11:]
     group = pl.program_id(0)
     rows, degrees, low = layout.rows, layout.degrees, layout.low
 
@@ -278,9 +294,10 @@
         for start, stop, top in groups():
             real_rows = real_ref[top:degrees, :]
             imag_rows = imag_ref[top:degrees, :]
+            held, offset = sources(start)
 
             def low_block(order, carry):
-                values = jnp.concatenate([own[order]] + [ref[order] for ref in others], axis=0)
+                values = jnp.concatenate([ref[order - offset] for ref in held], axis=0)
                 spectral = dot(analysis[order, top:degrees, :], values).astype(jnp.bfloat16)
                 spec_low[order, top:degrees, :] = spectral
                 return carry
@@ -299,10 +316,10 @@
 
         line = lax.broadcasted_iota(jnp.int32, (rows, LANES), 0)
 
+        held, offset = sources(low)
+
         def pair_block(pair, carry):
-            total = own[low + pair].astype(jnp.float32)
-            for ref in others:
-                total = total + ref[low + pair].astype(jnp.float32)
+            total = sum(ref[low + pair - offset].astype(jnp.float32) for ref in held)
             spectral = total.astype(jnp.bfloat16)
             spec_pair[pair] = spectral
             natural = line >= layout.first_natural + pair
@@ -404,11 +421,13 @@
     return pl.BlockSpec(memory_space=pltpu.VMEM)
 
 
-def forward_call(layout, chunk, index, fields, basis, pair_fwd):
-    work = 2 * 2 * layout.slots * NLON * layout.rows * LANES // 2
+def forward_call(layout, chunk, first, last, index, fields, pair_fwd):
+    basis = jnp.asarray(fourier_constants(layout, first, last)[0])
+    slots = basis.shape[0] // 2
+    work = 2 * 2 * slots * NLON * layout.rows * LANES // 2
     groups = layout.half // PAIRS
     return pl.pallas_call(
-        functools.partial(forward_kernel, layout, chunk),
+        functools.partial(forward_kernel, layout, chunk, first, last),
         in_specs=[
             pl.BlockSpec(memory_space=pltpu.SMEM),
             pl.BlockSpec(memory_space=pl.ANY),
@@ -416,9 +435,9 @@
             pl.BlockSpec(memory_space=pl.ANY),
         ],
         out_specs=whole(),
-        out_shape=jax.ShapeDtypeStruct((layout.blocks, layout.rows, LANES), jnp.bfloat16),
+        out_shape=jax.ShapeDtypeStruct((last - first, layout.rows, LANES), jnp.bfloat16),
         scratch_shapes=[
-            pltpu.VMEM((layout.slots * layout.pitch, LANES), jnp.float32),
+            pltpu.VMEM((slots * layout.pitch, LANES), jnp.float32),
             pltpu.VMEM((layout.rows, LANES // 2, NLON), jnp.bfloat16),
             pltpu.VMEM(pair_fwd.shape[1:], jnp.bfloat16),
             pltpu.SemaphoreType.DMA((2 * groups,)),
@@ -426,20 +445,20 @@
         ],
         compiler_params=pltpu.CompilerParams(vmem_limit_bytes=FORWARD_VMEM),
         cost_estimate=pl.CostEstimate(flops=2 * work, bytes_accessed=8_000_000, transcendentals=0),
-        name=f"forward_{chunk}",
+        name=f"forward_{chunk}_{first}",
     )(index, fields, basis, pair_fwd)
 
 
-def spectral_call(layout, chunk, coeffs, cotangent, tables, real_rows, imag_rows, ahead=None):
+def spectral_call(layout, chunk, bounds, coeffs, cotangent, tables, real_rows, imag_rows, ahead=None):
     work = 2 * 2 * layout.slots * NLON * layout.rows * LANES // 2
     operands = list(coeffs) + [cotangent, cotangent] + list(tables) + [real_rows, imag_rows]
-    specs = [whole()] * layout.parts + grid_specs(layout, chunk) + [whole()] * (len(tables) + 2)
+    specs = [whole()] * len(coeffs) + grid_specs(layout, chunk) + [whole()] * (len(tables) + 2)
     height = LANES
     if ahead is not None:
         operands, specs = [ahead] + operands, [whole()] + specs
         height += ahead.shape[0]
     return pl.pallas_call(
-        functools.partial(spectral_kernel, layout, ahead is not None),
+        functools.partial(spectral_kernel, layout, ahead is not None, bounds),
         grid=(layout.half // PAIRS,),
         in_specs=specs,
         out_specs=whole(),
@@ -468,19 +487,25 @@
     return found
 
 
-def sum_over(value, axis):
+def sum_steps(axis):
     size = lax.axis_size(axis)
-    stride = 1
+    steps, stride = [], 1
     for radix in radices(size):
+        steps.append((axis, stride, radix))
+        stride *= radix
+    return steps
+
+
+def sum_over(value, steps):
+    for axis, stride, radix in steps:
         total = value
         for turn in range(1, radix):
             pairs = []
-            for index in range(size):
+            for index in range(lax.axis_size(axis)):
                 digit = index // stride % radix
                 pairs.append((index, index + ((digit + turn) % radix - digit) * stride))
             total = total + lax.ppermute(value, axis, pairs)
         value = total
-        stride *= radix
     return value
 
 
@@ -498,7 +523,7 @@
     layout = Layout(parts, fields.shape[1])
     width = LANES // 2
     chunks = fields.shape[-1] // width
-    basis, inverse = (jnp.asarray(a) for a in fourier_constants(parts, layout.local))
+    inverse = jnp.asarray(fourier_constants(layout, 0, layout.blocks)[1])
     constants = legendre_constants(parts, layout.local)
 
     def local_table(name):
@@ -523,30 +548,40 @@
 
     received = []
     for chunk in range(chunks):
-        own = forward_call(layout, chunk, place, fields, basis, pair_fwd)
-        blocks = [own]
-        for shift in range(1, parts):
-            route = [(source, (source + shift) % parts) for source in range(parts)]
-            blocks.append(lax.ppermute(own, "space", route))
-        received.append(blocks)
-
-    totals, ahead = [], None
+        bounds = [0, layout.blocks] if chunk else sorted({0, layout.split, layout.blocks})
+        blocks = []
+        for first, last in zip(bounds, bounds[1:]):
+            own = forward_call(layout, chunk, first, last, place, fields, pair_fwd)
+            blocks.append(own)
+            for shift in range(1, parts):
+                route = [(source, (source + shift) % parts) for source in range(parts)]
+                blocks.append(lax.ppermute(own, "space", route))
+        received.append((tuple(bounds), blocks))
+
+    steps = sum_steps("dp")
+    early = []
     for chunk in range(chunks):
         columns = slice(chunk * width, (chunk + 1) * width)
         real, imag = real_all[:, columns], imag_all[:, columns]
         real_rows = jnp.concatenate([real, real], axis=1)
         imag_rows = jnp.concatenate([-imag, imag], axis=1)
-        coeffs = received[chunk]
-        if totals:
-            coeffs[0], totals[-1] = lax.optimization_barrier((coeffs[0], totals[-1]))
-        grads = spectral_call(layout, chunk, coeffs, cotangent, tables, real_rows, imag_rows, ahead)
-        if chunk == chunks - 2:
-            ahead = grads
-        else:
-            totals.append(sum_over(sum_over(grads, "dp"), "space"))
+        bounds, coeffs = received[chunk]
+        if early:
+            coeffs[0], early = lax.optimization_barrier((coeffs[0], early))
+        ahead = grads if 0 < chunk == chunks - 1 else None
+        grads = spectral_call(
+            layout, chunk, bounds, coeffs, cotangent, tables, real_rows, imag_rows, ahead
+        )
+        half = len(steps) // 2
+        if 0 < chunk <= len(early):
+            early[chunk - 1], grads = lax.optimization_barrier((early[chunk - 1], grads))
+            early[chunk - 1] = sum_over(early[chunk - 1], steps[half:])
+        if chunk < chunks - 2:
+            early.append(sum_over(grads, steps[:half]))
+    rows = jnp.concatenate(early + [sum_over(grads, steps)], axis=0)
+    rows = sum_over(rows, sum_steps("space")).reshape(chunks, 2, width, layout.degrees)
 
     batch_total = fields.shape[0] * lax.axis_size("dp")
-    rows = jnp.concatenate(totals, axis=0).reshape(chunks, 2, width, layout.degrees)
     real, imag = (rows[:, part, :, :MODES].reshape(chunks * width, MODES) for part in range(2))
     return (real.T / batch_total, imag.T / batch_total)
 

time: 177 us -> 155 us (0.88)
  waiting for transfers between devices: 58.4 us -> 35.3 us
  other arithmetic: 1.38 us -> 4.1 us
    ppermute x10 -> x9, waiting for transfers between devices: 50.2 us -> 25 us  [sum_over(): total = total + lax.ppermute(value, axis, pairs)]
    pallas_call x3, Pallas kernels: 58.7 us -> 53.3 us  [spectral_call(): pl.pallas_call(functools.partial(spectral_kernel, layout, ahead is not No...]
    pallas_call x3 -> x4, Pallas kernels: 19.1 us -> 22.9 us  [forward_call(): pl.pallas_call(functools.partial(forward_kernel, layout, chunk, first, la...]
    ppermute x3 -> x4, waiting for transfers between devices: 8.19 us -> 10.4 us  [on_device(): blocks.append(lax.ppermute(own, 'space', route))]
    ppermute x10 -> x9, starting transfers between devices: 17.3 us -> 15.9 us  [sum_over(): total = total + lax.ppermute(value, axis, pairs)]
    ppermute x3 -> x4, starting transfers between devices: 5.18 us -> 5.41 us  [on_device(): blocks.append(lax.ppermute(own, 'space', route))]
    unnamed x28 -> x34, local copies, waits for them, and re-layouts: 4.45 us -> 4.28 us
  transfers between devices with their start and end apart: 13 -> 13, of which waited for: 11 -> 11; matrix products, arithmetic and copies ran while one was open for 7% -> 10% of each run, Pallas kernels for 29% -> 34%
where the time goes in v4:
time: 155 us; the launch traced here: 154 us
  Pallas kernels  76.2 us (49%)
  waiting for transfers between devices  35.3 us (23%)
  starting transfers between devices  21.3 us (14%)
  local copies, waits for them, and re-layouts  16.5 us (11%)
  other arithmetic  4.1 us (3%)
    pallas_call x3, Pallas kernels, spectral_call(): pl.pallas_call(functools.partial(spectral_kernel, layout, ahead is not No...  53.3 us
    ppermute x9, waiting for transfers between devices, sum_over(): total = total + lax.ppermute(value, axis, pairs)  25 us
    pallas_call x4, Pallas kernels, forward_call(): pl.pallas_call(functools.partial(forward_kernel, layout, chunk, first, la...  22.9 us
    ppermute x9, starting transfers between devices, sum_over(): total = total + lax.ppermute(value, axis, pairs)  15.9 us
    ppermute x4, waiting for transfers between devices, on_device(): blocks.append(lax.ppermute(own, 'space', route))  10.4 us
    dynamic_slice x2, local copies, waits for them, and re-layouts, bands(): lax.dynamic_slice_in_dim(table, first * layout.rows, count * layout.rows, 1)  6.25 us
    ppermute x4, starting transfers between devices, on_device(): blocks.append(lax.ppermute(own, 'space', route))  5.41 us
    unnamed x34, local copies, waits for them, and re-layouts  4.28 us
  transfers between devices with their start and end apart: 13, of which 11 were waited for; matrix products, arithmetic and copies ran while one was open for 10% of the time, Pallas kernels for 34%

profile of v4, /device:TPU:0, one launch (start us, length us, event | category | flops | bytes accessed | tf_op | source)
XLA Modules:
  0.0 154.4 jit_solution(3578072401534843095)
XLA Ops:
  0.6 5.8 %forward_0_32.1.refs_2_ = bf16[63,64,128]{2,1,0:T(8,128)(2,1)} custom-call(s32[1]{0:T(128)} %bitcast.index, bf16[1,63,192,252]{3,2,1,0:T(8,128)(2,1)} %bitcast.30, bf16[192,252]{1,0:T(8,128)(2,1)} %constant.57.clone.basis, bf16[2,32,64,128]{3,2,1,0:T(8,128)(2,1)} %constant.50.clone.pair_all), custom_call_target="tpu_custom_call" | custom-call | flops 792723456 | bytes 8000000 | tf_op jit(solution)/shard_map/forward_0_32/pallas_call | solution.py:429
  6.5 3.0 %collective-permute-start.1 = (bf16[63,64,128]{2,1,0:T(8,128)(2,1)}, bf16[63,64,128]{2,1,0:T(8,128)(2,1)}, u32[]{:S(2)}, u32[]{:S(2)}) collective-permute-start(bf16[63,64,128]{2,1,0:T(8,128)(2,1)} %forward_0_32.1.refs_2_), channel_id=1, source_target_pairs={{0,1},{1,0},{2,3},{3,2},{4,5},{5,4},{6,7},{7,6},{8,9},{9,8},{10,11... | collective-permute-start | bytes 3096584 | tf_op jit(solution)/shard_map/ppermute | solution.py:558
  9.5 4.3 %forward_0_0.1.refs_0_ = bf16[32,64,128]{2,1,0:T(8,128)(2,1)} custom-call(s32[1]{0:T(128)} %bitcast.index, bf16[1,63,192,252]{3,2,1,0:T(8,128)(2,1)} %bitcast.31, bf16[64,252]{1,0:T(8,128)(2,1)} %constant.56.clone.basis, bf16[2,32,64,128]{3,2,1,0:T(8,128)(2,1)} %constant.50.clone.pair_all), custom_call_target="tpu_custom_call" | custom-call | flops 264241152 | bytes 8000000 | tf_op jit(solution)/shard_map/forward_0_0/pallas_call | solution.py:429
  13.8 0.1 collective-permute-start
  13.9 6.4 %forward_1_0.1.refs_0_ = bf16[95,64,128]{2,1,0:T(8,128)(2,1)} custom-call(s32[1]{0:T(128)} %bitcast.index, bf16[1,63,192,252]{3,2,1,0:T(8,128)(2,1)} %bitcast.32, bf16[256,252]{1,0:T(8,128)(2,1)} %constant.58.clone.basis, bf16[2,32,64,128]{3,2,1,0:T(8,128)(2,1)} %constant.50.clone.pair_all), custom_call_target="tpu_custom_call" | custom-call | flops 1056964608 | bytes 8000000 | tf_op jit(solution)/shard_map/forward_1_0/pallas_call | solution.py:429
  20.2 0.0 copy-start.12
  20.2 0.0 copy-start.9
  20.3 2.1 %collective-permute-start.4 = (bf16[95,64,128]{2,1,0:T(8,128)(2,1)}, bf16[95,64,128]{2,1,0:T(8,128)(2,1)}, u32[]{:S(2)}, u32[]{:S(2)}) collective-permute-start(bf16[95,64,128]{2,1,0:T(8,128)(2,1)} %forward_1_0.1.refs_0_), channel_id=1, source_target_pairs={{0,1},{1,0},{2,3},{3,2},{4,5},{5,4},{6,7},{7,6},{8,9},{9,8},{10,11... | collective-permute-start | bytes 4669448 | tf_op jit(solution)/shard_map/ppermute | solution.py:558
  22.3 6.4 %forward_2_0.1.refs_1_ = bf16[95,64,128]{2,1,0:T(8,128)(2,1)} custom-call(s32[1]{0:T(128)} %bitcast.index, bf16[1,63,192,252]{3,2,1,0:T(8,128)(2,1)} %bitcast.33, bf16[256,252]{1,0:T(8,128)(2,1)} %constant.58.clone.basis, bf16[2,32,64,128]{3,2,1,0:T(8,128)(2,1)} %constant.50.clone.pair_all), custom_call_target="tpu_custom_call" | custom-call | flops 1056964608 | bytes 8000000 | tf_op jit(solution)/shard_map/forward_2_0/pallas_call | solution.py:429
  28.7 0.2 collective-permute-start.7
  29.0 0.0 copy-done.12
  29.0 0.1 copy.18
  29.1 0.1 rev.7
  29.2 0.0 copy-done.9
  29.2 2.0 %constant_dynamic-slice_fusion = bf16[63,64,128]{1,2,0:T(8,128)(2,1)} fusion(bf16[63,128,128]{1,2,0:T(8,128)(2,1)S(1)} %copy-done.9, s32[]{:T(128)S(6)} %select_n.13), kind=kLoop, calls=%fused_computation.20 | loop fusion | bytes 2064388 | tf_op jit(solution)/shard_map/dynamic_slice | solution.py:537
  31.2 4.3 %constant_dynamic-slice_fusion.1 = bf16[63,128,128]{1,2,0:T(8,128)(2,1)} fusion(bf16[63,256,128]{1,2,0:T(8,128)(2,1)} %constant.51.clone, s32[]{:T(128)S(6)} %select_n.12), kind=kLoop, calls=%fused_computation.21 | loop fusion | bytes 4128772 | tf_op jit(solution)/shard_map/dynamic_slice | solution.py:537
  35.5 0.7 fusion.7
  36.2 0.0 copy-done.13
  36.2 0.1 copy.16
  36.4 0.6 copy-done.10
  37.0 0.6 copy-done.11
  37.6 0.6 rev.6
  38.2 2.5 %copy.20.refs_8_.refs_6_.refs_7_ = bf16[63,64,128]{2,1,0:T(8,128)(2,1)S(1)} copy(bf16[63,64,128]{1,2,0:T(8,128)(2,1)} %constant_dynamic-slice_fusion) | data formatting | bytes 2064384 | tf_op jit(solution)/shard_map/optimization_barrier | solution.py:536
  40.8 0.0 copy-start.7
  40.8 0.9 fusion.4
  41.7 0.0 copy-start.5
  41.7 0.0 copy-start.6
  41.7 1.3 slice_negate_fusion
  43.0 0.1 fusion.9
  43.1 0.0 copy-start.8
  43.1 0.1 pad_maximum_fusion.1
  43.2 1.2 dynamic-slice_bitcast_fusion.1.refs_11_.refs_9_.refs_10_
  44.5 1.3 dynamic-slice_bitcast_fusion.refs_10_.refs_8_.refs_9_
  45.8 0.0 collective-permute-done.refs_1_
  45.8 0.0 collective-permute-done.1.refs_3_
  45.9 0.0 copy-start
  45.9 2.7 %copy-done = bf16[1,63,252,192]{2,3,1,0:T(8,128)(2,1)S(1)} copy-done((bf16[1,63,252,192]{2,3,1,0:T(8,128)(2,1)S(1)}, bf16[1,63,252,192]{2,3,1,0:T(8,128)(2,1)}, u32[]{:S(2)}) %copy-start) | copy-done | bytes 6096408
  48.6 17.8 %spectral_0.1 = f32[128,128]{1,0:T(8,128)S(1)} custom-call(bf16[32,64,128]{2,1,0:T(8,128)(2,1)S(1)} %copy-done.6, bf16[32,64,128]{2,1,0:T(8,128)(2,1)S(1)} %collective-permute-done.refs_1_, bf16[63,64,128]{2,1,0:T(8,128)(2,1)S(1)} %copy-done.5, bf16[63,64,128]{2,1,0:T(8,128)(2,1)} %collective-permute-done.1.refs_3_, bf16[1,63,192,252]{3,2,1,0:T(8,128)(2,1)S(1)} %bitcast.16, ...), custom_call_target="tpu_custom_call" | custom-call | flops 3170893824 | bytes 16000000 | tf_op jit(solution)/shard_map/spectral_0/pallas_call | solution.py:460
  66.5 0.1 collective-permute-start.2
  66.6 1.2 collective-permute-done.2
  67.8 2.0 %collective-permute-start.3 = (f32[128,128]{1,0:T(8,128)S(1)}, f32[128,128]{1,0:T(8,128)S(1)}, u32[]{:S(2)}, u32[]{:S(2)}) collective-permute-start(f32[128,128]{1,0:T(8,128)S(1)} %add.46), channel_id=1, source_target_pairs={{0,4},{2,6},{4,0},{6,2},{8,12},{10,14},{12,8},{14,10},{16,20},{18,... | collective-permute-start | bytes 196616 | tf_op jit(solution)/shard_map/ppermute | solution.py:507
  69.8 0.1 pad_maximum_fusion.3
  69.9 2.3 %collective-permute-done.3 = f32[128,128]{1,0:T(8,128)S(1)} collective-permute-done((f32[128,128]{1,0:T(8,128)S(1)}, f32[128,128]{1,0:T(8,128)S(1)}, u32[]{:S(2)}, u32[]{:S(2)}) %collective-permute-start.3) | collective-permute-done | bytes 65568 | tf_op jit(solution)/shard_map/ppermute | solution.py:507
  72.2 5.8 %collective-permute-done.4.refs_1_ = bf16[95,64,128]{2,1,0:T(8,128)(2,1)} collective-permute-done((bf16[95,64,128]{2,1,0:T(8,128)(2,1)}, bf16[95,64,128]{2,1,0:T(8,128)(2,1)}, u32[]{:S(2)}, u32[]{:S(2)}) %collective-permute-start.4) | collective-permute-done | bytes 1556512 | tf_op jit(solution)/shard_map/ppermute | solution.py:558
  78.1 0.0 copy-start.3
  78.1 17.8 %spectral_1.1.refs_0_ = f32[128,128]{1,0:T(8,128)S(1)} custom-call(bf16[95,64,128]{2,1,0:T(8,128)(2,1)S(1)} %copy-done.4, bf16[95,64,128]{2,1,0:T(8,128)(2,1)} %collective-permute-done.4.refs_1_, bf16[1,63,192,252]{3,2,1,0:T(8,128)(2,1)S(1)} %bitcast.20, bf16[1,63,192,252]{3,2,1,0:T(8,128)(2,1)S(1)} %bitcast.21, bf16[256,252]{1,0:T(8,128)(2,1)S(1)} %copy-done.7, ...), custom_call_target="tpu_custom_call" | custom-call | flops 3170893824 | bytes 16000000 | tf_op jit(solution)/shard_map/spectral_1/pallas_call | solution.py:460
  95.9 2.2 %collective-permute-start.5 = (f32[128,128]{1,0:T(8,128)S(1)}, f32[128,128]{1,0:T(8,128)S(1)}, u32[]{:S(2)}, u32[]{:S(2)}) collective-permute-start(f32[128,128]{1,0:T(8,128)S(1)} %add.47), channel_id=1, source_target_pairs={{0,8},{2,10},{4,12},{6,14},{8,0},{10,2},{12,4},{14,6},{16,24},{18,... | collective-permute-start | bytes 196616 | tf_op jit(solution)/shard_map/ppermute | solution.py:507
  98.1 2.2 %collective-permute-done.5 = f32[128,128]{1,0:T(8,128)S(1)} collective-permute-done((f32[128,128]{1,0:T(8,128)S(1)}, f32[128,128]{1,0:T(8,128)S(1)}, u32[]{:S(2)}, u32[]{:S(2)}) %collective-permute-start.5) | collective-permute-done | bytes 65568 | tf_op jit(solution)/shard_map/ppermute | solution.py:507
  100.3 3.5 %collective-permute-start.6 = (f32[128,128]{1,0:T(8,128)S(1)}, f32[128,128]{1,0:T(8,128)S(1)}, u32[]{:S(2)}, u32[]{:S(2)}) collective-permute-start(f32[128,128]{1,0:T(8,128)S(1)} %add.48), channel_id=1, source_target_pairs={{0,16},{2,18},{4,20},{6,22},{8,24},{10,26},{12,28},{14,30},{16,0},... | collective-permute-start | bytes 196616 | tf_op jit(solution)/shard_map/ppermute | solution.py:507
  103.8 0.1 pad_maximum_fusion.5
  103.9 2.1 %collective-permute-done.6 = f32[128,128]{1,0:T(8,128)S(1)} collective-permute-done((f32[128,128]{1,0:T(8,128)S(1)}, f32[128,128]{1,0:T(8,128)S(1)}, u32[]{:S(2)}, u32[]{:S(2)}) %collective-permute-start.6) | collective-permute-done | bytes 65568 | tf_op jit(solution)/shard_map/ppermute | solution.py:507
  106.1 4.5 %collective-permute-done.7.refs_2_ = bf16[95,64,128]{2,1,0:T(8,128)(2,1)} collective-permute-done((bf16[95,64,128]{2,1,0:T(8,128)(2,1)}, bf16[95,64,128]{2,1,0:T(8,128)(2,1)}, u32[]{:S(2)}, u32[]{:S(2)}) %collective-permute-start.7) | collective-permute-done | bytes 1556512 | tf_op jit(solution)/shard_map/ppermute | solution.py:558
  110.6 17.7 %spectral_2.1 = f32[256,128]{1,0:T(8,128)S(1)} custom-call(f32[128,128]{1,0:T(8,128)S(1)} %spectral_1.1.refs_0_, bf16[95,64,128]{2,1,0:T(8,128)(2,1)S(1)} %copy-done.3, bf16[95,64,128]{2,1,0:T(8,128)(2,1)} %collective-permute-done.7.refs_2_, bf16[1,63,192,252]{3,2,1,0:T(8,128)(2,1)S(1)} %bitcast.22, bf16[1,63,192,252]{3,2,1,0:T(8,128)(2,1)S(1)} %bitcast.23, ...), custom_call_target="tpu_custom_call" | custom-call | flops 3170893824 | bytes 16000000 | tf_op jit(solution)/shard_map/spectral_2/pallas_call | solution.py:460
  128.3 0.1 collective-permute-start.8
  128.3 1.3 collective-permute-done.8
  129.7 1.8 %collective-permute-start.9 = (f32[256,128]{1,0:T(8,128)S(1)}, f32[256,128]{1,0:T(8,128)S(1)}, u32[]{:S(2)}, u32[]{:S(2)}) collective-permute-start(f32[256,128]{1,0:T(8,128)S(1)} %add.50), channel_id=1, source_target_pairs={{0,4},{2,6},{4,0},{6,2},{8,12},{10,14},{12,8},{14,10},{16,20},{18,... | collective-permute-start | bytes 393224 | tf_op jit(solution)/shard_map/ppermute | solution.py:507
  131.5 3.8 %collective-permute-done.9 = f32[256,128]{1,0:T(8,128)S(1)} collective-permute-done((f32[256,128]{1,0:T(8,128)S(1)}, f32[256,128]{1,0:T(8,128)S(1)}, u32[]{:S(2)}, u32[]{:S(2)}) %collective-permute-start.9) | collective-permute-done | bytes 131104 | tf_op jit(solution)/shard_map/ppermute | solution.py:507
  135.3 1.9 %collective-permute-start.10 = (f32[256,128]{1,0:T(8,128)S(1)}, f32[256,128]{1,0:T(8,128)S(1)}, u32[]{:S(2)}, u32[]{:S(2)}) collective-permute-start(f32[256,128]{1,0:T(8,128)S(1)} %add.51), channel_id=1, source_target_pairs={{0,8},{2,10},{4,12},{6,14},{8,0},{10,2},{12,4},{14,6},{16,24},{18,... | collective-permute-start | bytes 393224 | tf_op jit(solution)/shard_map/ppermute | solution.py:507
  137.2 3.2 %collective-permute-done.10 = f32[256,128]{1,0:T(8,128)S(1)} collective-permute-done((f32[256,128]{1,0:T(8,128)S(1)}, f32[256,128]{1,0:T(8,128)S(1)}, u32[]{:S(2)}, u32[]{:S(2)}) %collective-permute-start.10) | collective-permute-done | bytes 131104 | tf_op jit(solution)/shard_map/ppermute | solution.py:507
  140.4 2.9 %collective-permute-start.11 = (f32[256,128]{1,0:T(8,128)S(1)}, f32[256,128]{1,0:T(8,128)S(1)}, u32[]{:S(2)}, u32[]{:S(2)}) collective-permute-start(f32[256,128]{1,0:T(8,128)S(1)} %add.52), channel_id=1, source_target_pairs={{0,16},{2,18},{4,20},{6,22},{8,24},{10,26},{12,28},{14,30},{16,0},... | collective-permute-start | bytes 393224 | tf_op jit(solution)/shard_map/ppermute | solution.py:507
  143.3 4.6 %collective-permute-done.11 = f32[256,128]{1,0:T(8,128)S(1)} collective-permute-done((f32[256,128]{1,0:T(8,128)S(1)}, f32[256,128]{1,0:T(8,128)S(1)}, u32[]{:S(2)}, u32[]{:S(2)}) %collective-permute-start.11) | collective-permute-done | bytes 131104 | tf_op jit(solution)/shard_map/ppermute | solution.py:507
  147.9 1.6 %collective-permute-start.12 = (f32[384,128]{1,0:T(8,128)S(1)}, f32[384,128]{1,0:T(8,128)S(1)}, u32[]{:S(2)}, u32[]{:S(2)}) collective-permute-start(f32[384,128]{1,0:T(8,128)S(1)} %pad_maximum_fusion), channel_id=1, source_target_pairs={{0,1},{1,0},{2,3},{3,2},{4,5},{5,4},{6,7},{7,6},{8,9},{9,8},{10,11... | collective-permute-start | bytes 589832 | tf_op jit(solution)/shard_map/ppermute | solution.py:507
  149.6 4.1 %collective-permute-done.12 = f32[384,128]{1,0:T(8,128)S(1)} collective-permute-done((f32[384,128]{1,0:T(8,128)S(1)}, f32[384,128]{1,0:T(8,128)S(1)}, u32[]{:S(2)}, u32[]{:S(2)}) %collective-permute-start.12) | collective-permute-done | bytes 196640 | tf_op jit(solution)/shard_map/ppermute | solution.py:507
  153.7 0.7 slice_multiply_fusion
  (31 shorter events, 0.2 us)
Async XLA Ops:
  6.5 39.3 %collective-permute-start.1 = (bf16[63,64,128]{2,1,0:T(8,128)(2,1)}, bf16[63,64,128]{2,1,0:T(8,128)(2,1)}, u32[]{:S(2)}, u32[]{:S(2)}) collective-permute-start(bf16[63,64,128]{2,1,0:T(8,128)(2,1)} %forward_0_32.1.refs_2_), channel_id=1, source_target_pairs={{0,1},{1,0},{2,3},{3,2},{4,5},{5,4},{6,7},{7,6},{8,9},{9,8},{10,11... | collective-permute-start | bytes 3096584 | tf_op jit(solution)/shard_map/ppermute | solution.py:558
  13.8 32.0 %collective-permute-start = (bf16[32,64,128]{2,1,0:T(8,128)(2,1)}, bf16[32,64,128]{2,1,0:T(8,128)(2,1)S(1)}, u32[]{:S(2)}, u32[]{:S(2)}) collective-permute-start(bf16[32,64,128]{2,1,0:T(8,128)(2,1)} %forward_0_0.1.refs_0_), channel_id=1, source_target_pairs={{0,1},{1,0},{2,3},{3,2},{4,5},{5,4},{6,7},{7,6},{8,9},{9,8},{10,11... | collective-permute-start | bytes 1572872 | tf_op jit(solution)/shard_map/ppermute | solution.py:558
  20.2 8.7 %copy-start.12 = (bf16[126,192]{0,1:T(8,128)(2,1)S(1)}, bf16[126,192]{0,1:T(8,128)(2,1)}, u32[]{:S(2)}) copy-start(bf16[126,192]{0,1:T(8,128)(2,1)} %param.17) | copy-start | bytes 145156
  20.2 9.0 %copy-start.9 = (bf16[63,128,128]{1,2,0:T(8,128)(2,1)S(1)}, bf16[63,128,128]{1,2,0:T(8,128)(2,1)}, u32[]{:S(2)}) copy-start(bf16[63,128,128]{1,2,0:T(8,128)(2,1)} %constant.52.clone) | copy-start | bytes 6193156
  20.3 57.8 %collective-permute-start.4 = (bf16[95,64,128]{2,1,0:T(8,128)(2,1)}, bf16[95,64,128]{2,1,0:T(8,128)(2,1)}, u32[]{:S(2)}, u32[]{:S(2)}) collective-permute-start(bf16[95,64,128]{2,1,0:T(8,128)(2,1)} %forward_1_0.1.refs_0_), channel_id=1, source_target_pairs={{0,1},{1,0},{2,3},{3,2},{4,5},{5,4},{6,7},{7,6},{8,9},{9,8},{10,11... | collective-permute-start | bytes 4669448 | tf_op jit(solution)/shard_map/ppermute | solution.py:558
  28.7 81.8 %collective-permute-start.7 = (bf16[95,64,128]{2,1,0:T(8,128)(2,1)}, bf16[95,64,128]{2,1,0:T(8,128)(2,1)}, u32[]{:S(2)}, u32[]{:S(2)}) collective-permute-start(bf16[95,64,128]{2,1,0:T(8,128)(2,1)} %forward_2_0.1.refs_1_), channel_id=1, source_target_pairs={{0,1},{1,0},{2,3},{3,2},{4,5},{5,4},{6,7},{7,6},{8,9},{9,8},{10,11... | collective-permute-start | bytes 4669448 | tf_op jit(solution)/shard_map/ppermute | solution.py:558
  31.2 5.0 %copy-start.13 = (bf16[126,192]{0,1:T(8,128)(2,1)S(1)}, bf16[126,192]{0,1:T(8,128)(2,1)}, u32[]{:S(2)}) copy-start(bf16[126,192]{0,1:T(8,128)(2,1)} %param.16) | copy-start | bytes 145156
  36.3 0.6 copy-start.10
  37.0 0.6 copy-start.11
  38.2 39.8 %slice-start = ((s8[6193152]{0:T(1024)(128)(4,1)}), s8[1998848]{0:T(1024)(128)(4,1)S(1)}, s32[]{:S(2)}) async-start(s8[6193152]{0:T(1024)(128)(4,1)} %bitcast.18), calls=%async_computation | async-start | bytes 3997696
  40.8 5.1 %copy-start.7 = (bf16[256,252]{1,0:T(8,128)(2,1)S(1)}, bf16[256,252]{1,0:T(8,128)(2,1)}, u32[]{:S(2)}) copy-start(bf16[256,252]{1,0:T(8,128)(2,1)} %constant.49.clone.refs_6_.refs_4_.refs_5_) | copy-start | bytes 387076
  41.7 4.2 %copy-start.5 = (bf16[63,64,128]{2,1,0:T(8,128)(2,1)S(1)}, bf16[63,64,128]{2,1,0:T(8,128)(2,1)}, u32[]{:S(2)}) copy-start(bf16[63,64,128]{2,1,0:T(8,128)(2,1)} %forward_0_32.1.refs_2_) | copy-start | bytes 3096580
  41.7 4.2 %copy-start.6 = (bf16[32,64,128]{2,1,0:T(8,128)(2,1)S(1)}, bf16[32,64,128]{2,1,0:T(8,128)(2,1)}, u32[]{:S(2)}) copy-start(bf16[32,64,128]{2,1,0:T(8,128)(2,1)} %forward_0_0.1.refs_0_) | copy-start | bytes 1572868
  43.0 2.9 %copy-start.2 = (bf16[63,128,128]{1,2,0:T(8,128)(2,1)S(1)}, bf16[63,128,128]{1,2,0:T(8,128)(2,1)}, u32[]{:S(2)}) copy-start(bf16[63,128,128]{1,2,0:T(8,128)(2,1)} %constant_dynamic-slice_fusion.1) | copy-start | bytes 6193156
  43.1 2.8 %copy-start.1 = (bf16[63,64,128]{1,2,0:T(8,128)(2,1)S(1)}, bf16[63,64,128]{1,2,0:T(8,128)(2,1)}, u32[]{:S(2)}) copy-start(bf16[63,64,128]{1,2,0:T(8,128)(2,1)} %constant_dynamic-slice_fusion) | copy-start | bytes 3096580
  43.1 2.8 %copy-start.8 = (f32[128,128]{1,0:T(8,128)S(1)}, f32[128,128]{1,0:T(8,128)}, u32[]{:S(2)}) copy-start(f32[128,128]{1,0:T(8,128)} %constant.55.clone.refs_12_.refs_10_.refs_11_) | copy-start | bytes 196612
  45.9 2.8 %copy-start = (bf16[1,63,252,192]{2,3,1,0:T(8,128)(2,1)S(1)}, bf16[1,63,252,192]{2,3,1,0:T(8,128)(2,1)}, u32[]{:S(2)}) copy-start(bf16[1,63,252,192]{2,3,1,0:T(8,128)(2,1)} %param.15) | copy-start | bytes 18289156
  48.6 29.4 %slice-start.1 = ((s8[6193152]{0:T(1024)(128)(4,1)}), s8[4194304]{0:T(1024)(128)(4,1)S(1)}, s32[]{:S(2)}) async-start(s8[6193152]{0:T(1024)(128)(4,1)} %bitcast.18), calls=%async_computation.1 | async-start | bytes 8388608
  48.6 29.4 %copy-start.4 = (bf16[95,64,128]{2,1,0:T(8,128)(2,1)S(1)}, bf16[95,64,128]{2,1,0:T(8,128)(2,1)}, u32[]{:S(2)}) copy-start(bf16[95,64,128]{2,1,0:T(8,128)(2,1)} %forward_1_0.1.refs_0_) | copy-start | bytes 4669444
  66.5 1.3 collective-permute-start.2
  67.8 4.4 %collective-permute-start.3 = (f32[128,128]{1,0:T(8,128)S(1)}, f32[128,128]{1,0:T(8,128)S(1)}, u32[]{:S(2)}, u32[]{:S(2)}) collective-permute-start(f32[128,128]{1,0:T(8,128)S(1)} %add.46), channel_id=1, source_target_pairs={{0,4},{2,6},{4,0},{6,2},{8,12},{10,14},{12,8},{14,10},{16,20},{18,... | collective-permute-start | bytes 196616 | tf_op jit(solution)/shard_map/ppermute | solution.py:507
  78.1 32.5 %copy-start.3 = (bf16[95,64,128]{2,1,0:T(8,128)(2,1)S(1)}, bf16[95,64,128]{2,1,0:T(8,128)(2,1)}, u32[]{:S(2)}) copy-start(bf16[95,64,128]{2,1,0:T(8,128)(2,1)} %forward_2_0.1.refs_1_) | copy-start | bytes 4669444
  95.9 4.4 %collective-permute-start.5 = (f32[128,128]{1,0:T(8,128)S(1)}, f32[128,128]{1,0:T(8,128)S(1)}, u32[]{:S(2)}, u32[]{:S(2)}) collective-permute-start(f32[128,128]{1,0:T(8,128)S(1)} %add.47), channel_id=1, source_target_pairs={{0,8},{2,10},{4,12},{6,14},{8,0},{10,2},{12,4},{14,6},{16,24},{18,... | collective-permute-start | bytes 196616 | tf_op jit(solution)/shard_map/ppermute | solution.py:507
  100.3 5.7 %collective-permute-start.6 = (f32[128,128]{1,0:T(8,128)S(1)}, f32[128,128]{1,0:T(8,128)S(1)}, u32[]{:S(2)}, u32[]{:S(2)}) collective-permute-start(f32[128,128]{1,0:T(8,128)S(1)} %add.48), channel_id=1, source_target_pairs={{0,16},{2,18},{4,20},{6,22},{8,24},{10,26},{12,28},{14,30},{16,0},... | collective-permute-start | bytes 196616 | tf_op jit(solution)/shard_map/ppermute | solution.py:507
  128.3 1.4 collective-permute-start.8
  129.7 5.6 %collective-permute-start.9 = (f32[256,128]{1,0:T(8,128)S(1)}, f32[256,128]{1,0:T(8,128)S(1)}, u32[]{:S(2)}, u32[]{:S(2)}) collective-permute-start(f32[256,128]{1,0:T(8,128)S(1)} %add.50), channel_id=1, source_target_pairs={{0,4},{2,6},{4,0},{6,2},{8,12},{10,14},{12,8},{14,10},{16,20},{18,... | collective-permute-start | bytes 393224 | tf_op jit(solution)/shard_map/ppermute | solution.py:507
  135.3 5.0 %collective-permute-start.10 = (f32[256,128]{1,0:T(8,128)S(1)}, f32[256,128]{1,0:T(8,128)S(1)}, u32[]{:S(2)}, u32[]{:S(2)}) collective-permute-start(f32[256,128]{1,0:T(8,128)S(1)} %add.51), channel_id=1, source_target_pairs={{0,8},{2,10},{4,12},{6,14},{8,0},{10,2},{12,4},{14,6},{16,24},{18,... | collective-permute-start | bytes 393224 | tf_op jit(solution)/shard_map/ppermute | solution.py:507
  140.4 7.5 %collective-permute-start.11 = (f32[256,128]{1,0:T(8,128)S(1)}, f32[256,128]{1,0:T(8,128)S(1)}, u32[]{:S(2)}, u32[]{:S(2)}) collective-permute-start(f32[256,128]{1,0:T(8,128)S(1)} %add.52), channel_id=1, source_target_pairs={{0,16},{2,18},{4,20},{6,22},{8,24},{10,26},{12,28},{14,30},{16,0},... | collective-permute-start | bytes 393224 | tf_op jit(solution)/shard_map/ppermute | solution.py:507
  147.9 5.7 %collective-permute-start.12 = (f32[384,128]{1,0:T(8,128)S(1)}, f32[384,128]{1,0:T(8,128)S(1)}, u32[]{:S(2)}, u32[]{:S(2)}) collective-permute-start(f32[384,128]{1,0:T(8,128)S(1)} %pad_maximum_fusion), channel_id=1, source_target_pairs={{0,1},{1,0},{2,3},{3,2},{4,5},{5,4},{6,7},{7,6},{8,9},{9,8},{10,11... | collective-permute-start | bytes 589832 | tf_op jit(solution)/shard_map/ppermute | solution.py:507

commit v5 on v3

--- a/solution.py
+++ b/solution.py
@@ -72,9 +72,7 @@
         self.orders = np.array(orders + [-1] * (self.slots - len(orders)))
 
 
-@functools.lru_cache(maxsize=None)
-def fourier_constants(parts, local):
-    layout = Layout(parts, local)
+def fourier_constants(layout):
     orders = np.maximum(layout.orders, 0)
     angles = 2.0 * math.pi / NLON * (orders[:, None] * np.arange(NLON)[None] % NLON)
     live = (layout.orders >= 0)[:, None]
@@ -144,14 +142,9 @@
 
 
 def gelu_slope(values):
-    size = jnp.abs(values)
-    step = 1.0 / (1.0 + 0.2316419 * size)
-    scale = 1.0 / math.sqrt(2.0 * math.pi)
-    series = 1.330274429 * scale
-    for term in (-1.821255978, 1.781477937, -0.356563782, 0.319381530):
-        series = series * step + term * scale
-    below = jnp.exp(-0.5 * values * values) * (series * step - scale * size)
-    return jnp.where(values >= 0.0, 1.0 - below, below)
+    cumulative = 0.5 * (1.0 + lax.erf(values / math.sqrt(2.0)))
+    density = jnp.exp(-0.5 * values * values) / math.sqrt(2.0 * math.pi)
+    return cumulative + values * density
 
 
 def grid_rows(layout, north, south, quad, group):
@@ -167,7 +160,7 @@
 
 
 def scatter_rows(layout, values, scratch, quad, group):
-    slots = layout.slots
+    slots = values.shape[0] // 2
     for which in range(2):
         columns = slice(which * LANES, (which + 1) * LANES)
         upper, lower = interleave(values[:slots, columns], values[slots:, columns])
@@ -219,7 +212,11 @@
     return copies
 
 
-def forward_kernel(layout, chunk, index, fields, basis, pair_all, out, scratch, buffer, pair_fwd, sems, pair_sem):
+def forward_kernel(layout, chunk, bounds, index, fields, basis_all, pair_all, *refs):
+    outs, refs = refs[: len(bounds) - 1], refs[len(bounds) - 1 :]
+    scratch, buffer, basis, stage, pair_fwd, sems, basis_sem, pair_sem, out_sems = refs
+    basis_copy = pltpu.make_async_copy(basis_all, basis, basis_sem)
+    basis_copy.start()
     copies = band_copies(layout, chunk, fields, buffer, sems)
     for started in copies:
         for copy in started:
@@ -229,6 +226,7 @@
     if layout.rows > layout.local:
         shape = (layout.rows - layout.local,) + buffer.shape[1:]
         buffer[layout.local :] = jnp.zeros(shape, buffer.dtype)
+    basis_copy.wait()
     for group, started in enumerate(copies):
         for copy in started:
             copy.wait()
@@ -239,70 +237,100 @@
                 rows += [buffer[latitude], buffer[latitude + layout.half]]
             grid = jnp.concatenate(rows, axis=0)
             scatter_rows(layout, dot(basis[...], grid, (1, 1)), scratch, quad, group)
-    tables.wait()
 
     def low_block(order, carry):
-        out[order] = order_rows(layout, scratch, order, 1)
+        stage[order] = order_rows(layout, scratch, order, 1)
         return carry
 
     def pair_block(pair, carry):
         values = order_rows(layout, scratch, layout.low + 2 * pair, 2)
-        out[layout.low + pair] = dot(pair_fwd[pair], values).astype(jnp.bfloat16)
+        stage[layout.low + pair] = dot(pair_fwd[pair], values).astype(jnp.bfloat16)
         return carry
 
-    lax.fori_loop(0, layout.low, low_block, 0, unroll=8)
+    flushes = []
+
+    def flush(first, last):
+        at = max(at for at in range(len(outs)) if bounds[at] <= first)
+        flushes.append(
+            pltpu.make_async_copy(
+                stage.at[pl.ds(first, last - first)],
+                outs[at].at[pl.ds(first - bounds[at], last - first)],
+                out_sems.at[len(flushes)],
+            )
+        )
+        flushes[-1].start()
+
+    middle = layout.low // 2
+    for first, last in ((0, middle), (middle, layout.low)):
+        lax.fori_loop(first, last, low_block, 0, unroll=8)
+        flush(first, last)
+    tables.wait()
     lax.fori_loop(0, layout.pairs, pair_block, 0, unroll=8)
+    flush(layout.low, layout.blocks)
+    for copy in flushes:
+        copy.wait()
 
 
 def mix(spectral, swapped, real_rows, imag_rows):
     return (spectral * real_rows + swapped * imag_rows).astype(jnp.bfloat16)
 
 
-def spectral_kernel(layout, carries, *refs):
-    ahead = None
-    if carries:
-        ahead, refs = refs[0], refs[1:]
-    own, others = refs[0], refs[1 : layout.parts]
-    north, south, basis, analysis, synth_low, back_low = refs[layout.parts : layout.parts + 6]
-    pair_synth, pair_back, place, real_ref, imag_ref = refs[layout.parts + 6 : layout.parts + 11]
-    out, scratch, returned, spec_low, swap_low, spec_pair, swap_pair = refs[layout.parts + 11 :]
+def order_groups(layout):
+    for start in range(0, layout.low, GROUP):
+        yield start, min(start + GROUP, layout.low), start // 16 * 16
+
+
+def low_kernel(layout, *refs):
+    low_orders(layout, refs[: layout.parts], *refs[layout.parts :])
+
+
+def low_orders(layout, held, analysis, synth_low, real_ref, imag_ref, grid_low, spec_low, swap_low):
+    degrees = layout.degrees
+    for start, stop, top in order_groups(layout):
+        real_rows = real_ref[top:degrees, :]
+        imag_rows = imag_ref[top:degrees, :]
+
+        def low_block(order, carry):
+            values = jnp.concatenate([ref[order] for ref in held], axis=0)
+            spectral = dot(analysis[order, top:degrees, :], values).astype(jnp.bfloat16)
+            spec_low[order, top:degrees, :] = spectral
+            return carry
+
+        def mix_block(order, carry):
+            spectral = spec_low[order, top:degrees, :].astype(jnp.float32)
+            swapped = swap_halves(spectral)
+            swap_low[order, top:degrees, :] = swapped.astype(jnp.bfloat16)
+            mixed = mix(spectral, swapped, real_rows, imag_rows)
+            begin = pl.multiple_of(order * layout.pitch, 8)
+            grid_low[pl.ds(begin, layout.rows), :] = dot(synth_low[order, :, top:degrees], mixed)
+            return carry
+
+        lax.fori_loop(start, stop, low_block, 0, unroll=8)
+        lax.fori_loop(start, stop, mix_block, 0, unroll=8)
+
+
+def spectral_kernel(layout, apart, *refs):
+    held, lows, refs = refs[: layout.parts], refs[layout.parts : layout.parts + 2 + apart], refs[layout.parts + 2 + apart :]
+    north, south, basis, back_low, pair_synth, pair_back, place, real_ref, imag_ref = refs[:9]
+    out, scratch, returned, spec_low, swap_low, spec_pair, swap_pair, sems = refs[9:]
+    offset = 0 if apart else layout.low
     group = pl.program_id(0)
     rows, degrees, low = layout.rows, layout.degrees, layout.low
-
-    def groups():
-        for start in range(0, low, GROUP):
-            yield start, min(start + GROUP, low), start // 16 * 16
+    if apart:
+        targets = (scratch.at[pl.ds(0, low * layout.pitch)], spec_low, swap_low)
+        copies = [pltpu.make_async_copy(lows[at], targets[at], sems.at[at]) for at in range(3)]
 
     @pl.when(group == 0)
     def _():
-        for start, stop, top in groups():
-            real_rows = real_ref[top:degrees, :]
-            imag_rows = imag_ref[top:degrees, :]
-
-            def low_block(order, carry):
-                values = jnp.concatenate([own[order]] + [ref[order] for ref in others], axis=0)
-                spectral = dot(analysis[order, top:degrees, :], values).astype(jnp.bfloat16)
-                spec_low[order, top:degrees, :] = spectral
-                return carry
-
-            def mix_block(order, carry):
-                spectral = spec_low[order, top:degrees, :].astype(jnp.float32)
-                swapped = swap_halves(spectral)
-                swap_low[order, top:degrees, :] = swapped.astype(jnp.bfloat16)
-                mixed = mix(spectral, swapped, real_rows, imag_rows)
-                begin = pl.multiple_of(order * layout.pitch, 8)
-                scratch[pl.ds(begin, rows), :] = dot(synth_low[order, :, top:degrees], mixed)
-                return carry
-
-            lax.fori_loop(start, stop, low_block, 0, unroll=8)
-            lax.fori_loop(start, stop, mix_block, 0, unroll=8)
-
+        if apart:
+            for copy in copies:
+                copy.start()
+        else:
+            low_orders(layout, held, *lows, real_ref, imag_ref, scratch, spec_low, swap_low)
         line = lax.broadcasted_iota(jnp.int32, (rows, LANES), 0)
 
         def pair_block(pair, carry):
-            total = own[low + pair].astype(jnp.float32)
-            for ref in others:
-                total = total + ref[low + pair].astype(jnp.float32)
+            total = sum(ref[offset + pair].astype(jnp.float32) for ref in held)
             spectral = total.astype(jnp.bfloat16)
             spec_pair[pair] = spectral
             natural = line >= layout.first_natural + pair
@@ -324,6 +352,8 @@
             scratch[used : layout.slots * layout.pitch, :] = jnp.zeros(
                 (layout.slots * layout.pitch - used, LANES), jnp.float32
             )
+        if apart:
+            copies[0].wait()
 
     for quad in range(PAIRS // 2):
         modes = gather_rows(layout, scratch, quad, group)
@@ -334,12 +364,16 @@
 
     @pl.when(group == pl.num_programs(0) - 1)
     def _():
+        if apart:
+            copies[1].wait()
+            copies[2].wait()
+
         def products(spectral, swapped, back):
             return spectral.astype(jnp.float32) * back, swapped.astype(jnp.float32) * back
 
         zeros = jnp.zeros((degrees, LANES), jnp.float32)
         same, cross = zeros, zeros
-        for start, stop, top in groups():
+        for start, stop, top in order_groups(layout):
 
             def low_block(order, carry):
                 back = dot(back_low[order, top:degrees, :], order_rows(layout, returned, order, 1))
@@ -384,10 +418,7 @@
         real = same + swap_halves(same)
         imag = cross - swap_halves(cross)
         lane = lax.broadcasted_iota(jnp.int32, real.shape, 1)
-        grads = jnp.where(lane < LANES // 2, real, imag)
-        out[out.shape[0] - LANES :, :] = grads.T
-        if ahead is not None:
-            out[: out.shape[0] - LANES, :] = ahead[...]
+        out[...] = jnp.where(lane < LANES // 2, real, imag).T
 
 
 def grid_specs(layout, chunk):
@@ -404,46 +435,59 @@
     return pl.BlockSpec(memory_space=pltpu.VMEM)
 
 
-def forward_call(layout, chunk, index, fields, basis, pair_fwd):
-    work = 2 * 2 * layout.slots * NLON * layout.rows * LANES // 2
+def forward_call(layout, chunk, bounds, index, fields, pair_fwd):
+    basis = jnp.asarray(fourier_constants(layout)[0])
+    slots = basis.shape[0] // 2
     groups = layout.half // PAIRS
+    anywhere = pl.BlockSpec(memory_space=pl.ANY)
+    counts = [last - first for first, last in zip(bounds, bounds[1:])]
     return pl.pallas_call(
-        functools.partial(forward_kernel, layout, chunk),
-        in_specs=[
-            pl.BlockSpec(memory_space=pltpu.SMEM),
-            pl.BlockSpec(memory_space=pl.ANY),
-            whole(),
-            pl.BlockSpec(memory_space=pl.ANY),
-        ],
-        out_specs=whole(),
-        out_shape=jax.ShapeDtypeStruct((layout.blocks, layout.rows, LANES), jnp.bfloat16),
+        functools.partial(forward_kernel, layout, chunk, bounds),
+        in_specs=[pl.BlockSpec(memory_space=pltpu.SMEM)] + [anywhere] * 3,
+        out_specs=[anywhere] * len(counts),
+        out_shape=[jax.ShapeDtypeStruct((count, layout.rows, LANES), jnp.bfloat16) for count in counts],
         scratch_shapes=[
-            pltpu.VMEM((layout.slots * layout.pitch, LANES), jnp.float32),
+            pltpu.VMEM((slots * layout.pitch, LANES), jnp.float32),
             pltpu.VMEM((layout.rows, LANES // 2, NLON), jnp.bfloat16),
+            pltpu.VMEM(basis.shape, jnp.bfloat16),
+            pltpu.VMEM((layout.blocks, layout.rows, LANES), jnp.bfloat16),
             pltpu.VMEM(pair_fwd.shape[1:], jnp.bfloat16),
             pltpu.SemaphoreType.DMA((2 * groups,)),
             pltpu.SemaphoreType.DMA,
+            pltpu.SemaphoreType.DMA,
+            pltpu.SemaphoreType.DMA((3,)),
         ],
         compiler_params=pltpu.CompilerParams(vmem_limit_bytes=FORWARD_VMEM),
-        cost_estimate=pl.CostEstimate(flops=2 * work, bytes_accessed=8_000_000, transcendentals=0),
+        cost_estimate=pl.CostEstimate(flops=1_000_000, bytes_accessed=100_000, transcendentals=0),
         name=f"forward_{chunk}",
     )(index, fields, basis, pair_fwd)
 
 
-def spectral_call(layout, chunk, coeffs, cotangent, tables, real_rows, imag_rows, ahead=None):
-    work = 2 * 2 * layout.slots * NLON * layout.rows * LANES // 2
-    operands = list(coeffs) + [cotangent, cotangent] + list(tables) + [real_rows, imag_rows]
-    specs = [whole()] * layout.parts + grid_specs(layout, chunk) + [whole()] * (len(tables) + 2)
-    height = LANES
-    if ahead is not None:
-        operands, specs = [ahead] + operands, [whole()] + specs
-        height += ahead.shape[0]
+def low_call(layout, chunk, coeffs, tables, real_rows, imag_rows):
+    operands = list(coeffs) + list(tables) + [real_rows, imag_rows]
+    spectra = jax.ShapeDtypeStruct((layout.low, layout.degrees, LANES), jnp.bfloat16)
     return pl.pallas_call(
-        functools.partial(spectral_kernel, layout, ahead is not None),
+        functools.partial(low_kernel, layout),
+        in_specs=[whole()] * len(operands),
+        out_specs=[whole()] * 3,
+        out_shape=[jax.ShapeDtypeStruct((layout.low * layout.pitch, LANES), jnp.float32), spectra, spectra],
+        compiler_params=pltpu.CompilerParams(vmem_limit_bytes=VMEM),
+        cost_estimate=pl.CostEstimate(flops=8_000_000_000, bytes_accessed=30_000_000, transcendentals=0),
+        name=f"low_{chunk}",
+    )(*operands)
+
+
+def spectral_call(layout, chunk, apart, blocks, lows, cotangent, tables, real_rows, imag_rows):
+    operands = list(blocks) + list(lows) + [cotangent, cotangent] + list(tables) + [real_rows, imag_rows]
+    low_spec = pl.BlockSpec(memory_space=pl.ANY) if apart else whole()
+    specs = [whole()] * len(blocks) + [low_spec] * len(lows)
+    specs += grid_specs(layout, chunk) + [whole()] * (len(tables) + 2)
+    return pl.pallas_call(
+        functools.partial(spectral_kernel, layout, apart),
         grid=(layout.half // PAIRS,),
         in_specs=specs,
         out_specs=whole(),
-        out_shape=jax.ShapeDtypeStruct((height, layout.degrees), jnp.float32),
+        out_shape=jax.ShapeDtypeStruct((LANES, layout.degrees), jnp.float32),
         scratch_shapes=[
             pltpu.VMEM((layout.slots * layout.pitch, LANES), jnp.float32),
             pltpu.VMEM((layout.slots * layout.pitch, LANES), jnp.float32),
@@ -451,9 +495,10 @@
             pltpu.VMEM((layout.low, layout.degrees, LANES), jnp.bfloat16),
             pltpu.VMEM((layout.pairs, layout.rows, LANES), jnp.bfloat16),
             pltpu.VMEM((layout.pairs, layout.rows, LANES), jnp.bfloat16),
+            pltpu.SemaphoreType.DMA((3,)),
         ],
         compiler_params=pltpu.CompilerParams(vmem_limit_bytes=VMEM),
-        cost_estimate=pl.CostEstimate(flops=6 * work, bytes_accessed=16_000_000, transcendentals=0),
+        cost_estimate=pl.CostEstimate(flops=8_000_000_000, bytes_accessed=30_000_000, transcendentals=0),
         name=f"spectral_{chunk}",
     )(*operands)
 
@@ -468,19 +513,30 @@
     return found
 
 
-def sum_over(value, axis):
+def sum_steps(axis):
     size = lax.axis_size(axis)
-    stride = 1
+    steps, stride = [], 1
     for radix in radices(size):
-        total = value
-        for turn in range(1, radix):
-            pairs = []
-            for index in range(size):
-                digit = index // stride % radix
-                pairs.append((index, index + ((digit + turn) % radix - digit) * stride))
-            total = total + lax.ppermute(value, axis, pairs)
-        value = total
+        steps.append((axis, stride, radix))
         stride *= radix
+    return steps
+
+
+def hop_parcels(value, step):
+    axis, stride, radix = step
+    parcels = []
+    for turn in range(1, radix):
+        pairs = []
+        for index in range(lax.axis_size(axis)):
+            digit = index // stride % radix
+            pairs.append((index, index + ((digit + turn) % radix - digit) * stride))
+        parcels.append(lax.ppermute(value, axis, pairs))
+    return parcels
+
+
+def sum_over(value, steps):
+    for step in steps:
+        value = sum(hop_parcels(value, step), value)
     return value
 
 
@@ -498,7 +554,7 @@
     layout = Layout(parts, fields.shape[1])
     width = LANES // 2
     chunks = fields.shape[-1] // width
-    basis, inverse = (jnp.asarray(a) for a in fourier_constants(parts, layout.local))
+    inverse = jnp.asarray(fourier_constants(layout)[1])
     constants = legendre_constants(parts, layout.local)
 
     def local_table(name):
@@ -516,37 +572,82 @@
     synth_low = bands("synth_low", index, 1)
     back_low = jnp.swapaxes(synth_low, 1, 2)
     pair_tables = [local_table(name) for name in ("pair_synth", "pair_back")]
-    tables = [inverse, analysis, synth_low, back_low] + pair_tables + [jnp.asarray(constants["place"])]
+    low_tables = [analysis, synth_low]
+    tables = [inverse, back_low] + pair_tables + [jnp.asarray(constants["place"])]
     fields, cotangent = jnp.swapaxes(fields, 2, 3), jnp.swapaxes(cotangent, 2, 3)
     real_all = filter_rows(layout, spec_real)
     imag_all = filter_rows(layout, spec_imag)
 
-    received = []
+    def others(sent):
+        routes = [[(source, (source + shift) % parts) for source in range(parts)] for shift in range(1, parts)]
+        return [lax.ppermute(sent, "space", route) for route in routes]
+
+    held = []
     for chunk in range(chunks):
-        own = forward_call(layout, chunk, place, fields, basis, pair_fwd)
-        blocks = [own]
-        for shift in range(1, parts):
-            route = [(source, (source + shift) % parts) for source in range(parts)]
-            blocks.append(lax.ppermute(own, "space", route))
-        received.append(blocks)
-
-    totals, ahead = [], None
+        if chunk == chunks - 1:
+            place, low_tables, tables = lax.optimization_barrier((place, low_tables, tables))
+        bounds = (0, layout.blocks) if chunk < chunks - 1 else (0, layout.low, layout.blocks)
+        made = forward_call(layout, chunk, bounds, place, fields, pair_fwd)
+        place, made = lax.optimization_barrier((place, list(made)))
+        if len(made) > 1 and held:
+            made[1], held[0][1] = lax.optimization_barrier((made[1], held[0][1]))
+        held += [[own] + others(own) for own in made]
+
+    hops, last_hops = sum_steps("dp"), sum_steps("space")
+    waiting = []
+
+    def hop_all(limit, tie):
+        moved = []
+        for value, done in waiting:
+            if done < limit:
+                parcels = hop_parcels(value, (hops + last_hops)[done])
+                parcels, value, tie = lax.optimization_barrier((parcels, value, tie))
+                value, done = sum(parcels, value), done + 1
+            moved.append((value, done))
+        waiting[:] = moved
+        return tie
+
+    def before(values):
+        if not waiting:
+            return values
+        values, sums = lax.optimization_barrier((values, [value for value, _ in waiting]))
+        waiting[:] = [(value, done) for value, (_, done) in zip(sums, waiting)]
+        return values
+
     for chunk in range(chunks):
         columns = slice(chunk * width, (chunk + 1) * width)
         real, imag = real_all[:, columns], imag_all[:, columns]
         real_rows = jnp.concatenate([real, real], axis=1)
         imag_rows = jnp.concatenate([-imag, imag], axis=1)
-        coeffs = received[chunk]
-        if totals:
-            coeffs[0], totals[-1] = lax.optimization_barrier((coeffs[0], totals[-1]))
-        grads = spectral_call(layout, chunk, coeffs, cotangent, tables, real_rows, imag_rows, ahead)
-        if chunk == chunks - 2:
-            ahead = grads
+        blocks, lows, apart = held[chunk], low_tables, chunk == chunks - 1
+        if apart:
+            lows = low_call(layout, chunk, blocks, low_tables, real_rows, imag_rows)
+            lows = before(hop_all(len(hops), lows))
+            blocks = held[-1]
+        grads = spectral_call(layout, chunk, apart, blocks, lows, cotangent, tables, real_rows, imag_rows)
+        if not apart:
+            grads = hop_all(len(hops), grads)
+            waiting.append((grads, 0))
+            if chunk < chunks - 2:
+                for _ in range(len(hops) // 2):
+                    waiting[-1] = (sum_over(waiting[-1][0], hops[waiting[-1][1] :][:1]), waiting[-1][1] + 1)
+                held[chunk + 1] = before(held[chunk + 1])
         else:
-            totals.append(sum_over(sum_over(grads, "dp"), "space"))
+            grads = hop_all(len(hops) + len(last_hops), grads)
+            waiting.append((grads, 0))
+
+    total, done = waiting.pop()
+    hops = hops + last_hops
+    while done < len(hops):
+        joined = [value for value, at in waiting if at == done]
+        waiting = [(value, at) for value, at in waiting if at != done]
+        if joined:
+            total = jnp.concatenate(joined + [total], axis=0)
+        total, done = sum_over(total, hops[done : done + 1]), done + 1
+    rows = jnp.concatenate([value for value, _ in waiting] + [total], axis=0)
+    rows = rows.reshape(chunks, 2, width, layout.degrees)
 
     batch_total = fields.shape[0] * lax.axis_size("dp")
-    rows = jnp.concatenate(totals, axis=0).reshape(chunks, 2, width, layout.degrees)
     real, imag = (rows[:, part, :, :MODES].reshape(chunks * width, MODES) for part in range(2))
     return (real.T / batch_total, imag.T / batch_total)
 

time: 177 us -> 147 us (0.83)
  waiting for transfers between devices: 58.4 us -> 31.6 us
  Pallas kernels: 77.8 us -> 71.7 us
    ppermute x13 -> x16, waiting for transfers between devices: 58.4 us -> 31.6 us  [the longest x12 18.7 us: hop_parcels(): parcels.append(lax.ppermute(value, axis, pairs))]
    pallas_call x6 -> x7, Pallas kernels: 77.8 us -> 71.7 us  [the longest x3 47.4 us: spectral_call(): pl.pallas_call(functools.partial(spectral_kernel, layout, apart), grid=(l...]
    unnamed x28 -> x32, local copies, waits for them, and re-layouts: 4.45 us -> 5.49 us
    ppermute x13 -> x16, starting transfers between devices: 22.5 us -> 22.9 us  [the longest x12 16.2 us: hop_parcels(): parcels.append(lax.ppermute(value, axis, pairs))]
  transfers between devices with their start and end apart: 13 -> 16, of which waited for: 11 -> 9; matrix products, arithmetic and copies ran while one was open for 7% -> 9% of each run, Pallas kernels for 29% -> 45%
where the time goes in v5:
time: 147 us
  Pallas kernels  71.7 us (49%)
  waiting for transfers between devices  31.6 us (21%)
  starting transfers between devices  22.9 us (16%)
  local copies, waits for them, and re-layouts  17.3 us (12%)
  other arithmetic  2.31 us (2%)
    pallas_call x3, Pallas kernels, spectral_call(): pl.pallas_call(functools.partial(spectral_kernel, layout, apart), grid=(l...  47.4 us
    ppermute x12, waiting for transfers between devices, hop_parcels(): parcels.append(lax.ppermute(value, axis, pairs))  18.7 us
    pallas_call x3, Pallas kernels, forward_call(): pl.pallas_call(functools.partial(forward_kernel, layout, chunk, bounds),...  16.9 us
    ppermute x12, starting transfers between devices, hop_parcels(): parcels.append(lax.ppermute(value, axis, pairs))  16.2 us
    ppermute x4, waiting for transfers between devices, others(): return [lax.ppermute(sent, 'space', route) for route in routes]  12.9 us
    pallas_call x1, Pallas kernels, low_call(): pl.pallas_call(functools.partial(low_kernel, layout), in_specs=[whole()]...  7.39 us
    ppermute x4, starting transfers between devices, others(): return [lax.ppermute(sent, 'space', route) for route in routes]  6.77 us
    dynamic_slice x2, local copies, waits for them, and re-layouts, bands(): lax.dynamic_slice_in_dim(table, first * layout.rows, count * layout.rows, 1)  6.62 us
  transfers between devices with their start and end apart: 16, of which 9 were waited for; matrix products, arithmetic and copies ran while one was open for 9% of the time, Pallas kernels for 45%

profile of v5, /device:TPU:0, one launch (start us, length us, event | category | flops | bytes accessed | tf_op | source)
XLA Modules:
  0.0 146.8 jit_solution(898291306905713219)
XLA Ops:
  0.6 5.7 %forward_0.1.refs_0_ = bf16[95,64,128]{2,1,0:T(8,128)(2,1)} custom-call(s32[1]{0:T(128)} %bitcast.index, bf16[1,63,192,252]{3,2,1,0:T(8,128)(2,1)} %bitcast.30, bf16[256,252]{1,0:T(8,128)(2,1)} %constant.52.clone.basis_all, bf16[2,32,64,128]{3,2,1,0:T(8,128)(2,1)} %constant.46.clone.pair_all), custom_call_target="tpu_custom_call" | custom-call | flops 1000000 | bytes 100000 | tf_op jit(solution)/shard_map/forward_0/pallas_call | solution.py:444
  6.3 3.0 %collective-permute-start.1 = (bf16[95,64,128]{2,1,0:T(8,128)(2,1)}, bf16[95,64,128]{2,1,0:T(8,128)(2,1)}, u32[]{:S(2)}, u32[]{:S(2)}) collective-permute-start(bf16[95,64,128]{2,1,0:T(8,128)(2,1)} %forward_0.1.refs_0_), channel_id=1, source_target_pairs={{0,1},{1,0},{2,3},{3,2},{4,5},{5,4},{6,7},{7,6},{8,9},{9,8},{10,11... | collective-permute-start | bytes 4669448 | tf_op jit(solution)/shard_map/ppermute | solution.py:583
  9.4 5.6 %forward_1.1.refs_0_ = bf16[95,64,128]{2,1,0:T(8,128)(2,1)} custom-call(s32[1]{0:T(128)} %bitcast.index, bf16[1,63,192,252]{3,2,1,0:T(8,128)(2,1)} %bitcast.31, bf16[256,252]{1,0:T(8,128)(2,1)} %constant.52.clone.basis_all, bf16[2,32,64,128]{3,2,1,0:T(8,128)(2,1)} %constant.46.clone.pair_all), custom_call_target="tpu_custom_call" | custom-call | flops 1000000 | bytes 100000 | tf_op jit(solution)/shard_map/forward_1/pallas_call | solution.py:444
  15.0 0.1 collective-permute-start
  15.1 4.3 %constant_dynamic-slice_fusion.1 = bf16[63,128,128]{1,2,0:T(8,128)(2,1)} fusion(bf16[63,256,128]{1,2,0:T(8,128)(2,1)} %constant.47.clone, s32[]{:T(128)S(6)} %select_n.12), kind=kLoop, calls=%fused_computation.22 | loop fusion | bytes 4128772 | tf_op jit(solution)/shard_map/dynamic_slice | solution.py:568
  19.4 2.3 %constant_dynamic-slice_fusion = bf16[63,64,128]{1,2,0:T(8,128)(2,1)S(1)} fusion(bf16[63,128,128]{1,2,0:T(8,128)(2,1)} %constant.48.clone, s32[]{:T(128)S(6)} %select_n.13), kind=kLoop, calls=%fused_computation.21 | loop fusion | bytes 2064388 | tf_op jit(solution)/shard_map/dynamic_slice | solution.py:568
  21.7 0.0 copy-done.10
  21.7 0.9 dynamic-slice_bitcast_fusion.1.refs_9_.refs_10_
  22.6 1.3 dynamic-slice_bitcast_fusion.refs_8_.refs_9_
  23.9 5.6 %forward_2.1 = (bf16[63,64,128]{2,1,0:T(8,128)(2,1)}, bf16[32,64,128]{2,1,0:T(8,128)(2,1)}) custom-call(s32[1]{0:T(128)} %bitcast.index, bf16[1,63,192,252]{3,2,1,0:T(8,128)(2,1)} %bitcast.32, bf16[256,252]{1,0:T(8,128)(2,1)} %constant.52.clone.basis_all, bf16[2,32,64,128]{3,2,1,0:T(8,128)(2,1)} %constant.46.clone.pair_all), custom_call_target="tpu_custom_call" | custom-call | flops 1000000 | bytes 100000 | tf_op jit(solution)/shard_map/forward_2/pallas_call | solution.py:444
  29.5 0.0 copy-start.11
  29.5 0.0 copy-start.12
  29.5 2.1 %collective-permute-start.7 = (bf16[63,64,128]{2,1,0:T(8,128)(2,1)}, bf16[63,64,128]{2,1,0:T(8,128)(2,1)}, u32[]{:S(2)}, u32[]{:S(2)}) collective-permute-start(bf16[63,64,128]{2,1,0:T(8,128)(2,1)} %get-tuple-element.72.refs_0_), channel_id=1, source_target_pairs={{0,1},{1,0},{2,3},{3,2},{4,5},{5,4},{6,7},{7,6},{8,9},{9,8},{10,11... | collective-permute-start | bytes 3096584 | tf_op jit(solution)/shard_map/ppermute | solution.py:583
  31.6 2.1 %copy.20.refs_3_ = bf16[63,64,128]{2,1,0:T(8,128)(2,1)} copy(bf16[63,64,128]{1,2,0:T(8,128)(2,1)S(1)} %constant_dynamic-slice_fusion) | data formatting | bytes 2064384 | tf_op jit(solution)/shard_map/optimization_barrier | solution.py:588
  33.7 0.1 copy.16
  33.9 0.7 rev.6
  34.6 0.1 copy.18
  34.7 0.1 rev.7
  34.8 0.0 copy-start
  34.8 0.0 copy-start.3
  34.8 0.9 fusion.4
  35.8 0.1 fusion.9
  35.9 0.1 slice_negate_fusion
  36.0 0.1 pad_maximum_fusion.1
  36.1 8.4 %collective-permute-done.1.refs_1_ = bf16[95,64,128]{2,1,0:T(8,128)(2,1)} collective-permute-done((bf16[95,64,128]{2,1,0:T(8,128)(2,1)}, bf16[95,64,128]{2,1,0:T(8,128)(2,1)}, u32[]{:S(2)}, u32[]{:S(2)}) %collective-permute-start.1) | collective-permute-done | bytes 1556512 | tf_op jit(solution)/shard_map/ppermute | solution.py:583
  44.5 0.0 copy-done.9
  44.6 1.4 copy-done.2
  46.0 1.0 copy-done.4
  47.0 2.8 %copy-done.5 = bf16[1,63,252,192]{2,3,1,0:T(8,128)(2,1)S(1)} copy-done((bf16[1,63,252,192]{2,3,1,0:T(8,128)(2,1)S(1)}, bf16[1,63,252,192]{2,3,1,0:T(8,128)(2,1)}, u32[]{:S(2)}) %copy-start.5) | copy-done | bytes 6096408
  49.8 17.8 %spectral_0.1 = f32[128,128]{1,0:T(8,128)S(1)} custom-call(bf16[95,64,128]{2,1,0:T(8,128)(2,1)S(1)} %copy-done.2, bf16[95,64,128]{2,1,0:T(8,128)(2,1)} %collective-permute-done.1.refs_1_, bf16[63,128,128]{2,1,0:T(8,128)(2,1)S(1)} %bitcast.19, bf16[63,64,128]{2,1,0:T(8,128)(2,1)S(1)} %copy-done.3, bf16[1,63,192,252]{3,2,1,0:T(8,128)(2,1)S(1)} %bitcast.22, ...), custom_call_target="tpu_custom_call" | custom-call | flops 8000000000 | bytes 30000000 | tf_op jit(solution)/shard_map/spectral_0/pallas_call | solution.py:485
  67.6 0.1 collective-permute-start.2
  67.7 0.1 pad_maximum_fusion.3
  67.8 1.1 collective-permute-done.2
  68.9 2.1 %collective-permute-start.3 = (f32[128,128]{1,0:T(8,128)S(1)}, f32[128,128]{1,0:T(8,128)S(1)}, u32[]{:S(2)}, u32[]{:S(2)}) collective-permute-start(f32[128,128]{1,0:T(8,128)S(1)} %add.55), channel_id=1, source_target_pairs={{0,4},{2,6},{4,0},{6,2},{8,12},{10,14},{12,8},{14,10},{16,20},{18,... | collective-permute-start | bytes 196616 | tf_op jit(solution)/shard_map/ppermute | solution.py:533
  71.0 0.1 pad_maximum_fusion.5
  71.2 1.6 %collective-permute-start.9 = (bf16[32,64,128]{2,1,0:T(8,128)(2,1)S(1)}, bf16[32,64,128]{2,1,0:T(8,128)(2,1)S(1)}, u32[]{:S(2)}, u32[]{:S(2)}) collective-permute-start(bf16[32,64,128]{2,1,0:T(8,128)(2,1)S(1)} %copy-done.7), channel_id=1, source_target_pairs={{0,1},{1,0},{2,3},{3,2},{4,5},{5,4},{6,7},{7,6},{8,9},{9,8},{10,11... | collective-permute-start | bytes 1572872 | tf_op jit(solution)/shard_map/ppermute | solution.py:583
  72.8 0.7 collective-permute-done.3
  73.5 4.4 %collective-permute-done.refs_1_ = bf16[95,64,128]{2,1,0:T(8,128)(2,1)} collective-permute-done((bf16[95,64,128]{2,1,0:T(8,128)(2,1)}, bf16[95,64,128]{2,1,0:T(8,128)(2,1)}, u32[]{:S(2)}, u32[]{:S(2)}) %collective-permute-start) | collective-permute-done | bytes 1556512 | tf_op jit(solution)/shard_map/ppermute | solution.py:583
  77.9 2.1 %collective-permute-start.4 = (f32[128,128]{1,0:T(8,128)S(1)}, f32[128,128]{1,0:T(8,128)S(1)}, u32[]{:S(2)}, u32[]{:S(2)}) collective-permute-start(f32[128,128]{1,0:T(8,128)S(1)} %add.56), channel_id=1, source_target_pairs={{0,8},{2,10},{4,12},{6,14},{8,0},{10,2},{12,4},{14,6},{16,24},{18,... | collective-permute-start | bytes 196616 | tf_op jit(solution)/shard_map/ppermute | solution.py:533
  80.0 17.9 %spectral_1.1 = f32[128,128]{1,0:T(8,128)S(1)} custom-call(bf16[95,64,128]{2,1,0:T(8,128)(2,1)S(1)} %copy-done.1, bf16[95,64,128]{2,1,0:T(8,128)(2,1)} %collective-permute-done.refs_1_, bf16[63,128,128]{2,1,0:T(8,128)(2,1)S(1)} %bitcast.20, bf16[63,64,128]{2,1,0:T(8,128)(2,1)S(1)} %copy-done.3, bf16[1,63,192,252]{3,2,1,0:T(8,128)(2,1)S(1)} %bitcast.24, ...), custom_call_target="tpu_custom_call" | custom-call | flops 8000000000 | bytes 30000000 | tf_op jit(solution)/shard_map/spectral_1/pallas_call | solution.py:485
  97.9 0.0 collective-permute-done.4
  97.9 0.1 collective-permute-start.5
  98.0 2.7 %collective-permute-start.6 = (f32[128,128]{1,0:T(8,128)S(1)}, f32[128,128]{1,0:T(8,128)S(1)}, u32[]{:S(2)}, u32[]{:S(2)}) collective-permute-start(f32[128,128]{1,0:T(8,128)S(1)} %add.57), channel_id=1, source_target_pairs={{0,16},{2,18},{4,20},{6,22},{8,24},{10,26},{12,28},{14,30},{16,0},... | collective-permute-start | bytes 196616 | tf_op jit(solution)/shard_map/ppermute | solution.py:533
  100.7 0.0 collective-permute-done.7.refs_1_
  100.7 7.4 %low_2.1 = (f32[4536,128]{1,0:T(8,128)S(1)}, bf16[63,128,128]{2,1,0:T(8,128)(2,1)S(1)}, bf16[63,128,128]{2,1,0:T(8,128)(2,1)S(1)}) custom-call(bf16[63,64,128]{2,1,0:T(8,128)(2,1)S(1)} %copy-done.6, bf16[63,64,128]{2,1,0:T(8,128)(2,1)} %collective-permute-done.7.refs_1_, bf16[63,128,128]{2,1,0:T(8,128)(2,1)S(1)} %bitcast.21, ...), custom_call_target="tpu_custom_call" | custom-call | flops 8000000000 | bytes 30000000 | tf_op jit(solution)/shard_map/low_2/pallas_call | solution.py:469
  108.1 0.0 collective-permute-done.6
  108.1 0.0 collective-permute-done.5
  108.1 1.6 %collective-permute-start.10 = (f32[128,128]{1,0:T(8,128)S(1)}, f32[128,128]{1,0:T(8,128)S(1)}, u32[]{:S(2)}, u32[]{:S(2)}) collective-permute-start(f32[128,128]{1,0:T(8,128)S(1)} %add.59), channel_id=1, source_target_pairs={{0,4},{2,6},{4,0},{6,2},{8,12},{10,14},{12,8},{14,10},{16,20},{18,... | collective-permute-start | bytes 196616 | tf_op jit(solution)/shard_map/ppermute | solution.py:533
  109.7 1.5 %collective-permute-start.8 = (f32[128,128]{1,0:T(8,128)S(1)}, f32[128,128]{1,0:T(8,128)S(1)}, u32[]{:S(2)}, u32[]{:S(2)}) collective-permute-start(f32[128,128]{1,0:T(8,128)S(1)} %add.58), channel_id=1, source_target_pairs={{0,1},{1,0},{2,3},{3,2},{4,5},{5,4},{6,7},{7,6},{8,9},{9,8},{10,11... | collective-permute-start | bytes 196616 | tf_op jit(solution)/shard_map/ppermute | solution.py:533
  111.2 0.0 collective-permute-done.9.refs_1_
  111.2 11.7 %spectral_2.1 = f32[128,128]{1,0:T(8,128)S(1)} custom-call(bf16[32,64,128]{2,1,0:T(8,128)(2,1)S(1)} %copy-done.7, bf16[32,64,128]{2,1,0:T(8,128)(2,1)S(1)} %collective-permute-done.9.refs_1_, f32[4536,128]{1,0:T(8,128)S(1)} %get-tuple-element.88.refs_2_, bf16[63,128,128]{2,1,0:T(8,128)(2,1)S(1)} %get-tuple-element.89.refs_3_, ...), custom_call_target="tpu_custom_call" | custom-call | flops 8000000000 | bytes 30000000 | tf_op jit(solution)/shard_map/spectral_2/pallas_call | solution.py:485
  122.9 0.0 collective-permute-done.8
  122.9 0.0 collective-permute-done.10
  122.9 0.1 collective-permute-start.11
  123.0 1.2 collective-permute-done.11
  124.3 0.9 collective-permute-start.12
  125.1 3.5 %collective-permute-done.12 = f32[128,128]{1,0:T(8,128)S(1)} collective-permute-done((f32[128,128]{1,0:T(8,128)S(1)}, f32[128,128]{1,0:T(8,128)S(1)}, u32[]{:S(2)}, u32[]{:S(2)}) %collective-permute-start.12) | collective-permute-done | bytes 65568 | tf_op jit(solution)/shard_map/ppermute | solution.py:533
  128.6 1.5 %collective-permute-start.13 = (f32[256,128]{1,0:T(8,128)S(1)}, f32[256,128]{1,0:T(8,128)S(1)}, u32[]{:S(2)}, u32[]{:S(2)}) collective-permute-start(f32[256,128]{1,0:T(8,128)S(1)} %pad_maximum_fusion.7), channel_id=1, source_target_pairs={{0,8},{2,10},{4,12},{6,14},{8,0},{10,2},{12,4},{14,6},{16,24},{18,... | collective-permute-start | bytes 393224 | tf_op jit(solution)/shard_map/ppermute | solution.py:533
  130.1 3.5 %collective-permute-done.13 = f32[256,128]{1,0:T(8,128)S(1)} collective-permute-done((f32[256,128]{1,0:T(8,128)S(1)}, f32[256,128]{1,0:T(8,128)S(1)}, u32[]{:S(2)}, u32[]{:S(2)}) %collective-permute-start.13) | collective-permute-done | bytes 131104 | tf_op jit(solution)/shard_map/ppermute | solution.py:533
  133.7 2.5 %collective-permute-start.14 = (f32[256,128]{1,0:T(8,128)S(1)}, f32[256,128]{1,0:T(8,128)S(1)}, u32[]{:S(2)}, u32[]{:S(2)}) collective-permute-start(f32[256,128]{1,0:T(8,128)S(1)} %fusion.8), channel_id=1, source_target_pairs={{0,16},{2,18},{4,20},{6,22},{8,24},{10,26},{12,28},{14,30},{16,0},... | collective-permute-start | bytes 393224 | tf_op jit(solution)/shard_map/ppermute | solution.py:533
  136.2 4.8 %collective-permute-done.14 = f32[256,128]{1,0:T(8,128)S(1)} collective-permute-done((f32[256,128]{1,0:T(8,128)S(1)}, f32[256,128]{1,0:T(8,128)S(1)}, u32[]{:S(2)}, u32[]{:S(2)}) %collective-permute-start.14) | collective-permute-done | bytes 131104 | tf_op jit(solution)/shard_map/ppermute | solution.py:533
  141.0 1.1 collective-permute-start.15
  142.1 3.9 %collective-permute-done.15 = f32[256,128]{1,0:T(8,128)S(1)} collective-permute-done((f32[256,128]{1,0:T(8,128)S(1)}, f32[256,128]{1,0:T(8,128)S(1)}, u32[]{:S(2)}, u32[]{:S(2)}) %collective-permute-start.15) | collective-permute-done | bytes 131104 | tf_op jit(solution)/shard_map/ppermute | solution.py:533
  146.1 0.7 slice_multiply_fusion
  (39 shorter events, 0.3 us)
Async XLA Ops:
  6.3 38.2 %collective-permute-start.1 = (bf16[95,64,128]{2,1,0:T(8,128)(2,1)}, bf16[95,64,128]{2,1,0:T(8,128)(2,1)}, u32[]{:S(2)}, u32[]{:S(2)}) collective-permute-start(bf16[95,64,128]{2,1,0:T(8,128)(2,1)} %forward_0.1.refs_0_), channel_id=1, source_target_pairs={{0,1},{1,0},{2,3},{3,2},{4,5},{5,4},{6,7},{7,6},{8,9},{9,8},{10,11... | collective-permute-start | bytes 4669448 | tf_op jit(solution)/shard_map/ppermute | solution.py:583
  15.0 62.9 %collective-permute-start = (bf16[95,64,128]{2,1,0:T(8,128)(2,1)}, bf16[95,64,128]{2,1,0:T(8,128)(2,1)}, u32[]{:S(2)}, u32[]{:S(2)}) collective-permute-start(bf16[95,64,128]{2,1,0:T(8,128)(2,1)} %forward_1.1.refs_0_), channel_id=1, source_target_pairs={{0,1},{1,0},{2,3},{3,2},{4,5},{5,4},{6,7},{7,6},{8,9},{9,8},{10,11... | collective-permute-start | bytes 4669448 | tf_op jit(solution)/shard_map/ppermute | solution.py:583
  19.4 2.3 %copy-start.10 = (bf16[2,32,64,128]{3,2,1,0:T(8,128)(2,1)S(1)}, bf16[2,32,64,128]{3,2,1,0:T(8,128)(2,1)}, u32[]{:S(2)}) copy-start(bf16[2,32,64,128]{3,2,1,0:T(8,128)(2,1)} %constant.50.clone) | copy-start | bytes 3145732
  29.5 4.2 %copy-start.11 = (bf16[126,192]{0,1:T(8,128)(2,1)S(1)}, bf16[126,192]{0,1:T(8,128)(2,1)}, u32[]{:S(2)}) copy-start(bf16[126,192]{0,1:T(8,128)(2,1)} %param.16) | copy-start | bytes 145156
  29.5 5.0 %copy-start.12 = (bf16[126,192]{0,1:T(8,128)(2,1)S(1)}, bf16[126,192]{0,1:T(8,128)(2,1)}, u32[]{:S(2)}) copy-start(bf16[126,192]{0,1:T(8,128)(2,1)} %param.17) | copy-start | bytes 145156
  29.5 71.1 %collective-permute-start.7 = (bf16[63,64,128]{2,1,0:T(8,128)(2,1)}, bf16[63,64,128]{2,1,0:T(8,128)(2,1)}, u32[]{:S(2)}, u32[]{:S(2)}) collective-permute-start(bf16[63,64,128]{2,1,0:T(8,128)(2,1)} %get-tuple-element.72.refs_0_), channel_id=1, source_target_pairs={{0,1},{1,0},{2,3},{3,2},{4,5},{5,4},{6,7},{7,6},{8,9},{9,8},{10,11... | collective-permute-start | bytes 3096584 | tf_op jit(solution)/shard_map/ppermute | solution.py:583
  33.7 10.8 %copy-start.8 = (bf16[256,252]{1,0:T(8,128)(2,1)S(1)}, bf16[256,252]{1,0:T(8,128)(2,1)}, u32[]{:S(2)}) copy-start(bf16[256,252]{1,0:T(8,128)(2,1)} %constant.45.clone.refs_6_.refs_7_) | copy-start | bytes 387076
  33.7 10.8 %copy-start.9 = (f32[128,128]{1,0:T(8,128)S(1)}, f32[128,128]{1,0:T(8,128)}, u32[]{:S(2)}) copy-start(f32[128,128]{1,0:T(8,128)} %constant.51.clone.refs_10_.refs_11_) | copy-start | bytes 196612
  34.8 9.8 %copy-start = (bf16[63,128,128]{1,2,0:T(8,128)(2,1)S(1)}, bf16[63,128,128]{1,2,0:T(8,128)(2,1)}, u32[]{:S(2)}) copy-start(bf16[63,128,128]{1,2,0:T(8,128)(2,1)} %constant_dynamic-slice_fusion.1) | copy-start | bytes 6193156
  34.8 9.7 %copy-start.3 = (bf16[63,64,128]{2,1,0:T(8,128)(2,1)S(1)}, bf16[63,64,128]{2,1,0:T(8,128)(2,1)}, u32[]{:S(2)}) copy-start(bf16[63,64,128]{2,1,0:T(8,128)(2,1)} %copy.20.refs_3_) | copy-start | bytes 3096580
  44.6 1.4 copy-start.2
  46.0 1.0 copy-start.4
  47.0 2.8 %copy-start.5 = (bf16[1,63,252,192]{2,3,1,0:T(8,128)(2,1)S(1)}, bf16[1,63,252,192]{2,3,1,0:T(8,128)(2,1)}, u32[]{:S(2)}) copy-start(bf16[1,63,252,192]{2,3,1,0:T(8,128)(2,1)} %param.15) | copy-start | bytes 18289156
  49.8 21.4 %copy-start.7 = (bf16[32,64,128]{2,1,0:T(8,128)(2,1)S(1)}, bf16[32,64,128]{2,1,0:T(8,128)(2,1)}, u32[]{:S(2)}) copy-start(bf16[32,64,128]{2,1,0:T(8,128)(2,1)} %get-tuple-element.87.refs_0_) | copy-start | bytes 1572868
  49.8 30.2 %copy-start.1 = (bf16[95,64,128]{2,1,0:T(8,128)(2,1)S(1)}, bf16[95,64,128]{2,1,0:T(8,128)(2,1)}, u32[]{:S(2)}) copy-start(bf16[95,64,128]{2,1,0:T(8,128)(2,1)} %forward_1.1.refs_0_) | copy-start | bytes 4669444
  67.6 1.3 collective-permute-start.2
  68.9 4.5 %collective-permute-start.3 = (f32[128,128]{1,0:T(8,128)S(1)}, f32[128,128]{1,0:T(8,128)S(1)}, u32[]{:S(2)}, u32[]{:S(2)}) collective-permute-start(f32[128,128]{1,0:T(8,128)S(1)} %add.55), channel_id=1, source_target_pairs={{0,4},{2,6},{4,0},{6,2},{8,12},{10,14},{12,8},{14,10},{16,20},{18,... | collective-permute-start | bytes 196616 | tf_op jit(solution)/shard_map/ppermute | solution.py:533
  71.2 40.0 %collective-permute-start.9 = (bf16[32,64,128]{2,1,0:T(8,128)(2,1)S(1)}, bf16[32,64,128]{2,1,0:T(8,128)(2,1)S(1)}, u32[]{:S(2)}, u32[]{:S(2)}) collective-permute-start(bf16[32,64,128]{2,1,0:T(8,128)(2,1)S(1)} %copy-done.7), channel_id=1, source_target_pairs={{0,1},{1,0},{2,3},{3,2},{4,5},{5,4},{6,7},{7,6},{8,9},{9,8},{10,11... | collective-permute-start | bytes 1572872 | tf_op jit(solution)/shard_map/ppermute | solution.py:583
  77.9 20.0 %collective-permute-start.4 = (f32[128,128]{1,0:T(8,128)S(1)}, f32[128,128]{1,0:T(8,128)S(1)}, u32[]{:S(2)}, u32[]{:S(2)}) collective-permute-start(f32[128,128]{1,0:T(8,128)S(1)} %add.56), channel_id=1, source_target_pairs={{0,8},{2,10},{4,12},{6,14},{8,0},{10,2},{12,4},{14,6},{16,24},{18,... | collective-permute-start | bytes 196616 | tf_op jit(solution)/shard_map/ppermute | solution.py:533
  80.0 20.6 %copy-start.6 = (bf16[63,64,128]{2,1,0:T(8,128)(2,1)S(1)}, bf16[63,64,128]{2,1,0:T(8,128)(2,1)}, u32[]{:S(2)}) copy-start(bf16[63,64,128]{2,1,0:T(8,128)(2,1)} %get-tuple-element.72.refs_0_) | copy-start | bytes 3096580
  80.0 31.2 %slice-start = ((s8[6193152]{0:T(1024)(128)(4,1)}), s8[4194304]{0:T(1024)(128)(4,1)S(1)}, s32[]{:S(2)}) async-start(s8[6193152]{0:T(1024)(128)(4,1)} %bitcast.26), calls=%async_computation | async-start | bytes 8388608
  97.9 10.2 %collective-permute-start.5 = (f32[128,128]{1,0:T(8,128)S(1)}, f32[128,128]{1,0:T(8,128)S(1)}, u32[]{:S(2)}, u32[]{:S(2)}) collective-permute-start(f32[128,128]{1,0:T(8,128)S(1)} %spectral_1.1), channel_id=1, source_target_pairs={{0,2},{2,0},{4,6},{6,4},{8,10},{10,8},{12,14},{14,12},{16,18},{18,... | collective-permute-start | bytes 196616 | tf_op jit(solution)/shard_map/ppermute | solution.py:533
  98.0 10.1 %collective-permute-start.6 = (f32[128,128]{1,0:T(8,128)S(1)}, f32[128,128]{1,0:T(8,128)S(1)}, u32[]{:S(2)}, u32[]{:S(2)}) collective-permute-start(f32[128,128]{1,0:T(8,128)S(1)} %add.57), channel_id=1, source_target_pairs={{0,16},{2,18},{4,20},{6,22},{8,24},{10,26},{12,28},{14,30},{16,0},... | collective-permute-start | bytes 196616 | tf_op jit(solution)/shard_map/ppermute | solution.py:533
  100.7 10.5 %slice-start.1 = ((s8[6193152]{0:T(1024)(128)(4,1)}), s8[1998848]{0:T(1024)(128)(4,1)S(1)}, s32[]{:S(2)}) async-start(s8[6193152]{0:T(1024)(128)(4,1)} %bitcast.26), calls=%async_computation.1 | async-start | bytes 3997696
  108.1 14.8 %collective-permute-start.10 = (f32[128,128]{1,0:T(8,128)S(1)}, f32[128,128]{1,0:T(8,128)S(1)}, u32[]{:S(2)}, u32[]{:S(2)}) collective-permute-start(f32[128,128]{1,0:T(8,128)S(1)} %add.59), channel_id=1, source_target_pairs={{0,4},{2,6},{4,0},{6,2},{8,12},{10,14},{12,8},{14,10},{16,20},{18,... | collective-permute-start | bytes 196616 | tf_op jit(solution)/shard_map/ppermute | solution.py:533
  109.7 13.3 %collective-permute-start.8 = (f32[128,128]{1,0:T(8,128)S(1)}, f32[128,128]{1,0:T(8,128)S(1)}, u32[]{:S(2)}, u32[]{:S(2)}) collective-permute-start(f32[128,128]{1,0:T(8,128)S(1)} %add.58), channel_id=1, source_target_pairs={{0,1},{1,0},{2,3},{3,2},{4,5},{5,4},{6,7},{7,6},{8,9},{9,8},{10,11... | collective-permute-start | bytes 196616 | tf_op jit(solution)/shard_map/ppermute | solution.py:533
  122.9 1.3 collective-permute-start.11
  124.3 4.3 %collective-permute-start.12 = (f32[128,128]{1,0:T(8,128)S(1)}, f32[128,128]{1,0:T(8,128)S(1)}, u32[]{:S(2)}, u32[]{:S(2)}) collective-permute-start(f32[128,128]{1,0:T(8,128)S(1)} %add.62), channel_id=1, source_target_pairs={{0,4},{2,6},{4,0},{6,2},{8,12},{10,14},{12,8},{14,10},{16,20},{18,... | collective-permute-start | bytes 196616 | tf_op jit(solution)/shard_map/ppermute | solution.py:533
  128.6 5.0 %collective-permute-start.13 = (f32[256,128]{1,0:T(8,128)S(1)}, f32[256,128]{1,0:T(8,128)S(1)}, u32[]{:S(2)}, u32[]{:S(2)}) collective-permute-start(f32[256,128]{1,0:T(8,128)S(1)} %pad_maximum_fusion.7), channel_id=1, source_target_pairs={{0,8},{2,10},{4,12},{6,14},{8,0},{10,2},{12,4},{14,6},{16,24},{18,... | collective-permute-start | bytes 393224 | tf_op jit(solution)/shard_map/ppermute | solution.py:533
  133.7 7.3 %collective-permute-start.14 = (f32[256,128]{1,0:T(8,128)S(1)}, f32[256,128]{1,0:T(8,128)S(1)}, u32[]{:S(2)}, u32[]{:S(2)}) collective-permute-start(f32[256,128]{1,0:T(8,128)S(1)} %fusion.8), channel_id=1, source_target_pairs={{0,16},{2,18},{4,20},{6,22},{8,24},{10,26},{12,28},{14,30},{16,0},... | collective-permute-start | bytes 393224 | tf_op jit(solution)/shard_map/ppermute | solution.py:533
  141.0 5.0 %collective-permute-start.15 = (f32[256,128]{1,0:T(8,128)S(1)}, f32[256,128]{1,0:T(8,128)S(1)}, u32[]{:S(2)}, u32[]{:S(2)}) collective-permute-start(f32[256,128]{1,0:T(8,128)S(1)} %add.65), channel_id=1, source_target_pairs={{0,1},{1,0},{2,3},{3,2},{4,5},{5,4},{6,7},{7,6},{8,9},{9,8},{10,11... | collective-permute-start | bytes 393224 | tf_op jit(solution)/shard_map/ppermute | solution.py:533

commit v6 on v5

--- a/solution.py
+++ b/solution.py
@@ -59,7 +59,8 @@
         self.pitch = self.rows + 8
         self.low = max(MODES - local, 0)
         high = MODES - self.low
-        self.pairs = (high + 1) // 2
+        self.pairs = round_up((high + 1) // 2, 2)
+        self.twos = round_up(self.low, 2) // 2
         self.blocks = self.low + self.pairs
         self.slots = round_up(self.low + 2 * self.pairs, 8)
         self.degrees = round_up(MODES, 16)
@@ -67,8 +68,8 @@
         self.partner = MODES - 1 + self.low
         orders = list(range(self.low))
         for pair in range(self.pairs):
-            order = self.low + pair
-            orders += [order, self.partner - order if self.partner - order != order else -1]
+            order, mate = self.low + pair, self.partner - self.low - pair
+            orders += [order if order <= mate else -1, mate if order < mate else -1]
         self.orders = np.array(orders + [-1] * (self.slots - len(orders)))
 
 
@@ -87,26 +88,28 @@
     layout = Layout(parts, local)
     plain, weighted = legendre_table()
     rows, degrees, low, pairs = layout.rows, layout.degrees, layout.low, layout.pairs
-    analysis = np.zeros((low, 2 * parts * rows, degrees))
-    synth_low = np.zeros((low, parts * rows, degrees))
+    analysis = np.zeros((2 * layout.twos, 2 * parts * rows, degrees))
+    synth_low = np.zeros((2 * layout.twos, parts * rows, degrees))
     pair_fwd = np.zeros((parts, pairs, rows, 2 * rows))
     pair_back = np.zeros((parts, pairs, rows, 2 * rows))
     for part in range(parts):
         own = slice(part * local, (part + 1) * local)
         start = part * rows
-        synth_low[:, start : start + local, :MODES] = np.swapaxes(plain[:low, :, own], 1, 2)
+        synth_low[:low, start : start + local, :MODES] = np.swapaxes(plain[:low, :, own], 1, 2)
         for turn in (1, 2):
             start = (turn * parts - 1 - part) * rows
-            analysis[:, start : start + local, :MODES] = np.swapaxes(weighted[:low, :, own], 1, 2)
+            analysis[:low, start : start + local, :MODES] = np.swapaxes(weighted[:low, :, own], 1, 2)
         for pair in range(pairs):
             order = low + pair
             mate = layout.partner - order
             for target, table in ((pair_fwd, weighted), (pair_back, plain)):
-                count = MODES - order
-                target[part, pair, rows - count :, :local] = table[order, order:, own]
-                if mate != order:
+                if order <= mate:
+                    count = MODES - order
+                    target[part, pair, rows - count :, :local] = table[order, order:, own]
+                if order < mate:
                     count = MODES - mate
                     target[part, pair, :count, rows : rows + local] = table[mate, mate:, own][::-1]
+    pair_synth = np.swapaxes(pair_back, -1, -2)
     place = np.zeros((degrees, 2 * rows))
     for row in range(rows):
         if row >= rows - MODES + low:
@@ -117,8 +120,8 @@
         "analysis": to_bf16(analysis),
         "synth_low": to_bf16(synth_low),
         "pair_fwd": to_bf16(pair_fwd),
-        "pair_back": to_bf16(pair_back),
-        "pair_synth": to_bf16(np.swapaxes(pair_back, -1, -2)),
+        "pair_back": to_bf16(np.concatenate([pair_back[:, ::2], pair_back[:, 1::2]], axis=3)),
+        "pair_synth": to_bf16(np.concatenate([pair_synth[:, ::2], pair_synth[:, 1::2]], axis=3)),
         "place": place.astype(np.float32),
     }
 
@@ -126,6 +129,12 @@
 def dot(left, right, sides=(1, 0)):
     contract = (((sides[0],), (sides[1],)), ((), ()))
     return lax.dot_general(left, right, contract, preferred_element_type=jnp.float32)
+
+
+def dot_two(left, first, second):
+    upper = jnp.concatenate([first, jnp.zeros_like(first)], axis=1)
+    lower = jnp.concatenate([jnp.zeros_like(second), second], axis=1)
+    return dot(left, jnp.concatenate([upper, lower], axis=0))
 
 
 def swap_halves(values):
@@ -218,7 +227,7 @@
     basis_copy = pltpu.make_async_copy(basis_all, basis, basis_sem)
     basis_copy.start()
     copies = band_copies(layout, chunk, fields, buffer, sems)
-    for started in copies:
+    for started in copies[:2]:
         for copy in started:
             copy.start()
     tables = pltpu.make_async_copy(pair_all.at[index[0]], pair_fwd, pair_sem)
@@ -230,6 +239,8 @@
     for group, started in enumerate(copies):
         for copy in started:
             copy.wait()
+        for copy in sum(copies[group + 2 : group + 3], []):
+            copy.start()
         for quad in range(PAIRS // 2):
             rows = []
             for which in range(2):
@@ -277,7 +288,8 @@
 
 def order_groups(layout):
     for start in range(0, layout.low, GROUP):
-        yield start, min(start + GROUP, layout.low), start // 16 * 16
+        stop = min(start + GROUP, layout.low)
+        yield start // 2, (stop + 1) // 2, start // 16 * 16
 
 
 def low_kernel(layout, *refs):
@@ -290,23 +302,33 @@
         real_rows = real_ref[top:degrees, :]
         imag_rows = imag_ref[top:degrees, :]
 
-        def low_block(order, carry):
-            values = jnp.concatenate([ref[order] for ref in held], axis=0)
-            spectral = dot(analysis[order, top:degrees, :], values).astype(jnp.bfloat16)
-            spec_low[order, top:degrees, :] = spectral
+        def low_block(two, carry):
+            values = []
+            for order in (2 * two, jnp.minimum(2 * two + 1, layout.low - 1)):
+                values.append(jnp.concatenate([ref[order] for ref in held], axis=0))
+            spectral = dot_two(analysis[two, top:degrees, :], *values).astype(jnp.bfloat16)
+            for which in range(2):
+                spec_low[2 * two + which, top:degrees, :] = spectral[:, which * LANES : (which + 1) * LANES]
             return carry
 
-        def mix_block(order, carry):
-            spectral = spec_low[order, top:degrees, :].astype(jnp.float32)
-            swapped = swap_halves(spectral)
-            swap_low[order, top:degrees, :] = swapped.astype(jnp.bfloat16)
-            mixed = mix(spectral, swapped, real_rows, imag_rows)
-            begin = pl.multiple_of(order * layout.pitch, 8)
-            grid_low[pl.ds(begin, layout.rows), :] = dot(synth_low[order, :, top:degrees], mixed)
+        def mix_block(two, carry):
+            mixed = []
+            for order in (2 * two, 2 * two + 1):
+                spectral = spec_low[order, top:degrees, :].astype(jnp.float32)
+                swapped = swap_halves(spectral)
+                swap_low[order, top:degrees, :] = swapped.astype(jnp.bfloat16)
+                values = mix(spectral, swapped, real_rows, imag_rows)
+                if top:
+                    values = jnp.concatenate([jnp.zeros((top, LANES), values.dtype), values], axis=0)
+                mixed.append(values)
+            values = dot_two(synth_low[two], *mixed)
+            for which in range(2):
+                begin = pl.multiple_of((2 * two + which) * layout.pitch, 8)
+                grid_low[pl.ds(begin, layout.rows), :] = values[:, which * LANES : (which + 1) * LANES]
             return carry
 
-        lax.fori_loop(start, stop, low_block, 0, unroll=8)
-        lax.fori_loop(start, stop, mix_block, 0, unroll=8)
+        lax.fori_loop(start, stop, low_block, 0, unroll=4)
+        lax.fori_loop(start, stop, mix_block, 0, unroll=4)
 
 
 def spectral_kernel(layout, apart, *refs):
@@ -317,8 +339,9 @@
     group = pl.program_id(0)
     rows, degrees, low = layout.rows, layout.degrees, layout.low
     if apart:
+        sources = (lows[0].at[pl.ds(0, low * layout.pitch)], lows[1], lows[2])
         targets = (scratch.at[pl.ds(0, low * layout.pitch)], spec_low, swap_low)
-        copies = [pltpu.make_async_copy(lows[at], targets[at], sems.at[at]) for at in range(3)]
+        copies = [pltpu.make_async_copy(*ends, sems.at[at]) for at, ends in enumerate(zip(sources, targets))]
 
     @pl.when(group == 0)
     def _():
@@ -329,24 +352,27 @@
             low_orders(layout, held, *lows, real_ref, imag_ref, scratch, spec_low, swap_low)
         line = lax.broadcasted_iota(jnp.int32, (rows, LANES), 0)
 
-        def pair_block(pair, carry):
-            total = sum(ref[offset + pair].astype(jnp.float32) for ref in held)
-            spectral = total.astype(jnp.bfloat16)
-            spec_pair[pair] = spectral
-            natural = line >= layout.first_natural + pair
-            real_rows = jnp.where(natural, real_ref[degrees : degrees + rows, :], real_ref[degrees + rows :, :])
-            imag_rows = jnp.where(natural, imag_ref[degrees : degrees + rows, :], imag_ref[degrees + rows :, :])
-            spectral = spectral.astype(jnp.float32)
-            swapped = swap_halves(spectral)
-            swap_pair[pair] = swapped.astype(jnp.bfloat16)
-            mixed = mix(spectral, swapped, real_rows, imag_rows)
-            values = dot(pair_synth[pair], mixed)
-            for which in range(2):
-                begin = pl.multiple_of((low + 2 * pair + which) * layout.pitch, 8)
-                scratch[pl.ds(begin, rows), :] = values[which * rows : (which + 1) * rows]
+        def pair_block(two, carry):
+            mixed = []
+            for pair in (2 * two, 2 * two + 1):
+                total = sum(ref[offset + pair].astype(jnp.float32) for ref in held)
+                spectral = total.astype(jnp.bfloat16)
+                spec_pair[pair] = spectral
+                natural = line >= layout.first_natural + pair
+                real_rows = jnp.where(natural, real_ref[degrees : degrees + rows, :], real_ref[degrees + rows :, :])
+                imag_rows = jnp.where(natural, imag_ref[degrees : degrees + rows, :], imag_ref[degrees + rows :, :])
+                spectral = spectral.astype(jnp.float32)
+                swapped = swap_halves(spectral)
+                swap_pair[pair] = swapped.astype(jnp.bfloat16)
+                mixed.append(mix(spectral, swapped, real_rows, imag_rows))
+            values = dot_two(pair_synth[two], *mixed)
+            for which in range(4):
+                begin = pl.multiple_of((low + 4 * two + which) * layout.pitch, 8)
+                columns = slice(which // 2 * LANES, (which // 2 + 1) * LANES)
+                scratch[pl.ds(begin, rows), :] = values[which % 2 * rows : (which % 2 + 1) * rows, columns]
             return carry
 
-        lax.fori_loop(0, layout.pairs, pair_block, 0, unroll=8)
+        lax.fori_loop(0, layout.pairs // 2, pair_block, 0, unroll=4)
         used = (low + 2 * layout.pairs) * layout.pitch
         if used < layout.slots * layout.pitch:
             scratch[used : layout.slots * layout.pitch, :] = jnp.zeros(
@@ -375,15 +401,21 @@
         same, cross = zeros, zeros
         for start, stop, top in order_groups(layout):
 
-            def low_block(order, carry):
-                back = dot(back_low[order, top:degrees, :], order_rows(layout, returned, order, 1))
-                first, second = products(
-                    spec_low[order, top:degrees, :], swap_low[order, top:degrees, :], back
-                )
-                return carry[0] + first, carry[1] + second
+            def low_block(two, carry):
+                values = [order_rows(layout, returned, 2 * two + which, 1) for which in range(2)]
+                back = dot_two(back_low[two, top:degrees, :], *values)
+                for which in range(2):
+                    order = 2 * two + which
+                    first, second = products(
+                        spec_low[order, top:degrees, :],
+                        swap_low[order, top:degrees, :],
+                        back[:, which * LANES : (which + 1) * LANES],
+                    )
+                    carry = carry[0] + first, carry[1] + second
+                return carry
 
             part = jnp.zeros((degrees - top, LANES), jnp.float32)
-            first, second = lax.fori_loop(start, stop, low_block, (part, part), unroll=8)
+            first, second = lax.fori_loop(start, stop, low_block, (part, part), unroll=4)
             if top:
                 empty = jnp.zeros((top, LANES), jnp.float32)
                 first = jnp.concatenate([empty, first], axis=0)
@@ -392,19 +424,25 @@
 
         line = lax.broadcasted_iota(jnp.int32, (rows, LANES), 0)
 
-        def pair_block(pair, carry):
-            back = dot(pair_back[pair], order_rows(layout, returned, low + 2 * pair, 2))
-            first, second = products(spec_pair[pair], swap_pair[pair], back)
-            natural = line >= layout.first_natural + pair
-            return (
-                carry[0] + jnp.where(natural, first, 0.0),
-                carry[1] + jnp.where(natural, second, 0.0),
-                carry[2] + jnp.where(natural, 0.0, first),
-                carry[3] + jnp.where(natural, 0.0, second),
-            )
+        def pair_block(two, carry):
+            values = [order_rows(layout, returned, low + 4 * two + 2 * which, 2) for which in range(2)]
+            back = dot_two(pair_back[two], *values)
+            for which in range(2):
+                pair = 2 * two + which
+                first, second = products(
+                    spec_pair[pair], swap_pair[pair], back[:, which * LANES : (which + 1) * LANES]
+                )
+                natural = line >= layout.first_natural + pair
+                carry = (
+                    carry[0] + jnp.where(natural, first, 0.0),
+                    carry[1] + jnp.where(natural, second, 0.0),
+                    carry[2] + jnp.where(natural, 0.0, first),
+                    carry[3] + jnp.where(natural, 0.0, second),
+                )
+            return carry
 
         part = jnp.zeros((rows, LANES), jnp.float32)
-        sums = lax.fori_loop(0, layout.pairs, pair_block, (part,) * 4, unroll=8)
+        sums = lax.fori_loop(0, layout.pairs // 2, pair_block, (part,) * 4, unroll=4)
         placed = jnp.dot(
             place[...],
             jnp.concatenate(
@@ -465,12 +503,12 @@
 
 def low_call(layout, chunk, coeffs, tables, real_rows, imag_rows):
     operands = list(coeffs) + list(tables) + [real_rows, imag_rows]
-    spectra = jax.ShapeDtypeStruct((layout.low, layout.degrees, LANES), jnp.bfloat16)
+    spectra = jax.ShapeDtypeStruct((2 * layout.twos, layout.degrees, LANES), jnp.bfloat16)
     return pl.pallas_call(
         functools.partial(low_kernel, layout),
         in_specs=[whole()] * len(operands),
         out_specs=[whole()] * 3,
-        out_shape=[jax.ShapeDtypeStruct((layout.low * layout.pitch, LANES), jnp.float32), spectra, spectra],
+        out_shape=[jax.ShapeDtypeStruct((2 * layout.twos * layout.pitch, LANES), jnp.float32), spectra, spectra],
         compiler_params=pltpu.CompilerParams(vmem_limit_bytes=VMEM),
         cost_estimate=pl.CostEstimate(flops=8_000_000_000, bytes_accessed=30_000_000, transcendentals=0),
         name=f"low_{chunk}",
@@ -491,8 +529,8 @@
         scratch_shapes=[
             pltpu.VMEM((layout.slots * layout.pitch, LANES), jnp.float32),
             pltpu.VMEM((layout.slots * layout.pitch, LANES), jnp.float32),
-            pltpu.VMEM((layout.low, layout.degrees, LANES), jnp.bfloat16),
-            pltpu.VMEM((layout.low, layout.degrees, LANES), jnp.bfloat16),
+            pltpu.VMEM((2 * layout.twos, layout.degrees, LANES), jnp.bfloat16),
+            pltpu.VMEM((2 * layout.twos, layout.degrees, LANES), jnp.bfloat16),
             pltpu.VMEM((layout.pairs, layout.rows, LANES), jnp.bfloat16),
             pltpu.VMEM((layout.pairs, layout.rows, LANES), jnp.bfloat16),
             pltpu.SemaphoreType.DMA((3,)),
@@ -568,9 +606,14 @@
             lax.dynamic_slice_in_dim(table, first * layout.rows, count * layout.rows, 1)
         )
 
-    analysis = jnp.swapaxes(bands("analysis", parts - 1 - index, parts), 1, 2)
-    synth_low = bands("synth_low", index, 1)
-    back_low = jnp.swapaxes(synth_low, 1, 2)
+    def side_by_side(table):
+        return jnp.concatenate([table[::2], table[1::2]], axis=2)
+
+    synth_own = bands("synth_low", index, 1)
+    analysis = bands("analysis", parts - 1 - index, parts).reshape(layout.twos, -1, layout.degrees)
+    analysis = jnp.swapaxes(analysis, 1, 2)
+    back_low = jnp.swapaxes(synth_own.reshape(layout.twos, -1, layout.degrees), 1, 2)
+    synth_low = side_by_side(synth_own)
     pair_tables = [local_table(name) for name in ("pair_synth", "pair_back")]
     low_tables = [analysis, synth_low]
     tables = [inverse, back_low] + pair_tables + [jnp.asarray(constants["place"])]
@@ -584,7 +627,7 @@
 
     held = []
     for chunk in range(chunks):
-        if chunk == chunks - 1:
+        if chunk == 1:
             place, low_tables, tables = lax.optimization_barrier((place, low_tables, tables))
         bounds = (0, layout.blocks) if chunk < chunks - 1 else (0, layout.low, layout.blocks)
         made = forward_call(layout, chunk, bounds, place, fields, pair_fwd)

time: 147 us -> 146 us (level)
  Pallas kernels: 71.7 us -> 62.4 us
  local copies, waits for them, and re-layouts: 17.3 us -> 22.4 us
  starting transfers between devices: 22.9 us -> 25.9 us
  waiting for transfers between devices: 31.6 us -> 29.6 us
  other arithmetic: 2.31 us -> 4.21 us
    pallas_call x3, Pallas kernels: 47.4 us -> 40.9 us  [spectral_call(): pl.pallas_call(functools.partial(spectral_kernel, layout, apart), grid=(l...]
    reshape x0 -> x2, local copies, waits for them, and re-layouts: none -> 4.88 us  [the longest x1 3.27 us: on_device(): bands('analysis', parts - 1 - index, parts)]
    ppermute x12, starting transfers between devices: 16.2 us -> 19.2 us  [hop_parcels(): parcels.append(lax.ppermute(value, axis, pairs))]
    dynamic_slice x2, local copies, waits for them, and re-layouts: 6.62 us -> 4.43 us  [bands(): lax.dynamic_slice_in_dim(table, first * layout.rows, count * layout.rows, 1)]
    unnamed x32 -> x36, local copies, waits for them, and re-layouts: 5.49 us -> 7.64 us
    optimization_barrier x1 -> x0, local copies, waits for them, and re-layouts: 2.14 us -> none  [on_device(): lax.optimization_barrier((place, low_tables, tables))]
    pallas_call x1, Pallas kernels: 7.39 us -> 5.57 us  [low_call(): pl.pallas_call(functools.partial(low_kernel, layout), in_specs=[whole()]...]
    ppermute x12, waiting for transfers between devices: 18.7 us -> 17 us  [hop_parcels(): parcels.append(lax.ppermute(value, axis, pairs))]
  transfers between devices with their start and end apart: 16 -> 16, of which waited for: 9 -> 10; matrix products, arithmetic and copies ran while one was open for 9% -> 13% of each run, Pallas kernels for 45% -> 39%
where the time goes in v6:
time: 146 us; the launch traced here: 145 us
  Pallas kernels  62.4 us (43%)
  waiting for transfers between devices  29.6 us (20%)
  starting transfers between devices  25.9 us (18%)
  local copies, waits for them, and re-layouts  22.4 us (15%)
  other arithmetic  4.21 us (3%)
    pallas_call x3, Pallas kernels, spectral_call(): pl.pallas_call(functools.partial(spectral_kernel, layout, apart), grid=(l...  40.9 us
    ppermute x12, starting transfers between devices, hop_parcels(): parcels.append(lax.ppermute(value, axis, pairs))  19.2 us
    ppermute x12, waiting for transfers between devices, hop_parcels(): parcels.append(lax.ppermute(value, axis, pairs))  17 us
    pallas_call x3, Pallas kernels, forward_call(): pl.pallas_call(functools.partial(forward_kernel, layout, chunk, bounds),...  15.9 us
    ppermute x4, waiting for transfers between devices, others(): return [lax.ppermute(sent, 'space', route) for route in routes]  12.6 us
    unnamed x36, local copies, waits for them, and re-layouts  7.64 us
    ppermute x4, starting transfers between devices, others(): return [lax.ppermute(sent, 'space', route) for route in routes]  6.76 us
    pallas_call x1, Pallas kernels, low_call(): pl.pallas_call(functools.partial(low_kernel, layout), in_specs=[whole()]...  5.57 us
  transfers between devices with their start and end apart: 16, of which 10 were waited for; matrix products, arithmetic and copies ran while one was open for 13% of the time, Pallas kernels for 39%

profile of v6, /device:TPU:0, one launch (start us, length us, event | category | flops | bytes accessed | tf_op | source)
XLA Modules:
  0.0 145.5 jit_solution(15736574751534795209)
XLA Ops:
  0.6 5.3 %forward_0.1.refs_0_ = bf16[95,64,128]{2,1,0:T(8,128)(2,1)} custom-call(s32[1]{0:T(128)} %bitcast.index, bf16[1,63,192,252]{3,2,1,0:T(8,128)(2,1)} %bitcast.32, bf16[256,252]{1,0:T(8,128)(2,1)} %constant.52.clone.basis_all, bf16[2,32,64,128]{3,2,1,0:T(8,128)(2,1)} %constant.46.clone.pair_all), custom_call_target="tpu_custom_call" | custom-call | flops 1000000 | bytes 100000 | tf_op jit(solution)/shard_map/forward_0/pallas_call | solution.py:482
  5.9 3.0 %collective-permute-start.1 = (bf16[95,64,128]{2,1,0:T(8,128)(2,1)}, bf16[95,64,128]{2,1,0:T(8,128)(2,1)}, u32[]{:S(2)}, u32[]{:S(2)}) collective-permute-start(bf16[95,64,128]{2,1,0:T(8,128)(2,1)} %forward_0.1.refs_0_), channel_id=1, source_target_pairs={{0,1},{1,0},{2,3},{3,2},{4,5},{5,4},{6,7},{7,6},{8,9},{9,8},{10,11... | collective-permute-start | bytes 4669448 | tf_op jit(solution)/shard_map/ppermute | solution.py:626
  9.0 3.3 %constant_dynamic-slice_fusion.1 = bf16[64,128,128]{2,1,0:T(8,128)(2,1)} fusion(bf16[64,256,128]{2,1,0:T(8,128)(2,1)} %constant.48.clone, s32[]{:T(128)S(6)} %select_n.12), kind=kLoop, calls=%fused_computation.23 | loop fusion | bytes 4194308 | tf_op jit(solution)/shard_map/dynamic_slice | solution.py:606
  12.3 1.1 constant_dynamic-slice_fusion
  13.4 3.3 %copy.20 = bf16[32,256,128]{1,2,0:T(8,128)(2,1)S(1)} copy(bf16[32,256,128]{2,1,0:T(8,128)(2,1)} %bitcast.36) | data formatting | bytes 4194304 | tf_op jit(solution)/shard_map/reshape | solution.py:613
  16.7 1.6 %copy.21 = bf16[32,128,128]{1,2,0:T(8,128)(2,1)S(1)} copy(bf16[32,128,128]{2,1,0:T(8,128)(2,1)} %bitcast.35) | data formatting | bytes 2097152 | tf_op jit(solution)/shard_map/reshape | solution.py:615
  18.3 2.0 %dynamic-slice_bitcast_fusion.1.refs_8_.refs_9_ = bf16[16,128,128]{2,1,0:T(8,128)(2,1)} fusion(bf16[2,16,128,128]{3,2,1,0:T(8,128)(2,1)} %constant.49.clone, s32[]{:T(128)S(6)} %select_n.14), kind=kLoop, calls=%fused_computation.2 | loop fusion | bytes 1048580 | tf_op jit(solution)/shard_map/jit(dynamic_index_in_dim)/squeeze | solution.py:599
  20.3 1.9 %dynamic-slice_bitcast_fusion.refs_9_.refs_10_ = bf16[16,64,256]{2,1,0:T(8,128)(2,1)} fusion(bf16[2,16,64,256]{3,2,1,0:T(8,128)(2,1)} %constant.50.clone, s32[]{:T(128)S(6)} %select_n.14), kind=kLoop, calls=%fused_computation.1 | loop fusion | bytes 1048580 | tf_op jit(solution)/shard_map/jit(dynamic_index_in_dim)/squeeze | solution.py:599
  22.2 0.1 fusion.9
  22.3 1.1 pad_maximum_fusion.refs_3_
  23.4 5.3 %forward_1.1.refs_0_ = bf16[95,64,128]{2,1,0:T(8,128)(2,1)} custom-call(s32[1]{0:T(128)} %bitcast.index, bf16[1,63,192,252]{3,2,1,0:T(8,128)(2,1)} %bitcast.33, bf16[256,252]{1,0:T(8,128)(2,1)} %constant.52.clone.basis_all, bf16[2,32,64,128]{3,2,1,0:T(8,128)(2,1)} %constant.46.clone.pair_all), custom_call_target="tpu_custom_call" | custom-call | flops 1000000 | bytes 100000 | tf_op jit(solution)/shard_map/forward_1/pallas_call | solution.py:482
  28.7 0.0 copy-start.14
  28.7 0.1 collective-permute-start
  28.8 5.3 %forward_2.1 = (bf16[63,64,128]{2,1,0:T(8,128)(2,1)}, bf16[32,64,128]{2,1,0:T(8,128)(2,1)}) custom-call(s32[1]{0:T(128)} %bitcast.index, bf16[1,63,192,252]{3,2,1,0:T(8,128)(2,1)} %bitcast.34, bf16[256,252]{1,0:T(8,128)(2,1)} %constant.52.clone.basis_all, bf16[2,32,64,128]{3,2,1,0:T(8,128)(2,1)} %constant.46.clone.pair_all), custom_call_target="tpu_custom_call" | custom-call | flops 1000000 | bytes 100000 | tf_op jit(solution)/shard_map/forward_2/pallas_call | solution.py:482
  34.2 0.0 copy-start.10
  34.2 0.0 copy-start.11
  34.2 2.0 %collective-permute-start.7 = (bf16[63,64,128]{2,1,0:T(8,128)(2,1)}, bf16[63,64,128]{2,1,0:T(8,128)(2,1)}, u32[]{:S(2)}, u32[]{:S(2)}) collective-permute-start(bf16[63,64,128]{2,1,0:T(8,128)(2,1)} %get-tuple-element.72.refs_0_), channel_id=1, source_target_pairs={{0,1},{1,0},{2,3},{3,2},{4,5},{5,4},{6,7},{7,6},{8,9},{9,8},{10,11... | collective-permute-start | bytes 3096584 | tf_op jit(solution)/shard_map/ppermute | solution.py:626
  36.2 0.1 copy.22
  36.4 0.7 rev.6
  37.0 0.9 copy.24
  38.0 0.7 rev.7
  38.6 0.9 fusion.4
  39.6 0.8 fusion.7
  40.4 0.1 fusion.10
  40.5 0.1 slice_negate_fusion
  40.6 0.1 pad_maximum_fusion.2
  40.7 3.4 %collective-permute-done.1.refs_1_ = bf16[95,64,128]{2,1,0:T(8,128)(2,1)} collective-permute-done((bf16[95,64,128]{2,1,0:T(8,128)(2,1)}, bf16[95,64,128]{2,1,0:T(8,128)(2,1)}, u32[]{:S(2)}, u32[]{:S(2)}) %collective-permute-start.1) | collective-permute-done | bytes 1556512 | tf_op jit(solution)/shard_map/ppermute | solution.py:626
  44.2 1.0 copy-done.4
  45.2 2.8 %copy-done.6 = bf16[1,63,252,192]{2,3,1,0:T(8,128)(2,1)S(1)} copy-done((bf16[1,63,252,192]{2,3,1,0:T(8,128)(2,1)S(1)}, bf16[1,63,252,192]{2,3,1,0:T(8,128)(2,1)}, u32[]{:S(2)}) %copy-start.6) | copy-done | bytes 6096408
  48.0 15.2 %spectral_0.1 = f32[128,128]{1,0:T(8,128)S(1)} custom-call(bf16[95,64,128]{2,1,0:T(8,128)(2,1)S(1)} %copy-done, bf16[95,64,128]{2,1,0:T(8,128)(2,1)} %collective-permute-done.1.refs_1_, bf16[32,128,256]{2,1,0:T(8,128)(2,1)S(1)} %bitcast.18, bf16[32,64,256]{2,1,0:T(8,128)(2,1)S(1)} %copy-done.2, bf16[1,63,192,252]{3,2,1,0:T(8,128)(2,1)S(1)} %bitcast.24, ...), custom_call_target="tpu_custom_call" | custom-call | flops 8000000000 | bytes 30000000 | tf_op jit(solution)/shard_map/spectral_0/pallas_call | solution.py:523
  63.3 0.1 collective-permute-start.2
  63.3 0.1 pad_maximum_fusion.4
  63.5 1.1 collective-permute-done.2
  64.6 2.1 %collective-permute-start.3 = (f32[128,128]{1,0:T(8,128)S(1)}, f32[128,128]{1,0:T(8,128)S(1)}, u32[]{:S(2)}, u32[]{:S(2)}) collective-permute-start(f32[128,128]{1,0:T(8,128)S(1)} %add.55), channel_id=1, source_target_pairs={{0,4},{2,6},{4,0},{6,2},{8,12},{10,14},{12,8},{14,10},{16,20},{18,... | collective-permute-start | bytes 196616 | tf_op jit(solution)/shard_map/ppermute | solution.py:571
  66.7 0.1 pad_maximum_fusion.6
  66.9 1.6 %collective-permute-start.9 = (bf16[32,64,128]{2,1,0:T(8,128)(2,1)S(1)}, bf16[32,64,128]{2,1,0:T(8,128)(2,1)S(1)}, u32[]{:S(2)}, u32[]{:S(2)}) collective-permute-start(bf16[32,64,128]{2,1,0:T(8,128)(2,1)S(1)} %copy-done.9), channel_id=1, source_target_pairs={{0,1},{1,0},{2,3},{3,2},{4,5},{5,4},{6,7},{7,6},{8,9},{9,8},{10,11... | collective-permute-start | bytes 1572872 | tf_op jit(solution)/shard_map/ppermute | solution.py:626
  68.4 0.7 collective-permute-done.3
  69.1 8.4 %collective-permute-done.refs_1_ = bf16[95,64,128]{2,1,0:T(8,128)(2,1)} collective-permute-done((bf16[95,64,128]{2,1,0:T(8,128)(2,1)}, bf16[95,64,128]{2,1,0:T(8,128)(2,1)}, u32[]{:S(2)}, u32[]{:S(2)}) %collective-permute-start) | collective-permute-done | bytes 1556512 | tf_op jit(solution)/shard_map/ppermute | solution.py:626
  77.5 2.1 %collective-permute-start.4 = (f32[128,128]{1,0:T(8,128)S(1)}, f32[128,128]{1,0:T(8,128)S(1)}, u32[]{:S(2)}, u32[]{:S(2)}) collective-permute-start(f32[128,128]{1,0:T(8,128)S(1)} %add.56), channel_id=1, source_target_pairs={{0,8},{2,10},{4,12},{6,14},{8,0},{10,2},{12,4},{14,6},{16,24},{18,... | collective-permute-start | bytes 196616 | tf_op jit(solution)/shard_map/ppermute | solution.py:571
  79.7 2.8 %copy-done.7 = bf16[1,63,252,192]{2,3,1,0:T(8,128)(2,1)S(1)} copy-done((bf16[1,63,252,192]{2,3,1,0:T(8,128)(2,1)S(1)}, bf16[1,63,252,192]{2,3,1,0:T(8,128)(2,1)}, u32[]{:S(2)}) %copy-start.7) | copy-done | bytes 6096408
  82.4 15.3 %spectral_1.1 = f32[128,128]{1,0:T(8,128)S(1)} custom-call(bf16[95,64,128]{2,1,0:T(8,128)(2,1)S(1)} %copy-done.1, bf16[95,64,128]{2,1,0:T(8,128)(2,1)} %collective-permute-done.refs_1_, bf16[32,128,256]{2,1,0:T(8,128)(2,1)S(1)} %bitcast.19, bf16[32,64,256]{2,1,0:T(8,128)(2,1)S(1)} %copy-done.2, bf16[1,63,192,252]{3,2,1,0:T(8,128)(2,1)S(1)} %bitcast.26, ...), custom_call_target="tpu_custom_call" | custom-call | flops 8000000000 | bytes 30000000 | tf_op jit(solution)/shard_map/spectral_1/pallas_call | solution.py:523
  97.7 0.0 collective-permute-done.4
  97.7 0.1 collective-permute-start.5
  97.8 2.6 %collective-permute-start.6 = (f32[128,128]{1,0:T(8,128)S(1)}, f32[128,128]{1,0:T(8,128)S(1)}, u32[]{:S(2)}, u32[]{:S(2)}) collective-permute-start(f32[128,128]{1,0:T(8,128)S(1)} %add.57), channel_id=1, source_target_pairs={{0,16},{2,18},{4,20},{6,22},{8,24},{10,26},{12,28},{14,30},{16,0},... | collective-permute-start | bytes 196616 | tf_op jit(solution)/shard_map/ppermute | solution.py:571
  100.5 0.0 collective-permute-done.7.refs_1_
  100.5 5.6 %low_2.1 = (f32[4608,128]{1,0:T(8,128)S(1)}, bf16[64,128,128]{2,1,0:T(8,128)(2,1)S(1)}, bf16[64,128,128]{2,1,0:T(8,128)(2,1)S(1)}) custom-call(bf16[63,64,128]{2,1,0:T(8,128)(2,1)S(1)} %copy-done.8, bf16[63,64,128]{2,1,0:T(8,128)(2,1)} %collective-permute-done.7.refs_1_, bf16[32,128,256]{2,1,0:T(8,128)(2,1)S(1)} %bitcast.20, ...), custom_call_target="tpu_custom_call" | custom-call | flops 8000000000 | bytes 30000000 | tf_op jit(solution)/shard_map/low_2/pallas_call | solution.py:507
  106.1 0.0 collective-permute-done.6
  106.1 1.6 %collective-permute-start.10 = (f32[128,128]{1,0:T(8,128)S(1)}, f32[128,128]{1,0:T(8,128)S(1)}, u32[]{:S(2)}, u32[]{:S(2)}) collective-permute-start(f32[128,128]{1,0:T(8,128)S(1)} %add.59), channel_id=1, source_target_pairs={{0,4},{2,6},{4,0},{6,2},{8,12},{10,14},{12,8},{14,10},{16,20},{18,... | collective-permute-start | bytes 196616 | tf_op jit(solution)/shard_map/ppermute | solution.py:571
  107.7 1.5 %collective-permute-start.8 = (f32[128,128]{1,0:T(8,128)S(1)}, f32[128,128]{1,0:T(8,128)S(1)}, u32[]{:S(2)}, u32[]{:S(2)}) collective-permute-start(f32[128,128]{1,0:T(8,128)S(1)} %add.58), channel_id=1, source_target_pairs={{0,1},{1,0},{2,3},{3,2},{4,5},{5,4},{6,7},{7,6},{8,9},{9,8},{10,11... | collective-permute-start | bytes 196616 | tf_op jit(solution)/shard_map/ppermute | solution.py:571
  109.2 0.8 collective-permute-done.9.refs_1_
  110.0 10.4 %spectral_2.1 = f32[128,128]{1,0:T(8,128)S(1)} custom-call(bf16[32,64,128]{2,1,0:T(8,128)(2,1)S(1)} %copy-done.9, bf16[32,64,128]{2,1,0:T(8,128)(2,1)S(1)} %collective-permute-done.9.refs_1_, f32[4608,128]{1,0:T(8,128)S(1)} %get-tuple-element.88.refs_2_, bf16[64,128,128]{2,1,0:T(8,128)(2,1)S(1)} %get-tuple-element.89.refs_3_, ...), custom_call_target="tpu_custom_call" | custom-call | flops 8000000000 | bytes 30000000 | tf_op jit(solution)/shard_map/spectral_2/pallas_call | solution.py:523
  120.4 0.0 collective-permute-done.8
  120.4 0.0 collective-permute-done.10
  120.4 0.1 collective-permute-start.11
  120.5 1.2 collective-permute-done.11
  121.7 2.5 %collective-permute-start.12 = (f32[128,128]{1,0:T(8,128)S(1)}, f32[128,128]{1,0:T(8,128)S(1)}, u32[]{:S(2)}, u32[]{:S(2)}) collective-permute-start(f32[128,128]{1,0:T(8,128)S(1)} %add.62), channel_id=1, source_target_pairs={{0,4},{2,6},{4,0},{6,2},{8,12},{10,14},{12,8},{14,10},{16,20},{18,... | collective-permute-start | bytes 196616 | tf_op jit(solution)/shard_map/ppermute | solution.py:571
  124.2 2.4 %collective-permute-done.12 = f32[128,128]{1,0:T(8,128)S(1)} collective-permute-done((f32[128,128]{1,0:T(8,128)S(1)}, f32[128,128]{1,0:T(8,128)S(1)}, u32[]{:S(2)}, u32[]{:S(2)}) %collective-permute-start.12) | collective-permute-done | bytes 65568 | tf_op jit(solution)/shard_map/ppermute | solution.py:571
  126.7 2.0 %collective-permute-start.13 = (f32[256,128]{1,0:T(8,128)S(1)}, f32[256,128]{1,0:T(8,128)S(1)}, u32[]{:S(2)}, u32[]{:S(2)}) collective-permute-start(f32[256,128]{1,0:T(8,128)S(1)} %pad_maximum_fusion.8), channel_id=1, source_target_pairs={{0,8},{2,10},{4,12},{6,14},{8,0},{10,2},{12,4},{14,6},{16,24},{18,... | collective-permute-start | bytes 393224 | tf_op jit(solution)/shard_map/ppermute | solution.py:571
  128.7 3.1 %collective-permute-done.13 = f32[256,128]{1,0:T(8,128)S(1)} collective-permute-done((f32[256,128]{1,0:T(8,128)S(1)}, f32[256,128]{1,0:T(8,128)S(1)}, u32[]{:S(2)}, u32[]{:S(2)}) %collective-permute-start.13) | collective-permute-done | bytes 131104 | tf_op jit(solution)/shard_map/ppermute | solution.py:571
  131.8 2.9 %collective-permute-start.14 = (f32[256,128]{1,0:T(8,128)S(1)}, f32[256,128]{1,0:T(8,128)S(1)}, u32[]{:S(2)}, u32[]{:S(2)}) collective-permute-start(f32[256,128]{1,0:T(8,128)S(1)} %fusion.8), channel_id=1, source_target_pairs={{0,16},{2,18},{4,20},{6,22},{8,24},{10,26},{12,28},{14,30},{16,0},... | collective-permute-start | bytes 393224 | tf_op jit(solution)/shard_map/ppermute | solution.py:571
  134.7 5.0 %collective-permute-done.14 = f32[256,128]{1,0:T(8,128)S(1)} collective-permute-done((f32[256,128]{1,0:T(8,128)S(1)}, f32[256,128]{1,0:T(8,128)S(1)}, u32[]{:S(2)}, u32[]{:S(2)}) %collective-permute-start.14) | collective-permute-done | bytes 131104 | tf_op jit(solution)/shard_map/ppermute | solution.py:571
  139.7 1.6 %collective-permute-start.15 = (f32[256,128]{1,0:T(8,128)S(1)}, f32[256,128]{1,0:T(8,128)S(1)}, u32[]{:S(2)}, u32[]{:S(2)}) collective-permute-start(f32[256,128]{1,0:T(8,128)S(1)} %add.65), channel_id=1, source_target_pairs={{0,1},{1,0},{2,3},{3,2},{4,5},{5,4},{6,7},{7,6},{8,9},{9,8},{10,11... | collective-permute-start | bytes 393224 | tf_op jit(solution)/shard_map/ppermute | solution.py:571
  141.3 3.4 %collective-permute-done.15 = f32[256,128]{1,0:T(8,128)S(1)} collective-permute-done((f32[256,128]{1,0:T(8,128)S(1)}, f32[256,128]{1,0:T(8,128)S(1)}, u32[]{:S(2)}, u32[]{:S(2)}) %collective-permute-start.15) | collective-permute-done | bytes 131104 | tf_op jit(solution)/shard_map/ppermute | solution.py:571
  144.8 0.7 slice_multiply_fusion
  (46 shorter events, 0.2 us)
Async XLA Ops:
  5.9 38.2 %collective-permute-start.1 = (bf16[95,64,128]{2,1,0:T(8,128)(2,1)}, bf16[95,64,128]{2,1,0:T(8,128)(2,1)}, u32[]{:S(2)}, u32[]{:S(2)}) collective-permute-start(bf16[95,64,128]{2,1,0:T(8,128)(2,1)} %forward_0.1.refs_0_), channel_id=1, source_target_pairs={{0,1},{1,0},{2,3},{3,2},{4,5},{5,4},{6,7},{7,6},{8,9},{9,8},{10,11... | collective-permute-start | bytes 4669448 | tf_op jit(solution)/shard_map/ppermute | solution.py:626
  9.0 3.3 %copy-start.13 = (bf16[64,128,128]{2,1,0:T(8,128)(2,1)S(1)}, bf16[64,128,128]{2,1,0:T(8,128)(2,1)}, u32[]{:S(2)}) copy-start(bf16[64,128,128]{2,1,0:T(8,128)(2,1)} %constant.47.clone) | copy-start | bytes 6291460
  18.3 3.9 %copy-start.12 = (bf16[64,64,128]{2,1,0:T(8,128)(2,1)S(1)}, bf16[64,64,128]{2,1,0:T(8,128)(2,1)}, u32[]{:S(2)}) copy-start(bf16[64,64,128]{2,1,0:T(8,128)(2,1)} %constant_dynamic-slice_fusion) | copy-start | bytes 3145732
  28.7 7.5 %copy-start.14 = (bf16[126,192]{0,1:T(8,128)(2,1)S(1)}, bf16[126,192]{0,1:T(8,128)(2,1)}, u32[]{:S(2)}) copy-start(bf16[126,192]{0,1:T(8,128)(2,1)} %param.16) | copy-start | bytes 145156
  28.7 48.8 %collective-permute-start = (bf16[95,64,128]{2,1,0:T(8,128)(2,1)}, bf16[95,64,128]{2,1,0:T(8,128)(2,1)}, u32[]{:S(2)}, u32[]{:S(2)}) collective-permute-start(bf16[95,64,128]{2,1,0:T(8,128)(2,1)} %forward_1.1.refs_0_), channel_id=1, source_target_pairs={{0,1},{1,0},{2,3},{3,2},{4,5},{5,4},{6,7},{7,6},{8,9},{9,8},{10,11... | collective-permute-start | bytes 4669448 | tf_op jit(solution)/shard_map/ppermute | solution.py:626
  34.2 10.0 %copy-start.10 = (bf16[256,252]{1,0:T(8,128)(2,1)S(1)}, bf16[256,252]{1,0:T(8,128)(2,1)}, u32[]{:S(2)}) copy-start(bf16[256,252]{1,0:T(8,128)(2,1)} %constant.45.clone.refs_6_.refs_7_) | copy-start | bytes 387076
  34.2 10.0 %copy-start.11 = (f32[128,128]{1,0:T(8,128)S(1)}, f32[128,128]{1,0:T(8,128)}, u32[]{:S(2)}) copy-start(f32[128,128]{1,0:T(8,128)} %constant.51.clone.refs_10_.refs_11_) | copy-start | bytes 196612
  34.2 66.3 %collective-permute-start.7 = (bf16[63,64,128]{2,1,0:T(8,128)(2,1)}, bf16[63,64,128]{2,1,0:T(8,128)(2,1)}, u32[]{:S(2)}, u32[]{:S(2)}) collective-permute-start(bf16[63,64,128]{2,1,0:T(8,128)(2,1)} %get-tuple-element.72.refs_0_), channel_id=1, source_target_pairs={{0,1},{1,0},{2,3},{3,2},{4,5},{5,4},{6,7},{7,6},{8,9},{9,8},{10,11... | collective-permute-start | bytes 3096584 | tf_op jit(solution)/shard_map/ppermute | solution.py:626
  38.6 5.5 %copy-start = (bf16[95,64,128]{2,1,0:T(8,128)(2,1)S(1)}, bf16[95,64,128]{2,1,0:T(8,128)(2,1)}, u32[]{:S(2)}) copy-start(bf16[95,64,128]{2,1,0:T(8,128)(2,1)} %forward_0.1.refs_0_) | copy-start | bytes 4669444
  38.6 5.5 %copy-start.2 = (bf16[32,64,256]{2,1,0:T(8,128)(2,1)S(1)}, bf16[32,64,256]{2,1,0:T(8,128)(2,1)}, u32[]{:S(2)}) copy-start(bf16[32,64,256]{2,1,0:T(8,128)(2,1)} %pad_maximum_fusion.refs_3_) | copy-start | bytes 3145732
  38.6 5.5 %copy-start.3 = (bf16[16,128,128]{2,1,0:T(8,128)(2,1)S(1)}, bf16[16,128,128]{2,1,0:T(8,128)(2,1)}, u32[]{:S(2)}) copy-start(bf16[16,128,128]{2,1,0:T(8,128)(2,1)} %dynamic-slice_bitcast_fusion.1.refs_8_.refs_9_) | copy-start | bytes 1572868
  44.2 1.0 copy-start.4
  45.2 2.8 %copy-start.6 = (bf16[1,63,252,192]{2,3,1,0:T(8,128)(2,1)S(1)}, bf16[1,63,252,192]{2,3,1,0:T(8,128)(2,1)}, u32[]{:S(2)}) copy-start(bf16[1,63,252,192]{2,3,1,0:T(8,128)(2,1)} %param.15) | copy-start | bytes 18289156
  48.0 18.8 %copy-start.9 = (bf16[32,64,128]{2,1,0:T(8,128)(2,1)S(1)}, bf16[32,64,128]{2,1,0:T(8,128)(2,1)}, u32[]{:S(2)}) copy-start(bf16[32,64,128]{2,1,0:T(8,128)(2,1)} %get-tuple-element.87.refs_0_) | copy-start | bytes 1572868
  48.0 31.6 %copy-start.1 = (bf16[95,64,128]{2,1,0:T(8,128)(2,1)S(1)}, bf16[95,64,128]{2,1,0:T(8,128)(2,1)}, u32[]{:S(2)}) copy-start(bf16[95,64,128]{2,1,0:T(8,128)(2,1)} %forward_1.1.refs_0_) | copy-start | bytes 4669444
  63.3 1.3 collective-permute-start.2
  64.6 4.5 %collective-permute-start.3 = (f32[128,128]{1,0:T(8,128)S(1)}, f32[128,128]{1,0:T(8,128)S(1)}, u32[]{:S(2)}, u32[]{:S(2)}) collective-permute-start(f32[128,128]{1,0:T(8,128)S(1)} %add.55), channel_id=1, source_target_pairs={{0,4},{2,6},{4,0},{6,2},{8,12},{10,14},{12,8},{14,10},{16,20},{18,... | collective-permute-start | bytes 196616 | tf_op jit(solution)/shard_map/ppermute | solution.py:571
  66.9 43.1 %collective-permute-start.9 = (bf16[32,64,128]{2,1,0:T(8,128)(2,1)S(1)}, bf16[32,64,128]{2,1,0:T(8,128)(2,1)S(1)}, u32[]{:S(2)}, u32[]{:S(2)}) collective-permute-start(bf16[32,64,128]{2,1,0:T(8,128)(2,1)S(1)} %copy-done.9), channel_id=1, source_target_pairs={{0,1},{1,0},{2,3},{3,2},{4,5},{5,4},{6,7},{7,6},{8,9},{9,8},{10,11... | collective-permute-start | bytes 1572872 | tf_op jit(solution)/shard_map/ppermute | solution.py:626
  77.5 20.2 %collective-permute-start.4 = (f32[128,128]{1,0:T(8,128)S(1)}, f32[128,128]{1,0:T(8,128)S(1)}, u32[]{:S(2)}, u32[]{:S(2)}) collective-permute-start(f32[128,128]{1,0:T(8,128)S(1)} %add.56), channel_id=1, source_target_pairs={{0,8},{2,10},{4,12},{6,14},{8,0},{10,2},{12,4},{14,6},{16,24},{18,... | collective-permute-start | bytes 196616 | tf_op jit(solution)/shard_map/ppermute | solution.py:571
  79.6 2.8 %copy-start.7 = (bf16[1,63,252,192]{2,3,1,0:T(8,128)(2,1)S(1)}, bf16[1,63,252,192]{2,3,1,0:T(8,128)(2,1)}, u32[]{:S(2)}) copy-start(bf16[1,63,252,192]{2,3,1,0:T(8,128)(2,1)} %param.15) | copy-start | bytes 18289156
  82.4 18.1 %copy-start.8 = (bf16[63,64,128]{2,1,0:T(8,128)(2,1)S(1)}, bf16[63,64,128]{2,1,0:T(8,128)(2,1)}, u32[]{:S(2)}) copy-start(bf16[63,64,128]{2,1,0:T(8,128)(2,1)} %get-tuple-element.72.refs_0_) | copy-start | bytes 3096580
  82.4 27.5 %slice-start = ((s8[6193152]{0:T(1024)(128)(4,1)}), s8[4194304]{0:T(1024)(128)(4,1)S(1)}, s32[]{:S(2)}) async-start(s8[6193152]{0:T(1024)(128)(4,1)} %bitcast.28), calls=%async_computation | async-start | bytes 8388608
  97.7 8.4 %collective-permute-start.5 = (f32[128,128]{1,0:T(8,128)S(1)}, f32[128,128]{1,0:T(8,128)S(1)}, u32[]{:S(2)}, u32[]{:S(2)}) collective-permute-start(f32[128,128]{1,0:T(8,128)S(1)} %spectral_1.1), channel_id=1, source_target_pairs={{0,2},{2,0},{4,6},{6,4},{8,10},{10,8},{12,14},{14,12},{16,18},{18,... | collective-permute-start | bytes 196616 | tf_op jit(solution)/shard_map/ppermute | solution.py:571
  97.8 8.2 %collective-permute-start.6 = (f32[128,128]{1,0:T(8,128)S(1)}, f32[128,128]{1,0:T(8,128)S(1)}, u32[]{:S(2)}, u32[]{:S(2)}) collective-permute-start(f32[128,128]{1,0:T(8,128)S(1)} %add.57), channel_id=1, source_target_pairs={{0,16},{2,18},{4,20},{6,22},{8,24},{10,26},{12,28},{14,30},{16,0},... | collective-permute-start | bytes 196616 | tf_op jit(solution)/shard_map/ppermute | solution.py:571
  100.5 9.5 %copy-start.5 = (bf16[16,64,256]{2,1,0:T(8,128)(2,1)S(1)}, bf16[16,64,256]{2,1,0:T(8,128)(2,1)}, u32[]{:S(2)}) copy-start(bf16[16,64,256]{2,1,0:T(8,128)(2,1)} %dynamic-slice_bitcast_fusion.refs_9_.refs_10_) | copy-start | bytes 1572868
  100.5 9.5 %slice-start.1 = ((s8[6193152]{0:T(1024)(128)(4,1)}), s8[1998848]{0:T(1024)(128)(4,1)S(1)}, s32[]{:S(2)}) async-start(s8[6193152]{0:T(1024)(128)(4,1)} %bitcast.28), calls=%async_computation.1 | async-start | bytes 3997696
  106.1 14.3 %collective-permute-start.10 = (f32[128,128]{1,0:T(8,128)S(1)}, f32[128,128]{1,0:T(8,128)S(1)}, u32[]{:S(2)}, u32[]{:S(2)}) collective-permute-start(f32[128,128]{1,0:T(8,128)S(1)} %add.59), channel_id=1, source_target_pairs={{0,4},{2,6},{4,0},{6,2},{8,12},{10,14},{12,8},{14,10},{16,20},{18,... | collective-permute-start | bytes 196616 | tf_op jit(solution)/shard_map/ppermute | solution.py:571
  107.7 12.7 %collective-permute-start.8 = (f32[128,128]{1,0:T(8,128)S(1)}, f32[128,128]{1,0:T(8,128)S(1)}, u32[]{:S(2)}, u32[]{:S(2)}) collective-permute-start(f32[128,128]{1,0:T(8,128)S(1)} %add.58), channel_id=1, source_target_pairs={{0,1},{1,0},{2,3},{3,2},{4,5},{5,4},{6,7},{7,6},{8,9},{9,8},{10,11... | collective-permute-start | bytes 196616 | tf_op jit(solution)/shard_map/ppermute | solution.py:571
  120.4 1.3 collective-permute-start.11
  121.7 4.9 %collective-permute-start.12 = (f32[128,128]{1,0:T(8,128)S(1)}, f32[128,128]{1,0:T(8,128)S(1)}, u32[]{:S(2)}, u32[]{:S(2)}) collective-permute-start(f32[128,128]{1,0:T(8,128)S(1)} %add.62), channel_id=1, source_target_pairs={{0,4},{2,6},{4,0},{6,2},{8,12},{10,14},{12,8},{14,10},{16,20},{18,... | collective-permute-start | bytes 196616 | tf_op jit(solution)/shard_map/ppermute | solution.py:571
  126.7 5.1 %collective-permute-start.13 = (f32[256,128]{1,0:T(8,128)S(1)}, f32[256,128]{1,0:T(8,128)S(1)}, u32[]{:S(2)}, u32[]{:S(2)}) collective-permute-start(f32[256,128]{1,0:T(8,128)S(1)} %pad_maximum_fusion.8), channel_id=1, source_target_pairs={{0,8},{2,10},{4,12},{6,14},{8,0},{10,2},{12,4},{14,6},{16,24},{18,... | collective-permute-start | bytes 393224 | tf_op jit(solution)/shard_map/ppermute | solution.py:571
  131.8 7.9 %collective-permute-start.14 = (f32[256,128]{1,0:T(8,128)S(1)}, f32[256,128]{1,0:T(8,128)S(1)}, u32[]{:S(2)}, u32[]{:S(2)}) collective-permute-start(f32[256,128]{1,0:T(8,128)S(1)} %fusion.8), channel_id=1, source_target_pairs={{0,16},{2,18},{4,20},{6,22},{8,24},{10,26},{12,28},{14,30},{16,0},... | collective-permute-start | bytes 393224 | tf_op jit(solution)/shard_map/ppermute | solution.py:571
  139.7 5.0 %collective-permute-start.15 = (f32[256,128]{1,0:T(8,128)S(1)}, f32[256,128]{1,0:T(8,128)S(1)}, u32[]{:S(2)}, u32[]{:S(2)}) collective-permute-start(f32[256,128]{1,0:T(8,128)S(1)} %add.65), channel_id=1, source_target_pairs={{0,1},{1,0},{2,3},{3,2},{4,5},{5,4},{6,7},{7,6},{8,9},{9,8},{10,11... | collective-permute-start | bytes 393224 | tf_op jit(solution)/shard_map/ppermute | solution.py:571

commit v7 on v6

--- a/solution.py
+++ b/solution.py
@@ -331,10 +331,10 @@
         lax.fori_loop(start, stop, mix_block, 0, unroll=4)
 
 
-def spectral_kernel(layout, apart, *refs):
+def spectral_kernel(layout, apart, side, *refs):
     held, lows, refs = refs[: layout.parts], refs[layout.parts : layout.parts + 2 + apart], refs[layout.parts + 2 + apart :]
     north, south, basis, back_low, pair_synth, pair_back, place, real_ref, imag_ref = refs[:9]
-    out, scratch, returned, spec_low, swap_low, spec_pair, swap_pair, sems = refs[9:]
+    keep, send, scratch, returned, spec_low, swap_low, spec_pair, swap_pair, sems = refs[9:]
     offset = 0 if apart else layout.low
     group = pl.program_id(0)
     rows, degrees, low = layout.rows, layout.degrees, layout.low
@@ -456,7 +456,10 @@
         real = same + swap_halves(same)
         imag = cross - swap_halves(cross)
         lane = lax.broadcasted_iota(jnp.int32, real.shape, 1)
-        out[...] = jnp.where(lane < LANES // 2, real, imag).T
+        grads = jnp.where(lane < LANES // 2, real, imag).T
+        upper, lower = grads[: LANES // 2], grads[LANES // 2 :]
+        keep[...] = jnp.where(side[0] == 0, upper, lower)
+        send[...] = jnp.where(side[0] == 0, lower, upper)
 
 
 def grid_specs(layout, chunk):
@@ -515,17 +518,18 @@
     )(*operands)
 
 
-def spectral_call(layout, chunk, apart, blocks, lows, cotangent, tables, real_rows, imag_rows):
-    operands = list(blocks) + list(lows) + [cotangent, cotangent] + list(tables) + [real_rows, imag_rows]
+def spectral_call(layout, chunk, apart, side, blocks, lows, cotangent, tables, real_rows, imag_rows):
+    half = jax.ShapeDtypeStruct((LANES // 2, layout.degrees), jnp.float32)
+    operands = [side] + list(blocks) + list(lows) + [cotangent, cotangent] + list(tables) + [real_rows, imag_rows]
     low_spec = pl.BlockSpec(memory_space=pl.ANY) if apart else whole()
-    specs = [whole()] * len(blocks) + [low_spec] * len(lows)
+    specs = [pl.BlockSpec(memory_space=pltpu.SMEM)] + [whole()] * len(blocks) + [low_spec] * len(lows)
     specs += grid_specs(layout, chunk) + [whole()] * (len(tables) + 2)
     return pl.pallas_call(
         functools.partial(spectral_kernel, layout, apart),
         grid=(layout.half // PAIRS,),
         in_specs=specs,
-        out_specs=whole(),
-        out_shape=jax.ShapeDtypeStruct((LANES, layout.degrees), jnp.float32),
+        out_specs=[whole()] * 2,
+        out_shape=[half, half],
         scratch_shapes=[
             pltpu.VMEM((layout.slots * layout.pitch, LANES), jnp.float32),
             pltpu.VMEM((layout.slots * layout.pitch, LANES), jnp.float32),
@@ -572,12 +576,6 @@
     return parcels
 
 
-def sum_over(value, steps):
-    for step in steps:
-        value = sum(hop_parcels(value, step), value)
-    return value
-
-
 def filter_rows(layout, spec):
     padded = jnp.pad(spec, ((0, layout.degrees - MODES), (0, 0)))
     front = jnp.pad(spec, ((layout.rows, layout.rows), (0, 0)))
@@ -636,19 +634,34 @@
             made[1], held[0][1] = lax.optimization_barrier((made[1], held[0][1]))
         held += [[own] + others(own) for own in made]
 
-    hops, last_hops = sum_steps("dp"), sum_steps("space")
+    hops = sum_steps("dp") + sum_steps("space")
+    count_dp = len(sum_steps("dp"))
+    swap = [(device, device ^ 1) for device in range(lax.axis_size("dp"))]
+    side = lax.rem(lax.axis_index("dp"), 2).reshape((1,)).astype(jnp.int32)
     waiting = []
+
+    def launch(value, done):
+        if done:
+            return value, hop_parcels(value, hops[done])
+        keep, send = value
+        return keep, [lax.ppermute(send, "dp", swap)]
 
     def hop_all(limit, tie):
         moved = []
         for value, done in waiting:
             if done < limit:
-                parcels = hop_parcels(value, (hops + last_hops)[done])
+                value, parcels = launch(value, done)
                 parcels, value, tie = lax.optimization_barrier((parcels, value, tie))
                 value, done = sum(parcels, value), done + 1
             moved.append((value, done))
         waiting[:] = moved
         return tie
+
+    def hop_last(times):
+        for _ in range(times):
+            value, done = waiting[-1]
+            value, parcels = launch(value, done)
+            waiting[-1] = (sum(parcels, value), done + 1)
 
     def before(values):
         if not waiting:
@@ -665,33 +678,28 @@
         blocks, lows, apart = held[chunk], low_tables, chunk == chunks - 1
         if apart:
             lows = low_call(layout, chunk, blocks, low_tables, real_rows, imag_rows)
-            lows = before(hop_all(len(hops), lows))
+            lows = before(hop_all(count_dp, lows))
             blocks = held[-1]
-        grads = spectral_call(layout, chunk, apart, blocks, lows, cotangent, tables, real_rows, imag_rows)
-        if not apart:
-            grads = hop_all(len(hops), grads)
-            waiting.append((grads, 0))
-            if chunk < chunks - 2:
-                for _ in range(len(hops) // 2):
-                    waiting[-1] = (sum_over(waiting[-1][0], hops[waiting[-1][1] :][:1]), waiting[-1][1] + 1)
-                held[chunk + 1] = before(held[chunk + 1])
-        else:
-            grads = hop_all(len(hops) + len(last_hops), grads)
-            waiting.append((grads, 0))
-
+        grads = spectral_call(layout, chunk, apart, side, blocks, lows, cotangent, tables, real_rows, imag_rows)
+        grads = hop_all(len(hops) if apart else count_dp, grads)
+        waiting.append((grads, 0))
+        if chunk < chunks - 2:
+            hop_last(count_dp // 2)
+            held[chunk + 1] = before(held[chunk + 1])
+
+    hop_last(1)
     total, done = waiting.pop()
-    hops = hops + last_hops
     while done < len(hops):
         joined = [value for value, at in waiting if at == done]
         waiting = [(value, at) for value, at in waiting if at != done]
         if joined:
             total = jnp.concatenate(joined + [total], axis=0)
-        total, done = sum_over(total, hops[done : done + 1]), done + 1
-    rows = jnp.concatenate([value for value, _ in waiting] + [total], axis=0)
-    rows = rows.reshape(chunks, 2, width, layout.degrees)
-
+        total, done = sum(hop_parcels(total, hops[done]), total), done + 1
+    mine = jnp.concatenate([value for value, _ in waiting] + [total], axis=0)
+    other = lax.ppermute(mine, "dp", swap)
+    real = jnp.where(side[0] == 0, mine, other)[:, :MODES]
+    imag = jnp.where(side[0] == 0, other, mine)[:, :MODES]
     batch_total = fields.shape[0] * lax.axis_size("dp")
-    real, imag = (rows[:, part, :, :MODES].reshape(chunks * width, MODES) for part in range(2))
     return (real.T / batch_total, imag.T / batch_total)
 
 

time: 146 us -> 143 us (0.979)
  waiting for transfers between devices: 29.6 us -> 23 us
  local copies, waits for them, and re-layouts: 22.4 us -> 25.9 us
    ppermute x12 -> x9, waiting for transfers between devices: 17 us -> 9.71 us  [hop_parcels(): parcels.append(lax.ppermute(value, axis, pairs))]
    ppermute x0 -> x4, waiting for transfers between devices: none -> 3.67 us  [the longest x3 2.39 us: launch(): return (keep, [lax.ppermute(send, 'dp', swap)])]
    ppermute x4, waiting for transfers between devices: 12.6 us -> 9.61 us  [others(): return [lax.ppermute(sent, 'space', route) for route in routes]]
    ppermute x12 -> x9, starting transfers between devices: 19.2 us -> 18.1 us  [hop_parcels(): parcels.append(lax.ppermute(value, axis, pairs))]
    unnamed x36 -> x32, local copies, waits for them, and re-layouts: 7.64 us -> 8.67 us
  transfers between devices with their start and end apart: 16 -> 17, of which waited for: 10 -> 11; matrix products, arithmetic and copies ran while one was open for 13% -> 16% of each run, Pallas kernels for 39% -> 40%
where the time goes in v7:
time: 143 us; the launch traced here: 142 us
  Pallas kernels  62.4 us (44%)
  local copies, waits for them, and re-layouts  25.9 us (18%)
  starting transfers between devices  25.2 us (18%)
  waiting for transfers between devices  23 us (16%)
  other arithmetic  4.52 us (3%)
    pallas_call x3, Pallas kernels, spectral_call(): pl.pallas_call(functools.partial(spectral_kernel, layout, apart), grid=(l...  40.9 us
    ppermute x9, starting transfers between devices, hop_parcels(): parcels.append(lax.ppermute(value, axis, pairs))  18.1 us
    pallas_call x3, Pallas kernels, forward_call(): pl.pallas_call(functools.partial(forward_kernel, layout, chunk, bounds),...  16 us
    ppermute x9, waiting for transfers between devices, hop_parcels(): parcels.append(lax.ppermute(value, axis, pairs))  9.71 us
    ppermute x4, waiting for transfers between devices, others(): return [lax.ppermute(sent, 'space', route) for route in routes]  9.61 us
    unnamed x32, local copies, waits for them, and re-layouts  8.67 us
    ppermute x4, starting transfers between devices, others(): return [lax.ppermute(sent, 'space', route) for route in routes]  6.78 us
    pallas_call x1, Pallas kernels, low_call(): pl.pallas_call(functools.partial(low_kernel, layout), in_specs=[whole()]...  5.55 us
  transfers between devices with their start and end apart: 17, of which 11 were waited for; matrix products, arithmetic and copies ran while one was open for 16% of the time, Pallas kernels for 40%

profile of v7, /device:TPU:0, one launch (start us, length us, event | category | flops | bytes accessed | tf_op | source)
XLA Modules:
  0.0 142.0 jit_solution(2755038464703545731)
XLA Ops:
  0.6 5.4 %forward_0.1.refs_0_ = bf16[95,64,128]{2,1,0:T(8,128)(2,1)} custom-call(s32[1]{0:T(128)} %bitcast.index, bf16[1,63,192,252]{3,2,1,0:T(8,128)(2,1)} %bitcast.30, bf16[256,252]{1,0:T(8,128)(2,1)} %constant.59.clone.basis_all, bf16[2,32,64,128]{3,2,1,0:T(8,128)(2,1)} %constant.53.clone.pair_all), custom_call_target="tpu_custom_call" | custom-call | flops 1000000 | bytes 100000 | tf_op jit(solution)/shard_map/forward_0/pallas_call | solution.py:485
  6.0 3.0 %collective-permute-start.1 = (bf16[95,64,128]{2,1,0:T(8,128)(2,1)}, bf16[95,64,128]{2,1,0:T(8,128)(2,1)}, u32[]{:S(2)}, u32[]{:S(2)}) collective-permute-start(bf16[95,64,128]{2,1,0:T(8,128)(2,1)} %forward_0.1.refs_0_), channel_id=1, source_target_pairs={{0,1},{1,0},{2,3},{3,2},{4,5},{5,4},{6,7},{7,6},{8,9},{9,8},{10,11... | collective-permute-start | bytes 4669448 | tf_op jit(solution)/shard_map/ppermute | solution.py:624
  9.0 3.2 %constant_dynamic-slice_fusion.1 = bf16[64,128,128]{2,1,0:T(8,128)(2,1)} fusion(bf16[64,256,128]{2,1,0:T(8,128)(2,1)} %constant.55.clone, s32[]{:T(128)S(6)} %select_n.25), kind=kLoop, calls=%fused_computation.26 | loop fusion | bytes 4194308 | tf_op jit(solution)/shard_map/dynamic_slice | solution.py:604
  12.2 3.3 %copy.20 = bf16[32,256,128]{1,2,0:T(8,128)(2,1)S(1)} copy(bf16[32,256,128]{2,1,0:T(8,128)(2,1)} %bitcast.34) | data formatting | bytes 4194304 | tf_op jit(solution)/shard_map/reshape | solution.py:611
  15.5 2.3 %constant_dynamic-slice_fusion = bf16[64,64,128]{2,1,0:T(8,128)(2,1)} fusion(bf16[64,128,128]{2,1,0:T(8,128)(2,1)} %constant.54.clone, s32[]{:T(128)S(6)} %select_n.26), kind=kLoop, calls=%fused_computation.25 | loop fusion | bytes 2097156 | tf_op jit(solution)/shard_map/dynamic_slice | solution.py:604
  17.8 1.6 %copy.21 = bf16[32,128,128]{1,2,0:T(8,128)(2,1)S(1)} copy(bf16[32,128,128]{2,1,0:T(8,128)(2,1)} %bitcast.33) | data formatting | bytes 2097152 | tf_op jit(solution)/shard_map/reshape | solution.py:613
  19.4 2.0 %dynamic-slice_bitcast_fusion.1.refs_8_.refs_9_ = bf16[16,128,128]{2,1,0:T(8,128)(2,1)} fusion(bf16[2,16,128,128]{3,2,1,0:T(8,128)(2,1)} %constant.56.clone, s32[]{:T(128)S(6)} %select_n.27), kind=kLoop, calls=%fused_computation.2 | loop fusion | bytes 1048580 | tf_op jit(solution)/shard_map/jit(dynamic_index_in_dim)/squeeze | solution.py:597
  21.4 1.9 %dynamic-slice_bitcast_fusion.refs_9_.refs_10_ = bf16[16,64,256]{2,1,0:T(8,128)(2,1)} fusion(bf16[2,16,64,256]{3,2,1,0:T(8,128)(2,1)} %constant.57.clone, s32[]{:T(128)S(6)} %select_n.27), kind=kLoop, calls=%fused_computation.1 | loop fusion | bytes 1048580 | tf_op jit(solution)/shard_map/jit(dynamic_index_in_dim)/squeeze | solution.py:597
  23.4 0.1 fusion.10
  23.4 1.2 pad_maximum_fusion.refs_3_
  24.6 5.3 %forward_1.1.refs_0_ = bf16[95,64,128]{2,1,0:T(8,128)(2,1)} custom-call(s32[1]{0:T(128)} %bitcast.index, bf16[1,63,192,252]{3,2,1,0:T(8,128)(2,1)} %bitcast.31, bf16[256,252]{1,0:T(8,128)(2,1)} %constant.59.clone.basis_all, bf16[2,32,64,128]{3,2,1,0:T(8,128)(2,1)} %constant.53.clone.pair_all), custom_call_target="tpu_custom_call" | custom-call | flops 1000000 | bytes 100000 | tf_op jit(solution)/shard_map/forward_1/pallas_call | solution.py:485
  29.9 0.0 copy-start.12
  29.9 0.1 collective-permute-start
  30.0 5.3 %forward_2.1 = (bf16[63,64,128]{2,1,0:T(8,128)(2,1)}, bf16[32,64,128]{2,1,0:T(8,128)(2,1)}) custom-call(s32[1]{0:T(128)} %bitcast.index, bf16[1,63,192,252]{3,2,1,0:T(8,128)(2,1)} %bitcast.32, bf16[256,252]{1,0:T(8,128)(2,1)} %constant.59.clone.basis_all, bf16[2,32,64,128]{3,2,1,0:T(8,128)(2,1)} %constant.53.clone.pair_all), custom_call_target="tpu_custom_call" | custom-call | flops 1000000 | bytes 100000 | tf_op jit(solution)/shard_map/forward_2/pallas_call | solution.py:485
  35.3 2.1 %collective-permute-start.7 = (bf16[63,64,128]{2,1,0:T(8,128)(2,1)}, bf16[63,64,128]{2,1,0:T(8,128)(2,1)}, u32[]{:S(2)}, u32[]{:S(2)}) collective-permute-start(bf16[63,64,128]{2,1,0:T(8,128)(2,1)} %get-tuple-element.86.refs_0_), channel_id=1, source_target_pairs={{0,1},{1,0},{2,3},{3,2},{4,5},{5,4},{6,7},{7,6},{8,9},{9,8},{10,11... | collective-permute-start | bytes 3096584 | tf_op jit(solution)/shard_map/ppermute | solution.py:624
  37.4 0.1 copy.22
  37.6 0.1 rev.6
  37.6 0.0 copy-start.9
  37.7 0.0 copy-start.10
  37.7 0.8 fusion.11
  38.5 0.9 copy.24
  39.4 0.6 slice.54
  40.0 1.4 rev.7
  41.4 0.9 fusion.7
  42.3 1.2 pad_maximum_fusion.1
  43.5 0.1 slice_negate_fusion
  43.7 0.1 pad_maximum_fusion.2
  43.8 0.4 collective-permute-done.1.refs_1_
  44.3 1.0 copy-done.3
  45.3 1.0 copy-done.4
  46.3 2.8 %copy-done.5 = bf16[1,63,252,192]{2,3,1,0:T(8,128)(2,1)S(1)} copy-done((bf16[1,63,252,192]{2,3,1,0:T(8,128)(2,1)S(1)}, bf16[1,63,252,192]{2,3,1,0:T(8,128)(2,1)}, u32[]{:S(2)}) %copy-start.5) | copy-done | bytes 6096408
  49.1 15.3 %spectral_0.1 = (f32[64,128]{1,0:T(8,128)S(1)}, f32[64,128]{1,0:T(8,128)S(1)}) custom-call(s32[1]{0:T(128)} %bitcast.8.side, bf16[95,64,128]{2,1,0:T(8,128)(2,1)S(1)} %copy-done, bf16[95,64,128]{2,1,0:T(8,128)(2,1)} %collective-permute-done.1.refs_1_, bf16[32,128,256]{2,1,0:T(8,128)(2,1)S(1)} %bitcast.16, bf16[32,64,256]{2,1,0:T(8,128)(2,1)S(1)} %copy-done.2, ...), custom_call_target="tpu_custom_call" | custom-call | flops 8000000000 | bytes 30000000 | tf_op jit(solution)/shard_map/spectral_0/pallas_call | solution.py:527
  64.4 0.1 collective-permute-start.2
  64.4 1.2 collective-permute-done.2
  65.6 2.0 %collective-permute-start.3 = (f32[64,128]{1,0:T(8,128)S(1)}, f32[64,128]{1,0:T(8,128)S(1)}, u32[]{:S(2)}, u32[]{:S(2)}) collective-permute-start(f32[64,128]{1,0:T(8,128)S(1)} %add.55), channel_id=1, source_target_pairs={{0,4},{2,6},{4,0},{6,2},{8,12},{10,14},{12,8},{14,10},{16,20},{18,... | collective-permute-start | bytes 98312 | tf_op jit(solution)/shard_map/ppermute | solution.py:575
  67.7 0.1 pad_maximum_fusion.5
  67.8 1.6 %collective-permute-start.9 = (bf16[32,64,128]{2,1,0:T(8,128)(2,1)S(1)}, bf16[32,64,128]{2,1,0:T(8,128)(2,1)S(1)}, u32[]{:S(2)}, u32[]{:S(2)}) collective-permute-start(bf16[32,64,128]{2,1,0:T(8,128)(2,1)S(1)} %copy-done.8), channel_id=1, source_target_pairs={{0,1},{1,0},{2,3},{3,2},{4,5},{5,4},{6,7},{7,6},{8,9},{9,8},{10,11... | collective-permute-start | bytes 1572872 | tf_op jit(solution)/shard_map/ppermute | solution.py:624
  69.4 0.2 collective-permute-done.3
  69.6 8.0 %collective-permute-done.refs_1_ = bf16[95,64,128]{2,1,0:T(8,128)(2,1)} collective-permute-done((bf16[95,64,128]{2,1,0:T(8,128)(2,1)}, bf16[95,64,128]{2,1,0:T(8,128)(2,1)}, u32[]{:S(2)}, u32[]{:S(2)}) %collective-permute-start) | collective-permute-done | bytes 1556512 | tf_op jit(solution)/shard_map/ppermute | solution.py:624
  77.6 2.1 %collective-permute-start.4 = (f32[64,128]{1,0:T(8,128)S(1)}, f32[64,128]{1,0:T(8,128)S(1)}, u32[]{:S(2)}, u32[]{:S(2)}) collective-permute-start(f32[64,128]{1,0:T(8,128)S(1)} %add.56), channel_id=1, source_target_pairs={{0,8},{2,10},{4,12},{6,14},{8,0},{10,2},{12,4},{14,6},{16,24},{18,... | collective-permute-start | bytes 98312 | tf_op jit(solution)/shard_map/ppermute | solution.py:575
  79.7 2.8 %copy-done.6 = bf16[1,63,252,192]{2,3,1,0:T(8,128)(2,1)S(1)} copy-done((bf16[1,63,252,192]{2,3,1,0:T(8,128)(2,1)S(1)}, bf16[1,63,252,192]{2,3,1,0:T(8,128)(2,1)}, u32[]{:S(2)}) %copy-start.6) | copy-done | bytes 6096408
  82.5 15.3 %spectral_1.1 = (f32[64,128]{1,0:T(8,128)S(1)}, f32[64,128]{1,0:T(8,128)S(1)}) custom-call(s32[1]{0:T(128)} %bitcast.8.side, bf16[95,64,128]{2,1,0:T(8,128)(2,1)S(1)} %copy-done.1, bf16[95,64,128]{2,1,0:T(8,128)(2,1)} %collective-permute-done.refs_1_, bf16[32,128,256]{2,1,0:T(8,128)(2,1)S(1)} %bitcast.17, bf16[32,64,256]{2,1,0:T(8,128)(2,1)S(1)} %copy-done.2, ...), custom_call_target="tpu_custom_call" | custom-call | flops 8000000000 | bytes 30000000 | tf_op jit(solution)/shard_map/spectral_1/pallas_call | solution.py:527
  97.7 0.0 collective-permute-done.4
  97.7 0.1 collective-permute-start.5
  97.8 2.7 %collective-permute-start.6 = (f32[64,128]{1,0:T(8,128)S(1)}, f32[64,128]{1,0:T(8,128)S(1)}, u32[]{:S(2)}, u32[]{:S(2)}) collective-permute-start(f32[64,128]{1,0:T(8,128)S(1)} %add.57), channel_id=1, source_target_pairs={{0,16},{2,18},{4,20},{6,22},{8,24},{10,26},{12,28},{14,30},{16,0},... | collective-permute-start | bytes 98312 | tf_op jit(solution)/shard_map/ppermute | solution.py:575
  100.5 0.0 collective-permute-done.7.refs_1_
  100.5 5.5 %low_2.1 = (f32[4608,128]{1,0:T(8,128)S(1)}, bf16[64,128,128]{2,1,0:T(8,128)(2,1)S(1)}, bf16[64,128,128]{2,1,0:T(8,128)(2,1)S(1)}) custom-call(bf16[63,64,128]{2,1,0:T(8,128)(2,1)S(1)} %copy-done.7, bf16[63,64,128]{2,1,0:T(8,128)(2,1)} %collective-permute-done.7.refs_1_, bf16[32,128,256]{2,1,0:T(8,128)(2,1)S(1)} %bitcast.18, ...), custom_call_target="tpu_custom_call" | custom-call | flops 8000000000 | bytes 30000000 | tf_op jit(solution)/shard_map/low_2/pallas_call | solution.py:510
  106.1 1.6 %collective-permute-start.8 = (f32[64,128]{1,0:T(8,128)S(1)}, f32[64,128]{1,0:T(8,128)S(1)}, u32[]{:S(2)}, u32[]{:S(2)}) collective-permute-start(f32[64,128]{1,0:T(8,128)S(1)} %add.58), channel_id=1, source_target_pairs={{0,1},{1,0},{2,3},{3,2},{4,5},{5,4},{6,7},{7,6},{8,9},{9,8},{10,11... | collective-permute-start | bytes 98312 | tf_op jit(solution)/shard_map/ppermute | solution.py:575
  107.7 1.5 %collective-permute-start.10 = (f32[64,128]{1,0:T(8,128)S(1)}, f32[64,128]{1,0:T(8,128)S(1)}, u32[]{:S(2)}, u32[]{:S(2)}) collective-permute-start(f32[64,128]{1,0:T(8,128)S(1)} %add.59), channel_id=1, source_target_pairs={{0,4},{2,6},{4,0},{6,2},{8,12},{10,14},{12,8},{14,10},{16,20},{18,... | collective-permute-start | bytes 98312 | tf_op jit(solution)/shard_map/ppermute | solution.py:575
  109.2 1.2 collective-permute-done.9.refs_1_
  110.3 10.4 %spectral_2.1 = (f32[64,128]{1,0:T(8,128)S(1)}, f32[64,128]{1,0:T(8,128)S(1)}) custom-call(s32[1]{0:T(128)} %bitcast.8.side, bf16[32,64,128]{2,1,0:T(8,128)(2,1)S(1)} %copy-done.8, bf16[32,64,128]{2,1,0:T(8,128)(2,1)S(1)} %collective-permute-done.9.refs_1_, f32[4608,128]{1,0:T(8,128)S(1)} %get-tuple-element.102.refs_2_, ...), custom_call_target="tpu_custom_call" | custom-call | flops 8000000000 | bytes 30000000 | tf_op jit(solution)/shard_map/spectral_2/pallas_call | solution.py:527
  120.8 0.1 collective-permute-start.11
  120.8 1.2 collective-permute-done.11
  122.0 1.7 %collective-permute-start.12 = (f32[64,128]{1,0:T(8,128)S(1)}, f32[64,128]{1,0:T(8,128)S(1)}, u32[]{:S(2)}, u32[]{:S(2)}) collective-permute-start(f32[64,128]{1,0:T(8,128)S(1)} %add.62), channel_id=1, source_target_pairs={{0,4},{2,6},{4,0},{6,2},{8,12},{10,14},{12,8},{14,10},{16,20},{18,... | collective-permute-start | bytes 98312 | tf_op jit(solution)/shard_map/ppermute | solution.py:575
  123.7 2.2 %collective-permute-done.12 = f32[64,128]{1,0:T(8,128)S(1)} collective-permute-done((f32[64,128]{1,0:T(8,128)S(1)}, f32[64,128]{1,0:T(8,128)S(1)}, u32[]{:S(2)}, u32[]{:S(2)}) %collective-permute-start.12) | collective-permute-done | bytes 32800 | tf_op jit(solution)/shard_map/ppermute | solution.py:575
  126.0 1.9 %collective-permute-start.13 = (f32[128,128]{1,0:T(8,128)S(1)}, f32[128,128]{1,0:T(8,128)S(1)}, u32[]{:S(2)}, u32[]{:S(2)}) collective-permute-start(f32[128,128]{1,0:T(8,128)S(1)} %pad_maximum_fusion.8), channel_id=1, source_target_pairs={{0,8},{2,10},{4,12},{6,14},{8,0},{10,2},{12,4},{14,6},{16,24},{18,... | collective-permute-start | bytes 196616 | tf_op jit(solution)/shard_map/ppermute | solution.py:575
  127.8 2.5 %collective-permute-done.13 = f32[128,128]{1,0:T(8,128)S(1)} collective-permute-done((f32[128,128]{1,0:T(8,128)S(1)}, f32[128,128]{1,0:T(8,128)S(1)}, u32[]{:S(2)}, u32[]{:S(2)}) %collective-permute-start.13) | collective-permute-done | bytes 65568 | tf_op jit(solution)/shard_map/ppermute | solution.py:575
  130.3 2.9 %collective-permute-start.14 = (f32[128,128]{1,0:T(8,128)S(1)}, f32[128,128]{1,0:T(8,128)S(1)}, u32[]{:S(2)}, u32[]{:S(2)}) collective-permute-start(f32[128,128]{1,0:T(8,128)S(1)} %fusion.9), channel_id=1, source_target_pairs={{0,16},{2,18},{4,20},{6,22},{8,24},{10,26},{12,28},{14,30},{16,0},... | collective-permute-start | bytes 196616 | tf_op jit(solution)/shard_map/ppermute | solution.py:575
  133.2 2.3 %collective-permute-done.14 = f32[128,128]{1,0:T(8,128)S(1)} collective-permute-done((f32[128,128]{1,0:T(8,128)S(1)}, f32[128,128]{1,0:T(8,128)S(1)}, u32[]{:S(2)}, u32[]{:S(2)}) %collective-permute-start.14) | collective-permute-done | bytes 65568 | tf_op jit(solution)/shard_map/ppermute | solution.py:575
  135.5 1.8 %collective-permute-start.15 = (f32[128,128]{1,0:T(8,128)S(1)}, f32[128,128]{1,0:T(8,128)S(1)}, u32[]{:S(2)}, u32[]{:S(2)}) collective-permute-start(f32[128,128]{1,0:T(8,128)S(1)} %add.65), channel_id=1, source_target_pairs={{0,1},{1,0},{2,3},{3,2},{4,5},{5,4},{6,7},{7,6},{8,9},{9,8},{10,11... | collective-permute-start | bytes 196616 | tf_op jit(solution)/shard_map/ppermute | solution.py:575
  137.4 2.5 %collective-permute-done.15 = f32[128,128]{1,0:T(8,128)S(1)} collective-permute-done((f32[128,128]{1,0:T(8,128)S(1)}, f32[128,128]{1,0:T(8,128)S(1)}, u32[]{:S(2)}, u32[]{:S(2)}) %collective-permute-start.15) | collective-permute-done | bytes 65568 | tf_op jit(solution)/shard_map/ppermute | solution.py:575
  139.9 0.1 collective-permute-start.16
  140.0 1.3 collective-permute-done.16
  141.3 0.7 multiply_bitcast_fusion
  (44 shorter events, 0.2 us)
Async XLA Ops:
  6.0 38.2 %collective-permute-start.1 = (bf16[95,64,128]{2,1,0:T(8,128)(2,1)}, bf16[95,64,128]{2,1,0:T(8,128)(2,1)}, u32[]{:S(2)}, u32[]{:S(2)}) collective-permute-start(bf16[95,64,128]{2,1,0:T(8,128)(2,1)} %forward_0.1.refs_0_), channel_id=1, source_target_pairs={{0,1},{1,0},{2,3},{3,2},{4,5},{5,4},{6,7},{7,6},{8,9},{9,8},{10,11... | collective-permute-start | bytes 4669448 | tf_op jit(solution)/shard_map/ppermute | solution.py:624
  19.4 3.9 %copy-start.11 = (bf16[64,64,128]{2,1,0:T(8,128)(2,1)S(1)}, bf16[64,64,128]{2,1,0:T(8,128)(2,1)}, u32[]{:S(2)}) copy-start(bf16[64,64,128]{2,1,0:T(8,128)(2,1)} %constant_dynamic-slice_fusion) | copy-start | bytes 3145732
  29.9 7.5 %copy-start.12 = (bf16[126,192]{0,1:T(8,128)(2,1)S(1)}, bf16[126,192]{0,1:T(8,128)(2,1)}, u32[]{:S(2)}) copy-start(bf16[126,192]{0,1:T(8,128)(2,1)} %param.16) | copy-start | bytes 145156
  29.9 47.6 %collective-permute-start = (bf16[95,64,128]{2,1,0:T(8,128)(2,1)}, bf16[95,64,128]{2,1,0:T(8,128)(2,1)}, u32[]{:S(2)}, u32[]{:S(2)}) collective-permute-start(bf16[95,64,128]{2,1,0:T(8,128)(2,1)} %forward_1.1.refs_0_), channel_id=1, source_target_pairs={{0,1},{1,0},{2,3},{3,2},{4,5},{5,4},{6,7},{7,6},{8,9},{9,8},{10,11... | collective-permute-start | bytes 4669448 | tf_op jit(solution)/shard_map/ppermute | solution.py:624
  35.3 65.2 %collective-permute-start.7 = (bf16[63,64,128]{2,1,0:T(8,128)(2,1)}, bf16[63,64,128]{2,1,0:T(8,128)(2,1)}, u32[]{:S(2)}, u32[]{:S(2)}) collective-permute-start(bf16[63,64,128]{2,1,0:T(8,128)(2,1)} %get-tuple-element.86.refs_0_), channel_id=1, source_target_pairs={{0,1},{1,0},{2,3},{3,2},{4,5},{5,4},{6,7},{7,6},{8,9},{9,8},{10,11... | collective-permute-start | bytes 3096584 | tf_op jit(solution)/shard_map/ppermute | solution.py:624
  37.6 6.6 %copy-start.9 = (bf16[256,252]{1,0:T(8,128)(2,1)S(1)}, bf16[256,252]{1,0:T(8,128)(2,1)}, u32[]{:S(2)}) copy-start(bf16[256,252]{1,0:T(8,128)(2,1)} %constant.52.clone.refs_6_.refs_7_) | copy-start | bytes 387076
  37.7 6.6 %copy-start.10 = (f32[128,128]{1,0:T(8,128)S(1)}, f32[128,128]{1,0:T(8,128)}, u32[]{:S(2)}) copy-start(f32[128,128]{1,0:T(8,128)} %constant.58.clone.refs_10_.refs_11_) | copy-start | bytes 196612
  41.4 2.9 %copy-start = (bf16[95,64,128]{2,1,0:T(8,128)(2,1)S(1)}, bf16[95,64,128]{2,1,0:T(8,128)(2,1)}, u32[]{:S(2)}) copy-start(bf16[95,64,128]{2,1,0:T(8,128)(2,1)} %forward_0.1.refs_0_) | copy-start | bytes 4669444
  41.4 2.9 %copy-start.2 = (bf16[32,64,256]{2,1,0:T(8,128)(2,1)S(1)}, bf16[32,64,256]{2,1,0:T(8,128)(2,1)}, u32[]{:S(2)}) copy-start(bf16[32,64,256]{2,1,0:T(8,128)(2,1)} %pad_maximum_fusion.refs_3_) | copy-start | bytes 3145732
  44.2 1.0 copy-start.3
  45.3 1.0 copy-start.4
  46.3 2.8 %copy-start.5 = (bf16[1,63,252,192]{2,3,1,0:T(8,128)(2,1)S(1)}, bf16[1,63,252,192]{2,3,1,0:T(8,128)(2,1)}, u32[]{:S(2)}) copy-start(bf16[1,63,252,192]{2,3,1,0:T(8,128)(2,1)} %param.15) | copy-start | bytes 18289156
  49.1 18.7 %copy-start.8 = (bf16[32,64,128]{2,1,0:T(8,128)(2,1)S(1)}, bf16[32,64,128]{2,1,0:T(8,128)(2,1)}, u32[]{:S(2)}) copy-start(bf16[32,64,128]{2,1,0:T(8,128)(2,1)} %get-tuple-element.101.refs_0_) | copy-start | bytes 1572868
  49.1 30.6 %copy-start.1 = (bf16[95,64,128]{2,1,0:T(8,128)(2,1)S(1)}, bf16[95,64,128]{2,1,0:T(8,128)(2,1)}, u32[]{:S(2)}) copy-start(bf16[95,64,128]{2,1,0:T(8,128)(2,1)} %forward_1.1.refs_0_) | copy-start | bytes 4669444
  64.4 1.3 collective-permute-start.2
  65.6 3.9 %collective-permute-start.3 = (f32[64,128]{1,0:T(8,128)S(1)}, f32[64,128]{1,0:T(8,128)S(1)}, u32[]{:S(2)}, u32[]{:S(2)}) collective-permute-start(f32[64,128]{1,0:T(8,128)S(1)} %add.55), channel_id=1, source_target_pairs={{0,4},{2,6},{4,0},{6,2},{8,12},{10,14},{12,8},{14,10},{16,20},{18,... | collective-permute-start | bytes 98312 | tf_op jit(solution)/shard_map/ppermute | solution.py:575
  67.8 42.5 %collective-permute-start.9 = (bf16[32,64,128]{2,1,0:T(8,128)(2,1)S(1)}, bf16[32,64,128]{2,1,0:T(8,128)(2,1)S(1)}, u32[]{:S(2)}, u32[]{:S(2)}) collective-permute-start(bf16[32,64,128]{2,1,0:T(8,128)(2,1)S(1)} %copy-done.8), channel_id=1, source_target_pairs={{0,1},{1,0},{2,3},{3,2},{4,5},{5,4},{6,7},{7,6},{8,9},{9,8},{10,11... | collective-permute-start | bytes 1572872 | tf_op jit(solution)/shard_map/ppermute | solution.py:624
  77.6 20.1 %collective-permute-start.4 = (f32[64,128]{1,0:T(8,128)S(1)}, f32[64,128]{1,0:T(8,128)S(1)}, u32[]{:S(2)}, u32[]{:S(2)}) collective-permute-start(f32[64,128]{1,0:T(8,128)S(1)} %add.56), channel_id=1, source_target_pairs={{0,8},{2,10},{4,12},{6,14},{8,0},{10,2},{12,4},{14,6},{16,24},{18,... | collective-permute-start | bytes 98312 | tf_op jit(solution)/shard_map/ppermute | solution.py:575
  79.7 2.8 %copy-start.6 = (bf16[1,63,252,192]{2,3,1,0:T(8,128)(2,1)S(1)}, bf16[1,63,252,192]{2,3,1,0:T(8,128)(2,1)}, u32[]{:S(2)}) copy-start(bf16[1,63,252,192]{2,3,1,0:T(8,128)(2,1)} %param.15) | copy-start | bytes 18289156
  82.4 18.1 %copy-start.7 = (bf16[63,64,128]{2,1,0:T(8,128)(2,1)S(1)}, bf16[63,64,128]{2,1,0:T(8,128)(2,1)}, u32[]{:S(2)}) copy-start(bf16[63,64,128]{2,1,0:T(8,128)(2,1)} %get-tuple-element.86.refs_0_) | copy-start | bytes 3096580
  82.4 27.9 %slice-start = ((s8[6193152]{0:T(1024)(128)(4,1)}), s8[4194304]{0:T(1024)(128)(4,1)S(1)}, s32[]{:S(2)}) async-start(s8[6193152]{0:T(1024)(128)(4,1)} %bitcast.26), calls=%async_computation | async-start | bytes 8388608
  97.7 8.4 %collective-permute-start.5 = (f32[64,128]{1,0:T(8,128)S(1)}, f32[64,128]{1,0:T(8,128)S(1)}, u32[]{:S(2)}, u32[]{:S(2)}) collective-permute-start(f32[64,128]{1,0:T(8,128)S(1)} %get-tuple-element.82), channel_id=1, source_target_pairs={{0,2},{2,0},{4,6},{6,4},{8,10},{10,8},{12,14},{14,12},{16,18},{18,... | collective-permute-start | bytes 98312 | tf_op jit(solution)/shard_map/ppermute | solution.py:647
  97.8 8.3 %collective-permute-start.6 = (f32[64,128]{1,0:T(8,128)S(1)}, f32[64,128]{1,0:T(8,128)S(1)}, u32[]{:S(2)}, u32[]{:S(2)}) collective-permute-start(f32[64,128]{1,0:T(8,128)S(1)} %add.57), channel_id=1, source_target_pairs={{0,16},{2,18},{4,20},{6,22},{8,24},{10,26},{12,28},{14,30},{16,0},... | collective-permute-start | bytes 98312 | tf_op jit(solution)/shard_map/ppermute | solution.py:575
  100.5 9.8 %slice-start.1 = ((s8[6193152]{0:T(1024)(128)(4,1)}), s8[1998848]{0:T(1024)(128)(4,1)S(1)}, s32[]{:S(2)}) async-start(s8[6193152]{0:T(1024)(128)(4,1)} %bitcast.26), calls=%async_computation.1 | async-start | bytes 3997696
  106.1 14.6 %collective-permute-start.8 = (f32[64,128]{1,0:T(8,128)S(1)}, f32[64,128]{1,0:T(8,128)S(1)}, u32[]{:S(2)}, u32[]{:S(2)}) collective-permute-start(f32[64,128]{1,0:T(8,128)S(1)} %add.58), channel_id=1, source_target_pairs={{0,1},{1,0},{2,3},{3,2},{4,5},{5,4},{6,7},{7,6},{8,9},{9,8},{10,11... | collective-permute-start | bytes 98312 | tf_op jit(solution)/shard_map/ppermute | solution.py:575
  107.7 13.0 %collective-permute-start.10 = (f32[64,128]{1,0:T(8,128)S(1)}, f32[64,128]{1,0:T(8,128)S(1)}, u32[]{:S(2)}, u32[]{:S(2)}) collective-permute-start(f32[64,128]{1,0:T(8,128)S(1)} %add.59), channel_id=1, source_target_pairs={{0,4},{2,6},{4,0},{6,2},{8,12},{10,14},{12,8},{14,10},{16,20},{18,... | collective-permute-start | bytes 98312 | tf_op jit(solution)/shard_map/ppermute | solution.py:575
  120.8 1.3 collective-permute-start.11
  122.0 3.9 %collective-permute-start.12 = (f32[64,128]{1,0:T(8,128)S(1)}, f32[64,128]{1,0:T(8,128)S(1)}, u32[]{:S(2)}, u32[]{:S(2)}) collective-permute-start(f32[64,128]{1,0:T(8,128)S(1)} %add.62), channel_id=1, source_target_pairs={{0,4},{2,6},{4,0},{6,2},{8,12},{10,14},{12,8},{14,10},{16,20},{18,... | collective-permute-start | bytes 98312 | tf_op jit(solution)/shard_map/ppermute | solution.py:575
  126.0 4.3 %collective-permute-start.13 = (f32[128,128]{1,0:T(8,128)S(1)}, f32[128,128]{1,0:T(8,128)S(1)}, u32[]{:S(2)}, u32[]{:S(2)}) collective-permute-start(f32[128,128]{1,0:T(8,128)S(1)} %pad_maximum_fusion.8), channel_id=1, source_target_pairs={{0,8},{2,10},{4,12},{6,14},{8,0},{10,2},{12,4},{14,6},{16,24},{18,... | collective-permute-start | bytes 196616 | tf_op jit(solution)/shard_map/ppermute | solution.py:575
  130.3 5.2 %collective-permute-start.14 = (f32[128,128]{1,0:T(8,128)S(1)}, f32[128,128]{1,0:T(8,128)S(1)}, u32[]{:S(2)}, u32[]{:S(2)}) collective-permute-start(f32[128,128]{1,0:T(8,128)S(1)} %fusion.9), channel_id=1, source_target_pairs={{0,16},{2,18},{4,20},{6,22},{8,24},{10,26},{12,28},{14,30},{16,0},... | collective-permute-start | bytes 196616 | tf_op jit(solution)/shard_map/ppermute | solution.py:575
  135.5 4.3 %collective-permute-start.15 = (f32[128,128]{1,0:T(8,128)S(1)}, f32[128,128]{1,0:T(8,128)S(1)}, u32[]{:S(2)}, u32[]{:S(2)}) collective-permute-start(f32[128,128]{1,0:T(8,128)S(1)} %add.65), channel_id=1, source_target_pairs={{0,1},{1,0},{2,3},{3,2},{4,5},{5,4},{6,7},{7,6},{8,9},{9,8},{10,11... | collective-permute-start | bytes 196616 | tf_op jit(solution)/shard_map/ppermute | solution.py:575
  139.9 1.4 collective-permute-start.16

commit v8 on v7

--- a/solution.py
+++ b/solution.py
@@ -327,8 +327,8 @@
                 grid_low[pl.ds(begin, layout.rows), :] = values[:, which * LANES : (which + 1) * LANES]
             return carry
 
-        lax.fori_loop(start, stop, low_block, 0, unroll=4)
-        lax.fori_loop(start, stop, mix_block, 0, unroll=4)
+        lax.fori_loop(start, stop, low_block, 0, unroll=8)
+        lax.fori_loop(start, stop, mix_block, 0, unroll=8)
 
 
 def spectral_kernel(layout, apart, side, *refs):
@@ -372,7 +372,7 @@
                 scratch[pl.ds(begin, rows), :] = values[which % 2 * rows : (which % 2 + 1) * rows, columns]
             return carry
 
-        lax.fori_loop(0, layout.pairs // 2, pair_block, 0, unroll=4)
+        lax.fori_loop(0, layout.pairs // 2, pair_block, 0, unroll=8)
         used = (low + 2 * layout.pairs) * layout.pitch
         if used < layout.slots * layout.pitch:
             scratch[used : layout.slots * layout.pitch, :] = jnp.zeros(
@@ -415,7 +415,7 @@
                 return carry
 
             part = jnp.zeros((degrees - top, LANES), jnp.float32)
-            first, second = lax.fori_loop(start, stop, low_block, (part, part), unroll=4)
+            first, second = lax.fori_loop(start, stop, low_block, (part, part), unroll=8)
             if top:
                 empty = jnp.zeros((top, LANES), jnp.float32)
                 first = jnp.concatenate([empty, first], axis=0)
@@ -442,7 +442,7 @@
             return carry
 
         part = jnp.zeros((rows, LANES), jnp.float32)
-        sums = lax.fori_loop(0, layout.pairs // 2, pair_block, (part,) * 4, unroll=4)
+        sums = lax.fori_loop(0, layout.pairs // 2, pair_block, (part,) * 4, unroll=16)
         placed = jnp.dot(
             place[...],
             jnp.concatenate(

time: 143 us -> 141 us (0.986)
  Pallas kernels: 62.4 us -> 50.5 us
  waiting for transfers between devices: 23 us -> 32.5 us
    pallas_call x3, Pallas kernels: 40.9 us -> 31.1 us  [spectral_call(): pl.pallas_call(functools.partial(spectral_kernel, layout, apart), grid=(l...]
    ppermute x4, waiting for transfers between devices: 9.61 us -> 19.1 us  [others(): return [lax.ppermute(sent, 'space', route) for route in routes]]
    pallas_call x1, Pallas kernels: 5.55 us -> 3.39 us  [low_call(): pl.pallas_call(functools.partial(low_kernel, layout), in_specs=[whole()]...]
  transfers between devices with their start and end apart: 17 -> 17, of which waited for: 11 -> 12; matrix products, arithmetic and copies ran while one was open for 16% -> 16% of each run, Pallas kernels for 40% -> 32%
where the time goes in v8:
time: 141 us; the launch traced here: 140 us
  Pallas kernels  50.5 us (36%)
  waiting for transfers between devices  32.5 us (23%)
  local copies, waits for them, and re-layouts  25.9 us (18%)
  starting transfers between devices  25.7 us (18%)
  other arithmetic  4.52 us (3%)
    pallas_call x3, Pallas kernels, spectral_call(): pl.pallas_call(functools.partial(spectral_kernel, layout, apart), grid=(l...  31.1 us
    ppermute x4, waiting for transfers between devices, others(): return [lax.ppermute(sent, 'space', route) for route in routes]  19.1 us
    ppermute x9, starting transfers between devices, hop_parcels(): parcels.append(lax.ppermute(value, axis, pairs))  18.7 us
    pallas_call x3, Pallas kernels, forward_call(): pl.pallas_call(functools.partial(forward_kernel, layout, chunk, bounds),...  16 us
    ppermute x9, waiting for transfers between devices, hop_parcels(): parcels.append(lax.ppermute(value, axis, pairs))  9.72 us
    unnamed x32, local copies, waits for them, and re-layouts  8.67 us
    ppermute x4, starting transfers between devices, others(): return [lax.ppermute(sent, 'space', route) for route in routes]  6.77 us
    dynamic_slice x2, local copies, waits for them, and re-layouts, bands(): lax.dynamic_slice_in_dim(table, first * layout.rows, count * layout.rows, 1)  5.51 us
  transfers between devices with their start and end apart: 17, of which 12 were waited for; matrix products, arithmetic and copies ran while one was open for 16% of the time, Pallas kernels for 32%

profile of v8, /device:TPU:0, one launch (start us, length us, event | category | flops | bytes accessed | tf_op | source)
XLA Modules:
  0.0 140.1 jit_solution(12190398912745249114)
XLA Ops:
  0.6 5.4 %forward_0.1.refs_0_ = bf16[95,64,128]{2,1,0:T(8,128)(2,1)} custom-call(s32[1]{0:T(128)} %bitcast.index, bf16[1,63,192,252]{3,2,1,0:T(8,128)(2,1)} %bitcast.30, bf16[256,252]{1,0:T(8,128)(2,1)} %constant.59.clone.basis_all, bf16[2,32,64,128]{3,2,1,0:T(8,128)(2,1)} %constant.53.clone.pair_all), custom_call_target="tpu_custom_call" | custom-call | flops 1000000 | bytes 100000 | tf_op jit(solution)/shard_map/forward_0/pallas_call | solution.py:485
  6.0 3.0 %collective-permute-start.1 = (bf16[95,64,128]{2,1,0:T(8,128)(2,1)}, bf16[95,64,128]{2,1,0:T(8,128)(2,1)}, u32[]{:S(2)}, u32[]{:S(2)}) collective-permute-start(bf16[95,64,128]{2,1,0:T(8,128)(2,1)} %forward_0.1.refs_0_), channel_id=1, source_target_pairs={{0,1},{1,0},{2,3},{3,2},{4,5},{5,4},{6,7},{7,6},{8,9},{9,8},{10,11... | collective-permute-start | bytes 4669448 | tf_op jit(solution)/shard_map/ppermute | solution.py:624
  9.0 3.2 %constant_dynamic-slice_fusion.1 = bf16[64,128,128]{2,1,0:T(8,128)(2,1)} fusion(bf16[64,256,128]{2,1,0:T(8,128)(2,1)} %constant.55.clone, s32[]{:T(128)S(6)} %select_n.25), kind=kLoop, calls=%fused_computation.26 | loop fusion | bytes 4194308 | tf_op jit(solution)/shard_map/dynamic_slice | solution.py:604
  12.2 3.3 %copy.20 = bf16[32,256,128]{1,2,0:T(8,128)(2,1)S(1)} copy(bf16[32,256,128]{2,1,0:T(8,128)(2,1)} %bitcast.34) | data formatting | bytes 4194304 | tf_op jit(solution)/shard_map/reshape | solution.py:611
  15.5 2.3 %constant_dynamic-slice_fusion = bf16[64,64,128]{2,1,0:T(8,128)(2,1)} fusion(bf16[64,128,128]{2,1,0:T(8,128)(2,1)} %constant.54.clone, s32[]{:T(128)S(6)} %select_n.26), kind=kLoop, calls=%fused_computation.25 | loop fusion | bytes 2097156 | tf_op jit(solution)/shard_map/dynamic_slice | solution.py:604
  17.8 1.6 %copy.21 = bf16[32,128,128]{1,2,0:T(8,128)(2,1)S(1)} copy(bf16[32,128,128]{2,1,0:T(8,128)(2,1)} %bitcast.33) | data formatting | bytes 2097152 | tf_op jit(solution)/shard_map/reshape | solution.py:613
  19.4 2.0 %dynamic-slice_bitcast_fusion.1.refs_8_.refs_9_ = bf16[16,128,128]{2,1,0:T(8,128)(2,1)} fusion(bf16[2,16,128,128]{3,2,1,0:T(8,128)(2,1)} %constant.56.clone, s32[]{:T(128)S(6)} %select_n.27), kind=kLoop, calls=%fused_computation.2 | loop fusion | bytes 1048580 | tf_op jit(solution)/shard_map/jit(dynamic_index_in_dim)/squeeze | solution.py:597
  21.4 1.9 %dynamic-slice_bitcast_fusion.refs_9_.refs_10_ = bf16[16,64,256]{2,1,0:T(8,128)(2,1)} fusion(bf16[2,16,64,256]{3,2,1,0:T(8,128)(2,1)} %constant.57.clone, s32[]{:T(128)S(6)} %select_n.27), kind=kLoop, calls=%fused_computation.1 | loop fusion | bytes 1048580 | tf_op jit(solution)/shard_map/jit(dynamic_index_in_dim)/squeeze | solution.py:597
  23.4 0.1 fusion.10
  23.4 1.2 pad_maximum_fusion.refs_3_
  24.6 5.3 %forward_1.1.refs_0_ = bf16[95,64,128]{2,1,0:T(8,128)(2,1)} custom-call(s32[1]{0:T(128)} %bitcast.index, bf16[1,63,192,252]{3,2,1,0:T(8,128)(2,1)} %bitcast.31, bf16[256,252]{1,0:T(8,128)(2,1)} %constant.59.clone.basis_all, bf16[2,32,64,128]{3,2,1,0:T(8,128)(2,1)} %constant.53.clone.pair_all), custom_call_target="tpu_custom_call" | custom-call | flops 1000000 | bytes 100000 | tf_op jit(solution)/shard_map/forward_1/pallas_call | solution.py:485
  29.9 0.0 copy-start.12
  29.9 0.1 collective-permute-start
  30.0 5.3 %forward_2.1 = (bf16[63,64,128]{2,1,0:T(8,128)(2,1)}, bf16[32,64,128]{2,1,0:T(8,128)(2,1)}) custom-call(s32[1]{0:T(128)} %bitcast.index, bf16[1,63,192,252]{3,2,1,0:T(8,128)(2,1)} %bitcast.32, bf16[256,252]{1,0:T(8,128)(2,1)} %constant.59.clone.basis_all, bf16[2,32,64,128]{3,2,1,0:T(8,128)(2,1)} %constant.53.clone.pair_all), custom_call_target="tpu_custom_call" | custom-call | flops 1000000 | bytes 100000 | tf_op jit(solution)/shard_map/forward_2/pallas_call | solution.py:485
  35.3 2.1 %collective-permute-start.7 = (bf16[63,64,128]{2,1,0:T(8,128)(2,1)}, bf16[63,64,128]{2,1,0:T(8,128)(2,1)}, u32[]{:S(2)}, u32[]{:S(2)}) collective-permute-start(bf16[63,64,128]{2,1,0:T(8,128)(2,1)} %get-tuple-element.86.refs_0_), channel_id=1, source_target_pairs={{0,1},{1,0},{2,3},{3,2},{4,5},{5,4},{6,7},{7,6},{8,9},{9,8},{10,11... | collective-permute-start | bytes 3096584 | tf_op jit(solution)/shard_map/ppermute | solution.py:624
  37.4 0.1 copy.22
  37.6 0.1 rev.6
  37.6 0.0 copy-start.9
  37.7 0.0 copy-start.10
  37.7 0.8 fusion.11
  38.5 0.9 copy.24
  39.4 0.6 slice.54
  40.0 1.4 rev.7
  41.4 0.9 fusion.7
  42.3 1.2 pad_maximum_fusion.1
  43.5 0.1 slice_negate_fusion
  43.7 0.1 pad_maximum_fusion.2
  43.8 0.4 collective-permute-done.1.refs_1_
  44.3 1.0 copy-done.3
  45.3 1.0 copy-done.4
  46.3 2.8 %copy-done.5 = bf16[1,63,252,192]{2,3,1,0:T(8,128)(2,1)S(1)} copy-done((bf16[1,63,252,192]{2,3,1,0:T(8,128)(2,1)S(1)}, bf16[1,63,252,192]{2,3,1,0:T(8,128)(2,1)}, u32[]{:S(2)}) %copy-start.5) | copy-done | bytes 6096408
  49.1 11.3 %spectral_0.1 = (f32[64,128]{1,0:T(8,128)S(1)}, f32[64,128]{1,0:T(8,128)S(1)}) custom-call(s32[1]{0:T(128)} %bitcast.8.side, bf16[95,64,128]{2,1,0:T(8,128)(2,1)S(1)} %copy-done, bf16[95,64,128]{2,1,0:T(8,128)(2,1)} %collective-permute-done.1.refs_1_, bf16[32,128,256]{2,1,0:T(8,128)(2,1)S(1)} %bitcast.16, bf16[32,64,256]{2,1,0:T(8,128)(2,1)S(1)} %copy-done.2, ...), custom_call_target="tpu_custom_call" | custom-call | flops 8000000000 | bytes 30000000 | tf_op jit(solution)/shard_map/spectral_0/pallas_call | solution.py:527
  60.4 0.1 collective-permute-start.2
  60.5 1.2 collective-permute-done.2
  61.7 2.0 %collective-permute-start.3 = (f32[64,128]{1,0:T(8,128)S(1)}, f32[64,128]{1,0:T(8,128)S(1)}, u32[]{:S(2)}, u32[]{:S(2)}) collective-permute-start(f32[64,128]{1,0:T(8,128)S(1)} %add.55), channel_id=1, source_target_pairs={{0,4},{2,6},{4,0},{6,2},{8,12},{10,14},{12,8},{14,10},{16,20},{18,... | collective-permute-start | bytes 98312 | tf_op jit(solution)/shard_map/ppermute | solution.py:575
  63.7 0.1 pad_maximum_fusion.5
  63.9 1.6 %collective-permute-start.9 = (bf16[32,64,128]{2,1,0:T(8,128)(2,1)S(1)}, bf16[32,64,128]{2,1,0:T(8,128)(2,1)S(1)}, u32[]{:S(2)}, u32[]{:S(2)}) collective-permute-start(bf16[32,64,128]{2,1,0:T(8,128)(2,1)S(1)} %copy-done.8), channel_id=1, source_target_pairs={{0,1},{1,0},{2,3},{3,2},{4,5},{5,4},{6,7},{7,6},{8,9},{9,8},{10,11... | collective-permute-start | bytes 1572872 | tf_op jit(solution)/shard_map/ppermute | solution.py:624
  65.4 0.2 collective-permute-done.3
  65.6 12.0 %collective-permute-done.refs_1_ = bf16[95,64,128]{2,1,0:T(8,128)(2,1)} collective-permute-done((bf16[95,64,128]{2,1,0:T(8,128)(2,1)}, bf16[95,64,128]{2,1,0:T(8,128)(2,1)}, u32[]{:S(2)}, u32[]{:S(2)}) %collective-permute-start) | collective-permute-done | bytes 1556512 | tf_op jit(solution)/shard_map/ppermute | solution.py:624
  77.6 2.1 %collective-permute-start.4 = (f32[64,128]{1,0:T(8,128)S(1)}, f32[64,128]{1,0:T(8,128)S(1)}, u32[]{:S(2)}, u32[]{:S(2)}) collective-permute-start(f32[64,128]{1,0:T(8,128)S(1)} %add.56), channel_id=1, source_target_pairs={{0,8},{2,10},{4,12},{6,14},{8,0},{10,2},{12,4},{14,6},{16,24},{18,... | collective-permute-start | bytes 98312 | tf_op jit(solution)/shard_map/ppermute | solution.py:575
  79.7 2.8 %copy-done.6 = bf16[1,63,252,192]{2,3,1,0:T(8,128)(2,1)S(1)} copy-done((bf16[1,63,252,192]{2,3,1,0:T(8,128)(2,1)S(1)}, bf16[1,63,252,192]{2,3,1,0:T(8,128)(2,1)}, u32[]{:S(2)}) %copy-start.6) | copy-done | bytes 6096408
  82.5 11.3 %spectral_1.1 = (f32[64,128]{1,0:T(8,128)S(1)}, f32[64,128]{1,0:T(8,128)S(1)}) custom-call(s32[1]{0:T(128)} %bitcast.8.side, bf16[95,64,128]{2,1,0:T(8,128)(2,1)S(1)} %copy-done.1, bf16[95,64,128]{2,1,0:T(8,128)(2,1)} %collective-permute-done.refs_1_, bf16[32,128,256]{2,1,0:T(8,128)(2,1)S(1)} %bitcast.17, bf16[32,64,256]{2,1,0:T(8,128)(2,1)S(1)} %copy-done.2, ...), custom_call_target="tpu_custom_call" | custom-call | flops 8000000000 | bytes 30000000 | tf_op jit(solution)/shard_map/spectral_1/pallas_call | solution.py:527
  93.8 0.1 collective-permute-start.5
  93.9 2.7 %collective-permute-start.6 = (f32[64,128]{1,0:T(8,128)S(1)}, f32[64,128]{1,0:T(8,128)S(1)}, u32[]{:S(2)}, u32[]{:S(2)}) collective-permute-start(f32[64,128]{1,0:T(8,128)S(1)} %add.57), channel_id=1, source_target_pairs={{0,16},{2,18},{4,20},{6,22},{8,24},{10,26},{12,28},{14,30},{16,0},... | collective-permute-start | bytes 98312 | tf_op jit(solution)/shard_map/ppermute | solution.py:575
  96.6 3.1 %collective-permute-done.7.refs_1_ = bf16[63,64,128]{2,1,0:T(8,128)(2,1)} collective-permute-done((bf16[63,64,128]{2,1,0:T(8,128)(2,1)}, bf16[63,64,128]{2,1,0:T(8,128)(2,1)}, u32[]{:S(2)}, u32[]{:S(2)}) %collective-permute-start.7) | collective-permute-done | bytes 1032224 | tf_op jit(solution)/shard_map/ppermute | solution.py:624
  99.7 3.4 %low_2.1 = (f32[4608,128]{1,0:T(8,128)S(1)}, bf16[64,128,128]{2,1,0:T(8,128)(2,1)S(1)}, bf16[64,128,128]{2,1,0:T(8,128)(2,1)S(1)}) custom-call(bf16[63,64,128]{2,1,0:T(8,128)(2,1)S(1)} %copy-done.7, bf16[63,64,128]{2,1,0:T(8,128)(2,1)} %collective-permute-done.7.refs_1_, bf16[32,128,256]{2,1,0:T(8,128)(2,1)S(1)} %bitcast.18, ...), custom_call_target="tpu_custom_call" | custom-call | flops 8000000000 | bytes 30000000 | tf_op jit(solution)/shard_map/low_2/pallas_call | solution.py:510
  103.1 0.0 collective-permute-done.6
  103.1 2.1 %collective-permute-start.8 = (f32[64,128]{1,0:T(8,128)S(1)}, f32[64,128]{1,0:T(8,128)S(1)}, u32[]{:S(2)}, u32[]{:S(2)}) collective-permute-start(f32[64,128]{1,0:T(8,128)S(1)} %add.58), channel_id=1, source_target_pairs={{0,1},{1,0},{2,3},{3,2},{4,5},{5,4},{6,7},{7,6},{8,9},{9,8},{10,11... | collective-permute-start | bytes 98312 | tf_op jit(solution)/shard_map/ppermute | solution.py:575
  105.3 1.5 %collective-permute-start.10 = (f32[64,128]{1,0:T(8,128)S(1)}, f32[64,128]{1,0:T(8,128)S(1)}, u32[]{:S(2)}, u32[]{:S(2)}) collective-permute-start(f32[64,128]{1,0:T(8,128)S(1)} %add.59), channel_id=1, source_target_pairs={{0,4},{2,6},{4,0},{6,2},{8,12},{10,14},{12,8},{14,10},{16,20},{18,... | collective-permute-start | bytes 98312 | tf_op jit(solution)/shard_map/ppermute | solution.py:575
  106.8 3.6 %collective-permute-done.9.refs_1_ = bf16[32,64,128]{2,1,0:T(8,128)(2,1)S(1)} collective-permute-done((bf16[32,64,128]{2,1,0:T(8,128)(2,1)S(1)}, bf16[32,64,128]{2,1,0:T(8,128)(2,1)S(1)}, u32[]{:S(2)}, u32[]{:S(2)}) %collective-permute-start.9) | collective-permute-done | bytes 524320 | tf_op jit(solution)/shard_map/ppermute | solution.py:624
  110.3 8.5 %spectral_2.1 = (f32[64,128]{1,0:T(8,128)S(1)}, f32[64,128]{1,0:T(8,128)S(1)}) custom-call(s32[1]{0:T(128)} %bitcast.8.side, bf16[32,64,128]{2,1,0:T(8,128)(2,1)S(1)} %copy-done.8, bf16[32,64,128]{2,1,0:T(8,128)(2,1)S(1)} %collective-permute-done.9.refs_1_, f32[4608,128]{1,0:T(8,128)S(1)} %get-tuple-element.102.refs_2_, ...), custom_call_target="tpu_custom_call" | custom-call | flops 8000000000 | bytes 30000000 | tf_op jit(solution)/shard_map/spectral_2/pallas_call | solution.py:527
  118.9 0.1 collective-permute-start.11
  119.0 1.2 collective-permute-done.11
  120.2 1.7 %collective-permute-start.12 = (f32[64,128]{1,0:T(8,128)S(1)}, f32[64,128]{1,0:T(8,128)S(1)}, u32[]{:S(2)}, u32[]{:S(2)}) collective-permute-start(f32[64,128]{1,0:T(8,128)S(1)} %add.62), channel_id=1, source_target_pairs={{0,4},{2,6},{4,0},{6,2},{8,12},{10,14},{12,8},{14,10},{16,20},{18,... | collective-permute-start | bytes 98312 | tf_op jit(solution)/shard_map/ppermute | solution.py:575
  121.9 2.2 %collective-permute-done.12 = f32[64,128]{1,0:T(8,128)S(1)} collective-permute-done((f32[64,128]{1,0:T(8,128)S(1)}, f32[64,128]{1,0:T(8,128)S(1)}, u32[]{:S(2)}, u32[]{:S(2)}) %collective-permute-start.12) | collective-permute-done | bytes 32800 | tf_op jit(solution)/shard_map/ppermute | solution.py:575
  124.1 1.9 %collective-permute-start.13 = (f32[128,128]{1,0:T(8,128)S(1)}, f32[128,128]{1,0:T(8,128)S(1)}, u32[]{:S(2)}, u32[]{:S(2)}) collective-permute-start(f32[128,128]{1,0:T(8,128)S(1)} %pad_maximum_fusion.8), channel_id=1, source_target_pairs={{0,8},{2,10},{4,12},{6,14},{8,0},{10,2},{12,4},{14,6},{16,24},{18,... | collective-permute-start | bytes 196616 | tf_op jit(solution)/shard_map/ppermute | solution.py:575
  126.0 2.5 %collective-permute-done.13 = f32[128,128]{1,0:T(8,128)S(1)} collective-permute-done((f32[128,128]{1,0:T(8,128)S(1)}, f32[128,128]{1,0:T(8,128)S(1)}, u32[]{:S(2)}, u32[]{:S(2)}) %collective-permute-start.13) | collective-permute-done | bytes 65568 | tf_op jit(solution)/shard_map/ppermute | solution.py:575
  128.4 2.9 %collective-permute-start.14 = (f32[128,128]{1,0:T(8,128)S(1)}, f32[128,128]{1,0:T(8,128)S(1)}, u32[]{:S(2)}, u32[]{:S(2)}) collective-permute-start(f32[128,128]{1,0:T(8,128)S(1)} %fusion.9), channel_id=1, source_target_pairs={{0,16},{2,18},{4,20},{6,22},{8,24},{10,26},{12,28},{14,30},{16,0},... | collective-permute-start | bytes 196616 | tf_op jit(solution)/shard_map/ppermute | solution.py:575
  131.3 2.4 %collective-permute-done.14 = f32[128,128]{1,0:T(8,128)S(1)} collective-permute-done((f32[128,128]{1,0:T(8,128)S(1)}, f32[128,128]{1,0:T(8,128)S(1)}, u32[]{:S(2)}, u32[]{:S(2)}) %collective-permute-start.14) | collective-permute-done | bytes 65568 | tf_op jit(solution)/shard_map/ppermute | solution.py:575
  133.7 1.8 %collective-permute-start.15 = (f32[128,128]{1,0:T(8,128)S(1)}, f32[128,128]{1,0:T(8,128)S(1)}, u32[]{:S(2)}, u32[]{:S(2)}) collective-permute-start(f32[128,128]{1,0:T(8,128)S(1)} %add.65), channel_id=1, source_target_pairs={{0,1},{1,0},{2,3},{3,2},{4,5},{5,4},{6,7},{7,6},{8,9},{9,8},{10,11... | collective-permute-start | bytes 196616 | tf_op jit(solution)/shard_map/ppermute | solution.py:575
  135.5 2.5 %collective-permute-done.15 = f32[128,128]{1,0:T(8,128)S(1)} collective-permute-done((f32[128,128]{1,0:T(8,128)S(1)}, f32[128,128]{1,0:T(8,128)S(1)}, u32[]{:S(2)}, u32[]{:S(2)}) %collective-permute-start.15) | collective-permute-done | bytes 65568 | tf_op jit(solution)/shard_map/ppermute | solution.py:575
  138.0 0.1 collective-permute-start.16
  138.1 1.3 collective-permute-done.16
  139.4 0.7 multiply_bitcast_fusion
  (44 shorter events, 0.2 us)
Async XLA Ops:
  6.0 38.2 %collective-permute-start.1 = (bf16[95,64,128]{2,1,0:T(8,128)(2,1)}, bf16[95,64,128]{2,1,0:T(8,128)(2,1)}, u32[]{:S(2)}, u32[]{:S(2)}) collective-permute-start(bf16[95,64,128]{2,1,0:T(8,128)(2,1)} %forward_0.1.refs_0_), channel_id=1, source_target_pairs={{0,1},{1,0},{2,3},{3,2},{4,5},{5,4},{6,7},{7,6},{8,9},{9,8},{10,11... | collective-permute-start | bytes 4669448 | tf_op jit(solution)/shard_map/ppermute | solution.py:624
  19.4 3.9 %copy-start.11 = (bf16[64,64,128]{2,1,0:T(8,128)(2,1)S(1)}, bf16[64,64,128]{2,1,0:T(8,128)(2,1)}, u32[]{:S(2)}) copy-start(bf16[64,64,128]{2,1,0:T(8,128)(2,1)} %constant_dynamic-slice_fusion) | copy-start | bytes 3145732
  29.9 7.5 %copy-start.12 = (bf16[126,192]{0,1:T(8,128)(2,1)S(1)}, bf16[126,192]{0,1:T(8,128)(2,1)}, u32[]{:S(2)}) copy-start(bf16[126,192]{0,1:T(8,128)(2,1)} %param.16) | copy-start | bytes 145156
  29.9 47.6 %collective-permute-start = (bf16[95,64,128]{2,1,0:T(8,128)(2,1)}, bf16[95,64,128]{2,1,0:T(8,128)(2,1)}, u32[]{:S(2)}, u32[]{:S(2)}) collective-permute-start(bf16[95,64,128]{2,1,0:T(8,128)(2,1)} %forward_1.1.refs_0_), channel_id=1, source_target_pairs={{0,1},{1,0},{2,3},{3,2},{4,5},{5,4},{6,7},{7,6},{8,9},{9,8},{10,11... | collective-permute-start | bytes 4669448 | tf_op jit(solution)/shard_map/ppermute | solution.py:624
  35.3 64.4 %collective-permute-start.7 = (bf16[63,64,128]{2,1,0:T(8,128)(2,1)}, bf16[63,64,128]{2,1,0:T(8,128)(2,1)}, u32[]{:S(2)}, u32[]{:S(2)}) collective-permute-start(bf16[63,64,128]{2,1,0:T(8,128)(2,1)} %get-tuple-element.86.refs_0_), channel_id=1, source_target_pairs={{0,1},{1,0},{2,3},{3,2},{4,5},{5,4},{6,7},{7,6},{8,9},{9,8},{10,11... | collective-permute-start | bytes 3096584 | tf_op jit(solution)/shard_map/ppermute | solution.py:624
  37.6 6.6 %copy-start.9 = (bf16[256,252]{1,0:T(8,128)(2,1)S(1)}, bf16[256,252]{1,0:T(8,128)(2,1)}, u32[]{:S(2)}) copy-start(bf16[256,252]{1,0:T(8,128)(2,1)} %constant.52.clone.refs_6_.refs_7_) | copy-start | bytes 387076
  37.7 6.6 %copy-start.10 = (f32[128,128]{1,0:T(8,128)S(1)}, f32[128,128]{1,0:T(8,128)}, u32[]{:S(2)}) copy-start(f32[128,128]{1,0:T(8,128)} %constant.58.clone.refs_10_.refs_11_) | copy-start | bytes 196612
  41.4 2.9 %copy-start = (bf16[95,64,128]{2,1,0:T(8,128)(2,1)S(1)}, bf16[95,64,128]{2,1,0:T(8,128)(2,1)}, u32[]{:S(2)}) copy-start(bf16[95,64,128]{2,1,0:T(8,128)(2,1)} %forward_0.1.refs_0_) | copy-start | bytes 4669444
  41.4 2.9 %copy-start.2 = (bf16[32,64,256]{2,1,0:T(8,128)(2,1)S(1)}, bf16[32,64,256]{2,1,0:T(8,128)(2,1)}, u32[]{:S(2)}) copy-start(bf16[32,64,256]{2,1,0:T(8,128)(2,1)} %pad_maximum_fusion.refs_3_) | copy-start | bytes 3145732
  44.2 1.0 copy-start.3
  45.3 1.0 copy-start.4
  46.3 2.8 %copy-start.5 = (bf16[1,63,252,192]{2,3,1,0:T(8,128)(2,1)S(1)}, bf16[1,63,252,192]{2,3,1,0:T(8,128)(2,1)}, u32[]{:S(2)}) copy-start(bf16[1,63,252,192]{2,3,1,0:T(8,128)(2,1)} %param.15) | copy-start | bytes 18289156
  49.1 14.8 %copy-start.8 = (bf16[32,64,128]{2,1,0:T(8,128)(2,1)S(1)}, bf16[32,64,128]{2,1,0:T(8,128)(2,1)}, u32[]{:S(2)}) copy-start(bf16[32,64,128]{2,1,0:T(8,128)(2,1)} %get-tuple-element.101.refs_0_) | copy-start | bytes 1572868
  49.1 30.6 %copy-start.1 = (bf16[95,64,128]{2,1,0:T(8,128)(2,1)S(1)}, bf16[95,64,128]{2,1,0:T(8,128)(2,1)}, u32[]{:S(2)}) copy-start(bf16[95,64,128]{2,1,0:T(8,128)(2,1)} %forward_1.1.refs_0_) | copy-start | bytes 4669444
  60.4 1.3 collective-permute-start.2
  61.7 3.9 %collective-permute-start.3 = (f32[64,128]{1,0:T(8,128)S(1)}, f32[64,128]{1,0:T(8,128)S(1)}, u32[]{:S(2)}, u32[]{:S(2)}) collective-permute-start(f32[64,128]{1,0:T(8,128)S(1)} %add.55), channel_id=1, source_target_pairs={{0,4},{2,6},{4,0},{6,2},{8,12},{10,14},{12,8},{14,10},{16,20},{18,... | collective-permute-start | bytes 98312 | tf_op jit(solution)/shard_map/ppermute | solution.py:575
  63.9 46.5 %collective-permute-start.9 = (bf16[32,64,128]{2,1,0:T(8,128)(2,1)S(1)}, bf16[32,64,128]{2,1,0:T(8,128)(2,1)S(1)}, u32[]{:S(2)}, u32[]{:S(2)}) collective-permute-start(bf16[32,64,128]{2,1,0:T(8,128)(2,1)S(1)} %copy-done.8), channel_id=1, source_target_pairs={{0,1},{1,0},{2,3},{3,2},{4,5},{5,4},{6,7},{7,6},{8,9},{9,8},{10,11... | collective-permute-start | bytes 1572872 | tf_op jit(solution)/shard_map/ppermute | solution.py:624
  77.6 16.2 %collective-permute-start.4 = (f32[64,128]{1,0:T(8,128)S(1)}, f32[64,128]{1,0:T(8,128)S(1)}, u32[]{:S(2)}, u32[]{:S(2)}) collective-permute-start(f32[64,128]{1,0:T(8,128)S(1)} %add.56), channel_id=1, source_target_pairs={{0,8},{2,10},{4,12},{6,14},{8,0},{10,2},{12,4},{14,6},{16,24},{18,... | collective-permute-start | bytes 98312 | tf_op jit(solution)/shard_map/ppermute | solution.py:575
  79.7 2.8 %copy-start.6 = (bf16[1,63,252,192]{2,3,1,0:T(8,128)(2,1)S(1)}, bf16[1,63,252,192]{2,3,1,0:T(8,128)(2,1)}, u32[]{:S(2)}) copy-start(bf16[1,63,252,192]{2,3,1,0:T(8,128)(2,1)} %param.15) | copy-start | bytes 18289156
  82.4 17.3 %copy-start.7 = (bf16[63,64,128]{2,1,0:T(8,128)(2,1)S(1)}, bf16[63,64,128]{2,1,0:T(8,128)(2,1)}, u32[]{:S(2)}) copy-start(bf16[63,64,128]{2,1,0:T(8,128)(2,1)} %get-tuple-element.86.refs_0_) | copy-start | bytes 3096580
  82.4 27.9 %slice-start = ((s8[6193152]{0:T(1024)(128)(4,1)}), s8[4194304]{0:T(1024)(128)(4,1)S(1)}, s32[]{:S(2)}) async-start(s8[6193152]{0:T(1024)(128)(4,1)} %bitcast.26), calls=%async_computation | async-start | bytes 8388608
  93.8 9.3 %collective-permute-start.5 = (f32[64,128]{1,0:T(8,128)S(1)}, f32[64,128]{1,0:T(8,128)S(1)}, u32[]{:S(2)}, u32[]{:S(2)}) collective-permute-start(f32[64,128]{1,0:T(8,128)S(1)} %get-tuple-element.82), channel_id=1, source_target_pairs={{0,2},{2,0},{4,6},{6,4},{8,10},{10,8},{12,14},{14,12},{16,18},{18,... | collective-permute-start | bytes 98312 | tf_op jit(solution)/shard_map/ppermute | solution.py:647
  93.9 9.2 %collective-permute-start.6 = (f32[64,128]{1,0:T(8,128)S(1)}, f32[64,128]{1,0:T(8,128)S(1)}, u32[]{:S(2)}, u32[]{:S(2)}) collective-permute-start(f32[64,128]{1,0:T(8,128)S(1)} %add.57), channel_id=1, source_target_pairs={{0,16},{2,18},{4,20},{6,22},{8,24},{10,26},{12,28},{14,30},{16,0},... | collective-permute-start | bytes 98312 | tf_op jit(solution)/shard_map/ppermute | solution.py:575
  99.7 10.6 %slice-start.1 = ((s8[6193152]{0:T(1024)(128)(4,1)}), s8[1998848]{0:T(1024)(128)(4,1)S(1)}, s32[]{:S(2)}) async-start(s8[6193152]{0:T(1024)(128)(4,1)} %bitcast.26), calls=%async_computation.1 | async-start | bytes 3997696
  103.1 15.7 %collective-permute-start.8 = (f32[64,128]{1,0:T(8,128)S(1)}, f32[64,128]{1,0:T(8,128)S(1)}, u32[]{:S(2)}, u32[]{:S(2)}) collective-permute-start(f32[64,128]{1,0:T(8,128)S(1)} %add.58), channel_id=1, source_target_pairs={{0,1},{1,0},{2,3},{3,2},{4,5},{5,4},{6,7},{7,6},{8,9},{9,8},{10,11... | collective-permute-start | bytes 98312 | tf_op jit(solution)/shard_map/ppermute | solution.py:575
  105.3 13.6 %collective-permute-start.10 = (f32[64,128]{1,0:T(8,128)S(1)}, f32[64,128]{1,0:T(8,128)S(1)}, u32[]{:S(2)}, u32[]{:S(2)}) collective-permute-start(f32[64,128]{1,0:T(8,128)S(1)} %add.59), channel_id=1, source_target_pairs={{0,4},{2,6},{4,0},{6,2},{8,12},{10,14},{12,8},{14,10},{16,20},{18,... | collective-permute-start | bytes 98312 | tf_op jit(solution)/shard_map/ppermute | solution.py:575
  118.9 1.3 collective-permute-start.11
  120.2 3.9 %collective-permute-start.12 = (f32[64,128]{1,0:T(8,128)S(1)}, f32[64,128]{1,0:T(8,128)S(1)}, u32[]{:S(2)}, u32[]{:S(2)}) collective-permute-start(f32[64,128]{1,0:T(8,128)S(1)} %add.62), channel_id=1, source_target_pairs={{0,4},{2,6},{4,0},{6,2},{8,12},{10,14},{12,8},{14,10},{16,20},{18,... | collective-permute-start | bytes 98312 | tf_op jit(solution)/shard_map/ppermute | solution.py:575
  124.1 4.3 %collective-permute-start.13 = (f32[128,128]{1,0:T(8,128)S(1)}, f32[128,128]{1,0:T(8,128)S(1)}, u32[]{:S(2)}, u32[]{:S(2)}) collective-permute-start(f32[128,128]{1,0:T(8,128)S(1)} %pad_maximum_fusion.8), channel_id=1, source_target_pairs={{0,8},{2,10},{4,12},{6,14},{8,0},{10,2},{12,4},{14,6},{16,24},{18,... | collective-permute-start | bytes 196616 | tf_op jit(solution)/shard_map/ppermute | solution.py:575
  128.4 5.2 %collective-permute-start.14 = (f32[128,128]{1,0:T(8,128)S(1)}, f32[128,128]{1,0:T(8,128)S(1)}, u32[]{:S(2)}, u32[]{:S(2)}) collective-permute-start(f32[128,128]{1,0:T(8,128)S(1)} %fusion.9), channel_id=1, source_target_pairs={{0,16},{2,18},{4,20},{6,22},{8,24},{10,26},{12,28},{14,30},{16,0},... | collective-permute-start | bytes 196616 | tf_op jit(solution)/shard_map/ppermute | solution.py:575
  133.7 4.3 %collective-permute-start.15 = (f32[128,128]{1,0:T(8,128)S(1)}, f32[128,128]{1,0:T(8,128)S(1)}, u32[]{:S(2)}, u32[]{:S(2)}) collective-permute-start(f32[128,128]{1,0:T(8,128)S(1)} %add.65), channel_id=1, source_target_pairs={{0,1},{1,0},{2,3},{3,2},{4,5},{5,4},{6,7},{7,6},{8,9},{9,8},{10,11... | collective-permute-start | bytes 196616 | tf_op jit(solution)/shard_map/ppermute | solution.py:575
  138.0 1.4 collective-permute-start.16

commit v9 on v8

--- a/solution.py
+++ b/solution.py
@@ -16,6 +16,8 @@
 LANES = 128
 GROUP = 16
 PAIRS = 8
+MOVED = 3
+TAIL = 8
 VMEM = 30 * 1024 * 1024
 FORWARD_VMEM = 56 * 1024 * 1024
 
@@ -24,26 +26,32 @@
     return -(-value // step) * step
 
 
+@functools.lru_cache(maxsize=None)
 def legendre_table():
-    colatitude = math.pi * (np.arange(NLAT) + 0.5) / NLAT
+    single = np.float32
+    colatitude = single(math.pi) * (np.arange(NLAT, dtype=single) + single(0.5)) / single(NLAT)
     cos_theta, sin_theta = np.cos(colatitude), np.sin(colatitude)
-    counters = np.arange(1, MODES)
-    log_steps = 0.5 * np.log((2.0 * counters + 1.0) / (2.0 * counters))
-    log_table = np.concatenate([[0.0], np.cumsum(log_steps)])
-    table = np.zeros((MODES, MODES, NLAT))
-    for order in range(MODES):
-        table[order, order] = np.exp(
-            0.5 * math.log(1.0 / (4.0 * math.pi)) + log_table[order] + order * np.log(sin_theta)
+    counters = np.arange(1, MODES, dtype=single)
+    log_steps = single(0.5) * np.log((2 * counters + 1) / (2 * counters))
+    log_table = np.concatenate([np.zeros(1, single), np.cumsum(log_steps, dtype=single)])
+    order = np.arange(MODES, dtype=single)[:, None]
+    start = single(0.5 * math.log(1.0 / (4.0 * math.pi)))
+    diagonal = np.exp(start + log_table[:, None] + order * np.log(sin_theta)[None])
+    previous = earlier = np.zeros_like(diagonal)
+    table = np.zeros((MODES, MODES, NLAT), single)
+    for at in range(MODES):
+        degree, below = single(at), single(at - 1)
+        growth = np.sqrt(
+            np.maximum(4 * degree * degree - 1, single(0)) / np.maximum(degree * degree - order * order, single(1))
         )
-        for degree in range(order + 1, MODES):
-            growth = math.sqrt((4.0 * degree**2 - 1.0) / (degree**2 - order**2))
-            below = degree - 1
-            current = cos_theta * table[order, below]
-            if below > order:
-                damping = math.sqrt((below**2 - order**2) / (4.0 * below**2 - 1.0))
-                current = current - damping * table[order, degree - 2]
-            table[order, degree] = growth * current
-    weight = math.pi / NLAT * (2.0 * math.pi / NLON) * sin_theta
+        damping = np.sqrt(
+            np.maximum(below * below - order * order, single(0)) / np.maximum(4 * below * below - 1, single(1))
+        )
+        current = growth * (cos_theta[None] * previous - damping * earlier)
+        current = np.where(order == degree, diagonal, np.where(order < degree, current, single(0)))
+        table[:, at] = current
+        previous, earlier = current, previous
+    weight = single(math.pi / NLAT * (2.0 * math.pi / NLON)) * sin_theta
     return table, table * weight
 
 
@@ -56,12 +64,15 @@
         self.parts, self.local = parts, local
         self.rows = round_up(local + 1, 16)
         self.half = self.rows // 2
-        self.pitch = self.rows + 8
+        self.base = round_up(max(self.rows - local, 1), 8)
+        self.pitch = self.rows + self.base
         self.low = max(MODES - local, 0)
         high = MODES - self.low
         self.pairs = round_up((high + 1) // 2, 2)
         self.twos = round_up(self.low, 2) // 2
-        self.blocks = self.low + self.pairs
+        self.sent, self.runs = self.low, []
+        self.carry()
+        self.blocks = self.sent + self.pairs
         self.slots = round_up(self.low + 2 * self.pairs, 8)
         self.degrees = round_up(MODES, 16)
         self.first_natural = self.rows - MODES + self.low
@@ -71,6 +82,38 @@
             order, mate = self.low + pair, self.partner - self.low - pair
             orders += [order if order <= mate else -1, mate if order < mate else -1]
         self.orders = np.array(orders + [-1] * (self.slots - len(orders)))
+
+    def band(self, part):
+        latitudes = np.arange(part * self.local, (part + 1) * self.local)
+        return latitudes[::-1] if 2 * part < self.parts else latitudes
+
+    def carry(self):
+        plain = to_bf16(legendre_table()[0]).astype(np.float32)
+        live = np.zeros(self.low, int)
+        for part in range(self.parts):
+            used = np.abs(plain[: self.low][:, :, self.band(part)]).max(axis=1) > 0
+            for order in range(self.low):
+                live[order] = max(live[order], *(1 + np.flatnonzero(used[order])), 1)
+        sent = self.low - MOVED
+        places = []
+        for row in range(self.rows - 1, self.rows - TAIL - 1, -1):
+            free = live[: max(sent, 0)] <= row
+            first = int(np.flatnonzero(~free)[-1]) + 1 if (~free).any() else 0
+            if first < sent:
+                places.append((row, first, sent - first))
+        runs = []
+        for which in range(MOVED):
+            done = 0
+            while sent > 0 and done < live[sent + which] and places:
+                row, first, count = places.pop(0)
+                taken = min(count, live[sent + which] - done)
+                runs.append((which, int(done), row, first, int(taken)))
+                done += taken
+                if taken < count:
+                    places.insert(0, (row, int(first + taken), int(count - taken)))
+            if sent <= 0 or done < live[sent + which]:
+                return
+        self.sent, self.runs = sent, runs
 
 
 def fourier_constants(layout):
@@ -93,7 +136,7 @@
     pair_fwd = np.zeros((parts, pairs, rows, 2 * rows))
     pair_back = np.zeros((parts, pairs, rows, 2 * rows))
     for part in range(parts):
-        own = slice(part * local, (part + 1) * local)
+        own = layout.band(part)
         start = part * rows
         synth_low[:low, start : start + local, :MODES] = np.swapaxes(plain[:low, :, own], 1, 2)
         for turn in (1, 2):
@@ -105,10 +148,10 @@
             for target, table in ((pair_fwd, weighted), (pair_back, plain)):
                 if order <= mate:
                     count = MODES - order
-                    target[part, pair, rows - count :, :local] = table[order, order:, own]
+                    target[part, pair, rows - count :, :local] = table[order][order:, own]
                 if order < mate:
                     count = MODES - mate
-                    target[part, pair, :count, rows : rows + local] = table[mate, mate:, own][::-1]
+                    target[part, pair, :count, rows : rows + local] = table[mate][mate:, own][::-1]
     pair_synth = np.swapaxes(pair_back, -1, -2)
     place = np.zeros((degrees, 2 * rows))
     for row in range(rows):
@@ -168,23 +211,33 @@
     return jnp.concatenate(rows, axis=0)
 
 
-def scatter_rows(layout, values, scratch, quad, group):
+def row_of(layout, turned, group, place):
+    latitude = group * PAIRS + place
+    row = layout.local - 1 - latitude
+    if not isinstance(turned, bool):
+        row = jnp.where(turned, row, latitude) if latitude < layout.local else latitude
+    elif not turned:
+        row = latitude
+    return layout.base + row
+
+
+def scatter_rows(layout, turned, values, scratch, quad, group):
     slots = values.shape[0] // 2
     for which in range(2):
         columns = slice(which * LANES, (which + 1) * LANES)
         upper, lower = interleave(values[:slots, columns], values[slots:, columns])
-        latitude = group * PAIRS + 2 * quad + which
-        scratch[pl.ds(latitude, slots, stride=layout.pitch), :] = upper
-        scratch[pl.ds(latitude + layout.half, slots, stride=layout.pitch), :] = lower
-
-
-def gather_rows(layout, scratch, quad, group):
+        place = 2 * quad + which
+        scratch[pl.ds(row_of(layout, turned, group, place), slots, stride=layout.pitch), :] = upper
+        scratch[pl.ds(row_of(layout, turned, group, place + layout.half), slots, stride=layout.pitch), :] = lower
+
+
+def gather_rows(layout, turned, scratch, quad, group):
     slots = layout.slots
     cosine, sine = [], []
     for which in range(2):
-        latitude = group * PAIRS + 2 * quad + which
-        upper = scratch[pl.ds(latitude, slots, stride=layout.pitch), :]
-        lower = scratch[pl.ds(latitude + layout.half, slots, stride=layout.pitch), :]
+        place = 2 * quad + which
+        upper = scratch[pl.ds(row_of(layout, turned, group, place), slots, stride=layout.pitch), :]
+        lower = scratch[pl.ds(row_of(layout, turned, group, place + layout.half), slots, stride=layout.pitch), :]
         first, second = interleave(upper, lower)
         cosine.append(first.astype(jnp.bfloat16))
         sine.append(second.astype(jnp.bfloat16))
@@ -196,7 +249,7 @@
 def order_rows(layout, scratch, first, count):
     parts = []
     for order in range(count):
-        start = pl.multiple_of((first + order) * layout.pitch, 8)
+        start = pl.multiple_of((first + order) * layout.pitch + layout.base, 8)
         parts.append(scratch[pl.ds(start, layout.rows), :])
     return jnp.concatenate(parts, axis=0).astype(jnp.bfloat16)
 
@@ -236,6 +289,7 @@
         shape = (layout.rows - layout.local,) + buffer.shape[1:]
         buffer[layout.local :] = jnp.zeros(shape, buffer.dtype)
     basis_copy.wait()
+    turned = 2 * index[0] < layout.parts
     for group, started in enumerate(copies):
         for copy in started:
             copy.wait()
@@ -247,7 +301,7 @@
                 latitude = group * PAIRS + 2 * quad + which
                 rows += [buffer[latitude], buffer[latitude + layout.half]]
             grid = jnp.concatenate(rows, axis=0)
-            scatter_rows(layout, dot(basis[...], grid, (1, 1)), scratch, quad, group)
+            scatter_rows(layout, turned, dot(basis[...], grid, (1, 1)), scratch, quad, group)
 
     def low_block(order, carry):
         stage[order] = order_rows(layout, scratch, order, 1)
@@ -255,7 +309,7 @@
 
     def pair_block(pair, carry):
         values = order_rows(layout, scratch, layout.low + 2 * pair, 2)
-        stage[layout.low + pair] = dot(pair_fwd[pair], values).astype(jnp.bfloat16)
+        stage[layout.sent + pair] = dot(pair_fwd[pair], values).astype(jnp.bfloat16)
         return carry
 
     flushes = []
@@ -271,13 +325,16 @@
         )
         flushes[-1].start()
 
-    middle = layout.low // 2
-    for first, last in ((0, middle), (middle, layout.low)):
+    for which, start, row, first, count in layout.runs:
+        moved = scratch[pl.ds((layout.sent + which) * layout.pitch + layout.base + start, count), :]
+        scratch[pl.ds(first * layout.pitch + layout.base + row, count, stride=layout.pitch), :] = moved
+    middle = layout.sent // 2
+    for first, last in ((0, middle), (middle, layout.sent)):
         lax.fori_loop(first, last, low_block, 0, unroll=8)
         flush(first, last)
     tables.wait()
     lax.fori_loop(0, layout.pairs, pair_block, 0, unroll=8)
-    flush(layout.low, layout.blocks)
+    flush(layout.sent, layout.blocks)
     for copy in flushes:
         copy.wait()
 
@@ -296,16 +353,41 @@
     low_orders(layout, refs[: layout.parts], *refs[layout.parts :])
 
 
-def low_orders(layout, held, analysis, synth_low, real_ref, imag_ref, grid_low, spec_low, swap_low):
-    degrees = layout.degrees
+def low_orders(
+    layout, held, analysis, synth_low, real_ref, imag_ref, grid_low, spec_low, swap_low, tails, moved
+):
+    degrees, rows = layout.degrees, layout.rows
+    if layout.runs:
+        moved[...] = jnp.zeros_like(moved)
+    for at, ref in enumerate(held):
+        if layout.runs:
+
+            def tail_block(order, carry):
+                values = ref[order, rows - 16 :, :].astype(jnp.float32)
+                tails[pl.ds(pl.multiple_of(order * TAIL, TAIL), TAIL), :] = values[16 - TAIL :]
+                return carry
+
+            lax.fori_loop(0, layout.sent, tail_block, 0, unroll=10)
+        for which, start, row, first, count in layout.runs:
+            begin = (at * MOVED + which) * rows + start
+            source = pl.ds(first * TAIL + row - (rows - TAIL), count, stride=TAIL)
+            moved[pl.ds(begin, count), :] = tails[source, :]
+
+    def coefficients(order):
+        if isinstance(order, int) and order >= layout.sent:
+            which = min(order, layout.low - 1) - layout.sent
+            starts = [(at * MOVED + which) * rows for at in range(layout.parts)]
+            return jnp.concatenate([moved[start : start + rows, :] for start in starts], axis=0).astype(jnp.bfloat16)
+        return jnp.concatenate([ref[order] for ref in held], axis=0)
+
     for start, stop, top in order_groups(layout):
         real_rows = real_ref[top:degrees, :]
         imag_rows = imag_ref[top:degrees, :]
 
         def low_block(two, carry):
-            values = []
-            for order in (2 * two, jnp.minimum(2 * two + 1, layout.low - 1)):
-                values.append(jnp.concatenate([ref[order] for ref in held], axis=0))
+            last = layout.low - 1
+            second = min(2 * two + 1, last) if isinstance(two, int) else jnp.minimum(2 * two + 1, last)
+            values = [coefficients(2 * two), coefficients(second)]
             spectral = dot_two(analysis[two, top:degrees, :], *values).astype(jnp.bfloat16)
             for which in range(2):
                 spec_low[2 * two + which, top:degrees, :] = spectral[:, which * LANES : (which + 1) * LANES]
@@ -323,19 +405,22 @@
                 mixed.append(values)
             values = dot_two(synth_low[two], *mixed)
             for which in range(2):
-                begin = pl.multiple_of((2 * two + which) * layout.pitch, 8)
+                begin = pl.multiple_of((2 * two + which) * layout.pitch + layout.base, 8)
                 grid_low[pl.ds(begin, layout.rows), :] = values[:, which * LANES : (which + 1) * LANES]
             return carry
 
-        lax.fori_loop(start, stop, low_block, 0, unroll=8)
+        whole_twos = max(min(stop, layout.sent // 2 if layout.runs else stop), start)
+        lax.fori_loop(start, whole_twos, low_block, 0, unroll=8)
+        for two in range(whole_twos, stop):
+            low_block(two, 0)
         lax.fori_loop(start, stop, mix_block, 0, unroll=8)
 
 
 def spectral_kernel(layout, apart, side, *refs):
     held, lows, refs = refs[: layout.parts], refs[layout.parts : layout.parts + 2 + apart], refs[layout.parts + 2 + apart :]
     north, south, basis, back_low, pair_synth, pair_back, place, real_ref, imag_ref = refs[:9]
-    keep, send, scratch, returned, spec_low, swap_low, spec_pair, swap_pair, sems = refs[9:]
-    offset = 0 if apart else layout.low
+    keep, send, scratch, returned, spec_low, swap_low, spec_pair, swap_pair, tails, moved, sems = refs[9:]
+    offset = 0 if apart else layout.sent
     group = pl.program_id(0)
     rows, degrees, low = layout.rows, layout.degrees, layout.low
     if apart:
@@ -349,7 +434,7 @@
             for copy in copies:
                 copy.start()
         else:
-            low_orders(layout, held, *lows, real_ref, imag_ref, scratch, spec_low, swap_low)
+            low_orders(layout, held, *lows, real_ref, imag_ref, scratch, spec_low, swap_low, tails, moved)
         line = lax.broadcasted_iota(jnp.int32, (rows, LANES), 0)
 
         def pair_block(two, carry):
@@ -367,7 +452,7 @@
                 mixed.append(mix(spectral, swapped, real_rows, imag_rows))
             values = dot_two(pair_synth[two], *mixed)
             for which in range(4):
-                begin = pl.multiple_of((low + 4 * two + which) * layout.pitch, 8)
+                begin = pl.multiple_of((low + 4 * two + which) * layout.pitch + layout.base, 8)
                 columns = slice(which // 2 * LANES, (which // 2 + 1) * LANES)
                 scratch[pl.ds(begin, rows), :] = values[which % 2 * rows : (which % 2 + 1) * rows, columns]
             return carry
@@ -378,15 +463,21 @@
             scratch[used : layout.slots * layout.pitch, :] = jnp.zeros(
                 (layout.slots * layout.pitch - used, LANES), jnp.float32
             )
+        for row in range(layout.base + layout.local, layout.pitch):
+            returned[pl.ds(row, layout.slots, stride=layout.pitch), :] = jnp.zeros((layout.slots, LANES), jnp.float32)
         if apart:
             copies[0].wait()
 
-    for quad in range(PAIRS // 2):
-        modes = gather_rows(layout, scratch, quad, group)
-        signal = dot(modes, basis[...], (0, 0))
-        incoming = grid_rows(layout, north, south, quad, group).astype(jnp.float32)
-        upstream = (incoming * gelu_slope(signal)).astype(jnp.bfloat16)
-        scatter_rows(layout, dot(basis[...], upstream, (1, 1)), returned, quad, group)
+    def grid_step(turned):
+        for quad in range(PAIRS // 2):
+            modes = gather_rows(layout, turned, scratch, quad, group)
+            signal = dot(modes, basis[...], (0, 0))
+            incoming = grid_rows(layout, north, south, quad, group).astype(jnp.float32)
+            upstream = (incoming * gelu_slope(signal)).astype(jnp.bfloat16)
+            scatter_rows(layout, turned, dot(basis[...], upstream, (1, 1)), returned, quad, group)
+
+    pl.when(2 * side[1] < layout.parts)(functools.partial(grid_step, True))
+    pl.when(2 * side[1] >= layout.parts)(functools.partial(grid_step, False))
 
     @pl.when(group == pl.num_programs(0) - 1)
     def _():
@@ -512,6 +603,10 @@
         in_specs=[whole()] * len(operands),
         out_specs=[whole()] * 3,
         out_shape=[jax.ShapeDtypeStruct((2 * layout.twos * layout.pitch, LANES), jnp.float32), spectra, spectra],
+        scratch_shapes=[
+            pltpu.VMEM((layout.sent * TAIL, LANES), jnp.float32),
+            pltpu.VMEM((layout.parts * MOVED * layout.rows, LANES), jnp.float32),
+        ],
         compiler_params=pltpu.CompilerParams(vmem_limit_bytes=VMEM),
         cost_estimate=pl.CostEstimate(flops=8_000_000_000, bytes_accessed=30_000_000, transcendentals=0),
         name=f"low_{chunk}",
@@ -537,6 +632,8 @@
             pltpu.VMEM((2 * layout.twos, layout.degrees, LANES), jnp.bfloat16),
             pltpu.VMEM((layout.pairs, layout.rows, LANES), jnp.bfloat16),
             pltpu.VMEM((layout.pairs, layout.rows, LANES), jnp.bfloat16),
+            pltpu.VMEM((layout.sent * TAIL, LANES), jnp.float32),
+            pltpu.VMEM((layout.parts * MOVED * layout.rows, LANES), jnp.float32),
             pltpu.SemaphoreType.DMA((3,)),
         ],
         compiler_params=pltpu.CompilerParams(vmem_limit_bytes=VMEM),
@@ -627,7 +724,7 @@
     for chunk in range(chunks):
         if chunk == 1:
             place, low_tables, tables = lax.optimization_barrier((place, low_tables, tables))
-        bounds = (0, layout.blocks) if chunk < chunks - 1 else (0, layout.low, layout.blocks)
+        bounds = (0, layout.blocks) if chunk < chunks - 1 else (0, layout.sent, layout.blocks)
         made = forward_call(layout, chunk, bounds, place, fields, pair_fwd)
         place, made = lax.optimization_barrier((place, list(made)))
         if len(made) > 1 and held:
@@ -637,7 +734,7 @@
     hops = sum_steps("dp") + sum_steps("space")
     count_dp = len(sum_steps("dp"))
     swap = [(device, device ^ 1) for device in range(lax.axis_size("dp"))]
-    side = lax.rem(lax.axis_index("dp"), 2).reshape((1,)).astype(jnp.int32)
+    side = jnp.stack([lax.rem(lax.axis_index("dp"), 2), index]).astype(jnp.int32)
     waiting = []
 
     def launch(value, done):

time: 141 us -> 139 us (0.986)
  Pallas kernels: 50.5 us -> 57.3 us
  waiting for transfers between devices: 32.5 us -> 26.9 us
  starting transfers between devices: 25.7 us -> 24.1 us
    ppermute x4, waiting for transfers between devices: 19.1 us -> 11.8 us  [others(): return [lax.ppermute(sent, 'space', route) for route in routes]]
    pallas_call x3, Pallas kernels: 31.1 us -> 36.7 us  [spectral_call(): pl.pallas_call(functools.partial(spectral_kernel, layout, apart), grid=(l...]
    ppermute x9, waiting for transfers between devices: 9.72 us -> 11.3 us  [hop_parcels(): parcels.append(lax.ppermute(value, axis, pairs))]
    unnamed x32 -> x38, local copies, waits for them, and re-layouts: 8.67 us -> 8.68 us
  transfers between devices with their start and end apart: 17 -> 17, of which waited for: 12 -> 12; matrix products, arithmetic and copies ran while one was open for 16% -> 15% of each run, Pallas kernels for 32% -> 37%
where the time goes in v9:
time: 139 us
  Pallas kernels  57.3 us (41%)
  waiting for transfers between devices  26.9 us (19%)
  local copies, waits for them, and re-layouts  24.9 us (18%)
  starting transfers between devices  24.1 us (17%)
  other arithmetic  4.57 us (3%)
    pallas_call x3, Pallas kernels, spectral_call(): pl.pallas_call(functools.partial(spectral_kernel, layout, apart), grid=(l...  36.7 us
    ppermute x9, starting transfers between devices, hop_parcels(): parcels.append(lax.ppermute(value, axis, pairs))  17.8 us
    pallas_call x3, Pallas kernels, forward_call(): pl.pallas_call(functools.partial(forward_kernel, layout, chunk, bounds),...  16.1 us
    ppermute x4, waiting for transfers between devices, others(): return [lax.ppermute(sent, 'space', route) for route in routes]  11.8 us
    ppermute x9, waiting for transfers between devices, hop_parcels(): parcels.append(lax.ppermute(value, axis, pairs))  11.3 us
    unnamed x38, local copies, waits for them, and re-layouts  8.68 us
    ppermute x4, starting transfers between devices, others(): return [lax.ppermute(sent, 'space', route) for route in routes]  5.99 us
    dynamic_slice x2, local copies, waits for them, and re-layouts, bands(): lax.dynamic_slice_in_dim(table, first * layout.rows, count * layout.rows, 1)  4.46 us
  transfers between devices with their start and end apart: 17, of which 12 were waited for; matrix products, arithmetic and copies ran while one was open for 15% of the time, Pallas kernels for 37%

profile of v9, /device:TPU:0, one launch (start us, length us, event | category | flops | bytes accessed | tf_op | source)
XLA Modules:
  0.0 138.7 jit_solution(3231525698724399499)
XLA Ops:
  0.6 5.4 %forward_0.1.refs_0_ = bf16[92,64,128]{2,1,0:T(8,128)(2,1)} custom-call(s32[1]{0:T(128)} %bitcast.index, bf16[1,63,192,252]{3,2,1,0:T(8,128)(2,1)} %bitcast.30, bf16[256,252]{1,0:T(8,128)(2,1)} %constant.59.clone.basis_all, bf16[2,32,64,128]{3,2,1,0:T(8,128)(2,1)} %constant.53.clone.pair_all), custom_call_target="tpu_custom_call" | custom-call | flops 1000000 | bytes 100000 | tf_op jit(solution)/shard_map/forward_0/pallas_call | solution.py:576
  6.0 3.0 %collective-permute-start.1 = (bf16[92,64,128]{2,1,0:T(8,128)(2,1)}, bf16[92,64,128]{2,1,0:T(8,128)(2,1)}, u32[]{:S(2)}, u32[]{:S(2)}) collective-permute-start(bf16[92,64,128]{2,1,0:T(8,128)(2,1)} %forward_0.1.refs_0_), channel_id=1, source_target_pairs={{0,1},{1,0},{2,3},{3,2},{4,5},{5,4},{6,7},{7,6},{8,9},{9,8},{10,11... | collective-permute-start | bytes 4521992 | tf_op jit(solution)/shard_map/ppermute | solution.py:721
  9.1 3.4 %constant_dynamic-slice_fusion.1 = bf16[64,128,128]{2,1,0:T(8,128)(2,1)} fusion(bf16[64,256,128]{2,1,0:T(8,128)(2,1)} %constant.55.clone, s32[]{:T(128)S(6)} %select_n.25), kind=kLoop, calls=%fused_computation.26 | loop fusion | bytes 4194308 | tf_op jit(solution)/shard_map/dynamic_slice | solution.py:701
  12.4 1.1 constant_dynamic-slice_fusion
  13.5 1.9 %dynamic-slice_bitcast_fusion.1.refs_8_.refs_9_ = bf16[16,128,128]{2,1,0:T(8,128)(2,1)} fusion(bf16[2,16,128,128]{3,2,1,0:T(8,128)(2,1)} %constant.56.clone, s32[]{:T(128)S(6)} %select_n.27), kind=kLoop, calls=%fused_computation.2 | loop fusion | bytes 1048580 | tf_op jit(solution)/shard_map/jit(dynamic_index_in_dim)/squeeze | solution.py:694
  15.4 0.9 dynamic-slice_bitcast_fusion.refs_9_.refs_10_
  16.3 3.3 %copy.20 = bf16[32,256,128]{1,2,0:T(8,128)(2,1)S(1)} copy(bf16[32,256,128]{2,1,0:T(8,128)(2,1)} %bitcast.34) | data formatting | bytes 4194304 | tf_op jit(solution)/shard_map/reshape | solution.py:708
  19.6 1.6 %copy.21 = bf16[32,128,128]{1,2,0:T(8,128)(2,1)S(1)} copy(bf16[32,128,128]{2,1,0:T(8,128)(2,1)} %bitcast.33) | data formatting | bytes 2097152 | tf_op jit(solution)/shard_map/reshape | solution.py:710
  21.2 1.3 fusion.10
  22.5 1.1 pad_maximum_fusion.refs_3_
  23.6 5.3 %forward_1.1.refs_0_ = bf16[92,64,128]{2,1,0:T(8,128)(2,1)} custom-call(s32[1]{0:T(128)} %bitcast.index, bf16[1,63,192,252]{3,2,1,0:T(8,128)(2,1)} %bitcast.31, bf16[256,252]{1,0:T(8,128)(2,1)} %constant.59.clone.basis_all, bf16[2,32,64,128]{3,2,1,0:T(8,128)(2,1)} %constant.53.clone.pair_all), custom_call_target="tpu_custom_call" | custom-call | flops 1000000 | bytes 100000 | tf_op jit(solution)/shard_map/forward_1/pallas_call | solution.py:576
  29.0 0.0 copy-start.15
  29.0 0.1 collective-permute-start
  29.1 5.3 %forward_2.1 = (bf16[60,64,128]{2,1,0:T(8,128)(2,1)}, bf16[32,64,128]{2,1,0:T(8,128)(2,1)}) custom-call(s32[1]{0:T(128)} %bitcast.index, bf16[1,63,192,252]{3,2,1,0:T(8,128)(2,1)} %bitcast.32, bf16[256,252]{1,0:T(8,128)(2,1)} %constant.59.clone.basis_all, bf16[2,32,64,128]{3,2,1,0:T(8,128)(2,1)} %constant.53.clone.pair_all), custom_call_target="tpu_custom_call" | custom-call | flops 1000000 | bytes 100000 | tf_op jit(solution)/shard_map/forward_2/pallas_call | solution.py:576
  34.4 2.1 %collective-permute-start.7 = (bf16[60,64,128]{2,1,0:T(8,128)(2,1)}, bf16[60,64,128]{2,1,0:T(8,128)(2,1)}, u32[]{:S(2)}, u32[]{:S(2)}) collective-permute-start(bf16[60,64,128]{2,1,0:T(8,128)(2,1)} %get-tuple-element.86.refs_0_), channel_id=1, source_target_pairs={{0,1},{1,0},{2,3},{3,2},{4,5},{5,4},{6,7},{7,6},{8,9},{9,8},{10,11... | collective-permute-start | bytes 2949128 | tf_op jit(solution)/shard_map/ppermute | solution.py:721
  36.5 0.1 copy.22
  36.6 0.1 rev.6
  36.7 0.0 copy-start.11
  36.8 0.0 copy-start.12
  36.8 0.7 fusion.11
  37.5 0.1 pad_add_fusion.side
  37.6 0.9 copy.24
  38.5 0.6 slice.54
  39.2 1.4 rev.7
  40.5 0.9 fusion.7
  41.5 1.2 pad_maximum_fusion.1
  42.7 0.1 slice_negate_fusion
  42.8 0.1 pad_maximum_fusion.2
  43.0 0.2 collective-permute-done.1.refs_1_
  43.2 1.0 copy-done.3
  44.3 1.0 copy-done.5
  45.3 2.8 %copy-done.7 = bf16[1,63,252,192]{2,3,1,0:T(8,128)(2,1)S(1)} copy-done((bf16[1,63,252,192]{2,3,1,0:T(8,128)(2,1)S(1)}, bf16[1,63,252,192]{2,3,1,0:T(8,128)(2,1)}, u32[]{:S(2)}) %copy-start.7) | copy-done | bytes 6096408
  48.1 13.3 %spectral_0.1 = (f32[64,128]{1,0:T(8,128)S(1)}, f32[64,128]{1,0:T(8,128)S(1)}) custom-call(s32[2]{0:T(128)S(1)} %pad_add_fusion.side, bf16[92,64,128]{2,1,0:T(8,128)(2,1)S(1)} %copy-done, bf16[92,64,128]{2,1,0:T(8,128)(2,1)} %collective-permute-done.1.refs_1_, bf16[32,128,256]{2,1,0:T(8,128)(2,1)S(1)} %bitcast.16, bf16[32,64,256]{2,1,0:T(8,128)(2,1)S(1)} %copy-done.2, ...), custom_call_target="tpu_custom_call" | custom-call | flops 8000000000 | bytes 30000000 | tf_op jit(solution)/shard_map/spectral_0/pallas_call | solution.py:622
  61.3 0.1 collective-permute-start.2
  61.4 1.2 collective-permute-done.2
  62.6 2.0 %collective-permute-start.3 = (f32[64,128]{1,0:T(8,128)S(1)}, f32[64,128]{1,0:T(8,128)S(1)}, u32[]{:S(2)}, u32[]{:S(2)}) collective-permute-start(f32[64,128]{1,0:T(8,128)S(1)} %add.55), channel_id=1, source_target_pairs={{0,4},{2,6},{4,0},{6,2},{8,12},{10,14},{12,8},{14,10},{16,20},{18,... | collective-permute-start | bytes 98312 | tf_op jit(solution)/shard_map/ppermute | solution.py:672
  64.7 0.1 pad_maximum_fusion.5
  64.8 0.8 collective-permute-start.9
  65.6 1.0 collective-permute-done.3
  66.5 8.9 %collective-permute-done.refs_1_ = bf16[92,64,128]{2,1,0:T(8,128)(2,1)} collective-permute-done((bf16[92,64,128]{2,1,0:T(8,128)(2,1)}, bf16[92,64,128]{2,1,0:T(8,128)(2,1)}, u32[]{:S(2)}, u32[]{:S(2)}) %collective-permute-start) | collective-permute-done | bytes 1507360 | tf_op jit(solution)/shard_map/ppermute | solution.py:721
  75.5 2.1 %collective-permute-start.4 = (f32[64,128]{1,0:T(8,128)S(1)}, f32[64,128]{1,0:T(8,128)S(1)}, u32[]{:S(2)}, u32[]{:S(2)}) collective-permute-start(f32[64,128]{1,0:T(8,128)S(1)} %add.56), channel_id=1, source_target_pairs={{0,8},{2,10},{4,12},{6,14},{8,0},{10,2},{12,4},{14,6},{16,24},{18,... | collective-permute-start | bytes 98312 | tf_op jit(solution)/shard_map/ppermute | solution.py:672
  77.6 2.8 %copy-done.8 = bf16[1,63,252,192]{2,3,1,0:T(8,128)(2,1)S(1)} copy-done((bf16[1,63,252,192]{2,3,1,0:T(8,128)(2,1)S(1)}, bf16[1,63,252,192]{2,3,1,0:T(8,128)(2,1)}, u32[]{:S(2)}) %copy-start.8) | copy-done | bytes 6096408
  80.4 13.3 %spectral_1.1 = (f32[64,128]{1,0:T(8,128)S(1)}, f32[64,128]{1,0:T(8,128)S(1)}) custom-call(s32[2]{0:T(128)S(1)} %pad_add_fusion.side, bf16[92,64,128]{2,1,0:T(8,128)(2,1)S(1)} %copy-done.1, bf16[92,64,128]{2,1,0:T(8,128)(2,1)} %collective-permute-done.refs_1_, bf16[32,128,256]{2,1,0:T(8,128)(2,1)S(1)} %bitcast.17, bf16[32,64,256]{2,1,0:T(8,128)(2,1)S(1)} %copy-done.2, ...), custom_call_target="tpu_custom_call" | custom-call | flops 8000000000 | bytes 30000000 | tf_op jit(solution)/shard_map/spectral_1/pallas_call | solution.py:622
  93.7 0.1 collective-permute-start.5
  93.8 2.6 %collective-permute-start.6 = (f32[64,128]{1,0:T(8,128)S(1)}, f32[64,128]{1,0:T(8,128)S(1)}, u32[]{:S(2)}, u32[]{:S(2)}) collective-permute-start(f32[64,128]{1,0:T(8,128)S(1)} %add.57), channel_id=1, source_target_pairs={{0,16},{2,18},{4,20},{6,22},{8,24},{10,26},{12,28},{14,30},{16,0},... | collective-permute-start | bytes 98312 | tf_op jit(solution)/shard_map/ppermute | solution.py:672
  96.4 0.1 collective-permute-done.7.refs_1_
  96.6 4.5 %low_2.1 = (f32[4608,128]{1,0:T(8,128)S(1)}, bf16[64,128,128]{2,1,0:T(8,128)(2,1)S(1)}, bf16[64,128,128]{2,1,0:T(8,128)(2,1)S(1)}) custom-call(bf16[60,64,128]{2,1,0:T(8,128)(2,1)S(1)} %copy-done.9, bf16[60,64,128]{2,1,0:T(8,128)(2,1)} %collective-permute-done.7.refs_1_, bf16[32,128,256]{2,1,0:T(8,128)(2,1)S(1)} %bitcast.18, ...), custom_call_target="tpu_custom_call" | custom-call | flops 8000000000 | bytes 30000000 | tf_op jit(solution)/shard_map/low_2/pallas_call | solution.py:601
  101.1 2.1 %collective-permute-start.8 = (f32[64,128]{1,0:T(8,128)S(1)}, f32[64,128]{1,0:T(8,128)S(1)}, u32[]{:S(2)}, u32[]{:S(2)}) collective-permute-start(f32[64,128]{1,0:T(8,128)S(1)} %add.58), channel_id=1, source_target_pairs={{0,1},{1,0},{2,3},{3,2},{4,5},{5,4},{6,7},{7,6},{8,9},{9,8},{10,11... | collective-permute-start | bytes 98312 | tf_op jit(solution)/shard_map/ppermute | solution.py:672
  103.2 1.5 %collective-permute-start.10 = (f32[64,128]{1,0:T(8,128)S(1)}, f32[64,128]{1,0:T(8,128)S(1)}, u32[]{:S(2)}, u32[]{:S(2)}) collective-permute-start(f32[64,128]{1,0:T(8,128)S(1)} %add.59), channel_id=1, source_target_pairs={{0,4},{2,6},{4,0},{6,2},{8,12},{10,14},{12,8},{14,10},{16,20},{18,... | collective-permute-start | bytes 98312 | tf_op jit(solution)/shard_map/ppermute | solution.py:672
  104.7 2.5 %collective-permute-done.9.refs_1_ = bf16[32,64,128]{2,1,0:T(8,128)(2,1)S(1)} collective-permute-done((bf16[32,64,128]{2,1,0:T(8,128)(2,1)S(1)}, bf16[32,64,128]{2,1,0:T(8,128)(2,1)S(1)}, u32[]{:S(2)}, u32[]{:S(2)}) %collective-permute-start.9) | collective-permute-done | bytes 524320 | tf_op jit(solution)/shard_map/ppermute | solution.py:721
  107.2 10.2 %spectral_2.1 = (f32[64,128]{1,0:T(8,128)S(1)}, f32[64,128]{1,0:T(8,128)S(1)}) custom-call(s32[2]{0:T(128)S(1)} %pad_add_fusion.side, bf16[32,64,128]{2,1,0:T(8,128)(2,1)S(1)} %copy-done.10, bf16[32,64,128]{2,1,0:T(8,128)(2,1)S(1)} %collective-permute-done.9.refs_1_, f32[4608,128]{1,0:T(8,128)S(1)} %get-tuple-element.102.refs_2_, ...), custom_call_target="tpu_custom_call" | custom-call | flops 8000000000 | bytes 30000000 | tf_op jit(solution)/shard_map/spectral_2/pallas_call | solution.py:622
  117.4 0.1 collective-permute-start.11
  117.5 1.2 collective-permute-done.11
  118.7 1.7 %collective-permute-start.12 = (f32[64,128]{1,0:T(8,128)S(1)}, f32[64,128]{1,0:T(8,128)S(1)}, u32[]{:S(2)}, u32[]{:S(2)}) collective-permute-start(f32[64,128]{1,0:T(8,128)S(1)} %add.62), channel_id=1, source_target_pairs={{0,4},{2,6},{4,0},{6,2},{8,12},{10,14},{12,8},{14,10},{16,20},{18,... | collective-permute-start | bytes 98312 | tf_op jit(solution)/shard_map/ppermute | solution.py:672
  120.4 2.2 %collective-permute-done.12 = f32[64,128]{1,0:T(8,128)S(1)} collective-permute-done((f32[64,128]{1,0:T(8,128)S(1)}, f32[64,128]{1,0:T(8,128)S(1)}, u32[]{:S(2)}, u32[]{:S(2)}) %collective-permute-start.12) | collective-permute-done | bytes 32800 | tf_op jit(solution)/shard_map/ppermute | solution.py:672
  122.6 1.9 %collective-permute-start.13 = (f32[128,128]{1,0:T(8,128)S(1)}, f32[128,128]{1,0:T(8,128)S(1)}, u32[]{:S(2)}, u32[]{:S(2)}) collective-permute-start(f32[128,128]{1,0:T(8,128)S(1)} %pad_maximum_fusion.8), channel_id=1, source_target_pairs={{0,8},{2,10},{4,12},{6,14},{8,0},{10,2},{12,4},{14,6},{16,24},{18,... | collective-permute-start | bytes 196616 | tf_op jit(solution)/shard_map/ppermute | solution.py:672
  124.5 2.5 %collective-permute-done.13 = f32[128,128]{1,0:T(8,128)S(1)} collective-permute-done((f32[128,128]{1,0:T(8,128)S(1)}, f32[128,128]{1,0:T(8,128)S(1)}, u32[]{:S(2)}, u32[]{:S(2)}) %collective-permute-start.13) | collective-permute-done | bytes 65568 | tf_op jit(solution)/shard_map/ppermute | solution.py:672
  127.0 2.9 %collective-permute-start.14 = (f32[128,128]{1,0:T(8,128)S(1)}, f32[128,128]{1,0:T(8,128)S(1)}, u32[]{:S(2)}, u32[]{:S(2)}) collective-permute-start(f32[128,128]{1,0:T(8,128)S(1)} %fusion.9), channel_id=1, source_target_pairs={{0,16},{2,18},{4,20},{6,22},{8,24},{10,26},{12,28},{14,30},{16,0},... | collective-permute-start | bytes 196616 | tf_op jit(solution)/shard_map/ppermute | solution.py:672
  129.9 2.4 %collective-permute-done.14 = f32[128,128]{1,0:T(8,128)S(1)} collective-permute-done((f32[128,128]{1,0:T(8,128)S(1)}, f32[128,128]{1,0:T(8,128)S(1)}, u32[]{:S(2)}, u32[]{:S(2)}) %collective-permute-start.14) | collective-permute-done | bytes 65568 | tf_op jit(solution)/shard_map/ppermute | solution.py:672
  132.2 1.0 collective-permute-start.15
  133.2 3.3 %collective-permute-done.15 = f32[128,128]{1,0:T(8,128)S(1)} collective-permute-done((f32[128,128]{1,0:T(8,128)S(1)}, f32[128,128]{1,0:T(8,128)S(1)}, u32[]{:S(2)}, u32[]{:S(2)}) %collective-permute-start.15) | collective-permute-done | bytes 65568 | tf_op jit(solution)/shard_map/ppermute | solution.py:672
  136.6 0.1 collective-permute-start.16
  136.7 1.3 collective-permute-done.16
  138.0 0.7 multiply_bitcast_fusion
  (51 shorter events, 0.2 us)
Async XLA Ops:
  6.0 37.2 %collective-permute-start.1 = (bf16[92,64,128]{2,1,0:T(8,128)(2,1)}, bf16[92,64,128]{2,1,0:T(8,128)(2,1)}, u32[]{:S(2)}, u32[]{:S(2)}) collective-permute-start(bf16[92,64,128]{2,1,0:T(8,128)(2,1)} %forward_0.1.refs_0_), channel_id=1, source_target_pairs={{0,1},{1,0},{2,3},{3,2},{4,5},{5,4},{6,7},{7,6},{8,9},{9,8},{10,11... | collective-permute-start | bytes 4521992 | tf_op jit(solution)/shard_map/ppermute | solution.py:721
  9.1 3.4 %copy-start.13 = (bf16[64,128,128]{2,1,0:T(8,128)(2,1)S(1)}, bf16[64,128,128]{2,1,0:T(8,128)(2,1)}, u32[]{:S(2)}) copy-start(bf16[64,128,128]{2,1,0:T(8,128)(2,1)} %constant.54.clone) | copy-start | bytes 6291460
  12.4 3.0 %copy-start.14 = (bf16[2,16,64,256]{3,2,1,0:T(8,128)(2,1)S(1)}, bf16[2,16,64,256]{3,2,1,0:T(8,128)(2,1)}, u32[]{:S(2)}) copy-start(bf16[2,16,64,256]{3,2,1,0:T(8,128)(2,1)} %constant.57.clone) | copy-start | bytes 3145732
  29.0 7.5 %copy-start.15 = (bf16[126,192]{0,1:T(8,128)(2,1)S(1)}, bf16[126,192]{0,1:T(8,128)(2,1)}, u32[]{:S(2)}) copy-start(bf16[126,192]{0,1:T(8,128)(2,1)} %param.16) | copy-start | bytes 145156
  29.0 46.5 %collective-permute-start = (bf16[92,64,128]{2,1,0:T(8,128)(2,1)}, bf16[92,64,128]{2,1,0:T(8,128)(2,1)}, u32[]{:S(2)}, u32[]{:S(2)}) collective-permute-start(bf16[92,64,128]{2,1,0:T(8,128)(2,1)} %forward_1.1.refs_0_), channel_id=1, source_target_pairs={{0,1},{1,0},{2,3},{3,2},{4,5},{5,4},{6,7},{7,6},{8,9},{9,8},{10,11... | collective-permute-start | bytes 4521992 | tf_op jit(solution)/shard_map/ppermute | solution.py:721
  34.4 62.1 %collective-permute-start.7 = (bf16[60,64,128]{2,1,0:T(8,128)(2,1)}, bf16[60,64,128]{2,1,0:T(8,128)(2,1)}, u32[]{:S(2)}, u32[]{:S(2)}) collective-permute-start(bf16[60,64,128]{2,1,0:T(8,128)(2,1)} %get-tuple-element.86.refs_0_), channel_id=1, source_target_pairs={{0,1},{1,0},{2,3},{3,2},{4,5},{5,4},{6,7},{7,6},{8,9},{9,8},{10,11... | collective-permute-start | bytes 2949128 | tf_op jit(solution)/shard_map/ppermute | solution.py:721
  36.7 6.5 %copy-start.11 = (bf16[256,252]{1,0:T(8,128)(2,1)S(1)}, bf16[256,252]{1,0:T(8,128)(2,1)}, u32[]{:S(2)}) copy-start(bf16[256,252]{1,0:T(8,128)(2,1)} %constant.52.clone.refs_6_.refs_7_) | copy-start | bytes 387076
  36.8 6.4 %copy-start.12 = (f32[128,128]{1,0:T(8,128)S(1)}, f32[128,128]{1,0:T(8,128)}, u32[]{:S(2)}) copy-start(f32[128,128]{1,0:T(8,128)} %constant.58.clone.refs_10_.refs_11_) | copy-start | bytes 196612
  40.5 2.7 %copy-start = (bf16[92,64,128]{2,1,0:T(8,128)(2,1)S(1)}, bf16[92,64,128]{2,1,0:T(8,128)(2,1)}, u32[]{:S(2)}) copy-start(bf16[92,64,128]{2,1,0:T(8,128)(2,1)} %forward_0.1.refs_0_) | copy-start | bytes 4521988
  40.5 2.7 %copy-start.2 = (bf16[32,64,256]{2,1,0:T(8,128)(2,1)S(1)}, bf16[32,64,256]{2,1,0:T(8,128)(2,1)}, u32[]{:S(2)}) copy-start(bf16[32,64,256]{2,1,0:T(8,128)(2,1)} %pad_maximum_fusion.refs_3_) | copy-start | bytes 3145732
  43.2 1.0 copy-start.3
  44.3 1.0 copy-start.5
  45.3 2.8 %copy-start.7 = (bf16[1,63,252,192]{2,3,1,0:T(8,128)(2,1)S(1)}, bf16[1,63,252,192]{2,3,1,0:T(8,128)(2,1)}, u32[]{:S(2)}) copy-start(bf16[1,63,252,192]{2,3,1,0:T(8,128)(2,1)} %param.15) | copy-start | bytes 18289156
  48.1 16.7 %copy-start.10 = (bf16[32,64,128]{2,1,0:T(8,128)(2,1)S(1)}, bf16[32,64,128]{2,1,0:T(8,128)(2,1)}, u32[]{:S(2)}) copy-start(bf16[32,64,128]{2,1,0:T(8,128)(2,1)} %get-tuple-element.101.refs_0_) | copy-start | bytes 1572868
  48.1 29.5 %copy-start.1 = (bf16[92,64,128]{2,1,0:T(8,128)(2,1)S(1)}, bf16[92,64,128]{2,1,0:T(8,128)(2,1)}, u32[]{:S(2)}) copy-start(bf16[92,64,128]{2,1,0:T(8,128)(2,1)} %forward_1.1.refs_0_) | copy-start | bytes 4521988
  61.3 1.3 collective-permute-start.2
  62.6 3.9 %collective-permute-start.3 = (f32[64,128]{1,0:T(8,128)S(1)}, f32[64,128]{1,0:T(8,128)S(1)}, u32[]{:S(2)}, u32[]{:S(2)}) collective-permute-start(f32[64,128]{1,0:T(8,128)S(1)} %add.55), channel_id=1, source_target_pairs={{0,4},{2,6},{4,0},{6,2},{8,12},{10,14},{12,8},{14,10},{16,20},{18,... | collective-permute-start | bytes 98312 | tf_op jit(solution)/shard_map/ppermute | solution.py:672
  64.8 42.4 %collective-permute-start.9 = (bf16[32,64,128]{2,1,0:T(8,128)(2,1)S(1)}, bf16[32,64,128]{2,1,0:T(8,128)(2,1)S(1)}, u32[]{:S(2)}, u32[]{:S(2)}) collective-permute-start(bf16[32,64,128]{2,1,0:T(8,128)(2,1)S(1)} %copy-done.10), channel_id=1, source_target_pairs={{0,1},{1,0},{2,3},{3,2},{4,5},{5,4},{6,7},{7,6},{8,9},{9,8},{10,11... | collective-permute-start | bytes 1572872 | tf_op jit(solution)/shard_map/ppermute | solution.py:721
  75.5 18.2 %collective-permute-start.4 = (f32[64,128]{1,0:T(8,128)S(1)}, f32[64,128]{1,0:T(8,128)S(1)}, u32[]{:S(2)}, u32[]{:S(2)}) collective-permute-start(f32[64,128]{1,0:T(8,128)S(1)} %add.56), channel_id=1, source_target_pairs={{0,8},{2,10},{4,12},{6,14},{8,0},{10,2},{12,4},{14,6},{16,24},{18,... | collective-permute-start | bytes 98312 | tf_op jit(solution)/shard_map/ppermute | solution.py:672
  77.6 2.8 %copy-start.8 = (bf16[1,63,252,192]{2,3,1,0:T(8,128)(2,1)S(1)}, bf16[1,63,252,192]{2,3,1,0:T(8,128)(2,1)}, u32[]{:S(2)}) copy-start(bf16[1,63,252,192]{2,3,1,0:T(8,128)(2,1)} %param.15) | copy-start | bytes 18289156
  80.4 16.2 %copy-start.9 = (bf16[60,64,128]{2,1,0:T(8,128)(2,1)S(1)}, bf16[60,64,128]{2,1,0:T(8,128)(2,1)}, u32[]{:S(2)}) copy-start(bf16[60,64,128]{2,1,0:T(8,128)(2,1)} %get-tuple-element.86.refs_0_) | copy-start | bytes 2949124
  80.4 26.8 %slice-start = ((s8[6193152]{0:T(1024)(128)(4,1)}), s8[4194304]{0:T(1024)(128)(4,1)S(1)}, s32[]{:S(2)}) async-start(s8[6193152]{0:T(1024)(128)(4,1)} %bitcast.26), calls=%async_computation | async-start | bytes 8388608
  93.7 7.4 %collective-permute-start.5 = (f32[64,128]{1,0:T(8,128)S(1)}, f32[64,128]{1,0:T(8,128)S(1)}, u32[]{:S(2)}, u32[]{:S(2)}) collective-permute-start(f32[64,128]{1,0:T(8,128)S(1)} %get-tuple-element.82), channel_id=1, source_target_pairs={{0,2},{2,0},{4,6},{6,4},{8,10},{10,8},{12,14},{14,12},{16,18},{18,... | collective-permute-start | bytes 98312 | tf_op jit(solution)/shard_map/ppermute | solution.py:744
  93.8 7.3 %collective-permute-start.6 = (f32[64,128]{1,0:T(8,128)S(1)}, f32[64,128]{1,0:T(8,128)S(1)}, u32[]{:S(2)}, u32[]{:S(2)}) collective-permute-start(f32[64,128]{1,0:T(8,128)S(1)} %add.57), channel_id=1, source_target_pairs={{0,16},{2,18},{4,20},{6,22},{8,24},{10,26},{12,28},{14,30},{16,0},... | collective-permute-start | bytes 98312 | tf_op jit(solution)/shard_map/ppermute | solution.py:672
  96.6 10.6 %copy-start.4 = (bf16[16,128,128]{2,1,0:T(8,128)(2,1)S(1)}, bf16[16,128,128]{2,1,0:T(8,128)(2,1)}, u32[]{:S(2)}) copy-start(bf16[16,128,128]{2,1,0:T(8,128)(2,1)} %dynamic-slice_bitcast_fusion.1.refs_8_.refs_9_) | copy-start | bytes 1572868
  96.6 10.6 %copy-start.6 = (bf16[16,64,256]{2,1,0:T(8,128)(2,1)S(1)}, bf16[16,64,256]{2,1,0:T(8,128)(2,1)}, u32[]{:S(2)}) copy-start(bf16[16,64,256]{2,1,0:T(8,128)(2,1)} %dynamic-slice_bitcast_fusion.refs_9_.refs_10_) | copy-start | bytes 1572868
  96.6 10.6 %slice-start.1 = ((s8[6193152]{0:T(1024)(128)(4,1)}), s8[1998848]{0:T(1024)(128)(4,1)S(1)}, s32[]{:S(2)}) async-start(s8[6193152]{0:T(1024)(128)(4,1)} %bitcast.26), calls=%async_computation.1 | async-start | bytes 3997696
  101.1 16.3 %collective-permute-start.8 = (f32[64,128]{1,0:T(8,128)S(1)}, f32[64,128]{1,0:T(8,128)S(1)}, u32[]{:S(2)}, u32[]{:S(2)}) collective-permute-start(f32[64,128]{1,0:T(8,128)S(1)} %add.58), channel_id=1, source_target_pairs={{0,1},{1,0},{2,3},{3,2},{4,5},{5,4},{6,7},{7,6},{8,9},{9,8},{10,11... | collective-permute-start | bytes 98312 | tf_op jit(solution)/shard_map/ppermute | solution.py:672
  103.2 14.2 %collective-permute-start.10 = (f32[64,128]{1,0:T(8,128)S(1)}, f32[64,128]{1,0:T(8,128)S(1)}, u32[]{:S(2)}, u32[]{:S(2)}) collective-permute-start(f32[64,128]{1,0:T(8,128)S(1)} %add.59), channel_id=1, source_target_pairs={{0,4},{2,6},{4,0},{6,2},{8,12},{10,14},{12,8},{14,10},{16,20},{18,... | collective-permute-start | bytes 98312 | tf_op jit(solution)/shard_map/ppermute | solution.py:672
  117.4 1.3 collective-permute-start.11
  118.7 3.9 %collective-permute-start.12 = (f32[64,128]{1,0:T(8,128)S(1)}, f32[64,128]{1,0:T(8,128)S(1)}, u32[]{:S(2)}, u32[]{:S(2)}) collective-permute-start(f32[64,128]{1,0:T(8,128)S(1)} %add.62), channel_id=1, source_target_pairs={{0,4},{2,6},{4,0},{6,2},{8,12},{10,14},{12,8},{14,10},{16,20},{18,... | collective-permute-start | bytes 98312 | tf_op jit(solution)/shard_map/ppermute | solution.py:672
  122.6 4.3 %collective-permute-start.13 = (f32[128,128]{1,0:T(8,128)S(1)}, f32[128,128]{1,0:T(8,128)S(1)}, u32[]{:S(2)}, u32[]{:S(2)}) collective-permute-start(f32[128,128]{1,0:T(8,128)S(1)} %pad_maximum_fusion.8), channel_id=1, source_target_pairs={{0,8},{2,10},{4,12},{6,14},{8,0},{10,2},{12,4},{14,6},{16,24},{18,... | collective-permute-start | bytes 196616 | tf_op jit(solution)/shard_map/ppermute | solution.py:672
  127.0 5.2 %collective-permute-start.14 = (f32[128,128]{1,0:T(8,128)S(1)}, f32[128,128]{1,0:T(8,128)S(1)}, u32[]{:S(2)}, u32[]{:S(2)}) collective-permute-start(f32[128,128]{1,0:T(8,128)S(1)} %fusion.9), channel_id=1, source_target_pairs={{0,16},{2,18},{4,20},{6,22},{8,24},{10,26},{12,28},{14,30},{16,0},... | collective-permute-start | bytes 196616 | tf_op jit(solution)/shard_map/ppermute | solution.py:672
  132.2 4.3 %collective-permute-start.15 = (f32[128,128]{1,0:T(8,128)S(1)}, f32[128,128]{1,0:T(8,128)S(1)}, u32[]{:S(2)}, u32[]{:S(2)}) collective-permute-start(f32[128,128]{1,0:T(8,128)S(1)} %add.65), channel_id=1, source_target_pairs={{0,1},{1,0},{2,3},{3,2},{4,5},{5,4},{6,7},{7,6},{8,9},{9,8},{10,11... | collective-permute-start | bytes 196616 | tf_op jit(solution)/shard_map/ppermute | solution.py:672
  136.6 1.4 collective-permute-start.16

commit v10 on v9

--- a/solution.py
+++ b/solution.py
@@ -212,12 +212,12 @@
 
 
 def row_of(layout, turned, group, place):
-    latitude = group * PAIRS + place
-    row = layout.local - 1 - latitude
-    if not isinstance(turned, bool):
-        row = jnp.where(turned, row, latitude) if latitude < layout.local else latitude
-    elif not turned:
-        row = latitude
+    if turned is True:
+        steps = layout.half // PAIRS - 1
+        return (steps - group) * PAIRS + (layout.base + layout.local - 1 - place - steps * PAIRS)
+    row = latitude = group * PAIRS + place
+    if turned is not False and latitude < layout.local:
+        row = jnp.where(turned, layout.local - 1 - latitude, latitude)
     return layout.base + row
 
 
@@ -431,8 +431,7 @@
     @pl.when(group == 0)
     def _():
         if apart:
-            for copy in copies:
-                copy.start()
+            copies[0].start()
         else:
             low_orders(layout, held, *lows, real_ref, imag_ref, scratch, spec_low, swap_low, tails, moved)
         line = lax.broadcasted_iota(jnp.int32, (rows, LANES), 0)
@@ -467,6 +466,8 @@
             returned[pl.ds(row, layout.slots, stride=layout.pitch), :] = jnp.zeros((layout.slots, LANES), jnp.float32)
         if apart:
             copies[0].wait()
+            copies[1].start()
+            copies[2].start()
 
     def grid_step(turned):
         for quad in range(PAIRS // 2):

time: 139 us -> 139 us (level)
  Pallas kernels: 57.3 us -> 54.8 us
  starting transfers between devices: 24.1 us -> 25.7 us
    pallas_call x3, Pallas kernels: 36.7 us -> 34.3 us  [spectral_call(): pl.pallas_call(functools.partial(spectral_kernel, layout, apart), grid=(l...]
    ppermute x4, waiting for transfers between devices: 11.8 us -> 13.5 us  [others(): return [lax.ppermute(sent, 'space', route) for route in routes]]
    ppermute x9, waiting for transfers between devices: 11.3 us -> 9.73 us  [hop_parcels(): parcels.append(lax.ppermute(value, axis, pairs))]
  transfers between devices with their start and end apart: 17 -> 17, of which waited for: 12 -> 12; matrix products, arithmetic and copies ran while one was open for 15% -> 15% of each run, Pallas kernels for 37% -> 36%
where the time goes in v10:
time: 139 us; the launch traced here: 138 us
  Pallas kernels  54.8 us (39%)
  waiting for transfers between devices  26.9 us (19%)
  starting transfers between devices  25.7 us (18%)
  local copies, waits for them, and re-layouts  24.9 us (18%)
  other arithmetic  4.57 us (3%)
    pallas_call x3, Pallas kernels, spectral_call(): pl.pallas_call(functools.partial(spectral_kernel, layout, apart), grid=(l...  34.3 us
    ppermute x9, starting transfers between devices, hop_parcels(): parcels.append(lax.ppermute(value, axis, pairs))  18.6 us
    pallas_call x3, Pallas kernels, forward_call(): pl.pallas_call(functools.partial(forward_kernel, layout, chunk, bounds),...  16.1 us
    ppermute x4, waiting for transfers between devices, others(): return [lax.ppermute(sent, 'space', route) for route in routes]  13.5 us
    ppermute x9, waiting for transfers between devices, hop_parcels(): parcels.append(lax.ppermute(value, axis, pairs))  9.73 us
    unnamed x38, local copies, waits for them, and re-layouts  8.68 us
    ppermute x4, starting transfers between devices, others(): return [lax.ppermute(sent, 'space', route) for route in routes]  6.8 us
    dynamic_slice x2, local copies, waits for them, and re-layouts, bands(): lax.dynamic_slice_in_dim(table, first * layout.rows, count * layout.rows, 1)  4.46 us
  transfers between devices with their start and end apart: 17, of which 12 were waited for; matrix products, arithmetic and copies ran while one was open for 15% of the time, Pallas kernels for 36%

profile of v10, /device:TPU:0, one launch (start us, length us, event | category | flops | bytes accessed | tf_op | source)
XLA Modules:
  0.0 137.8 jit_solution(16755393701026149309)
XLA Ops:
  0.6 5.4 %forward_0.1.refs_0_ = bf16[92,64,128]{2,1,0:T(8,128)(2,1)} custom-call(s32[1]{0:T(128)} %bitcast.index, bf16[1,63,192,252]{3,2,1,0:T(8,128)(2,1)} %bitcast.30, bf16[256,252]{1,0:T(8,128)(2,1)} %constant.59.clone.basis_all, bf16[2,32,64,128]{3,2,1,0:T(8,128)(2,1)} %constant.53.clone.pair_all), custom_call_target="tpu_custom_call" | custom-call | flops 1000000 | bytes 100000 | tf_op jit(solution)/shard_map/forward_0/pallas_call | solution.py:577
  6.0 3.0 %collective-permute-start.1 = (bf16[92,64,128]{2,1,0:T(8,128)(2,1)}, bf16[92,64,128]{2,1,0:T(8,128)(2,1)}, u32[]{:S(2)}, u32[]{:S(2)}) collective-permute-start(bf16[92,64,128]{2,1,0:T(8,128)(2,1)} %forward_0.1.refs_0_), channel_id=1, source_target_pairs={{0,1},{1,0},{2,3},{3,2},{4,5},{5,4},{6,7},{7,6},{8,9},{9,8},{10,11... | collective-permute-start | bytes 4521992 | tf_op jit(solution)/shard_map/ppermute | solution.py:722
  9.1 3.4 %constant_dynamic-slice_fusion.1 = bf16[64,128,128]{2,1,0:T(8,128)(2,1)} fusion(bf16[64,256,128]{2,1,0:T(8,128)(2,1)} %constant.55.clone, s32[]{:T(128)S(6)} %select_n.25), kind=kLoop, calls=%fused_computation.26 | loop fusion | bytes 4194308 | tf_op jit(solution)/shard_map/dynamic_slice | solution.py:702
  12.4 1.1 constant_dynamic-slice_fusion
  13.5 1.9 %dynamic-slice_bitcast_fusion.1.refs_8_.refs_9_ = bf16[16,128,128]{2,1,0:T(8,128)(2,1)} fusion(bf16[2,16,128,128]{3,2,1,0:T(8,128)(2,1)} %constant.56.clone, s32[]{:T(128)S(6)} %select_n.27), kind=kLoop, calls=%fused_computation.2 | loop fusion | bytes 1048580 | tf_op jit(solution)/shard_map/jit(dynamic_index_in_dim)/squeeze | solution.py:695
  15.4 0.9 dynamic-slice_bitcast_fusion.refs_9_.refs_10_
  16.3 3.3 %copy.20 = bf16[32,256,128]{1,2,0:T(8,128)(2,1)S(1)} copy(bf16[32,256,128]{2,1,0:T(8,128)(2,1)} %bitcast.34) | data formatting | bytes 4194304 | tf_op jit(solution)/shard_map/reshape | solution.py:709
  19.6 1.6 %copy.21 = bf16[32,128,128]{1,2,0:T(8,128)(2,1)S(1)} copy(bf16[32,128,128]{2,1,0:T(8,128)(2,1)} %bitcast.33) | data formatting | bytes 2097152 | tf_op jit(solution)/shard_map/reshape | solution.py:711
  21.2 1.3 fusion.10
  22.5 1.1 pad_maximum_fusion.refs_3_
  23.6 5.3 %forward_1.1.refs_0_ = bf16[92,64,128]{2,1,0:T(8,128)(2,1)} custom-call(s32[1]{0:T(128)} %bitcast.index, bf16[1,63,192,252]{3,2,1,0:T(8,128)(2,1)} %bitcast.31, bf16[256,252]{1,0:T(8,128)(2,1)} %constant.59.clone.basis_all, bf16[2,32,64,128]{3,2,1,0:T(8,128)(2,1)} %constant.53.clone.pair_all), custom_call_target="tpu_custom_call" | custom-call | flops 1000000 | bytes 100000 | tf_op jit(solution)/shard_map/forward_1/pallas_call | solution.py:577
  29.0 0.0 copy-start.15
  29.0 0.1 collective-permute-start
  29.1 5.3 %forward_2.1 = (bf16[60,64,128]{2,1,0:T(8,128)(2,1)}, bf16[32,64,128]{2,1,0:T(8,128)(2,1)}) custom-call(s32[1]{0:T(128)} %bitcast.index, bf16[1,63,192,252]{3,2,1,0:T(8,128)(2,1)} %bitcast.32, bf16[256,252]{1,0:T(8,128)(2,1)} %constant.59.clone.basis_all, bf16[2,32,64,128]{3,2,1,0:T(8,128)(2,1)} %constant.53.clone.pair_all), custom_call_target="tpu_custom_call" | custom-call | flops 1000000 | bytes 100000 | tf_op jit(solution)/shard_map/forward_2/pallas_call | solution.py:577
  34.4 2.1 %collective-permute-start.7 = (bf16[60,64,128]{2,1,0:T(8,128)(2,1)}, bf16[60,64,128]{2,1,0:T(8,128)(2,1)}, u32[]{:S(2)}, u32[]{:S(2)}) collective-permute-start(bf16[60,64,128]{2,1,0:T(8,128)(2,1)} %get-tuple-element.86.refs_0_), channel_id=1, source_target_pairs={{0,1},{1,0},{2,3},{3,2},{4,5},{5,4},{6,7},{7,6},{8,9},{9,8},{10,11... | collective-permute-start | bytes 2949128 | tf_op jit(solution)/shard_map/ppermute | solution.py:722
  36.5 0.1 copy.22
  36.6 0.1 rev.6
  36.7 0.0 copy-start.11
  36.8 0.0 copy-start.12
  36.8 0.7 fusion.11
  37.5 0.1 pad_add_fusion.side
  37.6 0.9 copy.24
  38.5 0.6 slice.54
  39.2 1.4 rev.7
  40.5 0.9 fusion.7
  41.5 1.2 pad_maximum_fusion.1
  42.7 0.1 slice_negate_fusion
  42.8 0.1 pad_maximum_fusion.2
  43.0 0.2 collective-permute-done.1.refs_1_
  43.2 1.0 copy-done.3
  44.3 1.0 copy-done.5
  45.3 2.8 %copy-done.7 = bf16[1,63,252,192]{2,3,1,0:T(8,128)(2,1)S(1)} copy-done((bf16[1,63,252,192]{2,3,1,0:T(8,128)(2,1)S(1)}, bf16[1,63,252,192]{2,3,1,0:T(8,128)(2,1)}, u32[]{:S(2)}) %copy-start.7) | copy-done | bytes 6096408
  48.1 12.5 %spectral_0.1 = (f32[64,128]{1,0:T(8,128)S(1)}, f32[64,128]{1,0:T(8,128)S(1)}) custom-call(s32[2]{0:T(128)S(1)} %pad_add_fusion.side, bf16[92,64,128]{2,1,0:T(8,128)(2,1)S(1)} %copy-done, bf16[92,64,128]{2,1,0:T(8,128)(2,1)} %collective-permute-done.1.refs_1_, bf16[32,128,256]{2,1,0:T(8,128)(2,1)S(1)} %bitcast.16, bf16[32,64,256]{2,1,0:T(8,128)(2,1)S(1)} %copy-done.2, ...), custom_call_target="tpu_custom_call" | custom-call | flops 8000000000 | bytes 30000000 | tf_op jit(solution)/shard_map/spectral_0/pallas_call | solution.py:623
  60.5 0.1 collective-permute-start.2
  60.6 1.2 collective-permute-done.2
  61.8 2.0 %collective-permute-start.3 = (f32[64,128]{1,0:T(8,128)S(1)}, f32[64,128]{1,0:T(8,128)S(1)}, u32[]{:S(2)}, u32[]{:S(2)}) collective-permute-start(f32[64,128]{1,0:T(8,128)S(1)} %add.55), channel_id=1, source_target_pairs={{0,4},{2,6},{4,0},{6,2},{8,12},{10,14},{12,8},{14,10},{16,20},{18,... | collective-permute-start | bytes 98312 | tf_op jit(solution)/shard_map/ppermute | solution.py:673
  63.8 0.1 pad_maximum_fusion.5
  64.0 1.6 %collective-permute-start.9 = (bf16[32,64,128]{2,1,0:T(8,128)(2,1)S(1)}, bf16[32,64,128]{2,1,0:T(8,128)(2,1)S(1)}, u32[]{:S(2)}, u32[]{:S(2)}) collective-permute-start(bf16[32,64,128]{2,1,0:T(8,128)(2,1)S(1)} %copy-done.10), channel_id=1, source_target_pairs={{0,1},{1,0},{2,3},{3,2},{4,5},{5,4},{6,7},{7,6},{8,9},{9,8},{10,11... | collective-permute-start | bytes 1572872 | tf_op jit(solution)/shard_map/ppermute | solution.py:722
  65.6 0.1 collective-permute-done.3
  65.7 9.8 %collective-permute-done.refs_1_ = bf16[92,64,128]{2,1,0:T(8,128)(2,1)} collective-permute-done((bf16[92,64,128]{2,1,0:T(8,128)(2,1)}, bf16[92,64,128]{2,1,0:T(8,128)(2,1)}, u32[]{:S(2)}, u32[]{:S(2)}) %collective-permute-start) | collective-permute-done | bytes 1507360 | tf_op jit(solution)/shard_map/ppermute | solution.py:722
  75.5 2.1 %collective-permute-start.4 = (f32[64,128]{1,0:T(8,128)S(1)}, f32[64,128]{1,0:T(8,128)S(1)}, u32[]{:S(2)}, u32[]{:S(2)}) collective-permute-start(f32[64,128]{1,0:T(8,128)S(1)} %add.56), channel_id=1, source_target_pairs={{0,8},{2,10},{4,12},{6,14},{8,0},{10,2},{12,4},{14,6},{16,24},{18,... | collective-permute-start | bytes 98312 | tf_op jit(solution)/shard_map/ppermute | solution.py:673
  77.6 2.8 %copy-done.8 = bf16[1,63,252,192]{2,3,1,0:T(8,128)(2,1)S(1)} copy-done((bf16[1,63,252,192]{2,3,1,0:T(8,128)(2,1)S(1)}, bf16[1,63,252,192]{2,3,1,0:T(8,128)(2,1)}, u32[]{:S(2)}) %copy-start.8) | copy-done | bytes 6096408
  80.4 12.5 %spectral_1.1 = (f32[64,128]{1,0:T(8,128)S(1)}, f32[64,128]{1,0:T(8,128)S(1)}) custom-call(s32[2]{0:T(128)S(1)} %pad_add_fusion.side, bf16[92,64,128]{2,1,0:T(8,128)(2,1)S(1)} %copy-done.1, bf16[92,64,128]{2,1,0:T(8,128)(2,1)} %collective-permute-done.refs_1_, bf16[32,128,256]{2,1,0:T(8,128)(2,1)S(1)} %bitcast.17, bf16[32,64,256]{2,1,0:T(8,128)(2,1)S(1)} %copy-done.2, ...), custom_call_target="tpu_custom_call" | custom-call | flops 8000000000 | bytes 30000000 | tf_op jit(solution)/shard_map/spectral_1/pallas_call | solution.py:623
  92.9 0.1 collective-permute-start.5
  93.0 2.6 %collective-permute-start.6 = (f32[64,128]{1,0:T(8,128)S(1)}, f32[64,128]{1,0:T(8,128)S(1)}, u32[]{:S(2)}, u32[]{:S(2)}) collective-permute-start(f32[64,128]{1,0:T(8,128)S(1)} %add.57), channel_id=1, source_target_pairs={{0,16},{2,18},{4,20},{6,22},{8,24},{10,26},{12,28},{14,30},{16,0},... | collective-permute-start | bytes 98312 | tf_op jit(solution)/shard_map/ppermute | solution.py:673
  95.6 1.0 collective-permute-done.7.refs_1_
  96.6 4.5 %low_2.1 = (f32[4608,128]{1,0:T(8,128)S(1)}, bf16[64,128,128]{2,1,0:T(8,128)(2,1)S(1)}, bf16[64,128,128]{2,1,0:T(8,128)(2,1)S(1)}) custom-call(bf16[60,64,128]{2,1,0:T(8,128)(2,1)S(1)} %copy-done.9, bf16[60,64,128]{2,1,0:T(8,128)(2,1)} %collective-permute-done.7.refs_1_, bf16[32,128,256]{2,1,0:T(8,128)(2,1)S(1)} %bitcast.18, ...), custom_call_target="tpu_custom_call" | custom-call | flops 8000000000 | bytes 30000000 | tf_op jit(solution)/shard_map/low_2/pallas_call | solution.py:602
  101.1 2.1 %collective-permute-start.8 = (f32[64,128]{1,0:T(8,128)S(1)}, f32[64,128]{1,0:T(8,128)S(1)}, u32[]{:S(2)}, u32[]{:S(2)}) collective-permute-start(f32[64,128]{1,0:T(8,128)S(1)} %add.58), channel_id=1, source_target_pairs={{0,1},{1,0},{2,3},{3,2},{4,5},{5,4},{6,7},{7,6},{8,9},{9,8},{10,11... | collective-permute-start | bytes 98312 | tf_op jit(solution)/shard_map/ppermute | solution.py:673
  103.2 1.5 %collective-permute-start.10 = (f32[64,128]{1,0:T(8,128)S(1)}, f32[64,128]{1,0:T(8,128)S(1)}, u32[]{:S(2)}, u32[]{:S(2)}) collective-permute-start(f32[64,128]{1,0:T(8,128)S(1)} %add.59), channel_id=1, source_target_pairs={{0,4},{2,6},{4,0},{6,2},{8,12},{10,14},{12,8},{14,10},{16,20},{18,... | collective-permute-start | bytes 98312 | tf_op jit(solution)/shard_map/ppermute | solution.py:673
  104.7 2.5 %collective-permute-done.9.refs_1_ = bf16[32,64,128]{2,1,0:T(8,128)(2,1)S(1)} collective-permute-done((bf16[32,64,128]{2,1,0:T(8,128)(2,1)S(1)}, bf16[32,64,128]{2,1,0:T(8,128)(2,1)S(1)}, u32[]{:S(2)}, u32[]{:S(2)}) %collective-permute-start.9) | collective-permute-done | bytes 524320 | tf_op jit(solution)/shard_map/ppermute | solution.py:722
  107.2 9.4 %spectral_2.1 = (f32[64,128]{1,0:T(8,128)S(1)}, f32[64,128]{1,0:T(8,128)S(1)}) custom-call(s32[2]{0:T(128)S(1)} %pad_add_fusion.side, bf16[32,64,128]{2,1,0:T(8,128)(2,1)S(1)} %copy-done.10, bf16[32,64,128]{2,1,0:T(8,128)(2,1)S(1)} %collective-permute-done.9.refs_1_, f32[4608,128]{1,0:T(8,128)S(1)} %get-tuple-element.102.refs_2_, ...), custom_call_target="tpu_custom_call" | custom-call | flops 8000000000 | bytes 30000000 | tf_op jit(solution)/shard_map/spectral_2/pallas_call | solution.py:623
  116.6 0.1 collective-permute-start.11
  116.7 1.2 collective-permute-done.11
  117.9 1.7 %collective-permute-start.12 = (f32[64,128]{1,0:T(8,128)S(1)}, f32[64,128]{1,0:T(8,128)S(1)}, u32[]{:S(2)}, u32[]{:S(2)}) collective-permute-start(f32[64,128]{1,0:T(8,128)S(1)} %add.62), channel_id=1, source_target_pairs={{0,4},{2,6},{4,0},{6,2},{8,12},{10,14},{12,8},{14,10},{16,20},{18,... | collective-permute-start | bytes 98312 | tf_op jit(solution)/shard_map/ppermute | solution.py:673
  119.6 2.2 %collective-permute-done.12 = f32[64,128]{1,0:T(8,128)S(1)} collective-permute-done((f32[64,128]{1,0:T(8,128)S(1)}, f32[64,128]{1,0:T(8,128)S(1)}, u32[]{:S(2)}, u32[]{:S(2)}) %collective-permute-start.12) | collective-permute-done | bytes 32800 | tf_op jit(solution)/shard_map/ppermute | solution.py:673
  121.8 1.9 %collective-permute-start.13 = (f32[128,128]{1,0:T(8,128)S(1)}, f32[128,128]{1,0:T(8,128)S(1)}, u32[]{:S(2)}, u32[]{:S(2)}) collective-permute-start(f32[128,128]{1,0:T(8,128)S(1)} %pad_maximum_fusion.8), channel_id=1, source_target_pairs={{0,8},{2,10},{4,12},{6,14},{8,0},{10,2},{12,4},{14,6},{16,24},{18,... | collective-permute-start | bytes 196616 | tf_op jit(solution)/shard_map/ppermute | solution.py:673
  123.7 2.5 %collective-permute-done.13 = f32[128,128]{1,0:T(8,128)S(1)} collective-permute-done((f32[128,128]{1,0:T(8,128)S(1)}, f32[128,128]{1,0:T(8,128)S(1)}, u32[]{:S(2)}, u32[]{:S(2)}) %collective-permute-start.13) | collective-permute-done | bytes 65568 | tf_op jit(solution)/shard_map/ppermute | solution.py:673
  126.2 2.9 %collective-permute-start.14 = (f32[128,128]{1,0:T(8,128)S(1)}, f32[128,128]{1,0:T(8,128)S(1)}, u32[]{:S(2)}, u32[]{:S(2)}) collective-permute-start(f32[128,128]{1,0:T(8,128)S(1)} %fusion.9), channel_id=1, source_target_pairs={{0,16},{2,18},{4,20},{6,22},{8,24},{10,26},{12,28},{14,30},{16,0},... | collective-permute-start | bytes 196616 | tf_op jit(solution)/shard_map/ppermute | solution.py:673
  129.0 2.4 %collective-permute-done.14 = f32[128,128]{1,0:T(8,128)S(1)} collective-permute-done((f32[128,128]{1,0:T(8,128)S(1)}, f32[128,128]{1,0:T(8,128)S(1)}, u32[]{:S(2)}, u32[]{:S(2)}) %collective-permute-start.14) | collective-permute-done | bytes 65568 | tf_op jit(solution)/shard_map/ppermute | solution.py:673
  131.4 1.8 %collective-permute-start.15 = (f32[128,128]{1,0:T(8,128)S(1)}, f32[128,128]{1,0:T(8,128)S(1)}, u32[]{:S(2)}, u32[]{:S(2)}) collective-permute-start(f32[128,128]{1,0:T(8,128)S(1)} %add.65), channel_id=1, source_target_pairs={{0,1},{1,0},{2,3},{3,2},{4,5},{5,4},{6,7},{7,6},{8,9},{9,8},{10,11... | collective-permute-start | bytes 196616 | tf_op jit(solution)/shard_map/ppermute | solution.py:673
  133.2 2.5 %collective-permute-done.15 = f32[128,128]{1,0:T(8,128)S(1)} collective-permute-done((f32[128,128]{1,0:T(8,128)S(1)}, f32[128,128]{1,0:T(8,128)S(1)}, u32[]{:S(2)}, u32[]{:S(2)}) %collective-permute-start.15) | collective-permute-done | bytes 65568 | tf_op jit(solution)/shard_map/ppermute | solution.py:673
  135.8 0.1 collective-permute-start.16
  135.9 1.3 collective-permute-done.16
  137.2 0.7 multiply_bitcast_fusion
  (51 shorter events, 0.2 us)
Async XLA Ops:
  6.0 37.2 %collective-permute-start.1 = (bf16[92,64,128]{2,1,0:T(8,128)(2,1)}, bf16[92,64,128]{2,1,0:T(8,128)(2,1)}, u32[]{:S(2)}, u32[]{:S(2)}) collective-permute-start(bf16[92,64,128]{2,1,0:T(8,128)(2,1)} %forward_0.1.refs_0_), channel_id=1, source_target_pairs={{0,1},{1,0},{2,3},{3,2},{4,5},{5,4},{6,7},{7,6},{8,9},{9,8},{10,11... | collective-permute-start | bytes 4521992 | tf_op jit(solution)/shard_map/ppermute | solution.py:722
  9.1 3.4 %copy-start.13 = (bf16[64,128,128]{2,1,0:T(8,128)(2,1)S(1)}, bf16[64,128,128]{2,1,0:T(8,128)(2,1)}, u32[]{:S(2)}) copy-start(bf16[64,128,128]{2,1,0:T(8,128)(2,1)} %constant.54.clone) | copy-start | bytes 6291460
  12.4 3.0 %copy-start.14 = (bf16[2,16,64,256]{3,2,1,0:T(8,128)(2,1)S(1)}, bf16[2,16,64,256]{3,2,1,0:T(8,128)(2,1)}, u32[]{:S(2)}) copy-start(bf16[2,16,64,256]{3,2,1,0:T(8,128)(2,1)} %constant.57.clone) | copy-start | bytes 3145732
  29.0 7.5 %copy-start.15 = (bf16[126,192]{0,1:T(8,128)(2,1)S(1)}, bf16[126,192]{0,1:T(8,128)(2,1)}, u32[]{:S(2)}) copy-start(bf16[126,192]{0,1:T(8,128)(2,1)} %param.16) | copy-start | bytes 145156
  29.0 46.5 %collective-permute-start = (bf16[92,64,128]{2,1,0:T(8,128)(2,1)}, bf16[92,64,128]{2,1,0:T(8,128)(2,1)}, u32[]{:S(2)}, u32[]{:S(2)}) collective-permute-start(bf16[92,64,128]{2,1,0:T(8,128)(2,1)} %forward_1.1.refs_0_), channel_id=1, source_target_pairs={{0,1},{1,0},{2,3},{3,2},{4,5},{5,4},{6,7},{7,6},{8,9},{9,8},{10,11... | collective-permute-start | bytes 4521992 | tf_op jit(solution)/shard_map/ppermute | solution.py:722
  34.4 62.1 %collective-permute-start.7 = (bf16[60,64,128]{2,1,0:T(8,128)(2,1)}, bf16[60,64,128]{2,1,0:T(8,128)(2,1)}, u32[]{:S(2)}, u32[]{:S(2)}) collective-permute-start(bf16[60,64,128]{2,1,0:T(8,128)(2,1)} %get-tuple-element.86.refs_0_), channel_id=1, source_target_pairs={{0,1},{1,0},{2,3},{3,2},{4,5},{5,4},{6,7},{7,6},{8,9},{9,8},{10,11... | collective-permute-start | bytes 2949128 | tf_op jit(solution)/shard_map/ppermute | solution.py:722
  36.7 6.5 %copy-start.11 = (bf16[256,252]{1,0:T(8,128)(2,1)S(1)}, bf16[256,252]{1,0:T(8,128)(2,1)}, u32[]{:S(2)}) copy-start(bf16[256,252]{1,0:T(8,128)(2,1)} %constant.52.clone.refs_6_.refs_7_) | copy-start | bytes 387076
  36.8 6.4 %copy-start.12 = (f32[128,128]{1,0:T(8,128)S(1)}, f32[128,128]{1,0:T(8,128)}, u32[]{:S(2)}) copy-start(f32[128,128]{1,0:T(8,128)} %constant.58.clone.refs_10_.refs_11_) | copy-start | bytes 196612
  40.5 2.7 %copy-start = (bf16[92,64,128]{2,1,0:T(8,128)(2,1)S(1)}, bf16[92,64,128]{2,1,0:T(8,128)(2,1)}, u32[]{:S(2)}) copy-start(bf16[92,64,128]{2,1,0:T(8,128)(2,1)} %forward_0.1.refs_0_) | copy-start | bytes 4521988
  40.5 2.7 %copy-start.2 = (bf16[32,64,256]{2,1,0:T(8,128)(2,1)S(1)}, bf16[32,64,256]{2,1,0:T(8,128)(2,1)}, u32[]{:S(2)}) copy-start(bf16[32,64,256]{2,1,0:T(8,128)(2,1)} %pad_maximum_fusion.refs_3_) | copy-start | bytes 3145732
  43.2 1.0 copy-start.3
  44.3 1.0 copy-start.5
  45.3 2.8 %copy-start.7 = (bf16[1,63,252,192]{2,3,1,0:T(8,128)(2,1)S(1)}, bf16[1,63,252,192]{2,3,1,0:T(8,128)(2,1)}, u32[]{:S(2)}) copy-start(bf16[1,63,252,192]{2,3,1,0:T(8,128)(2,1)} %param.15) | copy-start | bytes 18289156
  48.1 15.9 %copy-start.10 = (bf16[32,64,128]{2,1,0:T(8,128)(2,1)S(1)}, bf16[32,64,128]{2,1,0:T(8,128)(2,1)}, u32[]{:S(2)}) copy-start(bf16[32,64,128]{2,1,0:T(8,128)(2,1)} %get-tuple-element.101.refs_0_) | copy-start | bytes 1572868
  48.1 29.5 %copy-start.1 = (bf16[92,64,128]{2,1,0:T(8,128)(2,1)S(1)}, bf16[92,64,128]{2,1,0:T(8,128)(2,1)}, u32[]{:S(2)}) copy-start(bf16[92,64,128]{2,1,0:T(8,128)(2,1)} %forward_1.1.refs_0_) | copy-start | bytes 4521988
  60.5 1.3 collective-permute-start.2
  61.8 3.9 %collective-permute-start.3 = (f32[64,128]{1,0:T(8,128)S(1)}, f32[64,128]{1,0:T(8,128)S(1)}, u32[]{:S(2)}, u32[]{:S(2)}) collective-permute-start(f32[64,128]{1,0:T(8,128)S(1)} %add.55), channel_id=1, source_target_pairs={{0,4},{2,6},{4,0},{6,2},{8,12},{10,14},{12,8},{14,10},{16,20},{18,... | collective-permute-start | bytes 98312 | tf_op jit(solution)/shard_map/ppermute | solution.py:673
  64.0 43.2 %collective-permute-start.9 = (bf16[32,64,128]{2,1,0:T(8,128)(2,1)S(1)}, bf16[32,64,128]{2,1,0:T(8,128)(2,1)S(1)}, u32[]{:S(2)}, u32[]{:S(2)}) collective-permute-start(bf16[32,64,128]{2,1,0:T(8,128)(2,1)S(1)} %copy-done.10), channel_id=1, source_target_pairs={{0,1},{1,0},{2,3},{3,2},{4,5},{5,4},{6,7},{7,6},{8,9},{9,8},{10,11... | collective-permute-start | bytes 1572872 | tf_op jit(solution)/shard_map/ppermute | solution.py:722
  75.5 17.4 %collective-permute-start.4 = (f32[64,128]{1,0:T(8,128)S(1)}, f32[64,128]{1,0:T(8,128)S(1)}, u32[]{:S(2)}, u32[]{:S(2)}) collective-permute-start(f32[64,128]{1,0:T(8,128)S(1)} %add.56), channel_id=1, source_target_pairs={{0,8},{2,10},{4,12},{6,14},{8,0},{10,2},{12,4},{14,6},{16,24},{18,... | collective-permute-start | bytes 98312 | tf_op jit(solution)/shard_map/ppermute | solution.py:673
  77.6 2.8 %copy-start.8 = (bf16[1,63,252,192]{2,3,1,0:T(8,128)(2,1)S(1)}, bf16[1,63,252,192]{2,3,1,0:T(8,128)(2,1)}, u32[]{:S(2)}) copy-start(bf16[1,63,252,192]{2,3,1,0:T(8,128)(2,1)} %param.15) | copy-start | bytes 18289156
  80.4 16.2 %copy-start.9 = (bf16[60,64,128]{2,1,0:T(8,128)(2,1)S(1)}, bf16[60,64,128]{2,1,0:T(8,128)(2,1)}, u32[]{:S(2)}) copy-start(bf16[60,64,128]{2,1,0:T(8,128)(2,1)} %get-tuple-element.86.refs_0_) | copy-start | bytes 2949124
  80.4 26.8 %slice-start = ((s8[6193152]{0:T(1024)(128)(4,1)}), s8[4194304]{0:T(1024)(128)(4,1)S(1)}, s32[]{:S(2)}) async-start(s8[6193152]{0:T(1024)(128)(4,1)} %bitcast.26), calls=%async_computation | async-start | bytes 8388608
  92.9 8.2 %collective-permute-start.5 = (f32[64,128]{1,0:T(8,128)S(1)}, f32[64,128]{1,0:T(8,128)S(1)}, u32[]{:S(2)}, u32[]{:S(2)}) collective-permute-start(f32[64,128]{1,0:T(8,128)S(1)} %get-tuple-element.82), channel_id=1, source_target_pairs={{0,2},{2,0},{4,6},{6,4},{8,10},{10,8},{12,14},{14,12},{16,18},{18,... | collective-permute-start | bytes 98312 | tf_op jit(solution)/shard_map/ppermute | solution.py:745
  93.0 8.1 %collective-permute-start.6 = (f32[64,128]{1,0:T(8,128)S(1)}, f32[64,128]{1,0:T(8,128)S(1)}, u32[]{:S(2)}, u32[]{:S(2)}) collective-permute-start(f32[64,128]{1,0:T(8,128)S(1)} %add.57), channel_id=1, source_target_pairs={{0,16},{2,18},{4,20},{6,22},{8,24},{10,26},{12,28},{14,30},{16,0},... | collective-permute-start | bytes 98312 | tf_op jit(solution)/shard_map/ppermute | solution.py:673
  96.6 10.6 %copy-start.4 = (bf16[16,128,128]{2,1,0:T(8,128)(2,1)S(1)}, bf16[16,128,128]{2,1,0:T(8,128)(2,1)}, u32[]{:S(2)}) copy-start(bf16[16,128,128]{2,1,0:T(8,128)(2,1)} %dynamic-slice_bitcast_fusion.1.refs_8_.refs_9_) | copy-start | bytes 1572868
  96.6 10.6 %copy-start.6 = (bf16[16,64,256]{2,1,0:T(8,128)(2,1)S(1)}, bf16[16,64,256]{2,1,0:T(8,128)(2,1)}, u32[]{:S(2)}) copy-start(bf16[16,64,256]{2,1,0:T(8,128)(2,1)} %dynamic-slice_bitcast_fusion.refs_9_.refs_10_) | copy-start | bytes 1572868
  96.6 10.6 %slice-start.1 = ((s8[6193152]{0:T(1024)(128)(4,1)}), s8[1998848]{0:T(1024)(128)(4,1)S(1)}, s32[]{:S(2)}) async-start(s8[6193152]{0:T(1024)(128)(4,1)} %bitcast.26), calls=%async_computation.1 | async-start | bytes 3997696
  101.1 15.5 %collective-permute-start.8 = (f32[64,128]{1,0:T(8,128)S(1)}, f32[64,128]{1,0:T(8,128)S(1)}, u32[]{:S(2)}, u32[]{:S(2)}) collective-permute-start(f32[64,128]{1,0:T(8,128)S(1)} %add.58), channel_id=1, source_target_pairs={{0,1},{1,0},{2,3},{3,2},{4,5},{5,4},{6,7},{7,6},{8,9},{9,8},{10,11... | collective-permute-start | bytes 98312 | tf_op jit(solution)/shard_map/ppermute | solution.py:673
  103.2 13.4 %collective-permute-start.10 = (f32[64,128]{1,0:T(8,128)S(1)}, f32[64,128]{1,0:T(8,128)S(1)}, u32[]{:S(2)}, u32[]{:S(2)}) collective-permute-start(f32[64,128]{1,0:T(8,128)S(1)} %add.59), channel_id=1, source_target_pairs={{0,4},{2,6},{4,0},{6,2},{8,12},{10,14},{12,8},{14,10},{16,20},{18,... | collective-permute-start | bytes 98312 | tf_op jit(solution)/shard_map/ppermute | solution.py:673
  116.6 1.3 collective-permute-start.11
  117.9 3.9 %collective-permute-start.12 = (f32[64,128]{1,0:T(8,128)S(1)}, f32[64,128]{1,0:T(8,128)S(1)}, u32[]{:S(2)}, u32[]{:S(2)}) collective-permute-start(f32[64,128]{1,0:T(8,128)S(1)} %add.62), channel_id=1, source_target_pairs={{0,4},{2,6},{4,0},{6,2},{8,12},{10,14},{12,8},{14,10},{16,20},{18,... | collective-permute-start | bytes 98312 | tf_op jit(solution)/shard_map/ppermute | solution.py:673
  121.8 4.3 %collective-permute-start.13 = (f32[128,128]{1,0:T(8,128)S(1)}, f32[128,128]{1,0:T(8,128)S(1)}, u32[]{:S(2)}, u32[]{:S(2)}) collective-permute-start(f32[128,128]{1,0:T(8,128)S(1)} %pad_maximum_fusion.8), channel_id=1, source_target_pairs={{0,8},{2,10},{4,12},{6,14},{8,0},{10,2},{12,4},{14,6},{16,24},{18,... | collective-permute-start | bytes 196616 | tf_op jit(solution)/shard_map/ppermute | solution.py:673
  126.2 5.2 %collective-permute-start.14 = (f32[128,128]{1,0:T(8,128)S(1)}, f32[128,128]{1,0:T(8,128)S(1)}, u32[]{:S(2)}, u32[]{:S(2)}) collective-permute-start(f32[128,128]{1,0:T(8,128)S(1)} %fusion.9), channel_id=1, source_target_pairs={{0,16},{2,18},{4,20},{6,22},{8,24},{10,26},{12,28},{14,30},{16,0},... | collective-permute-start | bytes 196616 | tf_op jit(solution)/shard_map/ppermute | solution.py:673
  131.4 4.3 %collective-permute-start.15 = (f32[128,128]{1,0:T(8,128)S(1)}, f32[128,128]{1,0:T(8,128)S(1)}, u32[]{:S(2)}, u32[]{:S(2)}) collective-permute-start(f32[128,128]{1,0:T(8,128)S(1)} %add.65), channel_id=1, source_target_pairs={{0,1},{1,0},{2,3},{3,2},{4,5},{5,4},{6,7},{7,6},{8,9},{9,8},{10,11... | collective-permute-start | bytes 196616 | tf_op jit(solution)/shard_map/ppermute | solution.py:673
  135.8 1.4 collective-permute-start.16

commit v11 on v10

--- a/solution.py
+++ b/solution.py
@@ -15,7 +15,7 @@
 MODES = 126
 LANES = 128
 GROUP = 16
-PAIRS = 8
+PAIRS = 16
 MOVED = 3
 TAIL = 8
 VMEM = 30 * 1024 * 1024

time: 139 us -> 138 us (level)
  Pallas kernels: 54.8 us -> 53 us
  transfers between devices with their start and end apart: 17 -> 17, of which waited for: 12 -> 12; matrix products, arithmetic and copies ran while one was open for 15% -> 15% of each run, Pallas kernels for 36% -> 35%
where the time goes in v11:
time: 138 us; the launch traced here: 137 us
  Pallas kernels  53 us (38%)
  waiting for transfers between devices  28.1 us (20%)
  starting transfers between devices  25.7 us (19%)
  local copies, waits for them, and re-layouts  24.9 us (18%)
  other arithmetic  4.57 us (3%)
    pallas_call x3, Pallas kernels, spectral_call(): pl.pallas_call(functools.partial(spectral_kernel, layout, apart), grid=(l...  33.2 us
    ppermute x9, starting transfers between devices, hop_parcels(): parcels.append(lax.ppermute(value, axis, pairs))  18.7 us
    pallas_call x3, Pallas kernels, forward_call(): pl.pallas_call(functools.partial(forward_kernel, layout, chunk, bounds),...  15.3 us
    ppermute x4, waiting for transfers between devices, others(): return [lax.ppermute(sent, 'space', route) for route in routes]  14.7 us
    ppermute x9, waiting for transfers between devices, hop_parcels(): parcels.append(lax.ppermute(value, axis, pairs))  9.67 us
    unnamed x38, local copies, waits for them, and re-layouts  8.68 us
    ppermute x4, starting transfers between devices, others(): return [lax.ppermute(sent, 'space', route) for route in routes]  6.78 us
    pallas_call x1, Pallas kernels, low_call(): pl.pallas_call(functools.partial(low_kernel, layout), in_specs=[whole()]...  4.46 us
  transfers between devices with their start and end apart: 17, of which 12 were waited for; matrix products, arithmetic and copies ran while one was open for 15% of the time, Pallas kernels for 35%

profile of v11, /device:TPU:0, one launch (start us, length us, event | category | flops | bytes accessed | tf_op | source)
XLA Modules:
  0.0 137.2 jit_solution(8788712338857746460)
XLA Ops:
  0.6 5.1 %forward_0.1.refs_0_ = bf16[92,64,128]{2,1,0:T(8,128)(2,1)} custom-call(s32[1]{0:T(128)} %bitcast.index, bf16[1,63,192,252]{3,2,1,0:T(8,128)(2,1)} %bitcast.30, bf16[256,252]{1,0:T(8,128)(2,1)} %constant.59.clone.basis_all, bf16[2,32,64,128]{3,2,1,0:T(8,128)(2,1)} %constant.53.clone.pair_all), custom_call_target="tpu_custom_call" | custom-call | flops 1000000 | bytes 100000 | tf_op jit(solution)/shard_map/forward_0/pallas_call | solution.py:577
  5.8 3.0 %collective-permute-start.1 = (bf16[92,64,128]{2,1,0:T(8,128)(2,1)}, bf16[92,64,128]{2,1,0:T(8,128)(2,1)}, u32[]{:S(2)}, u32[]{:S(2)}) collective-permute-start(bf16[92,64,128]{2,1,0:T(8,128)(2,1)} %forward_0.1.refs_0_), channel_id=1, source_target_pairs={{0,1},{1,0},{2,3},{3,2},{4,5},{5,4},{6,7},{7,6},{8,9},{9,8},{10,11... | collective-permute-start | bytes 4521992 | tf_op jit(solution)/shard_map/ppermute | solution.py:722
  8.8 3.4 %constant_dynamic-slice_fusion.1 = bf16[64,128,128]{2,1,0:T(8,128)(2,1)} fusion(bf16[64,256,128]{2,1,0:T(8,128)(2,1)} %constant.55.clone, s32[]{:T(128)S(6)} %select_n.25), kind=kLoop, calls=%fused_computation.26 | loop fusion | bytes 4194308 | tf_op jit(solution)/shard_map/dynamic_slice | solution.py:702
  12.2 1.1 constant_dynamic-slice_fusion
  13.3 1.9 %dynamic-slice_bitcast_fusion.1.refs_8_.refs_9_ = bf16[16,128,128]{2,1,0:T(8,128)(2,1)} fusion(bf16[2,16,128,128]{3,2,1,0:T(8,128)(2,1)} %constant.56.clone, s32[]{:T(128)S(6)} %select_n.27), kind=kLoop, calls=%fused_computation.2 | loop fusion | bytes 1048580 | tf_op jit(solution)/shard_map/jit(dynamic_index_in_dim)/squeeze | solution.py:695
  15.2 0.9 dynamic-slice_bitcast_fusion.refs_9_.refs_10_
  16.0 3.3 %copy.20 = bf16[32,256,128]{1,2,0:T(8,128)(2,1)S(1)} copy(bf16[32,256,128]{2,1,0:T(8,128)(2,1)} %bitcast.34) | data formatting | bytes 4194304 | tf_op jit(solution)/shard_map/reshape | solution.py:709
  19.3 1.6 %copy.21 = bf16[32,128,128]{1,2,0:T(8,128)(2,1)S(1)} copy(bf16[32,128,128]{2,1,0:T(8,128)(2,1)} %bitcast.33) | data formatting | bytes 2097152 | tf_op jit(solution)/shard_map/reshape | solution.py:711
  20.9 1.3 fusion.10
  22.2 1.1 pad_maximum_fusion.refs_3_
  23.4 5.1 %forward_1.1.refs_0_ = bf16[92,64,128]{2,1,0:T(8,128)(2,1)} custom-call(s32[1]{0:T(128)} %bitcast.index, bf16[1,63,192,252]{3,2,1,0:T(8,128)(2,1)} %bitcast.31, bf16[256,252]{1,0:T(8,128)(2,1)} %constant.59.clone.basis_all, bf16[2,32,64,128]{3,2,1,0:T(8,128)(2,1)} %constant.53.clone.pair_all), custom_call_target="tpu_custom_call" | custom-call | flops 1000000 | bytes 100000 | tf_op jit(solution)/shard_map/forward_1/pallas_call | solution.py:577
  28.5 0.0 copy-start.15
  28.5 0.1 collective-permute-start
  28.6 5.1 %forward_2.1 = (bf16[60,64,128]{2,1,0:T(8,128)(2,1)}, bf16[32,64,128]{2,1,0:T(8,128)(2,1)}) custom-call(s32[1]{0:T(128)} %bitcast.index, bf16[1,63,192,252]{3,2,1,0:T(8,128)(2,1)} %bitcast.32, bf16[256,252]{1,0:T(8,128)(2,1)} %constant.59.clone.basis_all, bf16[2,32,64,128]{3,2,1,0:T(8,128)(2,1)} %constant.53.clone.pair_all), custom_call_target="tpu_custom_call" | custom-call | flops 1000000 | bytes 100000 | tf_op jit(solution)/shard_map/forward_2/pallas_call | solution.py:577
  33.7 2.1 %collective-permute-start.7 = (bf16[60,64,128]{2,1,0:T(8,128)(2,1)}, bf16[60,64,128]{2,1,0:T(8,128)(2,1)}, u32[]{:S(2)}, u32[]{:S(2)}) collective-permute-start(bf16[60,64,128]{2,1,0:T(8,128)(2,1)} %get-tuple-element.86.refs_0_), channel_id=1, source_target_pairs={{0,1},{1,0},{2,3},{3,2},{4,5},{5,4},{6,7},{7,6},{8,9},{9,8},{10,11... | collective-permute-start | bytes 2949128 | tf_op jit(solution)/shard_map/ppermute | solution.py:722
  35.7 0.1 copy.22
  35.9 0.1 rev.6
  36.0 0.0 copy-start.11
  36.0 0.0 copy-start.12
  36.0 0.7 fusion.11
  36.8 0.1 pad_add_fusion.side
  36.9 0.9 copy.24
  37.8 0.6 slice.54
  38.4 1.4 rev.7
  39.8 0.9 fusion.7
  40.7 1.2 pad_maximum_fusion.1
  41.9 0.1 slice_negate_fusion
  42.1 0.1 pad_maximum_fusion.2
  42.2 0.7 collective-permute-done.1.refs_1_
  43.0 1.0 copy-done.3
  44.0 1.0 copy-done.5
  45.0 2.8 %copy-done.7 = bf16[1,63,252,192]{2,3,1,0:T(8,128)(2,1)S(1)} copy-done((bf16[1,63,252,192]{2,3,1,0:T(8,128)(2,1)S(1)}, bf16[1,63,252,192]{2,3,1,0:T(8,128)(2,1)}, u32[]{:S(2)}) %copy-start.7) | copy-done | bytes 6096408
  47.8 12.1 %spectral_0.1 = (f32[64,128]{1,0:T(8,128)S(1)}, f32[64,128]{1,0:T(8,128)S(1)}) custom-call(s32[2]{0:T(128)S(1)} %pad_add_fusion.side, bf16[92,64,128]{2,1,0:T(8,128)(2,1)S(1)} %copy-done, bf16[92,64,128]{2,1,0:T(8,128)(2,1)} %collective-permute-done.1.refs_1_, bf16[32,128,256]{2,1,0:T(8,128)(2,1)S(1)} %bitcast.16, bf16[32,64,256]{2,1,0:T(8,128)(2,1)S(1)} %copy-done.2, ...), custom_call_target="tpu_custom_call" | custom-call | flops 8000000000 | bytes 30000000 | tf_op jit(solution)/shard_map/spectral_0/pallas_call | solution.py:623
  59.9 0.1 collective-permute-start.2
  60.0 1.2 collective-permute-done.2
  61.2 2.0 %collective-permute-start.3 = (f32[64,128]{1,0:T(8,128)S(1)}, f32[64,128]{1,0:T(8,128)S(1)}, u32[]{:S(2)}, u32[]{:S(2)}) collective-permute-start(f32[64,128]{1,0:T(8,128)S(1)} %add.55), channel_id=1, source_target_pairs={{0,4},{2,6},{4,0},{6,2},{8,12},{10,14},{12,8},{14,10},{16,20},{18,... | collective-permute-start | bytes 98312 | tf_op jit(solution)/shard_map/ppermute | solution.py:673
  63.2 0.1 pad_maximum_fusion.5
  63.4 1.6 %collective-permute-start.9 = (bf16[32,64,128]{2,1,0:T(8,128)(2,1)S(1)}, bf16[32,64,128]{2,1,0:T(8,128)(2,1)S(1)}, u32[]{:S(2)}, u32[]{:S(2)}) collective-permute-start(bf16[32,64,128]{2,1,0:T(8,128)(2,1)S(1)} %copy-done.10), channel_id=1, source_target_pairs={{0,1},{1,0},{2,3},{3,2},{4,5},{5,4},{6,7},{7,6},{8,9},{9,8},{10,11... | collective-permute-start | bytes 1572872 | tf_op jit(solution)/shard_map/ppermute | solution.py:722
  64.9 0.1 collective-permute-done.3
  65.1 10.1 %collective-permute-done.refs_1_ = bf16[92,64,128]{2,1,0:T(8,128)(2,1)} collective-permute-done((bf16[92,64,128]{2,1,0:T(8,128)(2,1)}, bf16[92,64,128]{2,1,0:T(8,128)(2,1)}, u32[]{:S(2)}, u32[]{:S(2)}) %collective-permute-start) | collective-permute-done | bytes 1507360 | tf_op jit(solution)/shard_map/ppermute | solution.py:722
  75.2 2.1 %collective-permute-start.4 = (f32[64,128]{1,0:T(8,128)S(1)}, f32[64,128]{1,0:T(8,128)S(1)}, u32[]{:S(2)}, u32[]{:S(2)}) collective-permute-start(f32[64,128]{1,0:T(8,128)S(1)} %add.56), channel_id=1, source_target_pairs={{0,8},{2,10},{4,12},{6,14},{8,0},{10,2},{12,4},{14,6},{16,24},{18,... | collective-permute-start | bytes 98312 | tf_op jit(solution)/shard_map/ppermute | solution.py:673
  77.4 2.8 %copy-done.8 = bf16[1,63,252,192]{2,3,1,0:T(8,128)(2,1)S(1)} copy-done((bf16[1,63,252,192]{2,3,1,0:T(8,128)(2,1)S(1)}, bf16[1,63,252,192]{2,3,1,0:T(8,128)(2,1)}, u32[]{:S(2)}) %copy-start.8) | copy-done | bytes 6096408
  80.1 12.1 %spectral_1.1 = (f32[64,128]{1,0:T(8,128)S(1)}, f32[64,128]{1,0:T(8,128)S(1)}) custom-call(s32[2]{0:T(128)S(1)} %pad_add_fusion.side, bf16[92,64,128]{2,1,0:T(8,128)(2,1)S(1)} %copy-done.1, bf16[92,64,128]{2,1,0:T(8,128)(2,1)} %collective-permute-done.refs_1_, bf16[32,128,256]{2,1,0:T(8,128)(2,1)S(1)} %bitcast.17, bf16[32,64,256]{2,1,0:T(8,128)(2,1)S(1)} %copy-done.2, ...), custom_call_target="tpu_custom_call" | custom-call | flops 8000000000 | bytes 30000000 | tf_op jit(solution)/shard_map/spectral_1/pallas_call | solution.py:623
  92.3 0.1 collective-permute-start.5
  92.3 2.6 %collective-permute-start.6 = (f32[64,128]{1,0:T(8,128)S(1)}, f32[64,128]{1,0:T(8,128)S(1)}, u32[]{:S(2)}, u32[]{:S(2)}) collective-permute-start(f32[64,128]{1,0:T(8,128)S(1)} %add.57), channel_id=1, source_target_pairs={{0,16},{2,18},{4,20},{6,22},{8,24},{10,26},{12,28},{14,30},{16,0},... | collective-permute-start | bytes 98312 | tf_op jit(solution)/shard_map/ppermute | solution.py:673
  95.0 1.3 collective-permute-done.7.refs_1_
  96.3 4.5 %low_2.1 = (f32[4608,128]{1,0:T(8,128)S(1)}, bf16[64,128,128]{2,1,0:T(8,128)(2,1)S(1)}, bf16[64,128,128]{2,1,0:T(8,128)(2,1)S(1)}) custom-call(bf16[60,64,128]{2,1,0:T(8,128)(2,1)S(1)} %copy-done.9, bf16[60,64,128]{2,1,0:T(8,128)(2,1)} %collective-permute-done.7.refs_1_, bf16[32,128,256]{2,1,0:T(8,128)(2,1)S(1)} %bitcast.18, ...), custom_call_target="tpu_custom_call" | custom-call | flops 8000000000 | bytes 30000000 | tf_op jit(solution)/shard_map/low_2/pallas_call | solution.py:602
  100.8 2.1 %collective-permute-start.8 = (f32[64,128]{1,0:T(8,128)S(1)}, f32[64,128]{1,0:T(8,128)S(1)}, u32[]{:S(2)}, u32[]{:S(2)}) collective-permute-start(f32[64,128]{1,0:T(8,128)S(1)} %add.58), channel_id=1, source_target_pairs={{0,1},{1,0},{2,3},{3,2},{4,5},{5,4},{6,7},{7,6},{8,9},{9,8},{10,11... | collective-permute-start | bytes 98312 | tf_op jit(solution)/shard_map/ppermute | solution.py:673
  103.0 1.5 %collective-permute-start.10 = (f32[64,128]{1,0:T(8,128)S(1)}, f32[64,128]{1,0:T(8,128)S(1)}, u32[]{:S(2)}, u32[]{:S(2)}) collective-permute-start(f32[64,128]{1,0:T(8,128)S(1)} %add.59), channel_id=1, source_target_pairs={{0,4},{2,6},{4,0},{6,2},{8,12},{10,14},{12,8},{14,10},{16,20},{18,... | collective-permute-start | bytes 98312 | tf_op jit(solution)/shard_map/ppermute | solution.py:673
  104.4 2.5 %collective-permute-done.9.refs_1_ = bf16[32,64,128]{2,1,0:T(8,128)(2,1)S(1)} collective-permute-done((bf16[32,64,128]{2,1,0:T(8,128)(2,1)S(1)}, bf16[32,64,128]{2,1,0:T(8,128)(2,1)S(1)}, u32[]{:S(2)}, u32[]{:S(2)}) %collective-permute-start.9) | collective-permute-done | bytes 524320 | tf_op jit(solution)/shard_map/ppermute | solution.py:722
  107.0 9.0 %spectral_2.1 = (f32[64,128]{1,0:T(8,128)S(1)}, f32[64,128]{1,0:T(8,128)S(1)}) custom-call(s32[2]{0:T(128)S(1)} %pad_add_fusion.side, bf16[32,64,128]{2,1,0:T(8,128)(2,1)S(1)} %copy-done.10, bf16[32,64,128]{2,1,0:T(8,128)(2,1)S(1)} %collective-permute-done.9.refs_1_, f32[4608,128]{1,0:T(8,128)S(1)} %get-tuple-element.102.refs_2_, ...), custom_call_target="tpu_custom_call" | custom-call | flops 8000000000 | bytes 30000000 | tf_op jit(solution)/shard_map/spectral_2/pallas_call | solution.py:623
  116.0 0.1 collective-permute-start.11
  116.1 1.2 collective-permute-done.11
  117.3 1.7 %collective-permute-start.12 = (f32[64,128]{1,0:T(8,128)S(1)}, f32[64,128]{1,0:T(8,128)S(1)}, u32[]{:S(2)}, u32[]{:S(2)}) collective-permute-start(f32[64,128]{1,0:T(8,128)S(1)} %add.62), channel_id=1, source_target_pairs={{0,4},{2,6},{4,0},{6,2},{8,12},{10,14},{12,8},{14,10},{16,20},{18,... | collective-permute-start | bytes 98312 | tf_op jit(solution)/shard_map/ppermute | solution.py:673
  119.0 2.2 %collective-permute-done.12 = f32[64,128]{1,0:T(8,128)S(1)} collective-permute-done((f32[64,128]{1,0:T(8,128)S(1)}, f32[64,128]{1,0:T(8,128)S(1)}, u32[]{:S(2)}, u32[]{:S(2)}) %collective-permute-start.12) | collective-permute-done | bytes 32800 | tf_op jit(solution)/shard_map/ppermute | solution.py:673
  121.2 1.9 %collective-permute-start.13 = (f32[128,128]{1,0:T(8,128)S(1)}, f32[128,128]{1,0:T(8,128)S(1)}, u32[]{:S(2)}, u32[]{:S(2)}) collective-permute-start(f32[128,128]{1,0:T(8,128)S(1)} %pad_maximum_fusion.8), channel_id=1, source_target_pairs={{0,8},{2,10},{4,12},{6,14},{8,0},{10,2},{12,4},{14,6},{16,24},{18,... | collective-permute-start | bytes 196616 | tf_op jit(solution)/shard_map/ppermute | solution.py:673
  123.1 2.5 %collective-permute-done.13 = f32[128,128]{1,0:T(8,128)S(1)} collective-permute-done((f32[128,128]{1,0:T(8,128)S(1)}, f32[128,128]{1,0:T(8,128)S(1)}, u32[]{:S(2)}, u32[]{:S(2)}) %collective-permute-start.13) | collective-permute-done | bytes 65568 | tf_op jit(solution)/shard_map/ppermute | solution.py:673
  125.6 2.9 %collective-permute-start.14 = (f32[128,128]{1,0:T(8,128)S(1)}, f32[128,128]{1,0:T(8,128)S(1)}, u32[]{:S(2)}, u32[]{:S(2)}) collective-permute-start(f32[128,128]{1,0:T(8,128)S(1)} %fusion.9), channel_id=1, source_target_pairs={{0,16},{2,18},{4,20},{6,22},{8,24},{10,26},{12,28},{14,30},{16,0},... | collective-permute-start | bytes 196616 | tf_op jit(solution)/shard_map/ppermute | solution.py:673
  128.4 2.4 %collective-permute-done.14 = f32[128,128]{1,0:T(8,128)S(1)} collective-permute-done((f32[128,128]{1,0:T(8,128)S(1)}, f32[128,128]{1,0:T(8,128)S(1)}, u32[]{:S(2)}, u32[]{:S(2)}) %collective-permute-start.14) | collective-permute-done | bytes 65568 | tf_op jit(solution)/shard_map/ppermute | solution.py:673
  130.8 1.8 %collective-permute-start.15 = (f32[128,128]{1,0:T(8,128)S(1)}, f32[128,128]{1,0:T(8,128)S(1)}, u32[]{:S(2)}, u32[]{:S(2)}) collective-permute-start(f32[128,128]{1,0:T(8,128)S(1)} %add.65), channel_id=1, source_target_pairs={{0,1},{1,0},{2,3},{3,2},{4,5},{5,4},{6,7},{7,6},{8,9},{9,8},{10,11... | collective-permute-start | bytes 196616 | tf_op jit(solution)/shard_map/ppermute | solution.py:673
  132.6 2.5 %collective-permute-done.15 = f32[128,128]{1,0:T(8,128)S(1)} collective-permute-done((f32[128,128]{1,0:T(8,128)S(1)}, f32[128,128]{1,0:T(8,128)S(1)}, u32[]{:S(2)}, u32[]{:S(2)}) %collective-permute-start.15) | collective-permute-done | bytes 65568 | tf_op jit(solution)/shard_map/ppermute | solution.py:673
  135.2 0.1 collective-permute-start.16
  135.2 1.3 collective-permute-done.16
  136.5 0.7 multiply_bitcast_fusion
  (51 shorter events, 0.2 us)
Async XLA Ops:
  5.8 37.2 %collective-permute-start.1 = (bf16[92,64,128]{2,1,0:T(8,128)(2,1)}, bf16[92,64,128]{2,1,0:T(8,128)(2,1)}, u32[]{:S(2)}, u32[]{:S(2)}) collective-permute-start(bf16[92,64,128]{2,1,0:T(8,128)(2,1)} %forward_0.1.refs_0_), channel_id=1, source_target_pairs={{0,1},{1,0},{2,3},{3,2},{4,5},{5,4},{6,7},{7,6},{8,9},{9,8},{10,11... | collective-permute-start | bytes 4521992 | tf_op jit(solution)/shard_map/ppermute | solution.py:722
  8.8 3.4 %copy-start.13 = (bf16[64,128,128]{2,1,0:T(8,128)(2,1)S(1)}, bf16[64,128,128]{2,1,0:T(8,128)(2,1)}, u32[]{:S(2)}) copy-start(bf16[64,128,128]{2,1,0:T(8,128)(2,1)} %constant.54.clone) | copy-start | bytes 6291460
  12.2 3.0 %copy-start.14 = (bf16[2,16,64,256]{3,2,1,0:T(8,128)(2,1)S(1)}, bf16[2,16,64,256]{3,2,1,0:T(8,128)(2,1)}, u32[]{:S(2)}) copy-start(bf16[2,16,64,256]{3,2,1,0:T(8,128)(2,1)} %constant.57.clone) | copy-start | bytes 3145732
  28.5 7.3 %copy-start.15 = (bf16[126,192]{0,1:T(8,128)(2,1)S(1)}, bf16[126,192]{0,1:T(8,128)(2,1)}, u32[]{:S(2)}) copy-start(bf16[126,192]{0,1:T(8,128)(2,1)} %param.16) | copy-start | bytes 145156
  28.5 46.8 %collective-permute-start = (bf16[92,64,128]{2,1,0:T(8,128)(2,1)}, bf16[92,64,128]{2,1,0:T(8,128)(2,1)}, u32[]{:S(2)}, u32[]{:S(2)}) collective-permute-start(bf16[92,64,128]{2,1,0:T(8,128)(2,1)} %forward_1.1.refs_0_), channel_id=1, source_target_pairs={{0,1},{1,0},{2,3},{3,2},{4,5},{5,4},{6,7},{7,6},{8,9},{9,8},{10,11... | collective-permute-start | bytes 4521992 | tf_op jit(solution)/shard_map/ppermute | solution.py:722
  33.7 62.6 %collective-permute-start.7 = (bf16[60,64,128]{2,1,0:T(8,128)(2,1)}, bf16[60,64,128]{2,1,0:T(8,128)(2,1)}, u32[]{:S(2)}, u32[]{:S(2)}) collective-permute-start(bf16[60,64,128]{2,1,0:T(8,128)(2,1)} %get-tuple-element.86.refs_0_), channel_id=1, source_target_pairs={{0,1},{1,0},{2,3},{3,2},{4,5},{5,4},{6,7},{7,6},{8,9},{9,8},{10,11... | collective-permute-start | bytes 2949128 | tf_op jit(solution)/shard_map/ppermute | solution.py:722
  36.0 7.0 %copy-start.11 = (bf16[256,252]{1,0:T(8,128)(2,1)S(1)}, bf16[256,252]{1,0:T(8,128)(2,1)}, u32[]{:S(2)}) copy-start(bf16[256,252]{1,0:T(8,128)(2,1)} %constant.52.clone.refs_6_.refs_7_) | copy-start | bytes 387076
  36.0 6.9 %copy-start.12 = (f32[128,128]{1,0:T(8,128)S(1)}, f32[128,128]{1,0:T(8,128)}, u32[]{:S(2)}) copy-start(f32[128,128]{1,0:T(8,128)} %constant.58.clone.refs_10_.refs_11_) | copy-start | bytes 196612
  39.8 3.2 %copy-start = (bf16[92,64,128]{2,1,0:T(8,128)(2,1)S(1)}, bf16[92,64,128]{2,1,0:T(8,128)(2,1)}, u32[]{:S(2)}) copy-start(bf16[92,64,128]{2,1,0:T(8,128)(2,1)} %forward_0.1.refs_0_) | copy-start | bytes 4521988
  39.8 3.2 %copy-start.2 = (bf16[32,64,256]{2,1,0:T(8,128)(2,1)S(1)}, bf16[32,64,256]{2,1,0:T(8,128)(2,1)}, u32[]{:S(2)}) copy-start(bf16[32,64,256]{2,1,0:T(8,128)(2,1)} %pad_maximum_fusion.refs_3_) | copy-start | bytes 3145732
  43.0 1.0 copy-start.3
  44.0 1.0 copy-start.5
  45.0 2.8 %copy-start.7 = (bf16[1,63,252,192]{2,3,1,0:T(8,128)(2,1)S(1)}, bf16[1,63,252,192]{2,3,1,0:T(8,128)(2,1)}, u32[]{:S(2)}) copy-start(bf16[1,63,252,192]{2,3,1,0:T(8,128)(2,1)} %param.15) | copy-start | bytes 18289156
  47.8 15.5 %copy-start.10 = (bf16[32,64,128]{2,1,0:T(8,128)(2,1)S(1)}, bf16[32,64,128]{2,1,0:T(8,128)(2,1)}, u32[]{:S(2)}) copy-start(bf16[32,64,128]{2,1,0:T(8,128)(2,1)} %get-tuple-element.101.refs_0_) | copy-start | bytes 1572868
  47.8 29.6 %copy-start.1 = (bf16[92,64,128]{2,1,0:T(8,128)(2,1)S(1)}, bf16[92,64,128]{2,1,0:T(8,128)(2,1)}, u32[]{:S(2)}) copy-start(bf16[92,64,128]{2,1,0:T(8,128)(2,1)} %forward_1.1.refs_0_) | copy-start | bytes 4521988
  59.9 1.3 collective-permute-start.2
  61.2 3.9 %collective-permute-start.3 = (f32[64,128]{1,0:T(8,128)S(1)}, f32[64,128]{1,0:T(8,128)S(1)}, u32[]{:S(2)}, u32[]{:S(2)}) collective-permute-start(f32[64,128]{1,0:T(8,128)S(1)} %add.55), channel_id=1, source_target_pairs={{0,4},{2,6},{4,0},{6,2},{8,12},{10,14},{12,8},{14,10},{16,20},{18,... | collective-permute-start | bytes 98312 | tf_op jit(solution)/shard_map/ppermute | solution.py:673
  63.4 43.6 %collective-permute-start.9 = (bf16[32,64,128]{2,1,0:T(8,128)(2,1)S(1)}, bf16[32,64,128]{2,1,0:T(8,128)(2,1)S(1)}, u32[]{:S(2)}, u32[]{:S(2)}) collective-permute-start(bf16[32,64,128]{2,1,0:T(8,128)(2,1)S(1)} %copy-done.10), channel_id=1, source_target_pairs={{0,1},{1,0},{2,3},{3,2},{4,5},{5,4},{6,7},{7,6},{8,9},{9,8},{10,11... | collective-permute-start | bytes 1572872 | tf_op jit(solution)/shard_map/ppermute | solution.py:722
  75.2 17.0 %collective-permute-start.4 = (f32[64,128]{1,0:T(8,128)S(1)}, f32[64,128]{1,0:T(8,128)S(1)}, u32[]{:S(2)}, u32[]{:S(2)}) collective-permute-start(f32[64,128]{1,0:T(8,128)S(1)} %add.56), channel_id=1, source_target_pairs={{0,8},{2,10},{4,12},{6,14},{8,0},{10,2},{12,4},{14,6},{16,24},{18,... | collective-permute-start | bytes 98312 | tf_op jit(solution)/shard_map/ppermute | solution.py:673
  77.4 2.8 %copy-start.8 = (bf16[1,63,252,192]{2,3,1,0:T(8,128)(2,1)S(1)}, bf16[1,63,252,192]{2,3,1,0:T(8,128)(2,1)}, u32[]{:S(2)}) copy-start(bf16[1,63,252,192]{2,3,1,0:T(8,128)(2,1)} %param.15) | copy-start | bytes 18289156
  80.1 16.2 %copy-start.9 = (bf16[60,64,128]{2,1,0:T(8,128)(2,1)S(1)}, bf16[60,64,128]{2,1,0:T(8,128)(2,1)}, u32[]{:S(2)}) copy-start(bf16[60,64,128]{2,1,0:T(8,128)(2,1)} %get-tuple-element.86.refs_0_) | copy-start | bytes 2949124
  80.1 26.8 %slice-start = ((s8[6193152]{0:T(1024)(128)(4,1)}), s8[4194304]{0:T(1024)(128)(4,1)S(1)}, s32[]{:S(2)}) async-start(s8[6193152]{0:T(1024)(128)(4,1)} %bitcast.26), calls=%async_computation | async-start | bytes 8388608
  92.3 8.5 %collective-permute-start.5 = (f32[64,128]{1,0:T(8,128)S(1)}, f32[64,128]{1,0:T(8,128)S(1)}, u32[]{:S(2)}, u32[]{:S(2)}) collective-permute-start(f32[64,128]{1,0:T(8,128)S(1)} %get-tuple-element.82), channel_id=1, source_target_pairs={{0,2},{2,0},{4,6},{6,4},{8,10},{10,8},{12,14},{14,12},{16,18},{18,... | collective-permute-start | bytes 98312 | tf_op jit(solution)/shard_map/ppermute | solution.py:745
  92.3 8.4 %collective-permute-start.6 = (f32[64,128]{1,0:T(8,128)S(1)}, f32[64,128]{1,0:T(8,128)S(1)}, u32[]{:S(2)}, u32[]{:S(2)}) collective-permute-start(f32[64,128]{1,0:T(8,128)S(1)} %add.57), channel_id=1, source_target_pairs={{0,16},{2,18},{4,20},{6,22},{8,24},{10,26},{12,28},{14,30},{16,0},... | collective-permute-start | bytes 98312 | tf_op jit(solution)/shard_map/ppermute | solution.py:673
  96.3 10.7 %copy-start.4 = (bf16[16,128,128]{2,1,0:T(8,128)(2,1)S(1)}, bf16[16,128,128]{2,1,0:T(8,128)(2,1)}, u32[]{:S(2)}) copy-start(bf16[16,128,128]{2,1,0:T(8,128)(2,1)} %dynamic-slice_bitcast_fusion.1.refs_8_.refs_9_) | copy-start | bytes 1572868
  96.3 10.7 %copy-start.6 = (bf16[16,64,256]{2,1,0:T(8,128)(2,1)S(1)}, bf16[16,64,256]{2,1,0:T(8,128)(2,1)}, u32[]{:S(2)}) copy-start(bf16[16,64,256]{2,1,0:T(8,128)(2,1)} %dynamic-slice_bitcast_fusion.refs_9_.refs_10_) | copy-start | bytes 1572868
  96.3 10.7 %slice-start.1 = ((s8[6193152]{0:T(1024)(128)(4,1)}), s8[1998848]{0:T(1024)(128)(4,1)S(1)}, s32[]{:S(2)}) async-start(s8[6193152]{0:T(1024)(128)(4,1)} %bitcast.26), calls=%async_computation.1 | async-start | bytes 3997696
  100.8 15.2 %collective-permute-start.8 = (f32[64,128]{1,0:T(8,128)S(1)}, f32[64,128]{1,0:T(8,128)S(1)}, u32[]{:S(2)}, u32[]{:S(2)}) collective-permute-start(f32[64,128]{1,0:T(8,128)S(1)} %add.58), channel_id=1, source_target_pairs={{0,1},{1,0},{2,3},{3,2},{4,5},{5,4},{6,7},{7,6},{8,9},{9,8},{10,11... | collective-permute-start | bytes 98312 | tf_op jit(solution)/shard_map/ppermute | solution.py:673
  103.0 13.0 %collective-permute-start.10 = (f32[64,128]{1,0:T(8,128)S(1)}, f32[64,128]{1,0:T(8,128)S(1)}, u32[]{:S(2)}, u32[]{:S(2)}) collective-permute-start(f32[64,128]{1,0:T(8,128)S(1)} %add.59), channel_id=1, source_target_pairs={{0,4},{2,6},{4,0},{6,2},{8,12},{10,14},{12,8},{14,10},{16,20},{18,... | collective-permute-start | bytes 98312 | tf_op jit(solution)/shard_map/ppermute | solution.py:673
  116.0 1.3 collective-permute-start.11
  117.3 3.9 %collective-permute-start.12 = (f32[64,128]{1,0:T(8,128)S(1)}, f32[64,128]{1,0:T(8,128)S(1)}, u32[]{:S(2)}, u32[]{:S(2)}) collective-permute-start(f32[64,128]{1,0:T(8,128)S(1)} %add.62), channel_id=1, source_target_pairs={{0,4},{2,6},{4,0},{6,2},{8,12},{10,14},{12,8},{14,10},{16,20},{18,... | collective-permute-start | bytes 98312 | tf_op jit(solution)/shard_map/ppermute | solution.py:673
  121.2 4.3 %collective-permute-start.13 = (f32[128,128]{1,0:T(8,128)S(1)}, f32[128,128]{1,0:T(8,128)S(1)}, u32[]{:S(2)}, u32[]{:S(2)}) collective-permute-start(f32[128,128]{1,0:T(8,128)S(1)} %pad_maximum_fusion.8), channel_id=1, source_target_pairs={{0,8},{2,10},{4,12},{6,14},{8,0},{10,2},{12,4},{14,6},{16,24},{18,... | collective-permute-start | bytes 196616 | tf_op jit(solution)/shard_map/ppermute | solution.py:673
  125.6 5.2 %collective-permute-start.14 = (f32[128,128]{1,0:T(8,128)S(1)}, f32[128,128]{1,0:T(8,128)S(1)}, u32[]{:S(2)}, u32[]{:S(2)}) collective-permute-start(f32[128,128]{1,0:T(8,128)S(1)} %fusion.9), channel_id=1, source_target_pairs={{0,16},{2,18},{4,20},{6,22},{8,24},{10,26},{12,28},{14,30},{16,0},... | collective-permute-start | bytes 196616 | tf_op jit(solution)/shard_map/ppermute | solution.py:673
  130.8 4.3 %collective-permute-start.15 = (f32[128,128]{1,0:T(8,128)S(1)}, f32[128,128]{1,0:T(8,128)S(1)}, u32[]{:S(2)}, u32[]{:S(2)}) collective-permute-start(f32[128,128]{1,0:T(8,128)S(1)} %add.65), channel_id=1, source_target_pairs={{0,1},{1,0},{2,3},{3,2},{4,5},{5,4},{6,7},{7,6},{8,9},{9,8},{10,11... | collective-permute-start | bytes 196616 | tf_op jit(solution)/shard_map/ppermute | solution.py:673
  135.2 1.4 collective-permute-start.16

commit v12 on v11

--- a/solution.py
+++ b/solution.py
@@ -580,7 +580,7 @@
         out_specs=[anywhere] * len(counts),
         out_shape=[jax.ShapeDtypeStruct((count, layout.rows, LANES), jnp.bfloat16) for count in counts],
         scratch_shapes=[
-            pltpu.VMEM((slots * layout.pitch, LANES), jnp.float32),
+            pltpu.VMEM(((slots + 1) * layout.pitch, LANES), jnp.float32),
             pltpu.VMEM((layout.rows, LANES // 2, NLON), jnp.bfloat16),
             pltpu.VMEM(basis.shape, jnp.bfloat16),
             pltpu.VMEM((layout.blocks, layout.rows, LANES), jnp.bfloat16),
@@ -605,7 +605,7 @@
         out_specs=[whole()] * 3,
         out_shape=[jax.ShapeDtypeStruct((2 * layout.twos * layout.pitch, LANES), jnp.float32), spectra, spectra],
         scratch_shapes=[
-            pltpu.VMEM((layout.sent * TAIL, LANES), jnp.float32),
+            pltpu.VMEM(((layout.sent + 8) * TAIL, LANES), jnp.float32),
             pltpu.VMEM((layout.parts * MOVED * layout.rows, LANES), jnp.float32),
         ],
         compiler_params=pltpu.CompilerParams(vmem_limit_bytes=VMEM),
@@ -627,13 +627,13 @@
         out_specs=[whole()] * 2,
         out_shape=[half, half],
         scratch_shapes=[
-            pltpu.VMEM((layout.slots * layout.pitch, LANES), jnp.float32),
-            pltpu.VMEM((layout.slots * layout.pitch, LANES), jnp.float32),
+            pltpu.VMEM(((layout.slots + 1) * layout.pitch, LANES), jnp.float32),
+            pltpu.VMEM(((layout.slots + 1) * layout.pitch, LANES), jnp.float32),
             pltpu.VMEM((2 * layout.twos, layout.degrees, LANES), jnp.bfloat16),
             pltpu.VMEM((2 * layout.twos, layout.degrees, LANES), jnp.bfloat16),
             pltpu.VMEM((layout.pairs, layout.rows, LANES), jnp.bfloat16),
             pltpu.VMEM((layout.pairs, layout.rows, LANES), jnp.bfloat16),
-            pltpu.VMEM((layout.sent * TAIL, LANES), jnp.float32),
+            pltpu.VMEM(((layout.sent + 8) * TAIL, LANES), jnp.float32),
             pltpu.VMEM((layout.parts * MOVED * layout.rows, LANES), jnp.float32),
             pltpu.SemaphoreType.DMA((3,)),
         ],

time: 138 us -> 138 us (level)
  no operation moved by 1% of the time
where the time goes in v12:
time: 138 us; the launch traced here: 137 us
  Pallas kernels  53 us (38%)
  waiting for transfers between devices  28 us (20%)
  starting transfers between devices  25.7 us (19%)
  local copies, waits for them, and re-layouts  24.9 us (18%)
  other arithmetic  4.57 us (3%)
    pallas_call x3, Pallas kernels, spectral_call(): pl.pallas_call(functools.partial(spectral_kernel, layout, apart), grid=(l...  33.2 us
    ppermute x9, starting transfers between devices, hop_parcels(): parcels.append(lax.ppermute(value, axis, pairs))  18.7 us
    pallas_call x3, Pallas kernels, forward_call(): pl.pallas_call(functools.partial(forward_kernel, layout, chunk, bounds),...  15.4 us
    ppermute x4, waiting for transfers between devices, others(): return [lax.ppermute(sent, 'space', route) for route in routes]  14.7 us
    ppermute x9, waiting for transfers between devices, hop_parcels(): parcels.append(lax.ppermute(value, axis, pairs))  9.68 us
    unnamed x38, local copies, waits for them, and re-layouts  8.68 us
    ppermute x4, starting transfers between devices, others(): return [lax.ppermute(sent, 'space', route) for route in routes]  6.8 us
    pallas_call x1, Pallas kernels, low_call(): pl.pallas_call(functools.partial(low_kernel, layout), in_specs=[whole()]...  4.46 us
  transfers between devices with their start and end apart: 17, of which 12 were waited for; matrix products, arithmetic and copies ran while one was open for 15% of the time, Pallas kernels for 35%

profile of v12, /device:TPU:0, one launch (start us, length us, event | category | flops | bytes accessed | tf_op | source)
XLA Modules:
  0.0 137.2 jit_solution(12964661952249801281)
XLA Ops:
  0.6 5.1 %forward_0.1.refs_0_ = bf16[92,64,128]{2,1,0:T(8,128)(2,1)} custom-call(s32[1]{0:T(128)} %bitcast.index, bf16[1,63,192,252]{3,2,1,0:T(8,128)(2,1)} %bitcast.30, bf16[256,252]{1,0:T(8,128)(2,1)} %constant.59.clone.basis_all, bf16[2,32,64,128]{3,2,1,0:T(8,128)(2,1)} %constant.53.clone.pair_all), custom_call_target="tpu_custom_call" | custom-call | flops 1000000 | bytes 100000 | tf_op jit(solution)/shard_map/forward_0/pallas_call | solution.py:577
  5.8 3.0 %collective-permute-start.1 = (bf16[92,64,128]{2,1,0:T(8,128)(2,1)}, bf16[92,64,128]{2,1,0:T(8,128)(2,1)}, u32[]{:S(2)}, u32[]{:S(2)}) collective-permute-start(bf16[92,64,128]{2,1,0:T(8,128)(2,1)} %forward_0.1.refs_0_), channel_id=1, source_target_pairs={{0,1},{1,0},{2,3},{3,2},{4,5},{5,4},{6,7},{7,6},{8,9},{9,8},{10,11... | collective-permute-start | bytes 4521992 | tf_op jit(solution)/shard_map/ppermute | solution.py:722
  8.8 3.4 %constant_dynamic-slice_fusion.1 = bf16[64,128,128]{2,1,0:T(8,128)(2,1)} fusion(bf16[64,256,128]{2,1,0:T(8,128)(2,1)} %constant.55.clone, s32[]{:T(128)S(6)} %select_n.25), kind=kLoop, calls=%fused_computation.26 | loop fusion | bytes 4194308 | tf_op jit(solution)/shard_map/dynamic_slice | solution.py:702
  12.2 1.1 constant_dynamic-slice_fusion
  13.3 1.9 %dynamic-slice_bitcast_fusion.1.refs_8_.refs_9_ = bf16[16,128,128]{2,1,0:T(8,128)(2,1)} fusion(bf16[2,16,128,128]{3,2,1,0:T(8,128)(2,1)} %constant.56.clone, s32[]{:T(128)S(6)} %select_n.27), kind=kLoop, calls=%fused_computation.2 | loop fusion | bytes 1048580 | tf_op jit(solution)/shard_map/jit(dynamic_index_in_dim)/squeeze | solution.py:695
  15.2 0.9 dynamic-slice_bitcast_fusion.refs_9_.refs_10_
  16.0 3.3 %copy.20 = bf16[32,256,128]{1,2,0:T(8,128)(2,1)S(1)} copy(bf16[32,256,128]{2,1,0:T(8,128)(2,1)} %bitcast.34) | data formatting | bytes 4194304 | tf_op jit(solution)/shard_map/reshape | solution.py:709
  19.3 1.6 %copy.21 = bf16[32,128,128]{1,2,0:T(8,128)(2,1)S(1)} copy(bf16[32,128,128]{2,1,0:T(8,128)(2,1)} %bitcast.33) | data formatting | bytes 2097152 | tf_op jit(solution)/shard_map/reshape | solution.py:711
  20.9 1.3 fusion.10
  22.2 1.1 pad_maximum_fusion.refs_3_
  23.4 5.1 %forward_1.1.refs_0_ = bf16[92,64,128]{2,1,0:T(8,128)(2,1)} custom-call(s32[1]{0:T(128)} %bitcast.index, bf16[1,63,192,252]{3,2,1,0:T(8,128)(2,1)} %bitcast.31, bf16[256,252]{1,0:T(8,128)(2,1)} %constant.59.clone.basis_all, bf16[2,32,64,128]{3,2,1,0:T(8,128)(2,1)} %constant.53.clone.pair_all), custom_call_target="tpu_custom_call" | custom-call | flops 1000000 | bytes 100000 | tf_op jit(solution)/shard_map/forward_1/pallas_call | solution.py:577
  28.5 0.0 copy-start.15
  28.5 0.1 collective-permute-start
  28.6 5.1 %forward_2.1 = (bf16[60,64,128]{2,1,0:T(8,128)(2,1)}, bf16[32,64,128]{2,1,0:T(8,128)(2,1)}) custom-call(s32[1]{0:T(128)} %bitcast.index, bf16[1,63,192,252]{3,2,1,0:T(8,128)(2,1)} %bitcast.32, bf16[256,252]{1,0:T(8,128)(2,1)} %constant.59.clone.basis_all, bf16[2,32,64,128]{3,2,1,0:T(8,128)(2,1)} %constant.53.clone.pair_all), custom_call_target="tpu_custom_call" | custom-call | flops 1000000 | bytes 100000 | tf_op jit(solution)/shard_map/forward_2/pallas_call | solution.py:577
  33.7 2.1 %collective-permute-start.7 = (bf16[60,64,128]{2,1,0:T(8,128)(2,1)}, bf16[60,64,128]{2,1,0:T(8,128)(2,1)}, u32[]{:S(2)}, u32[]{:S(2)}) collective-permute-start(bf16[60,64,128]{2,1,0:T(8,128)(2,1)} %get-tuple-element.86.refs_0_), channel_id=1, source_target_pairs={{0,1},{1,0},{2,3},{3,2},{4,5},{5,4},{6,7},{7,6},{8,9},{9,8},{10,11... | collective-permute-start | bytes 2949128 | tf_op jit(solution)/shard_map/ppermute | solution.py:722
  35.8 0.1 copy.22
  35.9 0.1 rev.6
  36.0 0.0 copy-start.11
  36.0 0.0 copy-start.12
  36.1 0.7 fusion.11
  36.8 0.1 pad_add_fusion.side
  36.9 0.9 copy.24
  37.8 0.6 slice.54
  38.4 1.4 rev.7
  39.8 0.9 fusion.7
  40.7 1.2 pad_maximum_fusion.1
  42.0 0.1 slice_negate_fusion
  42.1 0.1 pad_maximum_fusion.2
  42.2 0.7 collective-permute-done.1.refs_1_
  43.0 1.0 copy-done.3
  44.0 1.0 copy-done.5
  45.1 2.8 %copy-done.7 = bf16[1,63,252,192]{2,3,1,0:T(8,128)(2,1)S(1)} copy-done((bf16[1,63,252,192]{2,3,1,0:T(8,128)(2,1)S(1)}, bf16[1,63,252,192]{2,3,1,0:T(8,128)(2,1)}, u32[]{:S(2)}) %copy-start.7) | copy-done | bytes 6096408
  47.8 12.1 %spectral_0.1 = (f32[64,128]{1,0:T(8,128)S(1)}, f32[64,128]{1,0:T(8,128)S(1)}) custom-call(s32[2]{0:T(128)S(1)} %pad_add_fusion.side, bf16[92,64,128]{2,1,0:T(8,128)(2,1)S(1)} %copy-done, bf16[92,64,128]{2,1,0:T(8,128)(2,1)} %collective-permute-done.1.refs_1_, bf16[32,128,256]{2,1,0:T(8,128)(2,1)S(1)} %bitcast.16, bf16[32,64,256]{2,1,0:T(8,128)(2,1)S(1)} %copy-done.2, ...), custom_call_target="tpu_custom_call" | custom-call | flops 8000000000 | bytes 30000000 | tf_op jit(solution)/shard_map/spectral_0/pallas_call | solution.py:623
  59.9 0.1 collective-permute-start.2
  60.0 1.2 collective-permute-done.2
  61.2 2.0 %collective-permute-start.3 = (f32[64,128]{1,0:T(8,128)S(1)}, f32[64,128]{1,0:T(8,128)S(1)}, u32[]{:S(2)}, u32[]{:S(2)}) collective-permute-start(f32[64,128]{1,0:T(8,128)S(1)} %add.55), channel_id=1, source_target_pairs={{0,4},{2,6},{4,0},{6,2},{8,12},{10,14},{12,8},{14,10},{16,20},{18,... | collective-permute-start | bytes 98312 | tf_op jit(solution)/shard_map/ppermute | solution.py:673
  63.2 0.1 pad_maximum_fusion.5
  63.4 1.6 %collective-permute-start.9 = (bf16[32,64,128]{2,1,0:T(8,128)(2,1)S(1)}, bf16[32,64,128]{2,1,0:T(8,128)(2,1)S(1)}, u32[]{:S(2)}, u32[]{:S(2)}) collective-permute-start(bf16[32,64,128]{2,1,0:T(8,128)(2,1)S(1)} %copy-done.10), channel_id=1, source_target_pairs={{0,1},{1,0},{2,3},{3,2},{4,5},{5,4},{6,7},{7,6},{8,9},{9,8},{10,11... | collective-permute-start | bytes 1572872 | tf_op jit(solution)/shard_map/ppermute | solution.py:722
  65.0 0.1 collective-permute-done.3
  65.1 10.1 %collective-permute-done.refs_1_ = bf16[92,64,128]{2,1,0:T(8,128)(2,1)} collective-permute-done((bf16[92,64,128]{2,1,0:T(8,128)(2,1)}, bf16[92,64,128]{2,1,0:T(8,128)(2,1)}, u32[]{:S(2)}, u32[]{:S(2)}) %collective-permute-start) | collective-permute-done | bytes 1507360 | tf_op jit(solution)/shard_map/ppermute | solution.py:722
  75.3 2.1 %collective-permute-start.4 = (f32[64,128]{1,0:T(8,128)S(1)}, f32[64,128]{1,0:T(8,128)S(1)}, u32[]{:S(2)}, u32[]{:S(2)}) collective-permute-start(f32[64,128]{1,0:T(8,128)S(1)} %add.56), channel_id=1, source_target_pairs={{0,8},{2,10},{4,12},{6,14},{8,0},{10,2},{12,4},{14,6},{16,24},{18,... | collective-permute-start | bytes 98312 | tf_op jit(solution)/shard_map/ppermute | solution.py:673
  77.4 2.8 %copy-done.8 = bf16[1,63,252,192]{2,3,1,0:T(8,128)(2,1)S(1)} copy-done((bf16[1,63,252,192]{2,3,1,0:T(8,128)(2,1)S(1)}, bf16[1,63,252,192]{2,3,1,0:T(8,128)(2,1)}, u32[]{:S(2)}) %copy-start.8) | copy-done | bytes 6096408
  80.1 12.1 %spectral_1.1 = (f32[64,128]{1,0:T(8,128)S(1)}, f32[64,128]{1,0:T(8,128)S(1)}) custom-call(s32[2]{0:T(128)S(1)} %pad_add_fusion.side, bf16[92,64,128]{2,1,0:T(8,128)(2,1)S(1)} %copy-done.1, bf16[92,64,128]{2,1,0:T(8,128)(2,1)} %collective-permute-done.refs_1_, bf16[32,128,256]{2,1,0:T(8,128)(2,1)S(1)} %bitcast.17, bf16[32,64,256]{2,1,0:T(8,128)(2,1)S(1)} %copy-done.2, ...), custom_call_target="tpu_custom_call" | custom-call | flops 8000000000 | bytes 30000000 | tf_op jit(solution)/shard_map/spectral_1/pallas_call | solution.py:623
  92.3 0.1 collective-permute-start.5
  92.4 2.6 %collective-permute-start.6 = (f32[64,128]{1,0:T(8,128)S(1)}, f32[64,128]{1,0:T(8,128)S(1)}, u32[]{:S(2)}, u32[]{:S(2)}) collective-permute-start(f32[64,128]{1,0:T(8,128)S(1)} %add.57), channel_id=1, source_target_pairs={{0,16},{2,18},{4,20},{6,22},{8,24},{10,26},{12,28},{14,30},{16,0},... | collective-permute-start | bytes 98312 | tf_op jit(solution)/shard_map/ppermute | solution.py:673
  95.0 1.3 collective-permute-done.7.refs_1_
  96.3 4.5 %low_2.1 = (f32[4608,128]{1,0:T(8,128)S(1)}, bf16[64,128,128]{2,1,0:T(8,128)(2,1)S(1)}, bf16[64,128,128]{2,1,0:T(8,128)(2,1)S(1)}) custom-call(bf16[60,64,128]{2,1,0:T(8,128)(2,1)S(1)} %copy-done.9, bf16[60,64,128]{2,1,0:T(8,128)(2,1)} %collective-permute-done.7.refs_1_, bf16[32,128,256]{2,1,0:T(8,128)(2,1)S(1)} %bitcast.18, ...), custom_call_target="tpu_custom_call" | custom-call | flops 8000000000 | bytes 30000000 | tf_op jit(solution)/shard_map/low_2/pallas_call | solution.py:602
  100.8 2.1 %collective-permute-start.8 = (f32[64,128]{1,0:T(8,128)S(1)}, f32[64,128]{1,0:T(8,128)S(1)}, u32[]{:S(2)}, u32[]{:S(2)}) collective-permute-start(f32[64,128]{1,0:T(8,128)S(1)} %add.58), channel_id=1, source_target_pairs={{0,1},{1,0},{2,3},{3,2},{4,5},{5,4},{6,7},{7,6},{8,9},{9,8},{10,11... | collective-permute-start | bytes 98312 | tf_op jit(solution)/shard_map/ppermute | solution.py:673
  103.0 1.5 %collective-permute-start.10 = (f32[64,128]{1,0:T(8,128)S(1)}, f32[64,128]{1,0:T(8,128)S(1)}, u32[]{:S(2)}, u32[]{:S(2)}) collective-permute-start(f32[64,128]{1,0:T(8,128)S(1)} %add.59), channel_id=1, source_target_pairs={{0,4},{2,6},{4,0},{6,2},{8,12},{10,14},{12,8},{14,10},{16,20},{18,... | collective-permute-start | bytes 98312 | tf_op jit(solution)/shard_map/ppermute | solution.py:673
  104.4 2.5 %collective-permute-done.9.refs_1_ = bf16[32,64,128]{2,1,0:T(8,128)(2,1)S(1)} collective-permute-done((bf16[32,64,128]{2,1,0:T(8,128)(2,1)S(1)}, bf16[32,64,128]{2,1,0:T(8,128)(2,1)S(1)}, u32[]{:S(2)}, u32[]{:S(2)}) %collective-permute-start.9) | collective-permute-done | bytes 524320 | tf_op jit(solution)/shard_map/ppermute | solution.py:722
  107.0 9.0 %spectral_2.1 = (f32[64,128]{1,0:T(8,128)S(1)}, f32[64,128]{1,0:T(8,128)S(1)}) custom-call(s32[2]{0:T(128)S(1)} %pad_add_fusion.side, bf16[32,64,128]{2,1,0:T(8,128)(2,1)S(1)} %copy-done.10, bf16[32,64,128]{2,1,0:T(8,128)(2,1)S(1)} %collective-permute-done.9.refs_1_, f32[4608,128]{1,0:T(8,128)S(1)} %get-tuple-element.102.refs_2_, ...), custom_call_target="tpu_custom_call" | custom-call | flops 8000000000 | bytes 30000000 | tf_op jit(solution)/shard_map/spectral_2/pallas_call | solution.py:623
  116.0 0.1 collective-permute-start.11
  116.1 1.2 collective-permute-done.11
  117.3 1.7 %collective-permute-start.12 = (f32[64,128]{1,0:T(8,128)S(1)}, f32[64,128]{1,0:T(8,128)S(1)}, u32[]{:S(2)}, u32[]{:S(2)}) collective-permute-start(f32[64,128]{1,0:T(8,128)S(1)} %add.62), channel_id=1, source_target_pairs={{0,4},{2,6},{4,0},{6,2},{8,12},{10,14},{12,8},{14,10},{16,20},{18,... | collective-permute-start | bytes 98312 | tf_op jit(solution)/shard_map/ppermute | solution.py:673
  119.0 2.2 %collective-permute-done.12 = f32[64,128]{1,0:T(8,128)S(1)} collective-permute-done((f32[64,128]{1,0:T(8,128)S(1)}, f32[64,128]{1,0:T(8,128)S(1)}, u32[]{:S(2)}, u32[]{:S(2)}) %collective-permute-start.12) | collective-permute-done | bytes 32800 | tf_op jit(solution)/shard_map/ppermute | solution.py:673
  121.2 1.9 %collective-permute-start.13 = (f32[128,128]{1,0:T(8,128)S(1)}, f32[128,128]{1,0:T(8,128)S(1)}, u32[]{:S(2)}, u32[]{:S(2)}) collective-permute-start(f32[128,128]{1,0:T(8,128)S(1)} %pad_maximum_fusion.8), channel_id=1, source_target_pairs={{0,8},{2,10},{4,12},{6,14},{8,0},{10,2},{12,4},{14,6},{16,24},{18,... | collective-permute-start | bytes 196616 | tf_op jit(solution)/shard_map/ppermute | solution.py:673
  123.1 2.5 %collective-permute-done.13 = f32[128,128]{1,0:T(8,128)S(1)} collective-permute-done((f32[128,128]{1,0:T(8,128)S(1)}, f32[128,128]{1,0:T(8,128)S(1)}, u32[]{:S(2)}, u32[]{:S(2)}) %collective-permute-start.13) | collective-permute-done | bytes 65568 | tf_op jit(solution)/shard_map/ppermute | solution.py:673
  125.6 2.9 %collective-permute-start.14 = (f32[128,128]{1,0:T(8,128)S(1)}, f32[128,128]{1,0:T(8,128)S(1)}, u32[]{:S(2)}, u32[]{:S(2)}) collective-permute-start(f32[128,128]{1,0:T(8,128)S(1)} %fusion.9), channel_id=1, source_target_pairs={{0,16},{2,18},{4,20},{6,22},{8,24},{10,26},{12,28},{14,30},{16,0},... | collective-permute-start | bytes 196616 | tf_op jit(solution)/shard_map/ppermute | solution.py:673
  128.5 2.4 %collective-permute-done.14 = f32[128,128]{1,0:T(8,128)S(1)} collective-permute-done((f32[128,128]{1,0:T(8,128)S(1)}, f32[128,128]{1,0:T(8,128)S(1)}, u32[]{:S(2)}, u32[]{:S(2)}) %collective-permute-start.14) | collective-permute-done | bytes 65568 | tf_op jit(solution)/shard_map/ppermute | solution.py:673
  130.8 1.8 %collective-permute-start.15 = (f32[128,128]{1,0:T(8,128)S(1)}, f32[128,128]{1,0:T(8,128)S(1)}, u32[]{:S(2)}, u32[]{:S(2)}) collective-permute-start(f32[128,128]{1,0:T(8,128)S(1)} %add.65), channel_id=1, source_target_pairs={{0,1},{1,0},{2,3},{3,2},{4,5},{5,4},{6,7},{7,6},{8,9},{9,8},{10,11... | collective-permute-start | bytes 196616 | tf_op jit(solution)/shard_map/ppermute | solution.py:673
  132.7 2.5 %collective-permute-done.15 = f32[128,128]{1,0:T(8,128)S(1)} collective-permute-done((f32[128,128]{1,0:T(8,128)S(1)}, f32[128,128]{1,0:T(8,128)S(1)}, u32[]{:S(2)}, u32[]{:S(2)}) %collective-permute-start.15) | collective-permute-done | bytes 65568 | tf_op jit(solution)/shard_map/ppermute | solution.py:673
  135.2 0.1 collective-permute-start.16
  135.3 1.3 collective-permute-done.16
  136.6 0.7 multiply_bitcast_fusion
  (51 shorter events, 0.2 us)
Async XLA Ops:
  5.8 37.2 %collective-permute-start.1 = (bf16[92,64,128]{2,1,0:T(8,128)(2,1)}, bf16[92,64,128]{2,1,0:T(8,128)(2,1)}, u32[]{:S(2)}, u32[]{:S(2)}) collective-permute-start(bf16[92,64,128]{2,1,0:T(8,128)(2,1)} %forward_0.1.refs_0_), channel_id=1, source_target_pairs={{0,1},{1,0},{2,3},{3,2},{4,5},{5,4},{6,7},{7,6},{8,9},{9,8},{10,11... | collective-permute-start | bytes 4521992 | tf_op jit(solution)/shard_map/ppermute | solution.py:722
  8.8 3.4 %copy-start.13 = (bf16[64,128,128]{2,1,0:T(8,128)(2,1)S(1)}, bf16[64,128,128]{2,1,0:T(8,128)(2,1)}, u32[]{:S(2)}) copy-start(bf16[64,128,128]{2,1,0:T(8,128)(2,1)} %constant.54.clone) | copy-start | bytes 6291460
  12.2 3.0 %copy-start.14 = (bf16[2,16,64,256]{3,2,1,0:T(8,128)(2,1)S(1)}, bf16[2,16,64,256]{3,2,1,0:T(8,128)(2,1)}, u32[]{:S(2)}) copy-start(bf16[2,16,64,256]{3,2,1,0:T(8,128)(2,1)} %constant.57.clone) | copy-start | bytes 3145732
  28.5 7.3 %copy-start.15 = (bf16[126,192]{0,1:T(8,128)(2,1)S(1)}, bf16[126,192]{0,1:T(8,128)(2,1)}, u32[]{:S(2)}) copy-start(bf16[126,192]{0,1:T(8,128)(2,1)} %param.16) | copy-start | bytes 145156
  28.5 46.8 %collective-permute-start = (bf16[92,64,128]{2,1,0:T(8,128)(2,1)}, bf16[92,64,128]{2,1,0:T(8,128)(2,1)}, u32[]{:S(2)}, u32[]{:S(2)}) collective-permute-start(bf16[92,64,128]{2,1,0:T(8,128)(2,1)} %forward_1.1.refs_0_), channel_id=1, source_target_pairs={{0,1},{1,0},{2,3},{3,2},{4,5},{5,4},{6,7},{7,6},{8,9},{9,8},{10,11... | collective-permute-start | bytes 4521992 | tf_op jit(solution)/shard_map/ppermute | solution.py:722
  33.7 62.6 %collective-permute-start.7 = (bf16[60,64,128]{2,1,0:T(8,128)(2,1)}, bf16[60,64,128]{2,1,0:T(8,128)(2,1)}, u32[]{:S(2)}, u32[]{:S(2)}) collective-permute-start(bf16[60,64,128]{2,1,0:T(8,128)(2,1)} %get-tuple-element.86.refs_0_), channel_id=1, source_target_pairs={{0,1},{1,0},{2,3},{3,2},{4,5},{5,4},{6,7},{7,6},{8,9},{9,8},{10,11... | collective-permute-start | bytes 2949128 | tf_op jit(solution)/shard_map/ppermute | solution.py:722
  36.0 6.9 %copy-start.11 = (bf16[256,252]{1,0:T(8,128)(2,1)S(1)}, bf16[256,252]{1,0:T(8,128)(2,1)}, u32[]{:S(2)}) copy-start(bf16[256,252]{1,0:T(8,128)(2,1)} %constant.52.clone.refs_6_.refs_7_) | copy-start | bytes 387076
  36.0 6.9 %copy-start.12 = (f32[128,128]{1,0:T(8,128)S(1)}, f32[128,128]{1,0:T(8,128)}, u32[]{:S(2)}) copy-start(f32[128,128]{1,0:T(8,128)} %constant.58.clone.refs_10_.refs_11_) | copy-start | bytes 196612
  39.8 3.2 %copy-start = (bf16[92,64,128]{2,1,0:T(8,128)(2,1)S(1)}, bf16[92,64,128]{2,1,0:T(8,128)(2,1)}, u32[]{:S(2)}) copy-start(bf16[92,64,128]{2,1,0:T(8,128)(2,1)} %forward_0.1.refs_0_) | copy-start | bytes 4521988
  39.8 3.2 %copy-start.2 = (bf16[32,64,256]{2,1,0:T(8,128)(2,1)S(1)}, bf16[32,64,256]{2,1,0:T(8,128)(2,1)}, u32[]{:S(2)}) copy-start(bf16[32,64,256]{2,1,0:T(8,128)(2,1)} %pad_maximum_fusion.refs_3_) | copy-start | bytes 3145732
  43.0 1.0 copy-start.3
  44.0 1.0 copy-start.5
  45.1 2.8 %copy-start.7 = (bf16[1,63,252,192]{2,3,1,0:T(8,128)(2,1)S(1)}, bf16[1,63,252,192]{2,3,1,0:T(8,128)(2,1)}, u32[]{:S(2)}) copy-start(bf16[1,63,252,192]{2,3,1,0:T(8,128)(2,1)} %param.15) | copy-start | bytes 18289156
  47.8 15.5 %copy-start.10 = (bf16[32,64,128]{2,1,0:T(8,128)(2,1)S(1)}, bf16[32,64,128]{2,1,0:T(8,128)(2,1)}, u32[]{:S(2)}) copy-start(bf16[32,64,128]{2,1,0:T(8,128)(2,1)} %get-tuple-element.101.refs_0_) | copy-start | bytes 1572868
  47.8 29.6 %copy-start.1 = (bf16[92,64,128]{2,1,0:T(8,128)(2,1)S(1)}, bf16[92,64,128]{2,1,0:T(8,128)(2,1)}, u32[]{:S(2)}) copy-start(bf16[92,64,128]{2,1,0:T(8,128)(2,1)} %forward_1.1.refs_0_) | copy-start | bytes 4521988
  59.9 1.3 collective-permute-start.2
  61.2 3.9 %collective-permute-start.3 = (f32[64,128]{1,0:T(8,128)S(1)}, f32[64,128]{1,0:T(8,128)S(1)}, u32[]{:S(2)}, u32[]{:S(2)}) collective-permute-start(f32[64,128]{1,0:T(8,128)S(1)} %add.55), channel_id=1, source_target_pairs={{0,4},{2,6},{4,0},{6,2},{8,12},{10,14},{12,8},{14,10},{16,20},{18,... | collective-permute-start | bytes 98312 | tf_op jit(solution)/shard_map/ppermute | solution.py:673
  63.4 43.6 %collective-permute-start.9 = (bf16[32,64,128]{2,1,0:T(8,128)(2,1)S(1)}, bf16[32,64,128]{2,1,0:T(8,128)(2,1)S(1)}, u32[]{:S(2)}, u32[]{:S(2)}) collective-permute-start(bf16[32,64,128]{2,1,0:T(8,128)(2,1)S(1)} %copy-done.10), channel_id=1, source_target_pairs={{0,1},{1,0},{2,3},{3,2},{4,5},{5,4},{6,7},{7,6},{8,9},{9,8},{10,11... | collective-permute-start | bytes 1572872 | tf_op jit(solution)/shard_map/ppermute | solution.py:722
  75.3 17.0 %collective-permute-start.4 = (f32[64,128]{1,0:T(8,128)S(1)}, f32[64,128]{1,0:T(8,128)S(1)}, u32[]{:S(2)}, u32[]{:S(2)}) collective-permute-start(f32[64,128]{1,0:T(8,128)S(1)} %add.56), channel_id=1, source_target_pairs={{0,8},{2,10},{4,12},{6,14},{8,0},{10,2},{12,4},{14,6},{16,24},{18,... | collective-permute-start | bytes 98312 | tf_op jit(solution)/shard_map/ppermute | solution.py:673
  77.4 2.8 %copy-start.8 = (bf16[1,63,252,192]{2,3,1,0:T(8,128)(2,1)S(1)}, bf16[1,63,252,192]{2,3,1,0:T(8,128)(2,1)}, u32[]{:S(2)}) copy-start(bf16[1,63,252,192]{2,3,1,0:T(8,128)(2,1)} %param.15) | copy-start | bytes 18289156
  80.1 16.2 %copy-start.9 = (bf16[60,64,128]{2,1,0:T(8,128)(2,1)S(1)}, bf16[60,64,128]{2,1,0:T(8,128)(2,1)}, u32[]{:S(2)}) copy-start(bf16[60,64,128]{2,1,0:T(8,128)(2,1)} %get-tuple-element.86.refs_0_) | copy-start | bytes 2949124
  80.1 26.8 %slice-start = ((s8[6193152]{0:T(1024)(128)(4,1)}), s8[4194304]{0:T(1024)(128)(4,1)S(1)}, s32[]{:S(2)}) async-start(s8[6193152]{0:T(1024)(128)(4,1)} %bitcast.26), calls=%async_computation | async-start | bytes 8388608
  92.3 8.5 %collective-permute-start.5 = (f32[64,128]{1,0:T(8,128)S(1)}, f32[64,128]{1,0:T(8,128)S(1)}, u32[]{:S(2)}, u32[]{:S(2)}) collective-permute-start(f32[64,128]{1,0:T(8,128)S(1)} %get-tuple-element.82), channel_id=1, source_target_pairs={{0,2},{2,0},{4,6},{6,4},{8,10},{10,8},{12,14},{14,12},{16,18},{18,... | collective-permute-start | bytes 98312 | tf_op jit(solution)/shard_map/ppermute | solution.py:745
  92.4 8.4 %collective-permute-start.6 = (f32[64,128]{1,0:T(8,128)S(1)}, f32[64,128]{1,0:T(8,128)S(1)}, u32[]{:S(2)}, u32[]{:S(2)}) collective-permute-start(f32[64,128]{1,0:T(8,128)S(1)} %add.57), channel_id=1, source_target_pairs={{0,16},{2,18},{4,20},{6,22},{8,24},{10,26},{12,28},{14,30},{16,0},... | collective-permute-start | bytes 98312 | tf_op jit(solution)/shard_map/ppermute | solution.py:673
  96.3 10.7 %copy-start.4 = (bf16[16,128,128]{2,1,0:T(8,128)(2,1)S(1)}, bf16[16,128,128]{2,1,0:T(8,128)(2,1)}, u32[]{:S(2)}) copy-start(bf16[16,128,128]{2,1,0:T(8,128)(2,1)} %dynamic-slice_bitcast_fusion.1.refs_8_.refs_9_) | copy-start | bytes 1572868
  96.3 10.7 %copy-start.6 = (bf16[16,64,256]{2,1,0:T(8,128)(2,1)S(1)}, bf16[16,64,256]{2,1,0:T(8,128)(2,1)}, u32[]{:S(2)}) copy-start(bf16[16,64,256]{2,1,0:T(8,128)(2,1)} %dynamic-slice_bitcast_fusion.refs_9_.refs_10_) | copy-start | bytes 1572868
  96.3 10.7 %slice-start.1 = ((s8[6193152]{0:T(1024)(128)(4,1)}), s8[1998848]{0:T(1024)(128)(4,1)S(1)}, s32[]{:S(2)}) async-start(s8[6193152]{0:T(1024)(128)(4,1)} %bitcast.26), calls=%async_computation.1 | async-start | bytes 3997696
  100.8 15.2 %collective-permute-start.8 = (f32[64,128]{1,0:T(8,128)S(1)}, f32[64,128]{1,0:T(8,128)S(1)}, u32[]{:S(2)}, u32[]{:S(2)}) collective-permute-start(f32[64,128]{1,0:T(8,128)S(1)} %add.58), channel_id=1, source_target_pairs={{0,1},{1,0},{2,3},{3,2},{4,5},{5,4},{6,7},{7,6},{8,9},{9,8},{10,11... | collective-permute-start | bytes 98312 | tf_op jit(solution)/shard_map/ppermute | solution.py:673
  103.0 13.1 %collective-permute-start.10 = (f32[64,128]{1,0:T(8,128)S(1)}, f32[64,128]{1,0:T(8,128)S(1)}, u32[]{:S(2)}, u32[]{:S(2)}) collective-permute-start(f32[64,128]{1,0:T(8,128)S(1)} %add.59), channel_id=1, source_target_pairs={{0,4},{2,6},{4,0},{6,2},{8,12},{10,14},{12,8},{14,10},{16,20},{18,... | collective-permute-start | bytes 98312 | tf_op jit(solution)/shard_map/ppermute | solution.py:673
  116.0 1.3 collective-permute-start.11
  117.3 3.9 %collective-permute-start.12 = (f32[64,128]{1,0:T(8,128)S(1)}, f32[64,128]{1,0:T(8,128)S(1)}, u32[]{:S(2)}, u32[]{:S(2)}) collective-permute-start(f32[64,128]{1,0:T(8,128)S(1)} %add.62), channel_id=1, source_target_pairs={{0,4},{2,6},{4,0},{6,2},{8,12},{10,14},{12,8},{14,10},{16,20},{18,... | collective-permute-start | bytes 98312 | tf_op jit(solution)/shard_map/ppermute | solution.py:673
  121.2 4.3 %collective-permute-start.13 = (f32[128,128]{1,0:T(8,128)S(1)}, f32[128,128]{1,0:T(8,128)S(1)}, u32[]{:S(2)}, u32[]{:S(2)}) collective-permute-start(f32[128,128]{1,0:T(8,128)S(1)} %pad_maximum_fusion.8), channel_id=1, source_target_pairs={{0,8},{2,10},{4,12},{6,14},{8,0},{10,2},{12,4},{14,6},{16,24},{18,... | collective-permute-start | bytes 196616 | tf_op jit(solution)/shard_map/ppermute | solution.py:673
  125.6 5.2 %collective-permute-start.14 = (f32[128,128]{1,0:T(8,128)S(1)}, f32[128,128]{1,0:T(8,128)S(1)}, u32[]{:S(2)}, u32[]{:S(2)}) collective-permute-start(f32[128,128]{1,0:T(8,128)S(1)} %fusion.9), channel_id=1, source_target_pairs={{0,16},{2,18},{4,20},{6,22},{8,24},{10,26},{12,28},{14,30},{16,0},... | collective-permute-start | bytes 196616 | tf_op jit(solution)/shard_map/ppermute | solution.py:673
  130.8 4.3 %collective-permute-start.15 = (f32[128,128]{1,0:T(8,128)S(1)}, f32[128,128]{1,0:T(8,128)S(1)}, u32[]{:S(2)}, u32[]{:S(2)}) collective-permute-start(f32[128,128]{1,0:T(8,128)S(1)} %add.65), channel_id=1, source_target_pairs={{0,1},{1,0},{2,3},{3,2},{4,5},{5,4},{6,7},{7,6},{8,9},{9,8},{10,11... | collective-permute-start | bytes 196616 | tf_op jit(solution)/shard_map/ppermute | solution.py:673
  135.2 1.4 collective-permute-start.16
